TPU v7x, 32 devices: a whole 2x2x4 slice. The times are simulated.
32 devices in a mesh: ctx: 4 (over z), fsdp: 8 (over y, x, core).
Axes of the slice: x: 2, y: 2, z: 4, core: 2. Of those that a mesh axis runs over, the one named last changes fastest.
Arguments:
- layer_input: bfloat16 [8, 1280, 2048], P('fsdp', 'ctx'), may hold values from -6 to 6
- grad_output: bfloat16 [8, 1280, 2048], P('fsdp', 'ctx'), may hold values from -6 to 6
- routes: int32 [8, 1280, 6], P('fsdp', 'ctx'), may hold values from 0 to 15, all different within a row
- continuation_prompt: int32 [8, 2], P('fsdp'), may hold values from 0 to 1
- block_order: int32 [8], replicated, may hold values from 0 to 7, each once
- query_weight: bfloat16 [2048, 3072], P('fsdp'), may hold values from -0.125 to 0.125
- latent_down: bfloat16 [2048, 576], P('fsdp'), may hold values from -0.125 to 0.125
- latent_up: bfloat16 [512, 4096], P('fsdp'), may hold values from -0.25 to 0.25
- output_weight: bfloat16 [2048, 2048], P('fsdp'), may hold values from -1 to 1
- router_weight: bfloat16 [2048, 16], P('fsdp'), may hold values from -0.0625 to 0.0625
- shared_gate: bfloat16 [2048, 2816], P('fsdp'), may hold values from -0.125 to 0.125
- shared_up: bfloat16 [2048, 2816], P('fsdp'), may hold values from -0.125 to 0.125
- shared_down: bfloat16 [2816, 2048], P('fsdp'), may hold values from -0.109375 to 0.109375
- attn_gain: bfloat16 [2048], P('fsdp'), may hold values from 0.5 to 1.5
- latent_gain: bfloat16 [512], P('fsdp'), may hold values from 0.5 to 1.5
- ffn_gain: bfloat16 [2048], P('fsdp'), may hold values from 0.5 to 1.5
- expert_gate: bfloat16 [32, 2048, 704], P(('ctx', 'fsdp')), may hold values from -0.125 to 0.125
- expert_up: bfloat16 [32, 2048, 704], P(('ctx', 'fsdp')), may hold values from -0.125 to 0.125
- expert_down: bfloat16 [32, 704, 2048], P(('ctx', 'fsdp')), may hold values from -0.15625 to 0.15625
Outputs:
- layer_output: bfloat16 [8, 1280, 2048], P('fsdp', 'ctx')
- grad_input: bfloat16 [8, 1280, 2048], P('fsdp', 'ctx')
- grad_query_weight: float32 [2048, 3072], P('fsdp')
- grad_latent_down: float32 [2048, 576], P('fsdp')
- grad_latent_up: float32 [512, 4096], P('fsdp')
- grad_output_weight: float32 [2048, 2048], P('fsdp')
- grad_router_weight: float32 [2048, 16], P('fsdp')
- grad_shared_gate: float32 [2048, 2816], P('fsdp')
- grad_shared_up: float32 [2048, 2816], P('fsdp')
- grad_shared_down: float32 [2816, 2048], P('fsdp')
- grad_attn_gain: float32 [2048], P('fsdp')
- grad_latent_gain: float32 [512], P('fsdp')
- grad_ffn_gain: float32 [2048], P('fsdp')
- grad_expert_gate: float32 [32, 2048, 704], P(('ctx', 'fsdp'))
- grad_expert_up: float32 [32, 2048, 704], P(('ctx', 'fsdp'))
- grad_expert_down: float32 [32, 704, 2048], P(('ctx', 'fsdp'))
Inputs may be any that keep to these rules, and one draw needn't show every extreme that they name: `routes`: within a row the 6 experts are distinct. `block_order`: each of the 8 prompt block numbers appears once.
All inputs are finite; a program needn't handle non-finite values.
Results may differ from a plain program's by a relative error of at most 0.023.
Values may be sent and summed in bfloat16 or wider, within the bound.
No kernel may reach another device: no remote copies, remote signals or barrier semaphores. Data moves between devices by JAX's collectives and lax.ppermute only.
A program may use at most 576 MiB of HBM per device.

v0:
```python
import jax
import jax.numpy as jnp
from jax import lax
from jax.sharding import PartitionSpec as P

HEADS = 16
NOPE = 128
ROPE = 64
VDIM = 128
KV_RANK = 512
TOP = 6
PROMPT = 512
PROMPTS = 2
CONT_LEN = 128
CONTS = 2


epsilon = 1e-06
masked_score = -1e30
bfloat = jnp.bfloat16
single = jnp.float32


def matmul(left, right):
    return jnp.dot(left, right, preferred_element_type=single)


def rms_forward(values, gain):
    inverse = lax.rsqrt(jnp.mean(values * values, axis=-1, keepdims=True) + epsilon)
    normal_part = values * inverse
    return (normal_part * gain, normal_part, inverse)


def rms_backward(grad_out, normal_part, inverse, gain):
    grad_normal = grad_out * gain
    grad_gain = jnp.sum(grad_out * normal_part, axis=0)
    grad_in = inverse * (
        grad_normal - normal_part * jnp.mean(grad_normal * normal_part, axis=-1, keepdims=True)
    )
    return (grad_in, grad_gain)


def rotary_tables(positions):
    exponent = jnp.arange(ROPE // 2, dtype=jnp.float32) * (2.0 / ROPE)
    frequency = jnp.exp(-jnp.log(10000.0) * exponent)
    angles = positions[:, None] * frequency[None, :]
    return (jnp.cos(angles), jnp.sin(angles))


def rotate(values, cos_table, sin_table):
    half_width = values.shape[-1] // 2
    first_half = values[..., :half_width]
    second = values[..., half_width:]
    return jnp.concatenate(
        [first_half * cos_table - second * sin_table, second * cos_table + first_half * sin_table],
        axis=-1,
    )


def lookup(table_values, wanted):
    matches = wanted[:, None] == jnp.arange(table_values.shape[0], dtype=jnp.int32)[None, :]
    return jnp.sum(jnp.where(matches, table_values[None, :], 0), axis=1)


def row_layout(device, local_row, block_order, link_table, block_len, cont_dev):
    prompt_rows = PROMPTS * 2 * block_len
    in_prompt = local_row < prompt_rows
    prompt_id = local_row // (2 * block_len)
    half_slot = local_row // block_len % 2
    prompt_pos = lookup(block_order, 2 * device + half_slot) * block_len + local_row % block_len
    cont_index = device * cont_dev + jnp.maximum(local_row - prompt_rows, 0)
    cont_id = jnp.minimum(cont_index // CONT_LEN, CONTS - 1)
    cont_pos = cont_index % CONT_LEN
    sequence = jnp.where(in_prompt, prompt_id, PROMPTS + cont_id)
    position = jnp.where(in_prompt, prompt_pos, cont_pos)
    linked = jnp.where(in_prompt, -1, lookup(link_table, cont_id))
    rotary = jnp.where(in_prompt, prompt_pos, PROMPT + cont_pos)
    return (sequence, position, linked, rotary)


def slot_tables(route_block, experts, capacity):
    flat_routes = route_block.reshape(-1)
    onehot = (flat_routes[:, None] == jnp.arange(experts, dtype=jnp.int32)[None, :]).astype(
        jnp.int32
    )
    slot_rank = jnp.sum((jnp.cumsum(onehot, axis=0, dtype=jnp.int32) - onehot) * onehot, axis=1)
    kept_pairs = slot_rank < capacity
    target = jnp.where(kept_pairs, flat_routes * capacity + slot_rank, experts * capacity)
    pair_count = flat_routes.shape[0]
    slot_owner = (
        jnp.full((experts * capacity + 1,), pair_count, jnp.int32)
        .at[target]
        .set(jnp.arange(pair_count, dtype=jnp.int32))
    )
    return (kept_pairs, target, slot_owner[: experts * capacity])


def silu_grads(grad_act, gate_pre, up_pre):
    sigmoid_gate = jax.nn.sigmoid(gate_pre)
    grad_gate = (grad_act * up_pre * sigmoid_gate * (1.0 + gate_pre * (1.0 - sigmoid_gate))).astype(
        bfloat
    )
    grad_up = (grad_act * gate_pre * sigmoid_gate).astype(bfloat)
    return (grad_gate, grad_up)


def attention_scores(query_nope, query_rope, key_nope, key_rope, allowed, score_scale):
    raw_scores = jnp.einsum(
        "qhd,khd->hqk", query_nope, key_nope, preferred_element_type=single
    ) + jnp.einsum("qhd,kd->hqk", query_rope, key_rope, preferred_element_type=single)
    return jnp.where(allowed[None], raw_scores * score_scale, masked_score)


def local(
    layer_input,
    grad_output,
    routes,
    continuation_prompt,
    block_order,
    query_weight,
    latent_down,
    latent_up,
    output_weight,
    router_weight,
    shared_gate,
    shared_up,
    shared_down,
    attn_gain,
    latent_gain,
    ffn_gain,
    expert_gate,
    expert_up,
    expert_down,
):
    ctx_size = lax.axis_size("ctx")
    device = lax.axis_index("ctx")
    tokens = layer_input.shape[1]
    model_width = layer_input.shape[2]
    experts = router_weight.shape[1]
    group_tok = tokens * ctx_size
    block_len = PROMPT // (2 * ctx_size)
    cont_dev = CONTS * CONT_LEN // ctx_size
    capacity = (5 * tokens * TOP + 4 * experts - 1) // (4 * experts)
    score_scale = (NOPE + ROPE) ** (-0.5)
    (
        full_query,
        full_down,
        full_up,
        full_output,
        full_router,
        full_sh_gate,
        full_sh_up,
        full_sh_down,
        gain_attn,
        gain_latent,
        gain_ffn,
    ) = (
        lax.all_gather(query_weight, "fsdp", axis=0, tiled=True),
        lax.all_gather(latent_down, "fsdp", axis=0, tiled=True),
        lax.all_gather(latent_up, "fsdp", axis=0, tiled=True),
        lax.all_gather(output_weight, "fsdp", axis=0, tiled=True),
        lax.all_gather(router_weight, "fsdp", axis=0, tiled=True),
        lax.all_gather(shared_gate, "fsdp", axis=0, tiled=True),
        lax.all_gather(shared_up, "fsdp", axis=0, tiled=True),
        lax.all_gather(shared_down, "fsdp", axis=0, tiled=True),
        lax.all_gather(attn_gain, "fsdp", axis=0, tiled=True),
        lax.all_gather(latent_gain, "fsdp", axis=0, tiled=True),
        lax.all_gather(ffn_gain, "fsdp", axis=0, tiled=True),
    )
    own_rows = jnp.arange(tokens, dtype=jnp.int32)
    link_table = continuation_prompt[0]
    own_seq, own_pos, own_link, own_rotary = row_layout(
        device, own_rows, block_order, link_table, block_len, cont_dev
    )
    group_rows = jnp.arange(group_tok, dtype=jnp.int32)
    key_seq, key_pos, key_link, key_rotary = row_layout(
        group_rows // tokens, group_rows % tokens, block_order, link_table, block_len, cont_dev
    )
    allowed = (key_seq[None, :] == own_seq[:, None]) & (key_pos[None, :] <= own_pos[:, None]) | (
        key_seq[None, :] == own_link[:, None]
    )
    cos_table, sin_table = rotary_tables(own_rotary.astype(single))
    inputs_full = layer_input[0].astype(single)
    normed, attn_normal, attn_inverse = rms_forward(inputs_full, gain_attn.astype(single))
    normed_low = normed.astype(bfloat)
    query_pre = matmul(normed_low, full_query)
    query_nope = query_pre[:, : HEADS * NOPE].reshape(tokens, HEADS, NOPE).astype(bfloat)
    query_rope = rotate(
        query_pre[:, HEADS * NOPE :].reshape(tokens, HEADS, ROPE),
        cos_table[:, None, :],
        sin_table[:, None, :],
    ).astype(bfloat)
    latent_pre = matmul(normed_low, full_down)
    latent, latent_normal, latent_inverse = rms_forward(
        latent_pre[:, :KV_RANK], gain_latent.astype(single)
    )
    latent_low = latent.astype(bfloat)
    key_rope_own = rotate(latent_pre[:, KV_RANK:], cos_table, sin_table).astype(bfloat)
    latent_group, rope_group = (
        lax.all_gather(latent_low, "ctx", axis=0, tiled=True),
        lax.all_gather(key_rope_own, "ctx", axis=0, tiled=True),
    )
    kv_group = matmul(latent_group, full_up).astype(bfloat)
    key_nope = kv_group[:, : HEADS * NOPE].reshape(group_tok, HEADS, NOPE)
    values = kv_group[:, HEADS * NOPE :].reshape(group_tok, HEADS, VDIM)
    scores = attention_scores(query_nope, query_rope, key_nope, rope_group, allowed, score_scale)
    top_score = jnp.max(scores, axis=2, keepdims=True)
    exps = jnp.exp(scores - top_score)
    row_total = jnp.sum(exps, axis=2, keepdims=True)
    log_total = top_score + jnp.log(row_total)
    probs_low = (exps / row_total).astype(bfloat)
    attended = jnp.einsum("hqk,khd->qhd", probs_low, values, preferred_element_type=single)
    attended_low = attended.reshape(tokens, HEADS * VDIM).astype(bfloat)
    hidden = inputs_full + matmul(attended_low, full_output)
    ffn_in, ffn_normal, ffn_inverse = rms_forward(hidden, gain_ffn.astype(single))
    ffn_low = ffn_in.astype(bfloat)
    logits = matmul(ffn_low, full_router)
    router_exps = jnp.exp(logits - jnp.max(logits, axis=1, keepdims=True))
    router = router_exps / jnp.sum(router_exps, axis=1, keepdims=True)
    route_rows = routes[0]
    route_match = route_rows[:, :, None] == jnp.arange(experts, dtype=jnp.int32)[None, None, :]
    chosen = jnp.sum(jnp.where(route_match, router[:, None, :], 0.0), axis=2)
    chosen_total = jnp.sum(chosen, axis=1, keepdims=True)
    gate_values = chosen / chosen_total
    sh_gate_pre = matmul(ffn_low, full_sh_gate)
    sh_up_pre = matmul(ffn_low, full_sh_up)
    shared_act = (jax.nn.silu(sh_gate_pre) * sh_up_pre).astype(bfloat)
    shared_out = matmul(shared_act, full_sh_down)
    kept_pairs, target, slot_owner = slot_tables(route_rows, experts, capacity)
    source_row = slot_owner // TOP
    padded_in = jnp.concatenate([ffn_low, jnp.zeros((1, model_width), bfloat)], axis=0)
    send_rows = padded_in[source_row].reshape(experts, 1, capacity, model_width)
    send_rows = jnp.broadcast_to(send_rows, (experts, 2, capacity, model_width)).reshape(
        2 * experts, capacity, model_width
    )
    arrived = lax.all_to_all(send_rows, ("ctx", "fsdp"), split_axis=0, concat_axis=0, tiled=True)
    sources = arrived.shape[0]
    slot_count = arrived.shape[1]
    arrived_rows = arrived.reshape(-1, model_width)
    gate_pre = matmul(arrived_rows, expert_gate[0])
    up_pre = matmul(arrived_rows, expert_up[0])
    activation = (jax.nn.silu(gate_pre) * up_pre).astype(bfloat)
    part_low = matmul(activation, expert_down[0]).astype(bfloat)
    part_low, piece_gate, piece_up, piece_rows = (
        part_low.reshape(sources, slot_count, model_width),
        gate_pre.reshape(sources, slot_count, -1),
        up_pre.reshape(sources, slot_count, -1),
        arrived,
    )
    returned = lax.all_to_all(part_low, ("ctx", "fsdp"), split_axis=0, concat_axis=0, tiled=True)
    returned = returned.reshape(experts, 2, capacity, model_width).astype(single)
    expert_out = (returned[:, 0] + returned[:, 1]).reshape(experts * capacity, model_width)
    padded_out = jnp.concatenate([expert_out, jnp.zeros((1, model_width), single)], axis=0)
    pair_out = padded_out[target].reshape(tokens, TOP, model_width)
    kept_float = kept_pairs.reshape(tokens, TOP).astype(single)
    pair_weight = gate_values * kept_float
    routed = jnp.sum(pair_out * pair_weight[:, :, None], axis=1)
    layer_output = (hidden + shared_out + routed).astype(bfloat)
    (
        full_query,
        full_down,
        full_up,
        full_output,
        full_router,
        full_sh_gate,
        full_sh_up,
        full_sh_down,
        gain_attn,
        gain_latent,
        gain_ffn,
    ) = (
        lax.all_gather(query_weight, "fsdp", axis=0, tiled=True),
        lax.all_gather(latent_down, "fsdp", axis=0, tiled=True),
        lax.all_gather(latent_up, "fsdp", axis=0, tiled=True),
        lax.all_gather(output_weight, "fsdp", axis=0, tiled=True),
        lax.all_gather(router_weight, "fsdp", axis=0, tiled=True),
        lax.all_gather(shared_gate, "fsdp", axis=0, tiled=True),
        lax.all_gather(shared_up, "fsdp", axis=0, tiled=True),
        lax.all_gather(shared_down, "fsdp", axis=0, tiled=True),
        lax.all_gather(attn_gain, "fsdp", axis=0, tiled=True),
        lax.all_gather(latent_gain, "fsdp", axis=0, tiled=True),
        lax.all_gather(ffn_gain, "fsdp", axis=0, tiled=True),
    )
    grad_low = grad_output[0]
    grad_top = grad_low.astype(single)
    grad_gate_pair = jnp.sum(pair_out * grad_top[:, None, :], axis=2) * kept_float
    padded_grad = jnp.concatenate([grad_top, jnp.zeros((1, model_width), single)], axis=0)
    padded_weight = jnp.concatenate([pair_weight.reshape(-1), jnp.zeros((1,), single)], axis=0)
    slot_grad = (padded_weight[slot_owner][:, None] * padded_grad[source_row]).astype(bfloat)
    slot_grad = jnp.broadcast_to(
        slot_grad.reshape(experts, 1, capacity, model_width), (experts, 2, capacity, model_width)
    )
    grad_arrived = lax.all_to_all(
        slot_grad.reshape(2 * experts, capacity, model_width),
        ("ctx", "fsdp"),
        split_axis=0,
        concat_axis=0,
        tiled=True,
    )
    grad_rows = grad_arrived.reshape(-1, model_width)
    gate_flat = piece_gate.reshape(grad_rows.shape[0], -1)
    up_flat = piece_up.reshape(grad_rows.shape[0], -1)
    rows_flat = piece_rows.reshape(-1, model_width)
    activation_low = (jax.nn.silu(gate_flat) * up_flat).astype(bfloat)
    grad_piece_down = jnp.einsum(
        "rf,rd->fd", activation_low, grad_rows, preferred_element_type=single
    )
    grad_act = jnp.einsum("rd,fd->rf", grad_rows, expert_down[0], preferred_element_type=single)
    grad_gate_low, grad_up_low = silu_grads(grad_act, gate_flat, up_flat)
    grad_piece_gate = jnp.einsum(
        "rd,rf->df", rows_flat, grad_gate_low, preferred_element_type=single
    )
    grad_piece_up = jnp.einsum("rd,rf->df", rows_flat, grad_up_low, preferred_element_type=single)
    grad_back = jnp.einsum(
        "rf,df->rd", grad_gate_low, expert_gate[0], preferred_element_type=single
    ) + jnp.einsum("rf,df->rd", grad_up_low, expert_up[0], preferred_element_type=single)
    grad_back = grad_back.astype(bfloat).reshape(grad_arrived.shape)
    grad_returned = lax.all_to_all(
        grad_back, ("ctx", "fsdp"), split_axis=0, concat_axis=0, tiled=True
    )
    grad_returned = grad_returned.reshape(experts, 2, capacity, model_width).astype(single)
    slot_in_grad = (grad_returned[:, 0] + grad_returned[:, 1]).reshape(
        experts * capacity, model_width
    )
    grad_ffn = (
        jnp.zeros((tokens + 1, model_width), single).at[source_row].add(slot_in_grad)[:tokens]
    )
    grad_chosen = (
        grad_gate_pair - jnp.sum(grad_gate_pair * gate_values, axis=1, keepdims=True)
    ) / chosen_total
    grad_router = jnp.sum(jnp.where(route_match, grad_chosen[:, :, None], 0.0), axis=1)
    grad_logits = (
        router * (grad_router - jnp.sum(router * grad_router, axis=1, keepdims=True))
    ).astype(bfloat)
    grad_w_router = jnp.einsum("td,te->de", ffn_low, grad_logits, preferred_element_type=single)
    grad_ffn = grad_ffn + jnp.einsum(
        "te,de->td", grad_logits, full_router, preferred_element_type=single
    )
    grad_w_sh_down = jnp.einsum("tf,td->fd", shared_act, grad_low, preferred_element_type=single)
    grad_sh_act = jnp.einsum("td,fd->tf", grad_low, full_sh_down, preferred_element_type=single)
    grad_sh_gate, grad_sh_up = silu_grads(grad_sh_act, sh_gate_pre, sh_up_pre)
    grad_w_sh_gate = jnp.einsum("td,tf->df", ffn_low, grad_sh_gate, preferred_element_type=single)
    grad_w_sh_up = jnp.einsum("td,tf->df", ffn_low, grad_sh_up, preferred_element_type=single)
    grad_ffn = (
        grad_ffn
        + jnp.einsum("tf,df->td", grad_sh_gate, full_sh_gate, preferred_element_type=single)
        + jnp.einsum("tf,df->td", grad_sh_up, full_sh_up, preferred_element_type=single)
    )
    grad_hidden_norm, grad_gain_ffn = rms_backward(
        grad_ffn, ffn_normal, ffn_inverse, gain_ffn.astype(single)
    )
    grad_hidden = grad_top + grad_hidden_norm
    grad_attn_low = grad_hidden.astype(bfloat)
    grad_w_output = jnp.einsum(
        "tv,td->vd", attended_low, grad_attn_low, preferred_element_type=single
    )
    grad_attended = (
        jnp.einsum("td,vd->tv", grad_attn_low, full_output, preferred_element_type=single)
        .astype(bfloat)
        .reshape(tokens, HEADS, VDIM)
    )
    scores_again = attention_scores(
        query_nope, query_rope, key_nope, rope_group, allowed, score_scale
    )
    probs_again = jnp.exp(scores_again - log_total)
    grad_probs = jnp.einsum("qhd,khd->hqk", grad_attended, values, preferred_element_type=single)
    row_delta = jnp.sum(probs_again * grad_probs, axis=2, keepdims=True)
    grad_scores = (probs_again * (grad_probs - row_delta)).astype(bfloat)
    grad_query_nope = (
        jnp.einsum("hqk,khd->qhd", grad_scores, key_nope, preferred_element_type=single)
        * score_scale
    )
    grad_query_rope = (
        jnp.einsum("hqk,kd->qhd", grad_scores, rope_group, preferred_element_type=single)
        * score_scale
    )
    grad_key_nope = (
        jnp.einsum("hqk,qhd->khd", grad_scores, query_nope, preferred_element_type=single)
        * score_scale
    )
    grad_key_rope = (
        jnp.einsum("hqk,qhd->kd", grad_scores, query_rope, preferred_element_type=single)
        * score_scale
    )
    grad_values = jnp.einsum(
        "hqk,qhd->khd", probs_low, grad_attended, preferred_element_type=single
    )
    grad_kv_part = jnp.concatenate(
        [grad_key_nope.reshape(group_tok, -1), grad_values.reshape(group_tok, -1)], axis=1
    )
    grad_kv_block = grad_kv_part.astype(bfloat)
    grad_w_up = jnp.einsum("tc,tk->ck", latent_group, grad_kv_block, preferred_element_type=single)
    grad_latent_group = jnp.einsum(
        "tk,ck->tc", grad_kv_block, full_up, preferred_element_type=single
    )
    grad_latent, grad_rope_own = (
        lax.psum_scatter(
            grad_latent_group.astype(jnp.bfloat16), "ctx", scatter_dimension=0, tiled=True
        ).astype(jnp.float32),
        lax.psum_scatter(
            grad_key_rope.astype(jnp.bfloat16), "ctx", scatter_dimension=0, tiled=True
        ).astype(jnp.float32),
    )
    grad_latent_in, grad_gain_latent = rms_backward(
        grad_latent, latent_normal, latent_inverse, gain_latent.astype(single)
    )
    grad_rope_in = rotate(grad_rope_own, cos_table, -sin_table)
    grad_latent_pre = jnp.concatenate([grad_latent_in, grad_rope_in], axis=1).astype(bfloat)
    grad_rope_query = rotate(grad_query_rope, cos_table[:, None, :], -sin_table[:, None, :])
    grad_query_pre = jnp.concatenate(
        [grad_query_nope.reshape(tokens, -1), grad_rope_query.reshape(tokens, -1)], axis=1
    ).astype(bfloat)
    grad_w_query = jnp.einsum(
        "td,tq->dq", normed_low, grad_query_pre, preferred_element_type=single
    )
    grad_w_down = jnp.einsum(
        "td,tk->dk", normed_low, grad_latent_pre, preferred_element_type=single
    )
    grad_normed = jnp.einsum(
        "tq,dq->td", grad_query_pre, full_query, preferred_element_type=single
    ) + jnp.einsum("tk,dk->td", grad_latent_pre, full_down, preferred_element_type=single)
    grad_x_norm, grad_gain_attn = rms_backward(
        grad_normed, attn_normal, attn_inverse, gain_attn.astype(single)
    )
    grad_input = (grad_hidden + grad_x_norm).astype(bfloat)
    reduced = (
        lax.psum_scatter(
            grad_w_query.astype(jnp.bfloat16), "fsdp", scatter_dimension=0, tiled=True
        ).astype(jnp.float32),
        lax.psum_scatter(
            grad_w_down.astype(jnp.bfloat16), "fsdp", scatter_dimension=0, tiled=True
        ).astype(jnp.float32),
        lax.psum_scatter(
            grad_w_up.astype(jnp.bfloat16), "fsdp", scatter_dimension=0, tiled=True
        ).astype(jnp.float32),
        lax.psum_scatter(
            grad_w_output.astype(jnp.bfloat16), "fsdp", scatter_dimension=0, tiled=True
        ).astype(jnp.float32),
        lax.psum_scatter(
            grad_w_router.astype(jnp.bfloat16), "fsdp", scatter_dimension=0, tiled=True
        ).astype(jnp.float32),
        lax.psum_scatter(
            grad_w_sh_gate.astype(jnp.bfloat16), "fsdp", scatter_dimension=0, tiled=True
        ).astype(jnp.float32),
        lax.psum_scatter(
            grad_w_sh_up.astype(jnp.bfloat16), "fsdp", scatter_dimension=0, tiled=True
        ).astype(jnp.float32),
        lax.psum_scatter(
            grad_w_sh_down.astype(jnp.bfloat16), "fsdp", scatter_dimension=0, tiled=True
        ).astype(jnp.float32),
        lax.psum_scatter(
            grad_gain_attn.astype(jnp.bfloat16), "fsdp", scatter_dimension=0, tiled=True
        ).astype(jnp.float32),
        lax.psum_scatter(
            grad_gain_latent.astype(jnp.bfloat16), "fsdp", scatter_dimension=0, tiled=True
        ).astype(jnp.float32),
        lax.psum_scatter(
            grad_gain_ffn.astype(jnp.bfloat16), "fsdp", scatter_dimension=0, tiled=True
        ).astype(jnp.float32),
    )
    summed = (
        lax.psum(reduced[0].astype(jnp.bfloat16), "ctx").astype(jnp.float32),
        lax.psum(reduced[1].astype(jnp.bfloat16), "ctx").astype(jnp.float32),
        lax.psum(reduced[2].astype(jnp.bfloat16), "ctx").astype(jnp.float32),
        lax.psum(reduced[3].astype(jnp.bfloat16), "ctx").astype(jnp.float32),
        lax.psum(reduced[4].astype(jnp.bfloat16), "ctx").astype(jnp.float32),
        lax.psum(reduced[5].astype(jnp.bfloat16), "ctx").astype(jnp.float32),
        lax.psum(reduced[6].astype(jnp.bfloat16), "ctx").astype(jnp.float32),
        lax.psum(reduced[7].astype(jnp.bfloat16), "ctx").astype(jnp.float32),
        lax.psum(reduced[8].astype(jnp.bfloat16), "ctx").astype(jnp.float32),
        lax.psum(reduced[9].astype(jnp.bfloat16), "ctx").astype(jnp.float32),
        lax.psum(reduced[10].astype(jnp.bfloat16), "ctx").astype(jnp.float32),
    )
    return (
        layer_output[None],
        grad_input[None],
        summed[0],
        summed[1],
        summed[2],
        summed[3],
        summed[4],
        summed[5],
        summed[6],
        summed[7],
        summed[8],
        summed[9],
        summed[10],
        grad_piece_gate[None],
        grad_piece_up[None],
        grad_piece_down[None],
    )


def solution(mesh):
    in_specs = (
        P("fsdp", "ctx", None),
        P("fsdp", "ctx", None),
        P("fsdp", "ctx", None),
        P("fsdp", None),
        P(),
        P("fsdp", None),
        P("fsdp", None),
        P("fsdp", None),
        P("fsdp", None),
        P("fsdp", None),
        P("fsdp", None),
        P("fsdp", None),
        P("fsdp", None),
        P("fsdp"),
        P("fsdp"),
        P("fsdp"),
        P(("ctx", "fsdp"), None, None),
        P(("ctx", "fsdp"), None, None),
        P(("ctx", "fsdp"), None, None),
    )
    out_specs = (
        P("fsdp", "ctx", None),
        P("fsdp", "ctx", None),
        P("fsdp", None),
        P("fsdp", None),
        P("fsdp", None),
        P("fsdp", None),
        P("fsdp", None),
        P("fsdp", None),
        P("fsdp", None),
        P("fsdp", None),
        P("fsdp"),
        P("fsdp"),
        P("fsdp"),
        P(("ctx", "fsdp"), None, None),
        P(("ctx", "fsdp"), None, None),
        P(("ctx", "fsdp"), None, None),
    )
    return jax.shard_map(local, mesh=mesh, in_specs=in_specs, out_specs=out_specs, check_vma=False)
```

profile of v0, /device:TPU:0, one launch (start us, length us, event | category | flops | bytes accessed | tf_op | source)
XLA Modules:
  0.0 3333.2 jit_solution(12885630473728473899)
XLA Ops:
  11.6 15.3 all-reduce.3
  83.2 13.7 all-gather.1
  99.0 18.7 all-gather.16.cloned.1.call-done
  117.6 10.9 convolution_convert_fusion.1
  128.5 13.4 slice_bitcast_fusion.2
  141.9 49.6 %all-gather.18.cloned.1.call-done = bf16[2048,3072]{1,0:T(8,128)(2,1)} async-done(((bf16[256,3072]{1,0:T(8,128)(2,1)}), bf16[2048,3072]{1,0:T(8,128)(2,1)}) %all-gather.18.cloned.1.call-update) | async-done | bytes 12582928 | tf_op jit(solution)/shard_map/all_gather | solution.py:158
  207.1 10.6 fusion.88
  217.8 19.4 fusion.172
  282.2 21.5 gather_fusion
  312.4 12.9 broadcast_in_dim.119
  334.9 21.0 gather_fusion.3
  355.9 20.8 gather.18
  376.8 93.9 %all_gather.62 = bf16[2048,16]{0,1:T(8,128)(2,1)S(1)} all-gather(bf16[256,16]{0,1:T(8,128)(2,1)S(1)} %copy-done.91), channel_id=1, replica_groups=mesh['ctx'=4,'fsdp'=8] {'fsdp'}, dimensions={0}, use_global_device_ids=true | all-gather | bytes 73728 | tf_op jit(solution)/shard_map/all_gather | solution.py:162
  474.7 13.0 gather_fusion.2
  487.8 11.8 multiply_convert_fusion.1
  499.6 273.8 %all-to-all-done = bf16[32,150,2048]{2,1,0:T(8,128)(2,1)} async-done(((bf16[32,150,2048]{2,1,0:T(8,128)(2,1)}), bf16[32,150,2048]{2,1,0:T(8,128)(2,1)}, u32[]{:S(2)}, u32[]{:S(2)}) %all-to-all-start) | async-done | bytes 19660832 | tf_op jit(solution)/shard_map/all_to_all | solution.py:236
  773.4 12.9 broadcast_in_dim.194
  790.4 17.1 reshape.707
  807.5 22.8 fusion.27
  830.3 17.4 fusion.31
  847.7 386.2 %all-to-all-done.2 = bf16[32,150,2048]{2,1,0:T(8,128)(2,1)} async-done(((bf16[32,150,2048]{2,1,0:T(8,128)(2,1)}), bf16[32,150,2048]{2,1,0:T(8,128)(2,1)}, u32[]{:S(2)}, u32[]{:S(2)}) %all-to-all-start.2) | async-done | bytes 19660832 | tf_op jit(solution)/shard_map/all_to_all | solution.py:293
  1233.8 17.0 reshape.711
  1250.8 39.8 %multiply_convert_fusion.2 = (bf16[4800,704]{0,1:T(8,128)(2,1)}, bf16[4800,704]{0,1:T(8,128)(2,1)}, bf16[4800,704]{0,1:T(8,128)(2,1)}) fusion(f32[4800,704]{0,1:T(8,128)} %fusion.31, f32[4800,704]{0,1:T(8,128)} %fusion.27, bf16[4800,2048]{1,0:T(8,128)(2,1)} %reshape.711, bf16[1,704,2048]{2,1,0:T(8,128)(2,1)S(1)} %copy-done), kind=kOutput, calls=%fused_computation.25 | convolution fusion | flops 13895270400 | bytes 69853184 | tf_op jit(solution)/shard_map/rd,fd->rf/dot_general | solution.py:308
  1290.6 21.4 convolution_convert_fusion
  1312.0 17.1 reshape.708
  1334.6 23.9 fusion.29
  1358.5 28.1 add_convert_fusion
  1386.7 17.0 reshape.712
  1403.7 382.9 %all-to-all-done.1 = bf16[32,150,2048]{2,1,0:T(8,128)(2,1)} async-done(((bf16[32,150,2048]{2,1,0:T(8,128)(2,1)}), bf16[32,150,2048]{2,1,0:T(8,128)(2,1)}, u32[]{:S(2)}, u32[]{:S(2)}) %all-to-all-start.1) | async-done | bytes 19660832 | tf_op jit(solution)/shard_map/all_to_all | solution.py:250
  1810.7 203.5 %all-gather.22.cloned.1.call-done = bf16[2048,2816]{1,0:T(8,128)(2,1)} async-done(((bf16[256,2816]{1,0:T(8,128)(2,1)}), bf16[2048,2816]{1,0:T(8,128)(2,1)}) %all-gather.22.cloned.1.call-update) | async-done | bytes 11534352 | tf_op jit(solution)/shard_map/all_gather | solution.py:163
  2014.2 11.8 multiply_convert_fusion.7
  2040.0 21.3 convert.64
  2061.3 20.9 fusion.3
  2082.1 20.8 add.478
  2102.9 15.5 concatenate.39
  2118.4 22.4 gather_fusion.1
  2140.8 17.9 reshape.709
  2158.8 14.3 multiply_reduce_fusion.1
  2173.4 70.1 %all-to-all-done.3 = bf16[32,150,2048]{2,1,0:T(8,128)(2,1)} async-done(((bf16[32,150,2048]{2,1,0:T(8,128)(2,1)}), bf16[32,150,2048]{2,1,0:T(8,128)(2,1)}, u32[]{:S(2)}, u32[]{:S(2)}) %all-to-all-start.3) | async-done | bytes 19660832 | tf_op jit(solution)/shard_map/all_to_all | solution.py:318
  2243.5 21.4 convert.65
  2264.8 20.8 slice_add_fusion
  2285.7 20.8 reshape.765
  2306.4 35.6 %scatter_custom_fusion.1 = f32[321,2048]{1,0:T(8,128)} fusion(s32[2400]{0:T(1024)} %copy-done.72, f32[2400,2048]{1,0:T(8,128)} %reshape.765, f32[]{:T(128)} %constant.183.clone.1), kind=kCustom, calls=%fused_computation.114 | custom fusion | flops 4915200 | bytes 2630144 | tf_op jit(solution)/shard_map/scatter-add | solution.py:326
  2361.6 18.7 multiply_reduce_fusion
  2380.3 17.3 multiply_convert_fusion
  2410.5 10.6 fusion.22
  2421.2 10.7 convolution_convert_fusion.4
  2433.2 10.4 convolution_convert_fusion.2
  2443.7 10.4 convolution_convert_fusion.3
  2466.7 13.9 fusion.6
  2490.7 10.0 fusion.56
  2510.4 11.4 convolution_convert_fusion.5
  2523.2 20.4 convolution_bitcast_fusion.2
  2544.8 20.5 convolution_bitcast_fusion
  2565.3 72.7 %reduce-scatter.29.cloned.1.call-done = bf16[352,2048]{1,0:T(8,128)(2,1)} async-done(((bf16[2816,2048]{1,0:T(8,128)(2,1)}), bf16[352,2048]{1,0:T(8,128)(2,1)}) %reduce-scatter.29.cloned.1.call-update) | async-done | bytes 1441808 | tf_op jit(solution)/shard_map/reduce_scatter | solution.py:448
  2638.0 90.3 %reduce-scatter.27.cloned.1.call-done = bf16[256,2816]{1,0:T(8,128)(2,1)} async-done(((bf16[2048,2816]{1,0:T(8,128)(2,1)}), bf16[256,2816]{1,0:T(8,128)(2,1)}) %reduce-scatter.27.cloned.1.call-update) | async-done | bytes 1441808 | tf_op jit(solution)/shard_map/reduce_scatter | solution.py:445
  2728.3 46.3 %reduce-scatter.17.cloned.1.call-done = bf16[256,576]{0,1:T(8,128)(2,1)} async-done(((bf16[2048,576]{0,1:T(8,128)(2,1)}), bf16[256,576]{0,1:T(8,128)(2,1)}) %reduce-scatter.17.cloned.1.call-update) | async-done | bytes 294928 | tf_op jit(solution)/shard_map/reduce_scatter | solution.py:430
  2774.6 54.9 %reduce-scatter.19.cloned.1.call-done = bf16[64,4096]{1,0:T(8,128)(2,1)} async-done(((bf16[512,4096]{1,0:T(8,128)(2,1)}), bf16[64,4096]{1,0:T(8,128)(2,1)}) %reduce-scatter.19.cloned.1.call-update) | async-done | bytes 524304 | tf_op jit(solution)/shard_map/reduce_scatter | solution.py:433
  2829.5 74.6 %reduce-scatter.21.cloned.1.call-done = bf16[256,2048]{1,0:T(8,128)(2,1)} async-done(((bf16[2048,2048]{1,0:T(8,128)(2,1)}), bf16[256,2048]{1,0:T(8,128)(2,1)}) %reduce-scatter.21.cloned.1.call-update) | async-done | bytes 1048592 | tf_op jit(solution)/shard_map/reduce_scatter | solution.py:436
  2904.1 96.2 %reduce-scatter.15.cloned.1.call-done = bf16[256,3072]{1,0:T(8,128)(2,1)} async-done(((bf16[2048,3072]{1,0:T(8,128)(2,1)}), bf16[256,3072]{1,0:T(8,128)(2,1)}) %reduce-scatter.15.cloned.1.call-update) | async-done | bytes 1572880 | tf_op jit(solution)/shard_map/reduce_scatter | solution.py:427
  3000.4 20.5 convolution_bitcast_fusion.1
  3041.1 13.7 all-reduce.7
  3055.0 13.2 all-reduce.8
  3074.5 237.3 %all-reduce.12.cloned.1.call-done = (bf16[256,3072]{1,0:T(8,128)(2,1)}, bf16[256,576]{0,1:T(8,128)(2,1)}, bf16[64,4096]{1,0:T(8,128)(2,1)}, bf16[256,2048]{1,0:T...) async-done(((bf16[256,3072]{1,0:T(8,128)(2,1)}, bf16[256,576]{0,1:T(8,128)(2,1)}, bf16[64,4096]{1,0:T(8,128)(2,1)}, ...) | async-done | bytes 7766032 | tf_op jit(solution)/shard_map/psum | solution.py:462
  (423 shorter events, 300.5 us)
Async XLA Ops:
  7.2 1243.6 %copy-start = (bf16[1,704,2048]{2,1,0:T(8,128)(2,1)S(1)}, bf16[1,704,2048]{2,1,0:T(8,128)(2,1)}, u32[]{:S(2)}) copy-start(bf16[1,704,2048]{2,1,0:T(8,128)(2,1)} %param.37) | copy-start | bytes 8650756
  7.2 34.8 %all-gather.12.cloned.1.call-start = ((), (), s32[]{:S(2)}) async-start(), calls=%async_computation.14 | async-start | bytes 2654208 | tf_op jit(solution)/shard_map/all_gather | solution.py:159
  7.9 91.0 %all-gather.14.cloned.1.call-start = ((), (), s32[]{:S(2)}) async-start(), calls=%async_computation.15 | async-start | bytes 1638400 | tf_op jit(solution)/shard_map/all_gather | solution.py:200
  26.8 18.8 copy-start.76
  45.5 21.8 copy-start.104
  47.1 70.5 %all-gather.16.cloned.1.call-start = ((), (), s32[]{:S(2)}) async-start(), calls=%async_computation.16 | async-start | bytes 4718592 | tf_op jit(solution)/shard_map/all_gather | solution.py:160
  47.9 143.7 %all-gather.18.cloned.1.call-start = ((), (), s32[]{:S(2)}) async-start(), calls=%async_computation.17 | async-start | bytes 14155776 | tf_op jit(solution)/shard_map/all_gather | solution.py:158
  48.4 222.7 %all-gather.20.cloned.1.call-start = ((), (), s32[]{:S(2)}) async-start(), calls=%async_computation.18 | async-start | bytes 9437184 | tf_op jit(solution)/shard_map/all_gather | solution.py:161
  67.4 12.4 copy-start.72
  83.2 122.1 %copy-start.40 = (f32[320,32]{0,1:T(8,128)}, f32[320,32]{0,1:T(8,128)S(1)}, u32[]{:S(2)}) copy-start(f32[320,32]{0,1:T(8,128)S(1)} %get-tuple-element.63) | copy-start | bytes 122884
  98.9 108.2 %copy-start.28 = (bf16[1280,64,1]{0,1,2:T(8,128)(2,1)}, bf16[1280,64,1]{0,1,2:T(8,128)(2,1)S(1)}, u32[]{:S(2)}) copy-start(bf16[1280,64,1]{0,1,2:T(8,128)(2,1)S(1)} %reshape.786) | copy-start | bytes 491524
  128.5 63.1 %copy-start.87 = (f32[8,1,256]{2,1,0:T(1,128)S(1)}, f32[8,1,256]{2,1,0:T(1,128)}, u32[]{:S(2)}) copy-start(f32[8,1,256]{2,1,0:T(1,128)} %copy-done.86) | copy-start | bytes 24580
  128.5 63.1 %copy-start.94 = (f32[320]{0:T(512)S(1)}, f32[320]{0:T(512)}, u32[]{:S(2)}) copy-start(f32[320]{0:T(512)} %copy-done.93) | copy-start | bytes 3844
  205.3 12.4 slice-start.4
  237.2 16.3 copy-start.2
  237.2 24.5 slice-start.6
  325.3 448.1 %all-to-all-start = ((bf16[32,150,2048]{2,1,0:T(8,128)(2,1)}), bf16[32,150,2048]{2,1,0:T(8,128)(2,1)}, u32[]{:S(2)}, u32[]{:S(2)}) async-start(bf16[32,150,2048]{2,1,0:T(8,128)(2,1)} %bitcast.235), calls=%async_computation | async-start | bytes 39845888 | tf_op jit(solution)/shard_map/all_to_all | solution.py:236
  330.0 143.1 %copy-start.55 = (s32[1,320,6]{1,2,0:T(8,128)}, s32[1,320,6]{1,2,0:T(8,128)S(1)}, u32[]{:S(2)}) copy-start(s32[1,320,6]{1,2,0:T(8,128)S(1)} %copy.291) | copy-start | bytes 23044
  355.9 20.8 copy-start.91
  355.9 118.1 %copy-start.66 = (s32[1920]{0:T(1024)S(1)}, s32[1920]{0:T(1024)}, u32[]{:S(2)}) copy-start(s32[1920]{0:T(1024)} %copy-done.65) | copy-start | bytes 23044
  355.9 118.7 %copy-start.75 = (s32[3072]{0:T(1024)S(1)}, s32[3072]{0:T(1024)}, u32[]{:S(2)}) copy-start(s32[3072]{0:T(1024)} %get-tuple-element.84) | copy-start | bytes 36868
  786.3 447.5 %all-to-all-start.2 = ((bf16[32,150,2048]{2,1,0:T(8,128)(2,1)}), bf16[32,150,2048]{2,1,0:T(8,128)(2,1)}, u32[]{:S(2)}, u32[]{:S(2)}) async-start(bf16[32,150,2048]{2,1,0:T(8,128)(2,1)} %bitcast.236), calls=%async_computation.2 | async-start | bytes 39845888 | tf_op jit(solution)/shard_map/all_to_all | solution.py:293
  807.5 22.8 copy-start.14
  807.5 22.8 copy-start.101
  1329.1 457.5 %all-to-all-start.1 = ((bf16[32,150,2048]{2,1,0:T(8,128)(2,1)}), bf16[32,150,2048]{2,1,0:T(8,128)(2,1)}, u32[]{:S(2)}, u32[]{:S(2)}) async-start(bf16[32,150,2048]{2,1,0:T(8,128)(2,1)} %reshape.708), calls=%async_computation.1 | async-start | bytes 39845888 | tf_op jit(solution)/shard_map/all_to_all | solution.py:250
  1333.3 458.2 %all-gather.26.cloned.1.call-start = ((), (), s32[]{:S(2)}) async-start(), calls=%async_computation.21 | async-start | bytes 12976128 | tf_op jit(solution)/shard_map/all_gather | solution.py:165
  1333.9 467.7 %all-gather.24.cloned.1.call-start = ((), (), s32[]{:S(2)}) async-start(), calls=%async_computation.20 | async-start | bytes 12976128 | tf_op jit(solution)/shard_map/all_gather | solution.py:164
  1403.7 387.7 %copy-start.83 = (s32[1920]{0:T(1024)S(1)}, s32[1920]{0:T(1024)}, u32[]{:S(2)}) copy-start(s32[1920]{0:T(1024)} %copy-done.82) | copy-start | bytes 23044
  1403.7 387.8 %copy-start.19 = (bf16[1,320,2048]{2,1,0:T(8,128)(2,1)S(1)}, bf16[1,320,2048]{2,1,0:T(8,128)(2,1)}, u32[]{:S(2)}) copy-start(bf16[1,320,2048]{2,1,0:T(8,128)(2,1)} %param.20) | copy-start | bytes 3932164
  1786.6 456.9 %all-to-all-start.3 = ((bf16[32,150,2048]{2,1,0:T(8,128)(2,1)}), bf16[32,150,2048]{2,1,0:T(8,128)(2,1)}, u32[]{:S(2)}, u32[]{:S(2)}) async-start(bf16[32,150,2048]{2,1,0:T(8,128)(2,1)} %reshape.712), calls=%async_computation.3 | async-start | bytes 39845888 | tf_op jit(solution)/shard_map/all_to_all | solution.py:318
  1790.6 223.6 %all-gather.22.cloned.1.call-start = ((), (), s32[]{:S(2)}) async-start(), calls=%async_computation.19 | async-start | bytes 12976128 | tf_op jit(solution)/shard_map/all_gather | solution.py:163
  1791.3 662.9 %reduce-scatter.31.cloned.1.call-start = ((), (), s32[]{:S(2)}) async-start(), calls=%async_computation.31 | async-start | bytes 409600
  2014.2 11.8 copy-start.100
  2140.8 17.9 copy-start.10
  2158.7 14.4 copy-start.50
  2158.7 14.4 copy-start.71
  2158.7 14.4 copy-start.74
  2158.7 14.5 copy-start.56
  2158.8 14.5 copy-start.37
  2158.8 14.5 copy-start.68
  2158.8 14.5 copy-start.81
  2173.4 168.7 %copy-start.57 = (bf16[320,16]{0,1:T(8,128)(2,1)}, bf16[320,16]{0,1:T(8,128)(2,1)S(1)}, u32[]{:S(2)}) copy-start(bf16[320,16]{0,1:T(8,128)(2,1)S(1)} %multiply_convert_fusion.12) | copy-start | bytes 30724
  2285.7 56.4 %copy-start.39 = (bf16[2048,16]{0,1:T(8,128)(2,1)S(1)}, bf16[2048,16]{0,1:T(8,128)(2,1)}, u32[]{:S(2)}) copy-start(bf16[2048,16]{0,1:T(8,128)(2,1)} %copy-done.38) | copy-start | bytes 196612
  2285.7 56.4 %copy-start.53 = (f32[8,1,256]{2,1,0:T(1,128)S(1)}, f32[8,1,256]{2,1,0:T(1,128)}, u32[]{:S(2)}) copy-start(f32[8,1,256]{2,1,0:T(1,128)} %convert_element_type.302) | copy-start | bytes 24580
  2285.7 56.4 %copy-start.85 = (f32[320]{0:T(512)S(1)}, f32[320]{0:T(512)}, u32[]{:S(2)}) copy-start(f32[320]{0:T(512)} %copy-done.84) | copy-start | bytes 3844
  2306.4 35.6 %copy-start.7 = (f32[320,2048]{1,0:T(8,128)S(1)}, f32[320,2048]{1,0:T(8,128)}, u32[]{:S(2)}) copy-start(f32[320,2048]{1,0:T(8,128)} %copy-done.6) | copy-start | bytes 7864324
  2380.3 17.3 copy-start.24
  2380.3 17.3 copy-start.26
  2410.4 48.3 %reduce-scatter.13.cloned.1.call-start = ((), (), s32[]{:S(2)}) async-start(), calls=%async_computation.22 | async-start | bytes 1638400 | tf_op jit(solution)/shard_map/reduce_scatter | solution.py:397
  2421.2 144.1 %reduce-scatter.25.cloned.1.call-start = ((), (), s32[]{:S(2)}) async-start(), calls=%async_computation.28 | async-start | bytes 12976128 | tf_op jit(solution)/shard_map/reduce_scatter | solution.py:442
  2432.0 206.1 %reduce-scatter.29.cloned.1.call-start = ((), (), s32[]{:S(2)}) async-start(), calls=%async_computation.30 | async-start | bytes 12976128 | tf_op jit(solution)/shard_map/reduce_scatter | solution.py:448
  2443.7 284.7 %reduce-scatter.27.cloned.1.call-start = ((), (), s32[]{:S(2)}) async-start(), calls=%async_computation.29 | async-start | bytes 12976128 | tf_op jit(solution)/shard_map/reduce_scatter | solution.py:445
  2454.2 320.5 %reduce-scatter.17.cloned.1.call-start = ((), (), s32[]{:S(2)}) async-start(), calls=%async_computation.24 | async-start | bytes 2654208 | tf_op jit(solution)/shard_map/reduce_scatter | solution.py:430
  2466.3 363.3 %reduce-scatter.19.cloned.1.call-start = ((), (), s32[]{:S(2)}) async-start(), calls=%async_computation.25 | async-start | bytes 4718592 | tf_op jit(solution)/shard_map/reduce_scatter | solution.py:433
  2480.7 423.5 %reduce-scatter.21.cloned.1.call-start = ((), (), s32[]{:S(2)}) async-start(), calls=%async_computation.26 | async-start | bytes 9437184 | tf_op jit(solution)/shard_map/reduce_scatter | solution.py:436
  2490.5 11.7 copy-start.29
  2490.5 509.9 %reduce-scatter.15.cloned.1.call-start = ((), (), s32[]{:S(2)}) async-start(), calls=%async_computation.23 | async-start | bytes 14155776 | tf_op jit(solution)/shard_map/reduce_scatter | solution.py:427
  2521.8 533.2 %reduce-scatter.23.cloned.1.call-start = ((), (), s32[]{:S(2)}) async-start(), calls=%async_computation.27 | async-start | bytes 73728 | tf_op jit(solution)/shard_map/reduce_scatter | solution.py:439
  2523.2 20.4 copy-start.58
  2544.5 767.3 %all-reduce.12.cloned.1.call-start = ((), (), s32[]{:S(2)}) async-start(), calls=%async_computation.32 | async-start | bytes 15532032 | tf_op jit(solution)/shard_map/psum | solution.py:462
  3000.3 20.5 copy-start.8
  3000.3 20.5 copy-start.27
  3000.4 20.5 copy-start.108
  3038.0 32.5 copy-start.18
  (76 other events, 436.5 us)
Sparse Core Ops, SparseCore 0:
  9.9 32.0 all-gather.11
  47.2 32.7 all-gather.13
  81.9 35.6 all-gather.15
  119.4 72.1 all-gather.17
  193.3 54.3 all-gather.19
  1335.7 220.7 all-gather.25
  1558.4 122.2 all-gather.23
  1793.3 220.8 all-gather.21
  2410.6 15.8 reduce-scatter.30
  2429.2 29.4 reduce-scatter.12
  2462.3 85.5 reduce-scatter.24
  2551.2 86.7 reduce-scatter.28
  2641.5 86.7 reduce-scatter.26
  2732.1 42.4 reduce-scatter.16
  2778.2 51.2 reduce-scatter.18
  2832.9 71.2 reduce-scatter.20
  2907.9 92.3 reduce-scatter.14
  3004.0 31.4 reduce-scatter.22
  3038.4 273.3 all-reduce.11
where the time goes:
time: 3340 us; the launch traced here: 3330 us
  waiting for transfers between devices  2070 us (62%)
  matrix products  493 us (15%)
  local copies, waits for them, and re-layouts  343 us (10%)
  other arithmetic  224 us (7%)
  blocking collectives  167 us (5%)
    all_to_all x1, waiting for transfers between devices, local(): lax.all_to_all(slot_grad.reshape(2 * experts, capacity, model_width), ('c...  386 us
    all_to_all x1, waiting for transfers between devices, local(): lax.all_to_all(part_low, ('ctx', 'fsdp'), split_axis=0, concat_axis=0, ti...  383 us
    all_to_all x1, waiting for transfers between devices, local(): lax.all_to_all(send_rows, ('ctx', 'fsdp'), split_axis=0, concat_axis=0, t...  274 us
    psum x1, waiting for transfers between devices, local(): lax.psum(reduced[0].astype(jnp.bfloat16), 'ctx').astype(jnp.float32)  237 us
    all_gather x1, waiting for transfers between devices, local(): lax.all_gather(shared_gate, 'fsdp', axis=0, tiled=True)  203 us
    dot_general x11, matrix products, matmul(): return jnp.dot(left, right, preferred_element_type=single)  123 us
    reduce_scatter x1, waiting for transfers between devices, local(): lax.psum_scatter(grad_w_query.astype(jnp.bfloat16), 'fsdp', scatter_dimen...  96.2 us
    all_gather x1, blocking collectives, local(): lax.all_gather(router_weight, 'fsdp', axis=0, tiled=True)  93.9 us
  transfers between devices with their start and end apart: 23, of which 16 were waited for; matrix products, arithmetic and copies ran while one was open for 21% of the time, Pallas kernels for 0%

commit v1 on v0

v1 whole, which is shorter than its diff:
```python
import jax
import jax.numpy as jnp
from jax import lax
from jax.sharding import PartitionSpec as P

HEADS = 16
NOPE = 128
ROPE = 64
VDIM = 128
KV_RANK = 512
TOP = 6
PROMPT = 512
PROMPTS = 2
CONT_LEN = 128
CONTS = 2


epsilon = 1e-06
masked_score = -1e30
bfloat = jnp.bfloat16
single = jnp.float32


def matmul(left, right):
    return jnp.dot(left, right, preferred_element_type=single)


def rms_forward(values, gain):
    inverse = lax.rsqrt(jnp.mean(values * values, axis=-1, keepdims=True) + epsilon)
    normal_part = values * inverse
    return (normal_part * gain, normal_part, inverse)


def rms_backward(grad_out, normal_part, inverse, gain):
    grad_normal = grad_out * gain
    grad_gain = jnp.sum(grad_out * normal_part, axis=0)
    grad_in = inverse * (
        grad_normal - normal_part * jnp.mean(grad_normal * normal_part, axis=-1, keepdims=True)
    )
    return (grad_in, grad_gain)


def rotary_tables(positions):
    exponent = jnp.arange(ROPE // 2, dtype=jnp.float32) * (2.0 / ROPE)
    frequency = jnp.exp(-jnp.log(10000.0) * exponent)
    angles = positions[:, None] * frequency[None, :]
    return (jnp.cos(angles), jnp.sin(angles))


def rotate(values, cos_table, sin_table):
    half_width = values.shape[-1] // 2
    first_half = values[..., :half_width]
    second = values[..., half_width:]
    return jnp.concatenate(
        [first_half * cos_table - second * sin_table, second * cos_table + first_half * sin_table],
        axis=-1,
    )


def lookup(table_values, wanted):
    matches = wanted[:, None] == jnp.arange(table_values.shape[0], dtype=jnp.int32)[None, :]
    return jnp.sum(jnp.where(matches, table_values[None, :], 0), axis=1)


def row_layout(device, local_row, block_order, link_table, block_len, cont_dev):
    prompt_rows = PROMPTS * 2 * block_len
    in_prompt = local_row < prompt_rows
    prompt_id = local_row // (2 * block_len)
    half_slot = local_row // block_len % 2
    prompt_pos = lookup(block_order, 2 * device + half_slot) * block_len + local_row % block_len
    cont_index = device * cont_dev + jnp.maximum(local_row - prompt_rows, 0)
    cont_id = jnp.minimum(cont_index // CONT_LEN, CONTS - 1)
    cont_pos = cont_index % CONT_LEN
    sequence = jnp.where(in_prompt, prompt_id, PROMPTS + cont_id)
    position = jnp.where(in_prompt, prompt_pos, cont_pos)
    linked = jnp.where(in_prompt, -1, lookup(link_table, cont_id))
    rotary = jnp.where(in_prompt, prompt_pos, PROMPT + cont_pos)
    return (sequence, position, linked, rotary)


def silu_grads(grad_act, gate_pre, up_pre):
    sigmoid_gate = jax.nn.sigmoid(gate_pre)
    grad_gate = (grad_act * up_pre * sigmoid_gate * (1.0 + gate_pre * (1.0 - sigmoid_gate))).astype(
        bfloat
    )
    grad_up = (grad_act * gate_pre * sigmoid_gate).astype(bfloat)
    return (grad_gate, grad_up)


def attention_scores(query_nope, query_rope, key_nope, key_rope, allowed, score_scale):
    raw_scores = jnp.einsum(
        "qhd,khd->hqk", query_nope, key_nope, preferred_element_type=single
    ) + jnp.einsum("qhd,kd->hqk", query_rope, key_rope, preferred_element_type=single)
    return jnp.where(allowed[None], raw_scores * score_scale, masked_score)


def ring_next(value):
    size = lax.axis_size("ctx")
    return lax.ppermute(value, "ctx", [(i, (i + 1) % size) for i in range(size)])


def to_chip(value, offset):
    if offset == 0:
        return value
    size = lax.axis_size("fsdp")
    return lax.ppermute(
        value, "fsdp", [(i, ((i // 2) ^ offset) * 2 + i % 2) for i in range(size)]
    )


def to_core(value):
    size = lax.axis_size("fsdp")
    return lax.ppermute(value, "fsdp", [(i, i ^ 1) for i in range(size)])


def gather_rows(value):
    return lax.all_gather(value, "fsdp", axis=0, tiled=True)


def scatter_rows(value):
    return lax.psum_scatter(value.astype(bfloat), "fsdp", scatter_dimension=0, tiled=True)


def sum_ctx(value):
    part = lax.psum_scatter(value, "ctx", scatter_dimension=0, tiled=True)
    return lax.all_gather(part, "ctx", axis=0, tiled=True).astype(single)


def rank_table(route_block, experts, capacity):
    tokens = route_block.shape[0]
    expert_ids = jnp.arange(experts, dtype=jnp.int32)
    named = jnp.any(route_block[:, :, None] == expert_ids[None, None, :], axis=1)
    order = jnp.arange(tokens, dtype=jnp.int32)
    earlier = (order[:, None] > order[None, :]).astype(bfloat)
    rank = matmul(earlier, named.astype(bfloat)).astype(jnp.int32)
    return jnp.where(named & (rank < capacity), rank, -1)


def dispatch(rows, chips):
    mine = [to_chip(rows[j], j) for j in range(chips)]
    theirs = [to_core(piece) for piece in mine]
    return jnp.concatenate(mine + theirs, axis=0)


def send_back(results, chips, kind):
    pieces = results.reshape((2 * chips, results.shape[0] // (2 * chips)) + results.shape[1:])
    other = to_core(pieces[chips:])
    total = (pieces[:chips].astype(single) + other.astype(single)).astype(kind)
    return jnp.stack([to_chip(total[j], j) for j in range(chips)])


def local(
    layer_input,
    grad_output,
    routes,
    continuation_prompt,
    block_order,
    query_weight,
    latent_down,
    latent_up,
    output_weight,
    router_weight,
    shared_gate,
    shared_up,
    shared_down,
    attn_gain,
    latent_gain,
    ffn_gain,
    expert_gate,
    expert_up,
    expert_down,
):
    ctx_size = lax.axis_size("ctx")
    fsdp_size = lax.axis_size("fsdp")
    chips = fsdp_size // 2
    device = lax.axis_index("ctx")
    chip = lax.axis_index("fsdp") // 2
    tokens = layer_input.shape[1]
    model_width = layer_input.shape[2]
    experts = router_weight.shape[1]
    group_tok = tokens * ctx_size
    block_len = PROMPT // (2 * ctx_size)
    cont_dev = CONTS * CONT_LEN // ctx_size
    capacity = (5 * tokens * TOP + 4 * experts - 1) // (4 * experts)
    slots = (capacity + 7) // 8 * 8
    score_scale = (NOPE + ROPE) ** (-0.5)
    shard_rows = latent_down.shape[0]
    down_width = latent_down.shape[1]
    hidden_dev = shared_down.shape[0] // ctx_size

    packed = gather_rows(
        jnp.concatenate(
            [
                latent_down,
                router_weight,
                attn_gain[:, None],
                ffn_gain[:, None],
                jnp.pad(latent_gain, (0, shard_rows - latent_gain.shape[0]))[:, None],
            ],
            axis=1,
        )
    )
    full_down = packed[:, :down_width]
    full_router = packed[:, down_width : down_width + experts]
    gain_attn = packed[:, down_width + experts].astype(single)
    gain_ffn = packed[:, down_width + experts + 1].astype(single)
    gain_latent = (
        packed[:, down_width + experts + 2]
        .reshape(fsdp_size, shard_rows)[:, : latent_gain.shape[0]]
        .reshape(-1)
        .astype(single)
    )
    full_query = gather_rows(query_weight)
    full_up = gather_rows(latent_up)
    full_output = gather_rows(output_weight)

    def hidden_columns(weight):
        parts = weight.reshape(shard_rows, fsdp_size, ctx_size, hidden_dev)
        return lax.dynamic_index_in_dim(parts, device, axis=2, keepdims=False).reshape(
            shard_rows, fsdp_size * hidden_dev
        )

    part_gate = gather_rows(hidden_columns(shared_gate))
    part_up = gather_rows(hidden_columns(shared_up))
    part_down = gather_rows(
        lax.dynamic_slice_in_dim(shared_down, device * hidden_dev, hidden_dev, axis=0)
    )

    own_rows = jnp.arange(tokens, dtype=jnp.int32)
    link_table = continuation_prompt[0]
    own_seq, own_pos, own_link, own_rotary = row_layout(
        device, own_rows, block_order, link_table, block_len, cont_dev
    )
    group_rows = jnp.arange(group_tok, dtype=jnp.int32)
    key_seq, key_pos, key_link, key_rotary = row_layout(
        group_rows // tokens, group_rows % tokens, block_order, link_table, block_len, cont_dev
    )
    allowed = (key_seq[None, :] == own_seq[:, None]) & (key_pos[None, :] <= own_pos[:, None]) | (
        key_seq[None, :] == own_link[:, None]
    )
    cos_table, sin_table = rotary_tables(own_rotary.astype(single))

    route_ring = [routes[0]]
    grad_ring = [grad_output[0]]
    for _ in range(ctx_size - 1):
        route_ring.append(ring_next(route_ring[-1]))
        grad_ring.append(ring_next(grad_ring[-1]))
    plane_experts = device * chips + (chip ^ jnp.arange(chips, dtype=jnp.int32))
    chosen_here = plane_experts[:, None] == jnp.arange(experts, dtype=jnp.int32)[None, :]
    rank_ring = [rank_table(block, experts, capacity) for block in route_ring]

    def here(table):
        return jnp.sum(jnp.where(chosen_here[:, None, :], table[None], 0), axis=2)

    slot_ids = jnp.arange(slots, dtype=jnp.int32)
    slot_match = [
        here(ranks)[:, None, :] == slot_ids[None, :, None] for ranks in rank_ring
    ]
    slot_pick = [match.astype(bfloat) for match in slot_match]

    def pick_rows(step, rows):
        return jnp.einsum(
            "jrt,td->jrd", slot_pick[step], rows, preferred_element_type=single
        ).astype(bfloat)

    def put_rows(step, results):
        return jnp.einsum("jrt,jrd->td", slot_pick[step], results, preferred_element_type=single)

    inputs_full = layer_input[0].astype(single)
    normed, attn_normal, attn_inverse = rms_forward(inputs_full, gain_attn)
    normed_low = normed.astype(bfloat)
    latent_pre = matmul(normed_low, full_down)
    latent, latent_normal, latent_inverse = rms_forward(latent_pre[:, :KV_RANK], gain_latent)
    latent_low = latent.astype(bfloat)
    key_rope_own = rotate(latent_pre[:, KV_RANK:], cos_table, sin_table).astype(bfloat)
    key_group = lax.all_gather(
        jnp.concatenate([latent_low, key_rope_own], axis=1), "ctx", axis=0, tiled=True
    )
    latent_group = key_group[:, :KV_RANK]
    rope_group = key_group[:, KV_RANK:]
    query_pre = matmul(normed_low, full_query)
    query_nope = query_pre[:, : HEADS * NOPE].reshape(tokens, HEADS, NOPE).astype(bfloat)
    query_rope = rotate(
        query_pre[:, HEADS * NOPE :].reshape(tokens, HEADS, ROPE),
        cos_table[:, None, :],
        sin_table[:, None, :],
    ).astype(bfloat)
    kv_group = matmul(latent_group, full_up).astype(bfloat)
    key_nope = kv_group[:, : HEADS * NOPE].reshape(group_tok, HEADS, NOPE)
    values = kv_group[:, HEADS * NOPE :].reshape(group_tok, HEADS, VDIM)
    scores = attention_scores(query_nope, query_rope, key_nope, rope_group, allowed, score_scale)
    top_score = jnp.max(scores, axis=2, keepdims=True)
    exps = jnp.exp(scores - top_score)
    row_total = jnp.sum(exps, axis=2, keepdims=True)
    log_total = top_score + jnp.log(row_total)
    probs_low = (exps / row_total).astype(bfloat)
    attended = jnp.einsum("hqk,khd->qhd", probs_low, values, preferred_element_type=single)
    attended_low = attended.reshape(tokens, HEADS * VDIM).astype(bfloat)
    hidden = inputs_full + matmul(attended_low, full_output)
    ffn_in, ffn_normal, ffn_inverse = rms_forward(hidden, gain_ffn)
    ffn_low = ffn_in.astype(bfloat)

    grad_rows_ring = [
        dispatch(pick_rows(step, grad_ring[step]), chips) for step in range(ctx_size)
    ]

    logits = matmul(ffn_low, full_router)
    router_exps = jnp.exp(logits - jnp.max(logits, axis=1, keepdims=True))
    router = router_exps / jnp.sum(router_exps, axis=1, keepdims=True)
    route_match = jnp.any(
        routes[0][:, :, None] == jnp.arange(experts, dtype=jnp.int32)[None, None, :], axis=1
    )
    chosen_total = jnp.sum(jnp.where(route_match, router, 0.0), axis=1, keepdims=True)
    gates = jnp.where(route_match, router, 0.0) / chosen_total
    pair_weight = jnp.where(rank_ring[0] >= 0, gates, 0.0)

    ffn_ring = [ffn_low]
    weight_ring = [pair_weight]
    for _ in range(ctx_size - 1):
        weight_ring.append(ring_next(weight_ring[-1]))
        ffn_ring.append(ring_next(ffn_ring[-1]))

    expert_steps = []
    grad_parts = []
    gate_parts = []
    shared_steps = []
    for step in range(ctx_size):
        slot_weight = jnp.sum(
            jnp.where(slot_match[step], here(weight_ring[step])[:, None, :], 0.0), axis=2
        )
        slot_weight = dispatch(slot_weight, chips)
        rows = dispatch(pick_rows(step, ffn_ring[step]), chips)
        grad_rows = grad_rows_ring[step]
        gate_pre = matmul(rows, expert_gate[0])
        up_pre = matmul(rows, expert_up[0])
        grad_act = jnp.einsum("rd,fd->rf", grad_rows, expert_down[0], preferred_element_type=single)
        sigmoid_gate = jax.nn.sigmoid(gate_pre)
        act = gate_pre * sigmoid_gate * up_pre
        grad_weight = jnp.sum(act.astype(bfloat).astype(single) * grad_act, axis=1)
        act_low = (act * slot_weight[:, None]).astype(bfloat)
        grad_gate_low, grad_up_low = silu_grads(grad_act * slot_weight[:, None], gate_pre, up_pre)
        grad_back = (
            jnp.einsum("rf,df->rd", grad_gate_low, expert_gate[0], preferred_element_type=single)
            + jnp.einsum("rf,df->rd", grad_up_low, expert_up[0], preferred_element_type=single)
        ).astype(bfloat)
        expert_steps.append((rows, grad_rows, act_low, grad_gate_low, grad_up_low))
        back_weight = send_back(grad_weight, chips, single)
        back_rows = send_back(grad_back, chips, bfloat)

        sh_gate_pre = matmul(ffn_ring[step], part_gate)
        sh_up_pre = matmul(ffn_ring[step], part_up)
        shared_act = (jax.nn.silu(sh_gate_pre) * sh_up_pre).astype(bfloat)
        grad_sh_act = jnp.einsum(
            "td,fd->tf", grad_ring[step], part_down, preferred_element_type=single
        )
        grad_sh_gate, grad_sh_up = silu_grads(grad_sh_act, sh_gate_pre, sh_up_pre)
        shared_steps.append((shared_act, grad_sh_gate, grad_sh_up))
        grad_parts.append(
            put_rows(step, back_rows)
            + jnp.einsum("tf,df->td", grad_sh_gate, part_gate, preferred_element_type=single)
            + jnp.einsum("tf,df->td", grad_sh_up, part_up, preferred_element_type=single)
        )
        token_weight = jnp.sum(
            jnp.where(slot_match[step], back_weight[:, :, None], 0.0), axis=1
        )
        gate_parts.append(
            jnp.sum(jnp.where(chosen_here[:, None, :], token_weight[:, :, None], 0.0), axis=0)
        )

    def ring_sum(parts, kind):
        moving = parts[1].astype(kind)
        for step in range(2, ctx_size):
            moving = (ring_next(moving).astype(single) + parts[step]).astype(kind)
        return ring_next(moving).astype(single) + parts[0]

    grad_gate_pair = jnp.where(rank_ring[0] >= 0, ring_sum(gate_parts, single), 0.0)
    grad_ffn = ring_sum(grad_parts, bfloat)

    grad_low = grad_output[0]
    grad_top = grad_low.astype(single)
    grad_chosen = (
        grad_gate_pair - jnp.sum(grad_gate_pair * gates, axis=1, keepdims=True)
    ) / chosen_total
    grad_router = jnp.where(route_match, grad_chosen, 0.0)
    grad_logits = (
        router * (grad_router - jnp.sum(router * grad_router, axis=1, keepdims=True))
    ).astype(bfloat)
    grad_w_router = jnp.einsum("td,te->de", ffn_low, grad_logits, preferred_element_type=single)
    grad_ffn = grad_ffn + jnp.einsum(
        "te,de->td", grad_logits, full_router, preferred_element_type=single
    )
    grad_hidden_norm, grad_gain_ffn = rms_backward(grad_ffn, ffn_normal, ffn_inverse, gain_ffn)
    grad_hidden = grad_top + grad_hidden_norm
    grad_attn_low = grad_hidden.astype(bfloat)

    out_parts = []
    for step in range(ctx_size):
        part_low = matmul(expert_steps[step][2], expert_down[0]).astype(bfloat)
        back_out = send_back(part_low, chips, bfloat)
        out_parts.append(put_rows(step, back_out) + matmul(shared_steps[step][0], part_down))
    layer_output = (hidden + ring_sum(out_parts, bfloat)).astype(bfloat)

    def over_steps(pairs):
        total = None
        for left, right in pairs:
            part = jnp.einsum("ra,rb->ab", left, right, preferred_element_type=single)
            total = part if total is None else total + part
        return total

    grad_piece_down = over_steps([(e[2], e[1]) for e in expert_steps])
    grad_piece_gate = over_steps([(e[0], e[3]) for e in expert_steps])
    grad_piece_up = over_steps([(e[0], e[4]) for e in expert_steps])
    grad_w_sh_down = over_steps([(s[0], g) for s, g in zip(shared_steps, grad_ring)])
    grad_w_sh_gate = over_steps([(x, s[1]) for s, x in zip(shared_steps, ffn_ring)])
    grad_w_sh_up = over_steps([(x, s[2]) for s, x in zip(shared_steps, ffn_ring)])

    grad_w_output = jnp.einsum(
        "tv,td->vd", attended_low, grad_attn_low, preferred_element_type=single
    )
    grad_attended = (
        jnp.einsum("td,vd->tv", grad_attn_low, full_output, preferred_element_type=single)
        .astype(bfloat)
        .reshape(tokens, HEADS, VDIM)
    )
    scores_again = attention_scores(
        query_nope, query_rope, key_nope, rope_group, allowed, score_scale
    )
    probs_again = jnp.exp(scores_again - log_total)
    grad_probs = jnp.einsum("qhd,khd->hqk", grad_attended, values, preferred_element_type=single)
    row_delta = jnp.sum(probs_again * grad_probs, axis=2, keepdims=True)
    grad_scores = (probs_again * (grad_probs - row_delta)).astype(bfloat)
    grad_query_nope = (
        jnp.einsum("hqk,khd->qhd", grad_scores, key_nope, preferred_element_type=single)
        * score_scale
    )
    grad_query_rope = (
        jnp.einsum("hqk,kd->qhd", grad_scores, rope_group, preferred_element_type=single)
        * score_scale
    )
    grad_key_nope = (
        jnp.einsum("hqk,qhd->khd", grad_scores, query_nope, preferred_element_type=single)
        * score_scale
    )
    grad_key_rope = (
        jnp.einsum("hqk,qhd->kd", grad_scores, query_rope, preferred_element_type=single)
        * score_scale
    )
    grad_values = jnp.einsum(
        "hqk,qhd->khd", probs_low, grad_attended, preferred_element_type=single
    )
    grad_kv_part = jnp.concatenate(
        [grad_key_nope.reshape(group_tok, -1), grad_values.reshape(group_tok, -1)], axis=1
    )
    grad_kv_block = grad_kv_part.astype(bfloat)
    grad_w_up = jnp.einsum("tc,tk->ck", latent_group, grad_kv_block, preferred_element_type=single)
    grad_latent_group = jnp.einsum(
        "tk,ck->tc", grad_kv_block, full_up, preferred_element_type=single
    )
    grad_keys_own = lax.psum_scatter(
        jnp.concatenate([grad_latent_group, grad_key_rope], axis=1).astype(bfloat),
        "ctx",
        scatter_dimension=0,
        tiled=True,
    ).astype(single)
    grad_latent = grad_keys_own[:, :KV_RANK]
    grad_rope_own = grad_keys_own[:, KV_RANK:]
    grad_latent_in, grad_gain_latent = rms_backward(
        grad_latent, latent_normal, latent_inverse, gain_latent
    )
    grad_rope_in = rotate(grad_rope_own, cos_table, -sin_table)
    grad_latent_pre = jnp.concatenate([grad_latent_in, grad_rope_in], axis=1).astype(bfloat)
    grad_rope_query = rotate(grad_query_rope, cos_table[:, None, :], -sin_table[:, None, :])
    grad_query_pre = jnp.concatenate(
        [grad_query_nope.reshape(tokens, -1), grad_rope_query.reshape(tokens, -1)], axis=1
    ).astype(bfloat)
    grad_w_query = jnp.einsum(
        "td,tq->dq", normed_low, grad_query_pre, preferred_element_type=single
    )
    grad_w_down = jnp.einsum(
        "td,tk->dk", normed_low, grad_latent_pre, preferred_element_type=single
    )
    grad_normed = jnp.einsum(
        "tq,dq->td", grad_query_pre, full_query, preferred_element_type=single
    ) + jnp.einsum("tk,dk->td", grad_latent_pre, full_down, preferred_element_type=single)
    grad_x_norm, grad_gain_attn = rms_backward(grad_normed, attn_normal, attn_inverse, gain_attn)
    grad_input = (grad_hidden + grad_x_norm).astype(bfloat)

    sum_output = sum_ctx(scatter_rows(grad_w_output))
    sum_up = sum_ctx(scatter_rows(grad_w_up))
    sum_query = sum_ctx(scatter_rows(grad_w_query))
    padded_latent = jnp.pad(
        grad_gain_latent.reshape(fsdp_size, -1),
        ((0, 0), (0, shard_rows - latent_gain.shape[0])),
    ).reshape(-1)
    sum_packed = sum_ctx(
        scatter_rows(
            jnp.concatenate(
                [
                    grad_w_down,
                    grad_w_router,
                    grad_gain_attn[:, None],
                    grad_gain_ffn[:, None],
                    padded_latent[:, None],
                ],
                axis=1,
            )
        )
    )
    sum_down = sum_packed[:, :down_width]
    sum_router = sum_packed[:, down_width : down_width + experts]
    sum_gain_attn = sum_packed[:, down_width + experts]
    sum_gain_ffn = sum_packed[:, down_width + experts + 1]
    sum_gain_latent = sum_packed[: latent_gain.shape[0], down_width + experts + 2]

    def all_columns(part):
        blocks = lax.all_gather(scatter_rows(part), "ctx", axis=0)
        blocks = blocks.reshape(ctx_size, shard_rows, fsdp_size, hidden_dev)
        return blocks.transpose(1, 2, 0, 3).reshape(shard_rows, -1).astype(single)

    sum_sh_gate = all_columns(grad_w_sh_gate)
    sum_sh_up = all_columns(grad_w_sh_up)
    sum_sh_down = lax.all_gather(
        scatter_rows(grad_w_sh_down), "ctx", axis=0, tiled=True
    ).astype(single)
    return (
        layer_output[None],
        grad_input[None],
        sum_query,
        sum_down,
        sum_up,
        sum_output,
        sum_router,
        sum_sh_gate,
        sum_sh_up,
        sum_sh_down,
        sum_gain_attn,
        sum_gain_latent,
        sum_gain_ffn,
        grad_piece_gate[None],
        grad_piece_up[None],
        grad_piece_down[None],
    )


def solution(mesh):
    in_specs = (
        P("fsdp", "ctx", None),
        P("fsdp", "ctx", None),
        P("fsdp", "ctx", None),
        P("fsdp", None),
        P(),
        P("fsdp", None),
        P("fsdp", None),
        P("fsdp", None),
        P("fsdp", None),
        P("fsdp", None),
        P("fsdp", None),
        P("fsdp", None),
        P("fsdp", None),
        P("fsdp"),
        P("fsdp"),
        P("fsdp"),
        P(("ctx", "fsdp"), None, None),
        P(("ctx", "fsdp"), None, None),
        P(("ctx", "fsdp"), None, None),
    )
    out_specs = (
        P("fsdp", "ctx", None),
        P("fsdp", "ctx", None),
        P("fsdp", None),
        P("fsdp", None),
        P("fsdp", None),
        P("fsdp", None),
        P("fsdp", None),
        P("fsdp", None),
        P("fsdp", None),
        P("fsdp", None),
        P("fsdp"),
        P("fsdp"),
        P("fsdp"),
        P(("ctx", "fsdp"), None, None),
        P(("ctx", "fsdp"), None, None),
        P(("ctx", "fsdp"), None, None),
    )
    return jax.shard_map(local, mesh=mesh, in_specs=in_specs, out_specs=out_specs, check_vma=False)
```

time: 3340 us -> 1920 us (0.57)
  waiting for transfers between devices: 2070 us -> 790 us
  matrix products: 493 us -> 640 us
  local copies, waits for them, and re-layouts: 343 us -> 196 us
  blocking collectives: 167 us -> 33.5 us
  other arithmetic: 224 us -> 113 us
  starting transfers between devices: 18.5 us -> 121 us
    all_to_all x4 -> x0, waiting for transfers between devices: 1110 us -> none  [the longest x1 386 us: local(): lax.all_to_all(slot_grad.reshape(2 * experts, capacity, model_width), ('c...]
    ppermute x0 -> x153, waiting for transfers between devices: none -> 382 us  [the longest x72 192 us: to_chip(): lax.ppermute(value, 'fsdp', [(i, (i // 2 ^ offset) * 2 + i % 2) for i in...]
    psum x1 -> x0, waiting for transfers between devices: 237 us -> none  [local(): lax.psum(reduced[0].astype(jnp.bfloat16), 'ctx').astype(jnp.float32)]
    reduce_scatter x9 -> x11, waiting for transfers between devices: 438 us -> 212 us  [the longest x7 154 us: scatter_rows(): lax.psum_scatter(value.astype(bfloat), 'fsdp', scatter_dimension=0, tiled...]
    dot_general x9 -> x52, matrix products: 116 us -> 248 us  [the longest x24 164 us: over_steps(): part = jnp.einsum('ra,rb->ab', left, right, preferred_element_type=single)]
    ppermute x0 -> x153, starting transfers between devices: none -> 118 us  [the longest x72 85.1 us: to_chip(): lax.ppermute(value, 'fsdp', [(i, (i // 2 ^ offset) * 2 + i % 2) for i in...]
    gather x5 -> x0, local copies, waits for them, and re-layouts: 98.7 us -> none  [the longest x2 41.9 us: local(): padded_grad[source_row]]
    all_gather x4 -> x2, blocking collectives: 124 us -> 33.5 us  [sum_ctx(): return lax.all_gather(part, 'ctx', axis=0, tiled=True).astype(single)]
  transfers between devices with their start and end apart: 23 -> 178, of which waited for: 16 -> 56; matrix products, arithmetic and copies ran while one was open for 21% -> 44% of each run, Pallas kernels for 0% -> 0%
where the time goes in v1:
time: 1920 us; the launch traced here: 1910 us
  waiting for transfers between devices  790 us (41%)
  matrix products  640 us (33%)
  local copies, waits for them, and re-layouts  196 us (10%)
  starting transfers between devices  121 us (6%)
  other arithmetic  113 us (6%)
  blocking collectives  33.5 us (2%)
    ppermute x72, waiting for transfers between devices, to_chip(): lax.ppermute(value, 'fsdp', [(i, (i // 2 ^ offset) * 2 + i % 2) for i in...  192 us
    ppermute x21, waiting for transfers between devices, ring_next(): lax.ppermute(value, 'ctx', [(i, (i + 1) % size) for i in range(size)])  183 us
    dot_general x24, matrix products, over_steps(): part = jnp.einsum('ra,rb->ab', left, right, preferred_element_type=single)  164 us
    reduce_scatter x7, waiting for transfers between devices, scatter_rows(): lax.psum_scatter(value.astype(bfloat), 'fsdp', scatter_dimension=0, tiled...  154 us
    dot_general x33, matrix products, matmul(): return jnp.dot(left, right, preferred_element_type=single)  141 us
    unnamed x587, local copies, waits for them, and re-layouts  86.5 us
    ppermute x72, starting transfers between devices, to_chip(): lax.ppermute(value, 'fsdp', [(i, (i // 2 ^ offset) * 2 + i % 2) for i in...  85.1 us
    all_gather x7, waiting for transfers between devices, gather_rows(): return lax.all_gather(value, 'fsdp', axis=0, tiled=True)  82.2 us
  transfers between devices with their start and end apart: 178, of which 56 were waited for; matrix products, arithmetic and copies ran while one was open for 44% of the time, Pallas kernels for 0%

profile of v1, /device:TPU:0, one launch (start us, length us, event | category | flops | bytes accessed | tf_op | source)
XLA Modules:
  0.0 1911.9 jit_solution(6362045526842403673)
XLA Ops:
  18.2 28.3 %all-gather.16.cloned.1.call-done = bf16[2048,595]{0,1:T(8,128)(2,1)} async-done(((bf16[256,595]{0,1:T(8,128)(2,1)}), bf16[2048,595]{0,1:T(8,128)(2,1)}) %all-gather.16.cloned.1.call-update) | async-done | bytes 2437136 | tf_op jit(solution)/shard_map/all_gather | solution.py:117
  67.2 26.6 %collective-permute-done.84 = bf16[320,2048]{1,0:T(8,128)(2,1)} collective-permute-done((bf16[320,2048]{1,0:T(8,128)(2,1)}, bf16[320,2048]{1,0:T(8,128)(2,1)}, u32[]{:S(2)}, u32[]{:S(2)}) %collective-permute-start.84) | collective-permute-done | bytes 1310752 | tf_op jit(solution)/shard_map/ppermute | solution.py:99
  97.0 52.2 %collective-permute-done.22 = s32[320,6]{0,1:T(8,128)S(1)} collective-permute-done((s32[320,6]{0,1:T(8,128)S(1)}, s32[320,6]{0,1:T(8,128)S(1)}, u32[]{:S(2)}, u32[]{:S(2)}) %collective-permute-start.22) | collective-permute-done | bytes 7712 | tf_op jit(solution)/shard_map/ppermute | solution.py:99
  166.1 19.9 %collective-permute-done.110 = bf16[320,2048]{1,0:T(8,128)(2,1)} collective-permute-done((bf16[320,2048]{1,0:T(8,128)(2,1)}, bf16[320,2048]{1,0:T(8,128)(2,1)}, u32[]{:S(2)}, u32[]{:S(2)}) %collective-permute-start.110) | collective-permute-done | bytes 1310752 | tf_op jit(solution)/shard_map/ppermute | solution.py:99
  189.6 11.4 convolution_convert_fusion
  201.0 13.0 slice_bitcast_fusion
  213.9 41.8 %all-gather.22.cloned.1.call-done = bf16[2048,3072]{1,0:T(8,128)(2,1)} async-done(((bf16[256,3072]{1,0:T(8,128)(2,1)}), bf16[2048,3072]{1,0:T(8,128)(2,1)}) %all-gather.22.cloned.1.call-update) | async-done | bytes 12582928 | tf_op jit(solution)/shard_map/all_gather | solution.py:117
  271.3 11.8 fusion.211
  283.1 19.3 %fusion.350 = (f32[16,320]{1,0:T(8,128)S(1)}, f32[16,320,1280]{2,1,0:T(8,128)}) fusion(f32[1280,320,16]{0,1,2:T(8,128)} %fusion.211, bf16[160,16,8,128]{3,2,1,0:T(8,128)(2,1)S(1)} %bitcast.645, pred[320,1280]{1,0:T(8,128)(4,1)S(1)} %compare_or_fusion, f32[320,3072]{1,0:T(8,128)S(1)} %copy-done.6), kind=kOutput, calls=%fused_computation.703 | convolution fusion | flops 1703930880 | bytes 59412480 | tf_op jit(solution)/shard_map/qhd,khd->hqk/dot_general | solution.py:91
  302.4 9.7 fusion.2
  318.7 8.3 divide_convert_fusion
  327.0 9.3 fusion.173
  386.3 12.1 all-gather.26.cloned.1.call-done
  429.8 14.0 collective-permute-done.67
  447.1 8.9 collective-permute-done.85
  458.5 13.5 collective-permute-done.86
  485.3 14.3 collective-permute-done.99
  510.3 15.7 collective-permute-done.112
  579.7 22.8 %collective-permute-done.53 = f32[320,16]{0,1:T(8,128)S(1)} collective-permute-done((f32[320,16]{0,1:T(8,128)S(1)}, f32[320,16]{0,1:T(8,128)S(1)}, u32[]{:S(2)}, u32[]{:S(2)}) %collective-permute-start.53) | collective-permute-done | bytes 20512 | tf_op jit(solution)/shard_map/ppermute | solution.py:99
  633.9 10.5 collective-permute-done.2
  644.4 13.8 collective-permute-done.3
  729.2 10.2 collective-permute-done.24
  740.0 12.2 collective-permute-done.26
  805.3 21.3 %collective-permute-done.45 = bf16[320,2048]{1,0:T(8,128)(2,1)} collective-permute-done((bf16[320,2048]{1,0:T(8,128)(2,1)}, bf16[320,2048]{1,0:T(8,128)(2,1)}, u32[]{:S(2)}, u32[]{:S(2)}) %collective-permute-start.45) | collective-permute-done | bytes 1310752 | tf_op jit(solution)/shard_map/ppermute | solution.py:99
  833.3 8.3 add_convert_fusion.2
  847.3 12.1 collective-permute-done.48
  945.4 9.0 collective-permute-done.106
  954.3 12.2 collective-permute-done.107
  976.3 10.5 collective-permute-done.119
  1008.7 22.4 %collective-permute-done.148 = f32[320,16]{0,1:T(8,128)S(1)} collective-permute-done((f32[320,16]{0,1:T(8,128)S(1)}, f32[320,16]{0,1:T(8,128)S(1)}, u32[]{:S(2)}, u32[]{:S(2)}) %collective-permute-start.148) | collective-permute-done | bytes 20512 | tf_op jit(solution)/shard_map/ppermute | solution.py:99
  1050.0 18.8 multiply_reduce_fusion
  1068.8 17.5 multiply_convert_fusion
  1086.3 9.1 multiply_convert_fusion.1
  1098.9 10.8 fusion.29
  1113.6 10.1 convolution_convert_fusion.2
  1124.0 9.9 fusion.176
  1135.3 10.4 multiply_bitcast_fusion
  1155.5 12.0 convolution_convert_fusion.1
  1220.0 9.1 fusion.196
  1239.6 12.0 concatenate.93
  1251.9 9.9 fusion.379
  1267.9 12.1 fusion.5
  1286.0 8.4 fusion.376
  1324.7 11.4 fusion.205
  1367.3 9.5 fusion.378
  1376.9 8.8 fusion.206
  1388.3 28.0 %reduce-scatter.31.cloned.1.call-done = bf16[256,704]{0,1:T(8,128)(2,1)} async-done(((bf16[2048,704]{0,1:T(8,128)(2,1)}), bf16[256,704]{0,1:T(8,128)(2,1)}) %reduce-scatter.31.cloned.1.call-update) | async-done | bytes 360464 | tf_op jit(solution)/shard_map/reduce_scatter | solution.py:121
  1431.2 42.1 %reduce-scatter.35.cloned.1.call-done = bf16[88,2048]{1,0:T(8,128)(2,1)} async-done(((bf16[704,2048]{1,0:T(8,128)(2,1)}), bf16[88,2048]{1,0:T(8,128)(2,1)}) %reduce-scatter.35.cloned.1.call-update) | async-done | bytes 360464 | tf_op jit(solution)/shard_map/reduce_scatter | solution.py:121
  1492.7 45.9 %reduce-scatter.21.cloned.1.call-done = bf16[256,595]{0,1:T(8,128)(2,1)} async-done(((bf16[2048,595]{0,1:T(8,128)(2,1)}), bf16[256,595]{0,1:T(8,128)(2,1)}) %reduce-scatter.21.cloned.1.call-update) | async-done | bytes 304656 | tf_op jit(solution)/shard_map/reduce_scatter | solution.py:121
  1540.5 17.1 add_bitcast_fusion
  1564.7 35.3 %reduce-scatter.23.cloned.1.call-done = bf16[64,4096]{1,0:T(8,128)(2,1)} async-done(((bf16[512,4096]{1,0:T(8,128)(2,1)}), bf16[64,4096]{1,0:T(8,128)(2,1)}) %reduce-scatter.23.cloned.1.call-update) | async-done | bytes 524304 | tf_op jit(solution)/shard_map/reduce_scatter | solution.py:121
  1608.5 20.8 %reduce-scatter.29.cloned.1.call-done = bf16[64,2048]{1,0:T(8,128)(2,1)} async-done(((bf16[256,2048]{1,0:T(8,128)(2,1)}), bf16[64,2048]{1,0:T(8,128)(2,1)}) %reduce-scatter.29.cloned.1.call-update) | async-done | bytes 262160 | tf_op jit(solution)/shard_map/reduce_scatter | solution.py:125
  1629.4 14.9 add_bitcast_fusion.1
  1651.8 22.1 %reduce-scatter.19.cloned.1.call-done = bf16[64,3072]{1,0:T(8,128)(2,1)} async-done(((bf16[256,3072]{1,0:T(8,128)(2,1)}), bf16[64,3072]{1,0:T(8,128)(2,1)}) %reduce-scatter.19.cloned.1.call-update) | async-done | bytes 393232 | tf_op jit(solution)/shard_map/reduce_scatter | solution.py:125
  1674.0 14.6 add_bitcast_fusion.2
  1688.6 10.2 collective-permute-done.65
  1703.2 14.8 all-gather.40.cloned.1.call-done
  1729.6 23.6 %all-gather.38.cloned.1.call-done = bf16[1024,704]{0,1:T(8,128)(2,1)} async-done(((bf16[256,704]{0,1:T(8,128)(2,1)}), bf16[1024,704]{0,1:T(8,128)(2,1)}) %all-gather.38.cloned.1.call-update) | async-done | bytes 1441808 | tf_op jit(solution)/shard_map/all_gather | solution.py:516
  1764.7 23.4 %all-gather.36.cloned.1.call-done = bf16[352,2048]{1,0:T(8,128)(2,1)} async-done(((bf16[88,2048]{1,0:T(8,128)(2,1)}), bf16[352,2048]{1,0:T(8,128)(2,1)}) %all-gather.36.cloned.1.call-update) | async-done | bytes 1441808 | tf_op jit(solution)/shard_map/all_gather | solution.py:522
  1795.1 14.9 reduce-scatter.39.cloned.1.call-done
  1810.0 16.0 all_gather.60
  1833.5 17.5 all_gather.61
  1852.1 10.5 all-gather.34.cloned.1.call-done
  1865.4 36.1 %all-gather.32.cloned.1.call-done = bf16[256,3072]{1,0:T(8,128)(2,1)} async-done(((bf16[64,3072]{1,0:T(8,128)(2,1)}), bf16[256,3072]{1,0:T(8,128)(2,1)}) %all-gather.32.cloned.1.call-update) | async-done | bytes 1572880 | tf_op jit(solution)/shard_map/all_gather | solution.py:126
  (1200 shorter events, 810.3 us)
Async XLA Ops:
  7.2 39.3 %all-gather.16.cloned.1.call-start = ((), (), s32[]{:S(2)}) async-start(), calls=%async_computation.12 | async-start | bytes 2764800 | tf_op jit(solution)/shard_map/all_gather | solution.py:117
  13.8 141.8 %all-gather.30.cloned.1.call-start = ((), (), s32[]{:S(2)}) async-start(), calls=%async_computation.19 | async-start | bytes 3244032 | tf_op jit(solution)/shard_map/all_gather | solution.py:117
  15.7 173.9 %all-gather.18.cloned.1.call-start = ((), (), s32[]{:S(2)}) async-start(), calls=%async_computation.13 | async-start | bytes 2048000 | tf_op jit(solution)/shard_map/all_gather | solution.py:276
  53.2 136.3 %all-gather.20.cloned.1.call-start = ((), (), s32[]{:S(2)}) async-start(), calls=%async_computation.14 | async-start | bytes 4718592 | tf_op jit(solution)/shard_map/all_gather | solution.py:117
  53.8 201.9 %all-gather.22.cloned.1.call-start = ((), (), s32[]{:S(2)}) async-start(), calls=%async_computation.15 | async-start | bytes 14155776 | tf_op jit(solution)/shard_map/all_gather | solution.py:117
  54.4 281.9 %all-gather.24.cloned.1.call-start = ((), (), s32[]{:S(2)}) async-start(), calls=%async_computation.16 | async-start | bytes 9437184 | tf_op jit(solution)/shard_map/all_gather | solution.py:117
  55.0 314.8 %all-gather.28.cloned.1.call-start = ((), (), s32[]{:S(2)}) async-start(), calls=%async_computation.18 | async-start | bytes 3244032 | tf_op jit(solution)/shard_map/all_gather | solution.py:117
  59.4 339.1 %all-gather.26.cloned.1.call-start = ((), (), s32[]{:S(2)}) async-start(), calls=%async_computation.17 | async-start | bytes 3244032 | tf_op jit(solution)/shard_map/all_gather | solution.py:117
  59.4 35.2 %collective-permute-start = (s32[320,6]{0,1:T(8,128)S(1)}, s32[320,6]{0,1:T(8,128)S(1)}, u32[]{:S(2)}, u32[]{:S(2)}) collective-permute-start(s32[320,6]{0,1:T(8,128)S(1)} %bitcast.688), channel_id=1, source_target_pairs={{0,8},{8,16},{16,24},{24,0},{1,9},{9,17},{17,25},{25,1},{2,10},{10... | collective-permute-start | bytes 23048 | tf_op jit(solution)/shard_map/ppermute | solution.py:99
  61.0 32.9 %collective-permute-start.84 = (bf16[320,2048]{1,0:T(8,128)(2,1)}, bf16[320,2048]{1,0:T(8,128)(2,1)}, u32[]{:S(2)}, u32[]{:S(2)}) collective-permute-start(bf16[320,2048]{1,0:T(8,128)(2,1)} %bitcast.663), channel_id=1, source_target_pairs={{0,8},{8,16},{16,24},{24,0},{1,9},{9,17},{17,25},{25,1},{2,10},{10... | collective-permute-start | bytes 3932168 | tf_op jit(solution)/shard_map/ppermute | solution.py:99
  66.8 1081.6 %reduce-scatter.37.cloned.1.call-start = ((), (), s32[]{:S(2)}) async-start(), calls=%async_computation.35 | async-start | bytes 2048000
  93.9 60.9 %collective-permute-start.97 = (bf16[320,2048]{1,0:T(8,128)(2,1)}, bf16[320,2048]{1,0:T(8,128)(2,1)}, u32[]{:S(2)}, u32[]{:S(2)}) collective-permute-start(bf16[320,2048]{1,0:T(8,128)(2,1)} %collective-permute-done.84), channel_id=1, source_target_pairs={{0,8},{8,16},{16,24},{24,0},{1,9},{9,17},{17,25},{25,1},{2,10},{10... | collective-permute-start | bytes 3932168 | tf_op jit(solution)/shard_map/ppermute | solution.py:99
  94.6 54.6 %collective-permute-start.22 = (s32[320,6]{0,1:T(8,128)S(1)}, s32[320,6]{0,1:T(8,128)S(1)}, u32[]{:S(2)}, u32[]{:S(2)}) collective-permute-start(s32[320,6]{0,1:T(8,128)S(1)} %collective-permute-done), channel_id=1, source_target_pairs={{0,8},{8,16},{16,24},{24,0},{1,9},{9,17},{17,25},{25,1},{2,10},{10... | collective-permute-start | bytes 23048 | tf_op jit(solution)/shard_map/ppermute | solution.py:99
  154.7 31.3 %collective-permute-start.110 = (bf16[320,2048]{1,0:T(8,128)(2,1)}, bf16[320,2048]{1,0:T(8,128)(2,1)}, u32[]{:S(2)}, u32[]{:S(2)}) collective-permute-start(bf16[320,2048]{1,0:T(8,128)(2,1)} %collective-permute-done.97), channel_id=1, source_target_pairs={{0,8},{8,16},{16,24},{24,0},{1,9},{9,17},{17,25},{25,1},{2,10},{10... | collective-permute-start | bytes 3932168 | tf_op jit(solution)/shard_map/ppermute | solution.py:99
  353.4 58.8 %collective-permute-start.123 = (bf16[152,2048]{1,0:T(8,128)(2,1)}, bf16[152,2048]{1,0:T(8,128)(2,1)}, u32[]{:S(2)}, u32[]{:S(2)}) collective-permute-start(bf16[152,2048]{1,0:T(8,128)(2,1)} %get-tuple-element.230), channel_id=1, source_target_pairs={{0,2},{1,3},{2,0},{3,1},{4,6},{5,7},{6,4},{7,5},{8,10},{9,11},{10,... | collective-permute-start | bytes 1867784 | tf_op jit(solution)/shard_map/ppermute | solution.py:106
  355.2 59.6 %collective-permute-start.124 = (bf16[152,2048]{1,0:T(8,128)(2,1)}, bf16[152,2048]{1,0:T(8,128)(2,1)}, u32[]{:S(2)}, u32[]{:S(2)}) collective-permute-start(bf16[152,2048]{1,0:T(8,128)(2,1)} %get-tuple-element.229), channel_id=1, source_target_pairs={{0,4},{1,5},{2,6},{3,7},{4,0},{5,1},{6,2},{7,3},{8,12},{9,13},{10,... | collective-permute-start | bytes 1867784 | tf_op jit(solution)/shard_map/ppermute | solution.py:106
  355.3 61.5 %collective-permute-start.125 = (bf16[152,2048]{1,0:T(8,128)(2,1)}, bf16[152,2048]{1,0:T(8,128)(2,1)S(1)}, u32[]{:S(2)}, u32[]{:S(2)}) collective-permute-start(bf16[152,2048]{1,0:T(8,128)(2,1)} %get-tuple-element.228), channel_id=1, source_target_pairs={{0,6},{1,7},{2,4},{3,5},{4,2},{5,3},{6,0},{7,1},{8,14},{9,15},{10,... | collective-permute-start | bytes 1867784 | tf_op jit(solution)/shard_map/ppermute | solution.py:106
  410.1 94.4 %collective-permute-start.9 = (f32[320,16]{0,1:T(8,128)S(1)}, f32[320,16]{0,1:T(8,128)S(1)}, u32[]{:S(2)}, u32[]{:S(2)}) collective-permute-start(f32[320,16]{0,1:T(8,128)S(1)} %copy-done.159), channel_id=1, source_target_pairs={{0,8},{8,16},{16,24},{24,0},{1,9},{9,17},{17,25},{25,1},{2,10},{10... | collective-permute-start | bytes 61448 | tf_op jit(solution)/shard_map/ppermute | solution.py:99
  447.0 32.0 %collective-permute-start.88 = (bf16[152,2048]{1,0:T(8,128)(2,1)S(1)}, bf16[152,2048]{1,0:T(8,128)(2,1)S(1)}, u32[]{:S(2)}, u32[]{:S(2)}) collective-permute-start(bf16[152,2048]{1,0:T(8,128)(2,1)S(1)} %copy-done.81), channel_id=1, source_target_pairs={{0,1},{1,0},{2,3},{3,2},{4,5},{5,4},{6,7},{7,6},{8,9},{9,8},{10,11... | collective-permute-start | bytes 1867784 | tf_op jit(solution)/shard_map/ppermute | solution.py:113
  504.5 65.5 %collective-permute-start.31 = (f32[320,16]{0,1:T(8,128)S(1)}, f32[320,16]{0,1:T(8,128)S(1)}, u32[]{:S(2)}, u32[]{:S(2)}) collective-permute-start(f32[320,16]{0,1:T(8,128)S(1)} %collective-permute-done.9), channel_id=1, source_target_pairs={{0,8},{8,16},{16,24},{24,0},{1,9},{9,17},{17,25},{25,1},{2,10},{10... | collective-permute-start | bytes 61448 | tf_op jit(solution)/shard_map/ppermute | solution.py:99
  570.0 54.4 %collective-permute-start.1 = (bf16[320,2048]{1,0:T(8,128)(2,1)}, bf16[320,2048]{1,0:T(8,128)(2,1)}, u32[]{:S(2)}, u32[]{:S(2)}) collective-permute-start(bf16[320,2048]{1,0:T(8,128)(2,1)} %copy-done.3), channel_id=1, source_target_pairs={{0,8},{8,16},{16,24},{24,0},{1,9},{9,17},{17,25},{25,1},{2,10},{10... | collective-permute-start | bytes 3932168 | tf_op jit(solution)/shard_map/ppermute | solution.py:99
  633.7 85.8 %collective-permute-start.23 = (bf16[320,2048]{1,0:T(8,128)(2,1)}, bf16[320,2048]{1,0:T(8,128)(2,1)}, u32[]{:S(2)}, u32[]{:S(2)}) collective-permute-start(bf16[320,2048]{1,0:T(8,128)(2,1)} %collective-permute-done.1), channel_id=1, source_target_pairs={{0,8},{8,16},{16,24},{24,0},{1,9},{9,17},{17,25},{25,1},{2,10},{10... | collective-permute-start | bytes 3932168 | tf_op jit(solution)/shard_map/ppermute | solution.py:99
  728.7 165.9 %collective-permute-start.92 = (bf16[4,152,2048]{2,1,0:T(8,128)(2,1)}, bf16[4,152,2048]{2,1,0:T(8,128)(2,1)}, u32[]{:S(2)}, u32[]{:S(2)}) collective-permute-start(bf16[4,152,2048]{2,1,0:T(8,128)(2,1)} %bitcast.96), channel_id=1, source_target_pairs={{0,1},{1,0},{2,3},{3,2},{4,5},{5,4},{6,7},{7,6},{8,9},{9,8},{10,11... | collective-permute-start | bytes 7471112 | tf_op jit(solution)/shard_map/ppermute | solution.py:113
  793.4 33.2 %collective-permute-start.45 = (bf16[320,2048]{1,0:T(8,128)(2,1)}, bf16[320,2048]{1,0:T(8,128)(2,1)}, u32[]{:S(2)}, u32[]{:S(2)}) collective-permute-start(bf16[320,2048]{1,0:T(8,128)(2,1)} %collective-permute-done.23), channel_id=1, source_target_pairs={{0,8},{8,16},{16,24},{24,0},{1,9},{9,17},{17,25},{25,1},{2,10},{10... | collective-permute-start | bytes 3932168 | tf_op jit(solution)/shard_map/ppermute | solution.py:99
  881.6 52.8 %collective-permute-start.105 = (bf16[4,152,2048]{2,1,0:T(8,128)(2,1)}, bf16[4,152,2048]{2,1,0:T(8,128)(2,1)}, u32[]{:S(2)}, u32[]{:S(2)}) collective-permute-start(bf16[4,152,2048]{2,1,0:T(8,128)(2,1)} %bitcast.111), channel_id=1, source_target_pairs={{0,1},{1,0},{2,3},{3,2},{4,5},{5,4},{6,7},{7,6},{8,9},{9,8},{10,11... | collective-permute-start | bytes 7471112 | tf_op jit(solution)/shard_map/ppermute | solution.py:113
  923.5 45.0 %collective-permute-start.118 = (bf16[4,152,2048]{2,1,0:T(8,128)(2,1)S(1)}, bf16[4,152,2048]{2,1,0:T(8,128)(2,1)S(1)}, u32[]{:S(2)}, u32[]{:S(2)}) collective-permute-start(bf16[4,152,2048]{2,1,0:T(8,128)(2,1)S(1)} %bitcast.666), channel_id=1, source_target_pairs={{0,1},{1,0},{2,3},{3,2},{4,5},{5,4},{6,7},{7,6},{8,9},{9,8},{10,11... | collective-permute-start | bytes 7471112 | tf_op jit(solution)/shard_map/ppermute | solution.py:113
  934.1 32.4 %collective-permute-start.96 = (bf16[320,2048]{1,0:T(8,128)(2,1)S(1)}, bf16[320,2048]{1,0:T(8,128)(2,1)S(1)}, u32[]{:S(2)}, u32[]{:S(2)}) collective-permute-start(bf16[320,2048]{1,0:T(8,128)(2,1)S(1)} %fusion.82), channel_id=1, source_target_pairs={{0,8},{8,16},{16,24},{24,0},{1,9},{9,17},{17,25},{25,1},{2,10},{10... | collective-permute-start | bytes 3932168 | tf_op jit(solution)/shard_map/ppermute | solution.py:99
  954.3 46.6 %collective-permute-start.130 = (bf16[4,152,2048]{2,1,0:T(8,128)(2,1)S(1)}, bf16[4,152,2048]{2,1,0:T(8,128)(2,1)S(1)}, u32[]{:S(2)}, u32[]{:S(2)}) collective-permute-start(bf16[4,152,2048]{2,1,0:T(8,128)(2,1)S(1)} %bitcast.665), channel_id=1, source_target_pairs={{0,1},{1,0},{2,3},{3,2},{4,5},{5,4},{6,7},{7,6},{8,9},{9,8},{10,11... | collective-permute-start | bytes 7471112 | tf_op jit(solution)/shard_map/ppermute | solution.py:113
  1000.9 31.8 %collective-permute-start.122 = (bf16[320,2048]{1,0:T(8,128)(2,1)S(1)}, bf16[320,2048]{1,0:T(8,128)(2,1)S(1)}, u32[]{:S(2)}, u32[]{:S(2)}) collective-permute-start(bf16[320,2048]{1,0:T(8,128)(2,1)S(1)} %add_convert_fusion.7), channel_id=1, source_target_pairs={{0,8},{8,16},{16,24},{24,0},{1,9},{9,17},{17,25},{25,1},{2,10},{10... | collective-permute-start | bytes 3932168 | tf_op jit(solution)/shard_map/ppermute | solution.py:99
  1113.6 210.6 %reduce-scatter.27.cloned.1.call-start = ((), (), s32[]{:S(2)}) async-start(), calls=%async_computation.26 | async-start | bytes 9437184 | tf_op jit(solution)/shard_map/reduce_scatter | solution.py:121
  1123.7 219.3 %reduce-scatter.17.cloned.1.call-start = ((), (), s32[]{:S(2)}) async-start(), calls=%async_computation.20 | async-start | bytes 14155776 | tf_op jit(solution)/shard_map/reduce_scatter | solution.py:121
  1167.5 199.6 %reduce-scatter.33.cloned.1.call-start = ((), (), s32[]{:S(2)}) async-start(), calls=%async_computation.30 | async-start | bytes 3244032 | tf_op jit(solution)/shard_map/reduce_scatter | solution.py:121
  1182.2 234.2 %reduce-scatter.31.cloned.1.call-start = ((), (), s32[]{:S(2)}) async-start(), calls=%async_computation.29 | async-start | bytes 3244032 | tf_op jit(solution)/shard_map/reduce_scatter | solution.py:121
  1196.9 276.4 %reduce-scatter.35.cloned.1.call-start = ((), (), s32[]{:S(2)}) async-start(), calls=%async_computation.31 | async-start | bytes 3244032 | tf_op jit(solution)/shard_map/reduce_scatter | solution.py:121
  1212.3 326.2 %reduce-scatter.21.cloned.1.call-start = ((), (), s32[]{:S(2)}) async-start(), calls=%async_computation.23 | async-start | bytes 2764800 | tf_op jit(solution)/shard_map/reduce_scatter | solution.py:121
  1251.7 348.4 %reduce-scatter.23.cloned.1.call-start = ((), (), s32[]{:S(2)}) async-start(), calls=%async_computation.24 | async-start | bytes 4718592 | tf_op jit(solution)/shard_map/reduce_scatter | solution.py:121
  1280.0 349.4 %reduce-scatter.29.cloned.1.call-start = ((), (), s32[]{:S(2)}) async-start(), calls=%async_computation.27 | async-start | bytes 1310720 | tf_op jit(solution)/shard_map/reduce_scatter | solution.py:125
  1285.9 53.0 %collective-permute-start.80 = (bf16[4,152,2048]{2,1,0:T(8,128)(2,1)}, bf16[4,152,2048]{2,1,0:T(8,128)(2,1)}, u32[]{:S(2)}, u32[]{:S(2)}) collective-permute-start(bf16[4,152,2048]{2,1,0:T(8,128)(2,1)} %bitcast.80), channel_id=1, source_target_pairs={{0,1},{1,0},{2,3},{3,2},{4,5},{5,4},{6,7},{7,6},{8,9},{9,8},{10,11... | collective-permute-start | bytes 7471112 | tf_op jit(solution)/shard_map/ppermute | solution.py:113
  1311.6 104.8 %collective-permute-start.17 = (bf16[4,152,2048]{2,1,0:T(8,128)(2,1)}, bf16[4,152,2048]{2,1,0:T(8,128)(2,1)}, u32[]{:S(2)}, u32[]{:S(2)}) collective-permute-start(bf16[4,152,2048]{2,1,0:T(8,128)(2,1)} %bitcast.22), channel_id=1, source_target_pairs={{0,1},{1,0},{2,3},{3,2},{4,5},{5,4},{6,7},{7,6},{8,9},{9,8},{10,11... | collective-permute-start | bytes 7471112 | tf_op jit(solution)/shard_map/ppermute | solution.py:113
  1324.2 349.7 %reduce-scatter.19.cloned.1.call-start = ((), (), s32[]{:S(2)}) async-start(), calls=%async_computation.21 | async-start | bytes 1966080 | tf_op jit(solution)/shard_map/reduce_scatter | solution.py:125
  1343.0 375.0 %all-gather.40.cloned.1.call-start = ((), (), s32[]{:S(2)}) async-start(), calls=%async_computation.34 | async-start | bytes 1802240 | tf_op jit(solution)/shard_map/all_gather | solution.py:516
  1355.7 129.1 %collective-permute-start.39 = (bf16[4,152,2048]{2,1,0:T(8,128)(2,1)}, bf16[4,152,2048]{2,1,0:T(8,128)(2,1)}, u32[]{:S(2)}, u32[]{:S(2)}) collective-permute-start(bf16[4,152,2048]{2,1,0:T(8,128)(2,1)} %bitcast.44), channel_id=1, source_target_pairs={{0,1},{1,0},{2,3},{3,2},{4,5},{5,4},{6,7},{7,6},{8,9},{9,8},{10,11... | collective-permute-start | bytes 7471112 | tf_op jit(solution)/shard_map/ppermute | solution.py:113
  1367.1 386.1 %all-gather.38.cloned.1.call-start = ((), (), s32[]{:S(2)}) async-start(), calls=%async_computation.33 | async-start | bytes 1802240 | tf_op jit(solution)/shard_map/all_gather | solution.py:516
  1416.4 371.7 %all-gather.36.cloned.1.call-start = ((), (), s32[]{:S(2)}) async-start(), calls=%async_computation.32 | async-start | bytes 1802240 | tf_op jit(solution)/shard_map/all_gather | solution.py:522
  1421.5 57.6 %collective-permute-start.18 = (bf16[152,2048]{1,0:T(8,128)(2,1)}, bf16[152,2048]{1,0:T(8,128)(2,1)}, u32[]{:S(2)}, u32[]{:S(2)}) collective-permute-start(bf16[152,2048]{1,0:T(8,128)(2,1)} %get-tuple-element.210), channel_id=1, source_target_pairs={{0,2},{1,3},{2,0},{3,1},{4,6},{5,7},{6,4},{7,5},{8,10},{9,11},{10,... | collective-permute-start | bytes 1867784 | tf_op jit(solution)/shard_map/ppermute | solution.py:106
  1422.9 56.1 %collective-permute-start.19 = (bf16[152,2048]{1,0:T(8,128)(2,1)}, bf16[152,2048]{1,0:T(8,128)(2,1)}, u32[]{:S(2)}, u32[]{:S(2)}) collective-permute-start(bf16[152,2048]{1,0:T(8,128)(2,1)} %get-tuple-element.209), channel_id=1, source_target_pairs={{0,4},{1,5},{2,6},{3,7},{4,0},{5,1},{6,2},{7,3},{8,12},{9,13},{10,... | collective-permute-start | bytes 1867784 | tf_op jit(solution)/shard_map/ppermute | solution.py:106
  1423.5 55.6 %collective-permute-start.20 = (bf16[152,2048]{1,0:T(8,128)(2,1)}, bf16[152,2048]{1,0:T(8,128)(2,1)}, u32[]{:S(2)}, u32[]{:S(2)}) collective-permute-start(bf16[152,2048]{1,0:T(8,128)(2,1)} %get-tuple-element.208), channel_id=1, source_target_pairs={{0,6},{1,7},{2,4},{3,5},{4,2},{5,3},{6,0},{7,1},{8,14},{9,15},{10,... | collective-permute-start | bytes 1867784 | tf_op jit(solution)/shard_map/ppermute | solution.py:106
  1473.4 336.6 %reduce-scatter.39.cloned.1.call-start = ((), (), s32[]{:S(2)}) async-start(), calls=%async_computation.36 | async-start | bytes 409600 | tf_op jit(solution)/shard_map/reduce_scatter | solution.py:125
  1479.1 121.0 %collective-permute-start.61 = (bf16[4,152,2048]{2,1,0:T(8,128)(2,1)}, bf16[4,152,2048]{2,1,0:T(8,128)(2,1)}, u32[]{:S(2)}, u32[]{:S(2)}) collective-permute-start(bf16[4,152,2048]{2,1,0:T(8,128)(2,1)} %bitcast.62), channel_id=1, source_target_pairs={{0,1},{1,0},{2,3},{3,2},{4,5},{5,4},{6,7},{7,6},{8,9},{9,8},{10,11... | collective-permute-start | bytes 7471112 | tf_op jit(solution)/shard_map/ppermute | solution.py:113
  1483.1 75.8 %collective-permute-start.21 = (bf16[320,2048]{1,0:T(8,128)(2,1)}, bf16[320,2048]{1,0:T(8,128)(2,1)}, u32[]{:S(2)}, u32[]{:S(2)}) collective-permute-start(bf16[320,2048]{1,0:T(8,128)(2,1)} %fusion.83), channel_id=1, source_target_pairs={{0,8},{8,16},{16,24},{24,0},{1,9},{9,17},{17,25},{25,1},{2,10},{10... | collective-permute-start | bytes 3932168 | tf_op jit(solution)/shard_map/ppermute | solution.py:99
  1489.2 68.4 %collective-permute-start.40 = (bf16[152,2048]{1,0:T(8,128)(2,1)}, bf16[152,2048]{1,0:T(8,128)(2,1)}, u32[]{:S(2)}, u32[]{:S(2)}) collective-permute-start(bf16[152,2048]{1,0:T(8,128)(2,1)} %get-tuple-element.198), channel_id=1, source_target_pairs={{0,2},{1,3},{2,0},{3,1},{4,6},{5,7},{6,4},{7,5},{8,10},{9,11},{10,... | collective-permute-start | bytes 1867784 | tf_op jit(solution)/shard_map/ppermute | solution.py:106
  1490.6 68.3 %collective-permute-start.41 = (bf16[152,2048]{1,0:T(8,128)(2,1)}, bf16[152,2048]{1,0:T(8,128)(2,1)}, u32[]{:S(2)}, u32[]{:S(2)}) collective-permute-start(bf16[152,2048]{1,0:T(8,128)(2,1)} %get-tuple-element.197), channel_id=1, source_target_pairs={{0,4},{1,5},{2,6},{3,7},{4,0},{5,1},{6,2},{7,3},{8,12},{9,13},{10,... | collective-permute-start | bytes 1867784 | tf_op jit(solution)/shard_map/ppermute | solution.py:106
  1491.2 67.7 %collective-permute-start.42 = (bf16[152,2048]{1,0:T(8,128)(2,1)}, bf16[152,2048]{1,0:T(8,128)(2,1)}, u32[]{:S(2)}, u32[]{:S(2)}) collective-permute-start(bf16[152,2048]{1,0:T(8,128)(2,1)} %get-tuple-element.196), channel_id=1, source_target_pairs={{0,6},{1,7},{2,4},{3,5},{4,2},{5,3},{6,0},{7,1},{8,14},{9,15},{10,... | collective-permute-start | bytes 1867784 | tf_op jit(solution)/shard_map/ppermute | solution.py:106
  1540.5 293.1 %reduce-scatter.25.cloned.1.call-start = ((), (), s32[]{:S(2)}) async-start(), calls=%async_computation.25 | async-start | bytes 655360 | tf_op jit(solution)/shard_map/reduce_scatter | solution.py:125
  1557.6 131.0 %collective-permute-start.81 = (bf16[152,2048]{1,0:T(8,128)(2,1)}, bf16[152,2048]{1,0:T(8,128)(2,1)}, u32[]{:S(2)}, u32[]{:S(2)}) collective-permute-start(bf16[152,2048]{1,0:T(8,128)(2,1)} %get-tuple-element.222), channel_id=1, source_target_pairs={{0,2},{1,3},{2,0},{3,1},{4,6},{5,7},{6,4},{7,5},{8,10},{9,11},{10,... | collective-permute-start | bytes 1867784 | tf_op jit(solution)/shard_map/ppermute | solution.py:106
  1563.3 84.0 %collective-permute-start.43 = (bf16[320,2048]{1,0:T(8,128)(2,1)}, bf16[320,2048]{1,0:T(8,128)(2,1)}, u32[]{:S(2)}, u32[]{:S(2)}) collective-permute-start(bf16[320,2048]{1,0:T(8,128)(2,1)} %add_convert_fusion.11), channel_id=1, source_target_pairs={{0,8},{8,16},{16,24},{24,0},{1,9},{9,17},{17,25},{25,1},{2,10},{10... | collective-permute-start | bytes 3932168 | tf_op jit(solution)/shard_map/ppermute | solution.py:99
  1600.1 262.5 %all-gather.34.cloned.1.call-start = ((), (), s32[]{:S(2)}) async-start(), calls=%async_computation.28 | async-start | bytes 1310720 | tf_op jit(solution)/shard_map/all_gather | solution.py:126
  1605.0 39.3 %collective-permute-start.62 = (bf16[152,2048]{1,0:T(8,128)(2,1)}, bf16[152,2048]{1,0:T(8,128)(2,1)}, u32[]{:S(2)}, u32[]{:S(2)}) collective-permute-start(bf16[152,2048]{1,0:T(8,128)(2,1)} %get-tuple-element.186), channel_id=1, source_target_pairs={{0,2},{1,3},{2,0},{3,1},{4,6},{5,7},{6,4},{7,5},{8,10},{9,11},{10,... | collective-permute-start | bytes 1867784 | tf_op jit(solution)/shard_map/ppermute | solution.py:106
  1606.5 39.4 %collective-permute-start.63 = (bf16[152,2048]{1,0:T(8,128)(2,1)}, bf16[152,2048]{1,0:T(8,128)(2,1)}, u32[]{:S(2)}, u32[]{:S(2)}) collective-permute-start(bf16[152,2048]{1,0:T(8,128)(2,1)} %get-tuple-element.185), channel_id=1, source_target_pairs={{0,4},{1,5},{2,6},{3,7},{4,0},{5,1},{6,2},{7,3},{8,12},{9,13},{10,... | collective-permute-start | bytes 1867784 | tf_op jit(solution)/shard_map/ppermute | solution.py:106
  1607.0 40.2 %collective-permute-start.64 = (bf16[152,2048]{1,0:T(8,128)(2,1)}, bf16[152,2048]{1,0:T(8,128)(2,1)}, u32[]{:S(2)}, u32[]{:S(2)}) collective-permute-start(bf16[152,2048]{1,0:T(8,128)(2,1)} %get-tuple-element.184), channel_id=1, source_target_pairs={{0,6},{1,7},{2,4},{3,5},{4,2},{5,3},{6,0},{7,1},{8,14},{9,15},{10,... | collective-permute-start | bytes 1867784 | tf_op jit(solution)/shard_map/ppermute | solution.py:106
  1629.4 272.2 %all-gather.32.cloned.1.call-start = ((), (), s32[]{:S(2)}) async-start(), calls=%async_computation.22 | async-start | bytes 1966080 | tf_op jit(solution)/shard_map/all_gather | solution.py:126
  1644.4 44.2 %collective-permute-start.82 = (bf16[152,2048]{1,0:T(8,128)(2,1)}, bf16[152,2048]{1,0:T(8,128)(2,1)}, u32[]{:S(2)}, u32[]{:S(2)}) collective-permute-start(bf16[152,2048]{1,0:T(8,128)(2,1)} %get-tuple-element.221), channel_id=1, source_target_pairs={{0,4},{1,5},{2,6},{3,7},{4,0},{5,1},{6,2},{7,3},{8,12},{9,13},{10,... | collective-permute-start | bytes 1867784 | tf_op jit(solution)/shard_map/ppermute | solution.py:106
  1645.8 42.8 %collective-permute-start.83 = (bf16[152,2048]{1,0:T(8,128)(2,1)}, bf16[152,2048]{1,0:T(8,128)(2,1)}, u32[]{:S(2)}, u32[]{:S(2)}) collective-permute-start(bf16[152,2048]{1,0:T(8,128)(2,1)} %get-tuple-element.220), channel_id=1, source_target_pairs={{0,6},{1,7},{2,4},{3,5},{4,2},{5,3},{6,0},{7,1},{8,14},{9,15},{10,... | collective-permute-start | bytes 1867784 | tf_op jit(solution)/shard_map/ppermute | solution.py:106
  1651.5 47.2 %collective-permute-start.65 = (bf16[320,2048]{1,0:T(8,128)(2,1)}, bf16[320,2048]{1,0:T(8,128)(2,1)}, u32[]{:S(2)}, u32[]{:S(2)}) collective-permute-start(bf16[320,2048]{1,0:T(8,128)(2,1)} %add_convert_fusion.10), channel_id=1, source_target_pairs={{0,8},{8,16},{16,24},{24,0},{1,9},{9,17},{17,25},{25,1},{2,10},{10... | collective-permute-start | bytes 3932168 | tf_op jit(solution)/shard_map/ppermute | solution.py:99
  (373 other events, 6366.7 us)
Sparse Core Ops, SparseCore 0:
  14.0 32.4 all-gather.15
  48.9 31.2 all-gather.29
  82.3 60.1 all-gather.17
  144.3 37.4 all-gather.19
  183.6 72.1 all-gather.21
  257.5 54.3 all-gather.23
  314.3 31.7 all-gather.27
  348.0 50.4 all-gather.25
  1113.7 34.5 reduce-scatter.36
  1152.0 70.2 reduce-scatter.26
  1225.9 92.4 reduce-scatter.16
  1322.1 44.8 reduce-scatter.32
  1371.4 44.8 reduce-scatter.30
  1420.2 53.1 reduce-scatter.34
  1477.0 61.5 reduce-scatter.20
  1542.2 57.8 reduce-scatter.22
  1602.2 27.1 reduce-scatter.28
  1631.6 42.2 reduce-scatter.18
  1675.5 42.4 all-gather.39
  1719.5 33.6 all-gather.37
  1754.9 33.1 all-gather.35
  1791.0 18.9 reduce-scatter.38
  1812.4 19.6 reduce-scatter.24
  1833.6 28.9 all-gather.33
  1864.3 37.2 all-gather.31

commit v2 on v1

v2 whole, which is shorter than its diff:
```python
import functools

import jax
import jax.numpy as jnp
from jax import lax
from jax.experimental import pallas as pl
from jax.experimental.layout import Layout, with_layout_constraint
from jax.experimental.pallas import tpu as pltpu
from jax.sharding import PartitionSpec as P

HEADS = 16
NOPE = 128
ROPE = 64
VDIM = 128
KV_RANK = 512
TOP = 6
PROMPT = 512
PROMPTS = 2
CONT_LEN = 128
CONTS = 2


epsilon = 1e-06
masked_score = -1e30
bfloat = jnp.bfloat16
single = jnp.float32


EXTRA = 128
by_rows = Layout(major_to_minor=(0, 1))


def matmul(left, right):
    return jnp.dot(left, right, preferred_element_type=single)


def rms_forward(values, gain):
    inverse = lax.rsqrt(jnp.mean(values * values, axis=-1, keepdims=True) + epsilon)
    normal_part = values * inverse
    return (normal_part * gain, normal_part, inverse)


def rms_backward(grad_out, normal_part, inverse, gain):
    grad_normal = grad_out * gain
    grad_gain = jnp.sum(grad_out * normal_part, axis=0)
    grad_in = inverse * (
        grad_normal - normal_part * jnp.mean(grad_normal * normal_part, axis=-1, keepdims=True)
    )
    return (grad_in, grad_gain)


def rotary_tables(positions):
    exponent = jnp.arange(ROPE // 2, dtype=jnp.float32) * (2.0 / ROPE)
    frequency = jnp.exp(-jnp.log(10000.0) * exponent)
    angles = positions[:, None] * frequency[None, :]
    return (jnp.cos(angles), jnp.sin(angles))


def rotate(values, cos_table, sin_table):
    half_width = values.shape[-1] // 2
    first_half = values[..., :half_width]
    second = values[..., half_width:]
    return jnp.concatenate(
        [first_half * cos_table - second * sin_table, second * cos_table + first_half * sin_table],
        axis=-1,
    )


def lookup(table_values, wanted):
    matches = wanted[:, None] == jnp.arange(table_values.shape[0], dtype=jnp.int32)[None, :]
    return jnp.sum(jnp.where(matches, table_values[None, :], 0), axis=1)


def row_layout(device, local_row, block_order, link_table, block_len, cont_dev):
    prompt_rows = PROMPTS * 2 * block_len
    in_prompt = local_row < prompt_rows
    prompt_id = local_row // (2 * block_len)
    half_slot = local_row // block_len % 2
    prompt_pos = lookup(block_order, 2 * device + half_slot) * block_len + local_row % block_len
    cont_index = device * cont_dev + jnp.maximum(local_row - prompt_rows, 0)
    cont_id = jnp.minimum(cont_index // CONT_LEN, CONTS - 1)
    cont_pos = cont_index % CONT_LEN
    sequence = jnp.where(in_prompt, prompt_id, PROMPTS + cont_id)
    position = jnp.where(in_prompt, prompt_pos, cont_pos)
    linked = jnp.where(in_prompt, -1, lookup(link_table, cont_id))
    rotary = jnp.where(in_prompt, prompt_pos, PROMPT + cont_pos)
    return (sequence, position, linked, rotary)


def silu_grads(grad_act, gate_pre, up_pre):
    sigmoid_gate = jax.nn.sigmoid(gate_pre)
    grad_gate = (grad_act * up_pre * sigmoid_gate * (1.0 + gate_pre * (1.0 - sigmoid_gate))).astype(
        bfloat
    )
    grad_up = (grad_act * gate_pre * sigmoid_gate).astype(bfloat)
    return (grad_gate, grad_up)


NT = (((1,), (1,)), ((), ()))
TN = (((0,), (0,)), ((), ()))


def product(left, right, dims):
    return lax.dot_general(left, right, dims, preferred_element_type=single)


def half_swap(values):
    width = values.shape[1]
    lane = lax.broadcasted_iota(jnp.int32, values.shape, 1)
    ahead = pltpu.roll(values, width - ROPE // 2, 1)
    behind = pltpu.roll(values, ROPE // 2, 1)
    return jnp.where(lane % ROPE < ROPE // 2, ahead, behind)


def head_query(nope, rotated, which):
    lane = lax.broadcasted_iota(jnp.int32, rotated.shape, 1)
    kept = jnp.where((lane >= ROPE) == (which == 1), rotated, 0.0)
    return jnp.concatenate(
        [nope[:, which * NOPE : (which + 1) * NOPE].astype(bfloat), kept.astype(bfloat)], axis=1
    )


def attend_kernel(
    rows, scale, link, nope, rope, cos, sin, keys, values, key_rope, prompt_mask, cont_mask, out, lse
):
    pair = pl.program_id(0)
    prompt_rows, cont_rows = rows
    first = prompt_rows * PROMPTS
    linked = pl.multiple_of(link[0] * PROMPT, PROMPT)
    rotated = rope[...] * cos[...] + half_swap(rope[...]) * sin[...]
    nopes = nope[...]

    @pl.when(pair == 0)
    def _():
        lse[...] = jnp.zeros_like(lse)

    def key_part(start, count, which):
        return jnp.concatenate(
            [keys[pl.ds(start, count), which * NOPE : (which + 1) * NOPE], key_rope[pl.ds(start, count), :]],
            axis=1,
        )

    def value_part(start, count, which):
        return values[pl.ds(start, count), which * VDIM : (which + 1) * VDIM]

    for which in range(2):
        query = head_query(nopes, rotated, which)
        outs = []
        logs = []
        for prompt in range(PROMPTS):
            part = query[prompt * prompt_rows : (prompt + 1) * prompt_rows]
            scores = product(part, key_part(prompt * PROMPT, PROMPT, which), NT) * scale
            scores = scores + prompt_mask[...]
            top = jnp.max(scores, axis=1, keepdims=True)
            exps = jnp.exp(scores - top)
            total = jnp.sum(exps, axis=1, keepdims=True)
            probs = (exps / total).astype(bfloat)
            outs.append(matmul(probs, value_part(prompt * PROMPT, PROMPT, which)))
            logs.append(top + jnp.log(total))
        part = query[first:]
        cont_keys = CONTS * CONT_LEN
        scores = product(part, key_part(linked, PROMPT, which), NT) * scale
        near = product(part, key_part(PROMPTS * PROMPT, cont_keys, which), NT) * scale
        near = near + cont_mask[...]
        top = jnp.maximum(
            jnp.max(scores, axis=1, keepdims=True), jnp.max(near, axis=1, keepdims=True)
        )
        exps = jnp.exp(scores - top)
        near_exps = jnp.exp(near - top)
        total = jnp.sum(exps, axis=1, keepdims=True) + jnp.sum(near_exps, axis=1, keepdims=True)
        outs.append(
            matmul((exps / total).astype(bfloat), value_part(linked, PROMPT, which))
            + matmul(
                (near_exps / total).astype(bfloat), value_part(PROMPTS * PROMPT, cont_keys, which)
            )
        )
        logs.append(top + jnp.log(total))
        out[:, which * VDIM : (which + 1) * VDIM] = jnp.concatenate(outs, axis=0).astype(bfloat)
        lane = lax.broadcasted_iota(jnp.int32, lse.shape, 1)
        lse[...] = jnp.where(lane == 2 * pair + which, jnp.concatenate(logs, axis=0), lse[...])


def attend_back_kernel(
    rows,
    scale,
    link,
    nope,
    rope,
    cos,
    sin,
    keys,
    values,
    key_rope,
    prompt_mask,
    cont_mask,
    lse,
    grad,
    grad_nope,
    grad_rope,
    grad_keys,
    grad_values,
    grad_key_rope,
    key_sum,
    value_sum,
    rope_sum,
):
    pair = pl.program_id(0)
    prompt_rows, cont_rows = rows
    first = prompt_rows * PROMPTS
    linked = pl.multiple_of(link[0] * PROMPT, PROMPT)
    cont_start = PROMPTS * PROMPT
    cont_keys = CONTS * CONT_LEN
    rotated = rope[...] * cos[...] + half_swap(rope[...]) * sin[...]
    nopes = nope[...]

    @pl.when(pair == 0)
    def _():
        rope_sum[...] = jnp.zeros_like(rope_sum)

    rope_grads = []
    for which in range(2):
        query = head_query(nopes, rotated, which)
        log_row = lse[which : which + 1, :]
        query_grads = []

        def one(lo, hi, start, count, mask):
            part = query[lo:hi]
            key_cat = jnp.concatenate(
                [
                    keys[pl.ds(start, count), which * NOPE : (which + 1) * NOPE],
                    key_rope[pl.ds(start, count), :],
                ],
                axis=1,
            )
            value = values[pl.ds(start, count), which * VDIM : (which + 1) * VDIM]
            grad_part = grad[lo:hi, which * VDIM : (which + 1) * VDIM]
            scores = product(key_cat, part, NT) * scale
            if mask is not None:
                scores = scores + mask
            probs = jnp.exp(scores - log_row[:, lo:hi])
            grad_probs = product(value, grad_part, NT)
            return part, key_cat, grad_part, probs, grad_probs

        def finish(parts, delta):
            part, key_cat, grad_part, probs, grad_probs = parts
            grad_scores = (probs * (grad_probs - delta)).astype(bfloat)
            query_grad = product(grad_scores, key_cat, TN)
            key_grad = matmul(grad_scores, part) * scale
            value_grad = matmul(probs.astype(bfloat), grad_part)
            return query_grad, key_grad, value_grad

        def delta_of(parts):
            return jnp.sum(parts[3] * parts[4], axis=0, keepdims=True)

        for prompt in range(PROMPTS):
            lo, hi = prompt * prompt_rows, (prompt + 1) * prompt_rows
            start = prompt * PROMPT
            parts = one(lo, hi, start, PROMPT, prompt_mask[...])
            query_grad, key_grad, value_grad = finish(parts, delta_of(parts))
            query_grads.append(query_grad)
            key_sum[start : start + PROMPT, :] = key_grad[:, :NOPE]
            value_sum[start : start + PROMPT, :] = value_grad
            rope_sum[start : start + PROMPT, :] += key_grad[:, NOPE:]
        far = one(first, first + cont_rows, linked, PROMPT, None)
        near = one(first, first + cont_rows, cont_start, cont_keys, cont_mask[...])
        delta = delta_of(far) + delta_of(near)
        far_query, far_key, far_value = finish(far, delta)
        near_query, near_key, near_value = finish(near, delta)
        query_grads.append(far_query + near_query)
        span = pl.ds(linked, PROMPT)
        key_sum[span, :] += far_key[:, :NOPE]
        value_sum[span, :] += far_value
        rope_sum[span, :] += far_key[:, NOPE:]
        key_sum[cont_start:, :] = near_key[:, :NOPE]
        value_sum[cont_start:, :] = near_value
        rope_sum[cont_start:, :] += near_key[:, NOPE:]
        query_grad = jnp.concatenate(query_grads, axis=0) * scale
        grad_nope[:, which * NOPE : (which + 1) * NOPE] = query_grad[:, :NOPE].astype(bfloat)
        rope_grads.append(query_grad[:, NOPE:])
        grad_keys[:, which * NOPE : (which + 1) * NOPE] = key_sum[...].astype(bfloat)
        grad_values[:, which * VDIM : (which + 1) * VDIM] = value_sum[...].astype(bfloat)
    lane = lax.broadcasted_iota(jnp.int32, rope_grads[0].shape, 1)
    both = jnp.where(lane < ROPE, rope_grads[0], rope_grads[1])
    grad_rope[...] = (both * cos[...] - half_swap(both) * sin[...]).astype(bfloat)
    grad_key_rope[...] = rope_sum[...]


def whole(shape):
    return pl.BlockSpec(shape, lambda pair: (0,) * len(shape))


def pair_specs(tokens, key_rows, prompt_mask, cont_mask):
    nope_blocks = HEADS * NOPE // (2 * ROPE)
    return [
        pl.BlockSpec(memory_space=pltpu.SMEM),
        pl.BlockSpec((tokens, 2 * NOPE), lambda pair: (0, pair)),
        pl.BlockSpec((tokens, 2 * ROPE), lambda pair: (0, nope_blocks + pair)),
        whole((tokens, 2 * ROPE)),
        whole((tokens, 2 * ROPE)),
        pl.BlockSpec((key_rows, 2 * NOPE), lambda pair: (0, pair)),
        pl.BlockSpec((key_rows, 2 * VDIM), lambda pair: (0, HEADS // 2 + pair)),
        whole((key_rows, 2 * ROPE)),
        whole(prompt_mask),
        whole(cont_mask),
    ]


def attend(rows, scale, link, query_pre, cos, sin, kv, key_rope, prompt_mask, cont_mask):
    tokens = query_pre.shape[0]
    key_rows = kv.shape[0]
    work = 2 * (rows[0] * PROMPT * PROMPTS + rows[1] * (PROMPT + CONTS * CONT_LEN)) * HEADS
    return pl.pallas_call(
        functools.partial(attend_kernel, rows, scale),
        grid=(HEADS // 2,),
        in_specs=pair_specs(tokens, key_rows, prompt_mask.shape, cont_mask.shape),
        out_specs=[
            pl.BlockSpec((tokens, 2 * VDIM), lambda pair: (0, pair)),
            whole((tokens, 128)),
        ],
        out_shape=[
            jax.ShapeDtypeStruct((tokens, HEADS * VDIM), bfloat),
            jax.ShapeDtypeStruct((tokens, 128), single),
        ],
        compiler_params=pltpu.CompilerParams(vmem_limit_bytes=40 * 2**20),
        cost_estimate=pl.CostEstimate(
            flops=work * 384, bytes_accessed=2 * kv.size + 6 * query_pre.size, transcendentals=work // 2
        ),
    )(link, query_pre, query_pre, cos, sin, kv, kv, key_rope, prompt_mask, cont_mask)


def attend_back(
    rows, scale, link, query_pre, cos, sin, kv, key_rope, prompt_mask, cont_mask, lse, grad
):
    tokens = query_pre.shape[0]
    key_rows = kv.shape[0]
    work = 2 * (rows[0] * PROMPT * PROMPTS + rows[1] * (PROMPT + CONTS * CONT_LEN)) * HEADS
    return pl.pallas_call(
        functools.partial(attend_back_kernel, rows, scale),
        grid=(HEADS // 2,),
        in_specs=pair_specs(tokens, key_rows, prompt_mask.shape, cont_mask.shape)
        + [
            pl.BlockSpec((None, 2, tokens), lambda pair: (pair, 0, 0)),
            pl.BlockSpec((tokens, 2 * VDIM), lambda pair: (0, pair)),
        ],
        out_specs=[
            pl.BlockSpec((tokens, 2 * NOPE), lambda pair: (0, pair)),
            pl.BlockSpec((tokens, 2 * ROPE), lambda pair: (0, pair)),
            pl.BlockSpec((key_rows, 2 * NOPE), lambda pair: (0, pair)),
            pl.BlockSpec((key_rows, 2 * VDIM), lambda pair: (0, pair)),
            whole((key_rows, 2 * ROPE)),
        ],
        out_shape=[
            jax.ShapeDtypeStruct((tokens, HEADS * NOPE), bfloat),
            jax.ShapeDtypeStruct((tokens, HEADS * ROPE), bfloat),
            jax.ShapeDtypeStruct((key_rows, HEADS * NOPE), bfloat),
            jax.ShapeDtypeStruct((key_rows, HEADS * VDIM), bfloat),
            jax.ShapeDtypeStruct((key_rows, 2 * ROPE), single),
        ],
        scratch_shapes=[
            pltpu.VMEM((key_rows, NOPE), single),
            pltpu.VMEM((key_rows, VDIM), single),
            pltpu.VMEM((key_rows, 2 * ROPE), single),
        ],
        compiler_params=pltpu.CompilerParams(vmem_limit_bytes=48 * 2**20),
        cost_estimate=pl.CostEstimate(
            flops=work * 1152, bytes_accessed=4 * kv.size + 10 * query_pre.size, transcendentals=work // 2
        ),
    )(link, query_pre, query_pre, cos, sin, kv, kv, key_rope, prompt_mask, cont_mask, lse, grad)


def expert_kernel(
    first_row,
    experts,
    expert,
    mine,
    theirs,
    grad_mine,
    grad_theirs,
    gate,
    up,
    down,
    *refs,
):
    back_mine, back_theirs, out_mine, out_theirs = refs[-21:-17]
    all_rows, all_grads, all_act, all_gate, all_up = refs[-17:-12]
    rows, grads, gate_w, up_w, down_w, act, grad_gate, grad_up, back, out = refs[-12:-2]
    in_sems, out_sems = refs[-2:]
    count = mine.shape[0]
    hidden, width = gate.shape
    lane = lax.broadcasted_iota(jnp.int32, (count, EXTRA), 1)
    here = lane == expert[0]
    loads = [
        pltpu.make_async_copy(source, target, in_sems.at[i])
        for i, (source, target) in enumerate(
            [
                (theirs, rows.at[1]),
                (gate, gate_w),
                (up, up_w),
                (grad_theirs, grads.at[1]),
                (down, down_w),
                (mine, rows.at[0]),
                (grad_mine, grads.at[0]),
            ]
        )
    ]
    for load in loads:
        load.start()

    def stores(half):
        span = pl.ds(first_row + half * count, count)
        pairs = [
            (back.at[half], (back_mine, back_theirs)[half]),
            (out.at[half], (out_mine, out_theirs)[half]),
            (rows.at[half, :, pl.ds(0, width)], all_rows.at[span, :]),
            (grads.at[half], all_grads.at[span, :]),
            (act.at[half], all_act.at[span, :]),
            (grad_gate.at[half], all_gate.at[span, :]),
            (grad_up.at[half], all_up.at[span, :]),
        ]
        return [
            pltpu.make_async_copy(source, target, out_sems.at[half, i])
            for i, (source, target) in enumerate(pairs)
        ]

    def one_half(turn, carry):
        half = 1 - turn

        @pl.when(turn == 0)
        def _():
            for load in loads[:5]:
                load.wait()

        @pl.when(turn == 1)
        def _():
            for load in loads[5:]:
                load.wait()

        extra = rows[half, :, width:].astype(single)
        slot_weight = jnp.sum(
            jnp.where(here | (lane == expert[0] + experts), extra, 0.0), axis=1, keepdims=True
        )
        total = jnp.zeros((count, 1), single)
        for lo in range(0, hidden, 256):
            hi = min(lo + 256, hidden)
            gate_pre = product(rows[half, :, :width], gate_w[lo:hi, :], NT)
            up_pre = product(rows[half, :, :width], up_w[lo:hi, :], NT)
            grad_act = product(grads[half], down_w[lo:hi, :], NT)
            sigmoid = 1.0 / (1.0 + jnp.exp(-gate_pre))
            silu = gate_pre * sigmoid
            value = silu * up_pre
            total = total + jnp.sum(
                value.astype(bfloat).astype(single) * grad_act, axis=1, keepdims=True
            )
            grad_act = grad_act * slot_weight
            act[half, :, lo:hi] = (value * slot_weight).astype(bfloat)
            grad_gate[half, :, lo:hi] = (
                grad_act * up_pre * sigmoid * (1.0 + gate_pre * (1.0 - sigmoid))
            ).astype(bfloat)
            grad_up[half, :, lo:hi] = (grad_act * silu).astype(bfloat)
        back[half, :, width:] = jnp.where(here, total, 0.0).astype(bfloat)
        step = min(512, width)
        for lo in range(0, width, step):
            hi = lo + step
            part = matmul(grad_gate[half], gate_w[:, lo:hi])
            part = part + matmul(grad_up[half], up_w[:, lo:hi])
            back[half, :, lo:hi] = part.astype(bfloat)
        for lo in range(0, width, step):
            hi = lo + step
            out[half, :, lo:hi] = matmul(act[half], down_w[:, lo:hi]).astype(bfloat)

        @pl.when(turn == 0)
        def _():
            for store in stores(1):
                store.start()

        @pl.when(turn == 1)
        def _():
            for store in stores(0):
                store.start()

        return carry

    lax.fori_loop(0, 2, one_half, 0)
    for half in range(2):
        for store in stores(half):
            store.wait()


def expert_call(
    step, steps, experts, expert, mine, theirs, grad_mine, grad_theirs, gate, up, down, kept
):
    count, wide = mine.shape
    hidden, width = gate.shape
    anywhere = pl.BlockSpec(memory_space=pl.ANY)
    back_shape = jax.ShapeDtypeStruct((count, wide), bfloat)
    out_shape = jax.ShapeDtypeStruct((count, width), bfloat)
    kept_shapes = [
        jax.ShapeDtypeStruct((steps * 2 * count, columns), bfloat)
        for columns in (width, width, hidden, hidden, hidden)
    ]
    outs = pl.pallas_call(
        functools.partial(expert_kernel, step * 2 * count, experts),
        in_specs=[pl.BlockSpec(memory_space=pltpu.SMEM)] + [anywhere] * (7 + len(kept)),
        out_specs=[anywhere] * 9,
        out_shape=[back_shape] * 2 + [out_shape] * 2 + kept_shapes,
        input_output_aliases={8 + i: 4 + i for i in range(len(kept))},
        scratch_shapes=[
            pltpu.VMEM((2, count, wide), bfloat),
            pltpu.VMEM((2, count, width), bfloat),
        ]
        + [pltpu.VMEM((hidden, width), bfloat)] * 3
        + [pltpu.VMEM((2, count, hidden), bfloat)] * 3
        + [pltpu.VMEM((2, count, wide), bfloat), pltpu.VMEM((2, count, width), bfloat)]
        + [pltpu.SemaphoreType.DMA((7,)), pltpu.SemaphoreType.DMA((2, 7))],
        compiler_params=pltpu.CompilerParams(vmem_limit_bytes=56 * 2**20),
        cost_estimate=pl.CostEstimate(
            flops=2 * 6 * 2 * count * width * hidden,
            bytes_accessed=2 * (12 * count * width + 3 * hidden * width + 6 * count * hidden),
            transcendentals=2 * count * hidden,
        ),
    )(expert, mine, theirs, grad_mine, grad_theirs, gate, up, down, *kept)
    return outs[:4], list(outs[4:])


def ring_next(value):
    size = lax.axis_size("ctx")
    return lax.ppermute(value, "ctx", [(i, (i + 1) % size) for i in range(size)])


def to_chips(value):
    size = lax.axis_size("fsdp")
    return lax.all_to_all(
        value,
        "fsdp",
        split_axis=0,
        concat_axis=0,
        tiled=True,
        axis_index_groups=[list(range(core, size, 2)) for core in range(2)],
    )


def to_core(value):
    size = lax.axis_size("fsdp")
    return lax.ppermute(value, "fsdp", [(i, i ^ 1) for i in range(size)])


def gather_rows(value):
    return lax.all_gather(value, "fsdp", axis=0, tiled=True)


def scatter_rows(value):
    return lax.psum_scatter(value.astype(bfloat), "fsdp", scatter_dimension=0, tiled=True)


def along_ctx(value, shift):
    size = lax.axis_size("ctx")
    return lax.ppermute(value, "ctx", [(i, (i + shift) % size) for i in range(size)])


def sum_ctx(value):
    size = lax.axis_size("ctx")
    device = lax.axis_index("ctx")
    low = ctx_total(value, device).astype(bfloat)
    pieces = [low] + [along_ctx(low, shift) for shift in range(1, size)]
    return in_order([piece.astype(single) for piece in pieces], device)


def in_order(pieces, device, axis=0):
    size = len(pieces)
    count = pieces[0].shape[axis]
    shape = list(pieces[0].shape)
    shape[axis] = size * count
    result = jnp.zeros(shape, pieces[0].dtype)
    for shift, piece in enumerate(pieces):
        owner = (device - shift + size) % size
        result = lax.dynamic_update_slice_in_dim(result, piece, owner * count, axis=axis)
    return result


def together(*values):
    return lax.optimization_barrier(values)


def ctx_total(group, device):
    size = lax.axis_size("ctx")
    count = group.shape[0] // size

    def share(owner):
        return lax.dynamic_slice_in_dim(group, owner % size * count, count, axis=0)

    total = share(device).astype(single)
    for shift in range(1, size):
        total = total + along_ctx(share(device + shift), shift).astype(single)
    return total


def rank_table(route_block, experts, capacity):
    tokens = route_block.shape[0]
    expert_ids = jnp.arange(experts, dtype=jnp.int32)
    named = jnp.any(route_block[:, :, None] == expert_ids[None, None, :], axis=1)
    order = jnp.arange(tokens, dtype=jnp.int32)
    earlier = (order[:, None] > order[None, :]).astype(bfloat)
    rank = matmul(earlier, named.astype(bfloat)).astype(jnp.int32)
    return jnp.where(named & (rank < capacity), rank, -1)


def dispatch(rows):
    mine = to_chips(rows)
    return mine, to_core(mine)


def add_halves(mine, theirs):
    return (mine.astype(single) + to_core(theirs).astype(single)).astype(bfloat)


def local(
    layer_input,
    grad_output,
    routes,
    continuation_prompt,
    block_order,
    query_weight,
    latent_down,
    latent_up,
    output_weight,
    router_weight,
    shared_gate,
    shared_up,
    shared_down,
    attn_gain,
    latent_gain,
    ffn_gain,
    expert_gate,
    expert_up,
    expert_down,
):
    ctx_size = lax.axis_size("ctx")
    fsdp_size = lax.axis_size("fsdp")
    chips = fsdp_size // 2
    device = lax.axis_index("ctx")
    tokens = layer_input.shape[1]
    model_width = layer_input.shape[2]
    experts = router_weight.shape[1]
    group_tok = tokens * ctx_size
    block_len = PROMPT // (2 * ctx_size)
    cont_dev = CONTS * CONT_LEN // ctx_size
    capacity = (5 * tokens * TOP + 4 * experts - 1) // (4 * experts)
    slots = (capacity + 7) // 8 * 8
    score_scale = (NOPE + ROPE) ** (-0.5)
    shard_rows = latent_down.shape[0]
    down_width = latent_down.shape[1]
    hidden_dev = shared_down.shape[0] // ctx_size

    def hidden_columns(weight):
        parts = weight.reshape(shard_rows, fsdp_size, ctx_size, hidden_dev)
        return lax.dynamic_index_in_dim(parts, device, axis=2, keepdims=False).reshape(
            shard_rows, fsdp_size * hidden_dev
        )

    hidden_part = fsdp_size * hidden_dev
    part_down = lax.dynamic_slice_in_dim(shared_down, device * hidden_dev, hidden_dev, axis=0)
    part_shared = jnp.concatenate(
        [
            hidden_columns(shared_gate),
            hidden_columns(shared_up),
            part_down.reshape(shard_rows, hidden_part),
        ],
        axis=1,
    )

    own_rows = jnp.arange(tokens, dtype=jnp.int32)
    link_table = continuation_prompt[0]
    own_seq, own_pos, own_link, own_rotary = row_layout(
        device, own_rows, block_order, link_table, block_len, cont_dev
    )
    prompt_rows = 2 * block_len
    first_cont = PROMPTS * prompt_rows
    link = lookup(link_table, (device * cont_dev // CONT_LEN)[None])
    key_pos = (block_order[:, None] * block_len + jnp.arange(block_len, dtype=jnp.int32)).reshape(-1)
    prompt_mask = jnp.where(key_pos[None, :] <= own_pos[:prompt_rows, None], 0.0, masked_score)
    cont_rows = device * cont_dev + jnp.arange(cont_dev, dtype=jnp.int32)
    cont_ids = jnp.arange(CONTS * CONT_LEN, dtype=jnp.int32)
    cont_mask = jnp.where(
        (cont_ids[None, :] // CONT_LEN == cont_rows[:, None] // CONT_LEN)
        & (cont_ids[None, :] <= cont_rows[:, None]),
        0.0,
        masked_score,
    )
    cos_table, sin_table = rotary_tables(own_rotary.astype(single))
    pair_cos = jnp.concatenate([cos_table] * 4, axis=1)
    pair_sin = jnp.concatenate([-sin_table, sin_table] * 2, axis=1)

    def by_sequence(group):
        blocks = group.reshape(ctx_size, tokens, -1)
        parts = [
            blocks[:, p * prompt_rows : (p + 1) * prompt_rows].reshape(PROMPT, -1)
            for p in range(PROMPTS)
        ]
        return jnp.concatenate(parts + [blocks[:, first_cont:].reshape(CONTS * CONT_LEN, -1)])

    def by_block(group):
        parts = [
            group[p * PROMPT : (p + 1) * PROMPT].reshape(ctx_size, prompt_rows, -1)
            for p in range(PROMPTS)
        ]
        last = group[PROMPTS * PROMPT :].reshape(ctx_size, cont_dev, -1)
        return jnp.concatenate(parts + [last], axis=1).reshape(group_tok, -1)

    plane_experts = device * chips + jnp.arange(chips, dtype=jnp.int32)
    chosen_here = plane_experts[:, None] == jnp.arange(experts, dtype=jnp.int32)[None, :]
    def here(table):
        return jnp.sum(jnp.where(chosen_here[:, None, :], table[None], 0), axis=2)

    slot_ids = jnp.arange(slots, dtype=jnp.int32)

    def pick_rows(step, rows):
        return jnp.einsum(
            "jrt,td->jrd", slot_pick[step], rows, preferred_element_type=single
        ).astype(bfloat)

    def put_rows(step, results):
        return jnp.einsum("jrt,jrd->td", slot_pick[step], results, preferred_element_type=single)

    def add_slots(route_block):
        ranks = rank_table(route_block, experts, capacity)
        match = here(ranks)[:, None, :] == slot_ids[None, :, None]
        slot_pick.append(match.astype(bfloat))
        return ranks

    slot_pick = []
    own_ranks = add_slots(routes[0])
    packed = gather_rows(
        jnp.concatenate(
            [
                latent_down,
                router_weight,
                attn_gain[:, None],
                ffn_gain[:, None],
                jnp.pad(latent_gain, (0, shard_rows - latent_gain.shape[0]))[:, None],
            ],
            axis=1,
        )
    )
    route_ring = [along_ctx(routes[0], s) for s in range(1, ctx_size)]
    grad_ring = [grad_output[0]]
    grad_next = ring_next(grad_ring[0])
    grad_mine = [to_chips(pick_rows(0, grad_ring[0]))]
    grad_theirs = []
    packed, query_shard, route_ring, grad_next, grad_mine[0] = together(
        packed, query_weight, route_ring, grad_next, grad_mine[0]
    )

    for route_block in route_ring:
        add_slots(route_block)
    full_down = packed[:, :down_width]
    full_router = packed[:, down_width : down_width + experts]
    gain_attn = packed[:, down_width + experts].astype(single)
    gain_ffn = packed[:, down_width + experts + 1].astype(single)
    gain_latent = (
        packed[:, down_width + experts + 2]
        .reshape(fsdp_size, shard_rows)[:, : latent_gain.shape[0]]
        .reshape(-1)
        .astype(single)
    )
    inputs_full = layer_input[0].astype(single)
    normed, attn_normal, attn_inverse = rms_forward(inputs_full, gain_attn)
    normed_low = normed.astype(bfloat)
    latent_pre = matmul(normed_low, full_down)
    latent, latent_normal, latent_inverse = rms_forward(latent_pre[:, :KV_RANK], gain_latent)
    latent_low = latent.astype(bfloat)
    key_rope_own = rotate(latent_pre[:, KV_RANK:], cos_table, sin_table).astype(bfloat)
    key_own = jnp.concatenate([latent_low, key_rope_own], axis=1)

    def more_grad_rows():
        step = len(grad_mine)
        grad_ring.append(grad_next)
        following = ring_next(grad_next) if step + 1 < ctx_size else grad_next
        theirs = to_core(grad_mine[-1])
        return following, theirs, to_chips(pick_rows(step, grad_ring[step]))

    full_query = gather_rows(query_shard)
    key_pieces = [key_own] + [along_ctx(key_own, s) for s in range(1, ctx_size)]
    grad_next, theirs, mine = more_grad_rows()
    full_query, up_shard, key_pieces, grad_next, theirs, mine = together(
        full_query, latent_up, key_pieces, grad_next, theirs, mine
    )
    grad_theirs.append(theirs)
    grad_mine.append(mine)

    full_up = gather_rows(up_shard)
    query_pre = matmul(normed_low, full_query)
    grad_next, theirs, mine = more_grad_rows()
    full_up, output_shard, query_pre, grad_next, theirs, mine = together(
        full_up, output_weight, query_pre, grad_next, theirs, mine
    )
    grad_theirs.append(theirs)
    grad_mine.append(mine)

    full_output = gather_rows(output_shard)
    key_group = by_sequence(in_order(key_pieces, device))
    latent_group = key_group[:, :KV_RANK]
    rope_pair = jnp.concatenate([key_group[:, KV_RANK:]] * 2, axis=1)
    kv_group = matmul(latent_group, full_up).astype(bfloat)
    rows_here = (prompt_rows, cont_dev)
    attended_low, log_total = attend(
        rows_here,
        score_scale,
        link,
        query_pre,
        pair_cos,
        pair_sin,
        kv_group,
        rope_pair,
        prompt_mask,
        cont_mask,
    )
    while len(grad_mine) < ctx_size:
        grad_next, theirs, mine = more_grad_rows()
        grad_theirs.append(theirs)
        grad_mine.append(mine)
    full_output, shared_shard, attended_low, grad_mine, grad_theirs = together(
        full_output, part_shared, attended_low, grad_mine, grad_theirs
    )
    grad_theirs.append(to_core(grad_mine[-1]))

    part_shared = gather_rows(shared_shard)
    hidden = inputs_full + matmul(attended_low, full_output)
    ffn_in, ffn_normal, ffn_inverse = rms_forward(hidden, gain_ffn)
    ffn_low = ffn_in.astype(bfloat)
    logits = matmul(ffn_low, full_router)
    router_exps = jnp.exp(logits - jnp.max(logits, axis=1, keepdims=True))
    router = router_exps / jnp.sum(router_exps, axis=1, keepdims=True)
    route_match = jnp.any(
        routes[0][:, :, None] == jnp.arange(experts, dtype=jnp.int32)[None, None, :], axis=1
    )
    chosen_total = jnp.sum(jnp.where(route_match, router, 0.0), axis=1, keepdims=True)
    gates = jnp.where(route_match, router, 0.0) / chosen_total
    pair_weight = jnp.where(own_ranks >= 0, gates, 0.0)

    weight_high = pair_weight.astype(bfloat)
    weight_low = (pair_weight - weight_high.astype(single)).astype(bfloat)
    ffn_wide = jnp.concatenate(
        [
            ffn_low,
            weight_high,
            weight_low,
            jnp.zeros((tokens, EXTRA - 2 * experts), bfloat),
        ],
        axis=1,
    )
    own_expert = (device * chips + lax.axis_index("fsdp") // 2)[None].astype(jnp.int32)
    kept = []
    out_sends = []

    def flat(rows):
        return rows.reshape(-1, rows.shape[-1])

    def expert_step(step, mine, theirs):
        results, kept[:] = expert_call(
            step,
            ctx_size,
            experts,
            own_expert,
            flat(mine),
            flat(theirs),
            flat(grad_mine[step]),
            flat(grad_theirs[step]),
            expert_gate[0].T,
            expert_up[0].T,
            expert_down[0],
            kept,
        )
        shaped = [rows.reshape(chips, slots, -1) for rows in results]
        out_sends.append(shaped[2:])
        return shaped[:2]

    def shared_step(first):
        rows = jnp.concatenate([block[:, :model_width] for block in ffn_ring[first : first + 2]])
        grads = jnp.concatenate(grad_ring[first : first + 2])
        gate_pre = matmul(rows, part_gate)
        up_pre = matmul(rows, part_up)
        act = (jax.nn.silu(gate_pre) * up_pre).astype(bfloat)
        grad_act = jnp.einsum("td,fd->tf", grads, part_down, preferred_element_type=single)
        grad_gate, grad_up = silu_grads(grad_act, gate_pre, up_pre)
        back = jnp.einsum("tf,df->td", grad_gate, part_gate, preferred_element_type=single)
        back = back + jnp.einsum("tf,df->td", grad_up, part_up, preferred_element_type=single)
        return rows, grads, act, grad_gate, grad_up, back

    def shared_grads():
        rows, grads, act, grad_gate, grad_up = [
            jnp.concatenate([part[i] for part in shared]) for i in range(5)
        ]
        pieces = [
            jnp.einsum("ta,tb->ab", left, right, preferred_element_type=single).astype(bfloat)
            for left, right in ((rows, grad_gate), (rows, grad_up), (act, grads))
        ]
        return jnp.concatenate(pieces[:2] + [pieces[2].reshape(model_width, hidden_part)], axis=1)

    def block_rows(parts, step):
        first = step % 2 * tokens
        return parts[step // 2][first : first + tokens]

    ffn_ring = [ffn_wide]
    shared = []
    mines, backs, added, returned, out_added = {}, {}, {}, {}, {}
    moving = None
    first_part = None

    def block_part(step):
        part = put_rows(step, returned[step])
        return part + jnp.pad(block_rows([p[5] for p in shared], step), ((0, 0), (0, EXTRA)))

    def hop(step):
        part = block_part(step)
        if moving is not None:
            part = part + moving.astype(single)
        return ring_next(part.astype(bfloat))

    for tick in range(ctx_size + 1):
        sent = {}
        if tick < ctx_size:
            sent["mine"] = to_chips(pick_rows(tick, ffn_ring[tick]))
            if tick + 1 < ctx_size:
                sent["ring"] = ring_next(ffn_ring[tick])
        else:
            sent["returned"] = to_chips(added[tick - 2])
        if tick >= 1:
            sent["back"] = expert_step(tick - 1, *mines[tick - 1])
        if 1 <= tick - 3 <= ctx_size - 3:
            sent["moving"] = hop(tick - 3)
        if tick == 0:
            sent["theirs"] = grad_theirs[-1]
        if tick == 1:
            sent["shared"] = part_shared
        names = sorted(sent)
        sent = dict(zip(names, together(*(sent[name] for name in names))))
        if tick + 1 < ctx_size:
            ffn_ring.append(sent["ring"])
        if tick >= 1:
            backs[tick - 1] = sent["back"]
        if tick == ctx_size:
            returned[tick - 2] = sent["returned"]
        moving = sent.get("moving", moving)
        if tick == 0:
            grad_theirs[-1] = sent["theirs"]
        if tick == 1:
            part_gate = sent["shared"][:, :hidden_part]
            part_up = sent["shared"][:, hidden_part : 2 * hidden_part]
            part_down = sent["shared"][:, 2 * hidden_part :].reshape(hidden_part, model_width)

        sends = {}
        if tick < ctx_size:
            sends["theirs"] = to_core(sent["mine"])
            sends["mine"] = sent["mine"]
        if tick >= 1:
            sends["added"] = add_halves(*backs[tick - 1])
        if 2 <= tick < ctx_size:
            sends["returned"] = to_chips(added[tick - 2])
        for pair in range(ctx_size // 2):
            if tick == min(2 * pair + 2, ctx_size - 1):
                shared.append(shared_step(2 * pair))
        if tick == 3:
            sends["first"] = block_part(0)
        if tick == ctx_size:
            sends["returned"] = to_chips(sends["added"])
            sends["moving"] = hop(ctx_size - 2)
            sends["shared_grads"] = shared_grads()
            sends["out"] = add_halves(*out_sends[1])
        names = sorted(sends)
        sends = dict(zip(names, together(*(sends[name] for name in names))))
        if tick < ctx_size:
            mines[tick] = (sends["mine"], sends["theirs"])
        if tick >= 1:
            added[tick - 1] = sends["added"]
        if 2 <= tick < ctx_size:
            returned[tick - 2] = sends["returned"]
        if tick == 3:
            first_part = sends["first"]
        if tick == ctx_size:
            returned[ctx_size - 1] = sends["returned"]
            moving = sends["moving"]
            out_added = sends["out"]

    shared_part = scatter_rows(sends["shared_grads"])
    out_steps = {}

    def next_out(step):
        ahead = (step + 1) % ctx_size
        return to_chips(out_added), add_halves(*out_sends[ahead]) if step else out_added

    moving, (out_steps[1], out_added) = together(hop(ctx_size - 1), next_out(1))
    grad_wide = moving.astype(single) + first_part
    grad_ffn = grad_wide[:, :model_width]
    grad_gate_pair = jnp.where(
        own_ranks >= 0, grad_wide[:, model_width : model_width + experts], 0.0
    )

    grad_low = grad_output[0]
    grad_top = grad_low.astype(single)
    grad_chosen = (
        grad_gate_pair - jnp.sum(grad_gate_pair * gates, axis=1, keepdims=True)
    ) / chosen_total
    grad_router = jnp.where(route_match, grad_chosen, 0.0)
    grad_logits = (
        router * (grad_router - jnp.sum(router * grad_router, axis=1, keepdims=True))
    ).astype(bfloat)
    grad_w_router = jnp.einsum("td,te->de", ffn_low, grad_logits, preferred_element_type=single)
    grad_ffn = grad_ffn + jnp.einsum(
        "te,de->td", grad_logits, full_router, preferred_element_type=single
    )
    grad_hidden_norm, grad_gain_ffn = rms_backward(grad_ffn, ffn_normal, ffn_inverse, gain_ffn)
    grad_hidden = grad_top + grad_hidden_norm
    grad_attn_low = grad_hidden.astype(bfloat)

    def out_hop(step, moving):
        part = put_rows(step, out_steps[step]) + block_rows(shared_out, step)
        if moving is not None:
            part = part + moving.astype(single)
        return ring_next(part.astype(bfloat))

    shared_out = [matmul(part[2], part_down) for part in shared]
    out_next = next_out(2)
    out_moving = out_hop(1, None)
    grad_attended = jnp.einsum(
        "td,vd->tv", grad_attn_low, full_output, preferred_element_type=single
    ).astype(bfloat)
    grad_w_output = jnp.einsum(
        "tv,td->vd", attended_low, grad_attn_low, preferred_element_type=single
    )
    grad_attended, out_next, shared_part, grad_w_output, out_moving = together(
        grad_attended, out_next, shared_part, grad_w_output, out_moving
    )
    out_steps[2], out_added = out_next
    output_part = scatter_rows(grad_w_output)
    shared_ring = [shared_part]

    out_moving = out_hop(2, out_moving)
    shared_next = ring_next(shared_part)

    def weight_grad(left, right):
        return jnp.einsum("ra,rb->ab", left, right, preferred_element_type=single)

    all_rows, all_grads, all_act, all_gate, all_up = kept
    grad_piece_down = weight_grad(all_act, all_grads)
    grad_piece_gate = weight_grad(all_rows, all_gate)
    grad_piece_up = weight_grad(all_rows, all_up)

    log_rows = log_total[:, :HEADS].T.reshape(HEADS // 2, 2, tokens)
    grad_nope, grad_rope, grad_key_part, grad_value_part, rope_pair_grad = attend_back(
        rows_here,
        score_scale,
        link,
        query_pre,
        pair_cos,
        pair_sin,
        kv_group,
        rope_pair,
        prompt_mask.T,
        cont_mask.T,
        log_rows,
        grad_attended,
    )
    out_next = next_out(3)
    (
        grad_nope,
        grad_rope,
        grad_key_part,
        grad_value_part,
        rope_pair_grad,
        out_next,
        out_moving,
        shared_next,
    ) = together(
        grad_nope,
        grad_rope,
        grad_key_part,
        grad_value_part,
        rope_pair_grad,
        out_next,
        out_moving,
        shared_next,
    )
    out_steps[3], out_added = out_next
    shared_ring.append(shared_next)
    shared_next = ring_next(shared_next)
    grad_kv_block = jnp.concatenate([grad_key_part, grad_value_part], axis=1)
    grad_key_rope = rope_pair_grad[:, :ROPE] + rope_pair_grad[:, ROPE:]
    grad_w_up = jnp.einsum("tc,tk->ck", latent_group, grad_kv_block, preferred_element_type=single)
    grad_latent_group = jnp.einsum(
        "tk,ck->tc", grad_kv_block, full_up, preferred_element_type=single
    )
    grad_query_pre = jnp.concatenate([grad_nope, grad_rope], axis=1)
    grad_w_query = jnp.einsum(
        "td,tq->dq", normed_low, grad_query_pre, preferred_element_type=single
    )
    grad_keys_own = ctx_total(
        by_block(jnp.concatenate([grad_latent_group, grad_key_rope], axis=1).astype(bfloat)), device
    )
    out_next = next_out(4 % ctx_size)
    grad_keys_own, output_part, grad_w_query, out_next, shared_next = together(
        grad_keys_own, output_part, grad_w_query, out_next, shared_next
    )
    out_steps[4 % ctx_size], out_added = out_next
    shared_ring.append(shared_next)
    out_moving = out_hop(3, out_moving)
    for step in range(4, ctx_size):
        out_moving = out_hop(step, out_moving)
        out_steps[(step + 1) % ctx_size], out_added = next_out((step + 1) % ctx_size)
    query_part = scatter_rows(grad_w_query)
    sum_output = sum_ctx(output_part)
    while len(shared_ring) < ctx_size:
        shared_ring.append(ring_next(shared_ring[-1]))
    grad_latent = grad_keys_own[:, :KV_RANK]
    grad_rope_own = grad_keys_own[:, KV_RANK:]
    grad_latent_in, grad_gain_latent = rms_backward(
        grad_latent, latent_normal, latent_inverse, gain_latent
    )
    grad_rope_in = rotate(grad_rope_own, cos_table, -sin_table)
    grad_latent_pre = jnp.concatenate([grad_latent_in, grad_rope_in], axis=1).astype(bfloat)
    grad_w_down = jnp.einsum(
        "td,tk->dk",
        normed_low,
        jnp.pad(grad_latent_pre, ((0, 0), (0, -down_width % 128))),
        preferred_element_type=single,
    )
    grad_normed = jnp.einsum(
        "tq,dq->td", grad_query_pre, full_query, preferred_element_type=single
    ) + jnp.einsum("tk,dk->td", grad_latent_pre, full_down, preferred_element_type=single)
    grad_x_norm, grad_gain_attn = rms_backward(grad_normed, attn_normal, attn_inverse, gain_attn)
    grad_input = (grad_hidden + grad_x_norm).astype(bfloat)

    padded_latent = jnp.pad(
        grad_gain_latent.reshape(fsdp_size, -1),
        ((0, 0), (0, shard_rows - latent_gain.shape[0])),
    ).reshape(-1)
    up_width = grad_w_up.size // model_width
    small = jnp.concatenate(
        [
            grad_w_router,
            grad_gain_attn[:, None],
            grad_gain_ffn[:, None],
            padded_latent[:, None],
        ],
        axis=1,
    ).astype(bfloat)
    packed_grads = jnp.concatenate(
        [
            grad_w_up.astype(bfloat).reshape(model_width, up_width),
            grad_w_down.astype(bfloat),
            jnp.pad(small, ((0, 0), (0, -small.shape[1] % 128))),
        ],
        axis=1,
    )
    query_part, out_moving, shared_ring, packed_grads, sum_output = together(
        query_part, out_moving, shared_ring, packed_grads, sum_output
    )
    first_out = put_rows(0, out_steps[0]) + block_rows(shared_out, 0)
    layer_output = (hidden + out_moving.astype(single) + first_out).astype(bfloat)
    packed_part = scatter_rows(with_layout_constraint(packed_grads, by_rows))
    sum_query = sum_ctx(query_part)
    packed_part, sum_query = together(packed_part, sum_query)
    sum_packed = with_layout_constraint(
        sum_ctx(with_layout_constraint(packed_part, by_rows)), by_rows
    )
    sum_up = sum_packed[:, :up_width].reshape(latent_up.shape)
    sum_down = sum_packed[:, up_width : up_width + down_width]
    sum_small = sum_packed[:, up_width + grad_w_down.shape[1] :]
    sum_router = sum_small[:, :experts]
    sum_gain_attn = sum_small[:, experts]
    sum_gain_ffn = sum_small[:, experts + 1]
    sum_gain_latent = sum_small[: latent_gain.shape[0], experts + 2]

    shared_blocks = in_order([piece[None] for piece in shared_ring], device)

    def all_columns(blocks):
        blocks = blocks.reshape(ctx_size, shard_rows, fsdp_size, hidden_dev)
        return blocks.transpose(1, 2, 0, 3).reshape(shard_rows, -1).astype(single)

    sum_sh_gate = all_columns(shared_blocks[:, :, :hidden_part])
    sum_sh_up = all_columns(shared_blocks[:, :, hidden_part : 2 * hidden_part])
    sum_sh_down = shared_blocks[:, :, 2 * hidden_part :].reshape(shared_down.shape).astype(single)
    return (
        layer_output[None],
        grad_input[None],
        sum_query,
        sum_down,
        sum_up,
        sum_output,
        sum_router,
        sum_sh_gate,
        sum_sh_up,
        sum_sh_down,
        sum_gain_attn,
        sum_gain_latent,
        sum_gain_ffn,
        grad_piece_gate[None],
        grad_piece_up[None],
        grad_piece_down[None],
    )


def solution(mesh):
    in_specs = (
        P("fsdp", "ctx", None),
        P("fsdp", "ctx", None),
        P("fsdp", "ctx", None),
        P("fsdp", None),
        P(),
        P("fsdp", None),
        P("fsdp", None),
        P("fsdp", None),
        P("fsdp", None),
        P("fsdp", None),
        P("fsdp", None),
        P("fsdp", None),
        P("fsdp", None),
        P("fsdp"),
        P("fsdp"),
        P("fsdp"),
        P(("ctx", "fsdp"), None, None),
        P(("ctx", "fsdp"), None, None),
        P(("ctx", "fsdp"), None, None),
    )
    out_specs = (
        P("fsdp", "ctx", None),
        P("fsdp", "ctx", None),
        P("fsdp", None),
        P("fsdp", None),
        P("fsdp", None),
        P("fsdp", None),
        P("fsdp", None),
        P("fsdp", None),
        P("fsdp", None),
        P("fsdp", None),
        P("fsdp"),
        P("fsdp"),
        P("fsdp"),
        P(("ctx", "fsdp"), None, None),
        P(("ctx", "fsdp"), None, None),
        P(("ctx", "fsdp"), None, None),
    )
    return jax.shard_map(local, mesh=mesh, in_specs=in_specs, out_specs=out_specs, check_vma=False)
```

time: 1920 us -> 1370 us (0.71)
  waiting for transfers between devices: 790 us -> 423 us
  matrix products: 640 us -> 325 us
  Pallas kernels: 0 us -> 200 us
  local copies, waits for them, and re-layouts: 196 us -> 118 us
  starting transfers between devices: 121 us -> 194 us
  blocking collectives: 33.5 us -> 0 us
  other arithmetic: 113 us -> 85.4 us
    dot_general x58 -> x13, matrix products: 379 us -> 125 us  [the longest x3 63.5 us: weight_grad(): return jnp.einsum('ra,rb->ab', left, right, preferred_element_type=single)]
    pallas_call x0 -> x6, Pallas kernels: none -> 200 us  [the longest x4 142 us: expert_call(): pl.pallas_call(functools.partial(expert_kernel, step * 2 * count, experts...]
    reduce_scatter x7 -> x4, waiting for transfers between devices: 154 us -> 6.08 us  [scatter_rows(): lax.psum_scatter(value.astype(bfloat), 'fsdp', scatter_dimension=0, tiled...]
    all_gather x6 -> x0, waiting for transfers between devices: 108 us -> none  [the longest x2 46.6 us: sum_ctx(): return lax.all_gather(part, 'ctx', axis=0, tiled=True).astype(single)]
    all_to_all x0 -> x16, starting transfers between devices: none -> 74.5 us  [to_chips(): lax.all_to_all(value, 'fsdp', split_axis=0, concat_axis=0, tiled=True, ax...]
    dot_general x33 -> x15, matrix products: 141 us -> 69.3 us  [matmul(): return jnp.dot(left, right, preferred_element_type=single)]
    unnamed x587 -> x291, local copies, waits for them, and re-layouts: 86.5 us -> 24 us
    reduce_scatter x4 -> x0, waiting for transfers between devices: 57.8 us -> none  [sum_ctx(): part = lax.psum_scatter(value, 'ctx', scatter_dimension=0, tiled=True)]
  transfers between devices with their start and end apart: 178 -> 83, of which waited for: 56 -> 35; matrix products, arithmetic and copies ran while one was open for 44% -> 35% of each run, Pallas kernels for 0% -> 15%
where the time goes in v2:
time: 1370 us; the launch traced here: 1360 us
  waiting for transfers between devices  423 us (31%)
  matrix products  325 us (24%)
  Pallas kernels  200 us (15%)
  starting transfers between devices  194 us (14%)
  local copies, waits for them, and re-layouts  118 us (9%)
  other arithmetic  85.4 us (6%)
  between operations  16.6 us (1%)
    ppermute x27, waiting for transfers between devices, along_ctx(): lax.ppermute(value, 'ctx', [(i, (i + shift) % size) for i in range(size)])  173 us
    ppermute x15, waiting for transfers between devices, ring_next(): lax.ppermute(value, 'ctx', [(i, (i + 1) % size) for i in range(size)])  142 us
    pallas_call x4, Pallas kernels, expert_call(): pl.pallas_call(functools.partial(expert_kernel, step * 2 * count, experts...  142 us
    ppermute x27, starting transfers between devices, along_ctx(): lax.ppermute(value, 'ctx', [(i, (i + shift) % size) for i in range(size)])  88.6 us
    all_to_all x16, starting transfers between devices, to_chips(): lax.all_to_all(value, 'fsdp', split_axis=0, concat_axis=0, tiled=True, ax...  74.5 us
    dot_general x15, matrix products, matmul(): return jnp.dot(left, right, preferred_element_type=single)  69.3 us
    dot_general x3, matrix products, weight_grad(): return jnp.einsum('ra,rb->ab', left, right, preferred_element_type=single)  63.5 us
    all_gather x5, waiting for transfers between devices, gather_rows(): return lax.all_gather(value, 'fsdp', axis=0, tiled=True)  53.6 us
  transfers between devices with their start and end apart: 83, of which 35 were waited for; matrix products, arithmetic and copies ran while one was open for 35% of the time, Pallas kernels for 15%

profile of v2, /device:TPU:0, one launch (start us, length us, event | category | flops | bytes accessed | tf_op | source)
XLA Modules:
  0.0 1363.2 jit_solution(2376524321275906629)
XLA Ops:
  32.8 26.2 %collective-permute-done = s32[320,6]{0,1:T(8,128)S(1)} collective-permute-done((s32[320,6]{0,1:T(8,128)S(1)}, s32[320,6]{0,1:T(8,128)S(1)}, u32[]{:S(2)}, u32[]{:S(2)}) %collective-permute-start) | collective-permute-done | bytes 7712 | tf_op jit(solution)/shard_map/ppermute | solution.py:557
  90.2 21.7 %collective-permute-done.4 = bf16[320,576]{1,0:T(8,128)(2,1)S(1)} collective-permute-done((bf16[320,576]{1,0:T(8,128)(2,1)S(1)}, bf16[320,576]{1,0:T(8,128)(2,1)S(1)}, u32[]{:S(2)}, u32[]{:S(2)}) %collective-permute-start.4) | collective-permute-done | bytes 368672 | tf_op jit(solution)/shard_map/ppermute | solution.py:557
  111.9 16.9 %collective-permute-done.5 = bf16[320,576]{1,0:T(8,128)(2,1)S(1)} collective-permute-done((bf16[320,576]{1,0:T(8,128)(2,1)S(1)}, bf16[320,576]{1,0:T(8,128)(2,1)S(1)}, u32[]{:S(2)}, u32[]{:S(2)}) %collective-permute-start.5) | collective-permute-done | bytes 368672 | tf_op jit(solution)/shard_map/ppermute | solution.py:557
  130.3 36.0 %all-gather.8.cloned.1.call-done = bf16[2048,3072]{1,0:T(8,128)(2,1)} async-done(((bf16[256,3072]{1,0:T(8,128)(2,1)}), bf16[2048,3072]{1,0:T(8,128)(2,1)}) %all-gather.8.cloned.1.call-update) | async-done | bytes 12582928 | tf_op jit(solution)/shard_map/all_gather | solution.py:548
  177.2 9.3 fusion.174.nope.rope
  186.5 22.3 %collective-permute-done.9 = bf16[320,2048]{1,0:T(8,128)(2,1)} collective-permute-done((bf16[320,2048]{1,0:T(8,128)(2,1)}, bf16[320,2048]{1,0:T(8,128)(2,1)}, u32[]{:S(2)}, u32[]{:S(2)}) %collective-permute-start.9) | collective-permute-done | bytes 1310752 | tf_op jit(solution)/shard_map/ppermute | solution.py:527
  211.7 12.0 all-gather.10.cloned.1.call-done
  252.9 11.7 convolution_convert_fusion.keys.values
  264.5 26.5 %shard_map.306 = (bf16[320,2048]{1,0:T(8,128)(2,1)S(1)}, f32[320,128]{1,0:T(8,128)S(1)}) custom-call(s32[1]{0:T(128)} %bitcast.11.link, f32[320,3072]{1,0:T(8,128)S(1)} %copy-done.2, f32[320,3072]{1,0:T(8,128)S(1)} %copy-done.2, f32[320,128]{1,0:T(8,128)S(1)} %get-tuple-element.458.cos, f32[320,128]{1,0:T(8,128)S(1)} %get-tuple-element.459.sin, ...), custom_call_target="tpu_custom_call" | custom-call | flops 2214592512 | bytes 16384000 | tf_op jit(solution)/shard_map/pallas_call | solution.py:312
  291.1 11.1 all-to-all-done.3
  323.2 33.1 %collective-permute-done.12 = bf16[320,2176]{1,0:T(8,128)(2,1)} collective-permute-done((bf16[320,2176]{1,0:T(8,128)(2,1)S(1)}, bf16[320,2176]{1,0:T(8,128)(2,1)}, u32[]{:S(2)}, u32[]{:S(2)}) %collective-permute-start.12) | collective-permute-done | bytes 1392672 | tf_op jit(solution)/shard_map/ppermute | solution.py:527
  373.6 35.4 %shard_map.307 = (bf16[608,2176]{1,0:T(8,128)(2,1)}, bf16[608,2176]{1,0:T(8,128)(2,1)}, bf16[608,2048]{1,0:T(8,128)(2,1)}, bf16[608,2048]{1,0:T(8,128)(2,1)}, bf...) custom-call(s32[1]{0:T(128)} %bitcast.18.expert, ...), custom_call_target="tpu_custom_call" | custom-call | flops 21038628864 | bytes 43671552 | tf_op jit(solution)/shard_map/pallas_call | solution.py:501
  417.5 7.0 reshape.498
  426.6 5.9 fusion.47
  447.1 7.1 multiply_convert_fusion.2
  454.2 6.8 fusion.69
  465.0 35.5 %shard_map.308 = (bf16[608,2176]{1,0:T(8,128)(2,1)}, bf16[608,2176]{1,0:T(8,128)(2,1)}, bf16[608,2048]{1,0:T(8,128)(2,1)}, bf16[608,2048]{1,0:T(8,128)(2,1)}, bf...) custom-call(s32[1]{0:T(128)} %bitcast.18.expert, ...), custom_call_target="tpu_custom_call", output_to_operand_aliasing={{4}: (8, {}), {5}: (9, {}), {6}: (10, {}), {7}: (11, {}), {... | custom-call | flops 21038628864 | bytes 43671552 | tf_op jit(solution)/shard_map/pallas_call | solution.py:501
  500.5 8.2 convolution_add_fusion.1
  514.0 6.5 fusion.51
  531.3 5.5 fusion.60
  536.8 8.6 all-to-all-done.7
  554.7 35.5 %shard_map.309 = (bf16[608,2176]{1,0:T(8,128)(2,1)}, bf16[608,2176]{1,0:T(8,128)(2,1)}, bf16[608,2048]{1,0:T(8,128)(2,1)}, bf16[608,2048]{1,0:T(8,128)(2,1)}, bf...) custom-call(s32[1]{0:T(128)} %bitcast.18.expert, ...), custom_call_target="tpu_custom_call", output_to_operand_aliasing={{4}: (8, {}), {5}: (9, {}), {6}: (10, {}), {7}: (11, {}), {... | custom-call | flops 21038628864 | bytes 43671552 | tf_op jit(solution)/shard_map/pallas_call | solution.py:501
  590.3 8.2 multiply_convert_fusion.1
  603.5 7.1 convolution_convert_fusion.7
  610.7 6.6 fusion.65
  626.0 9.0 all-to-all-done.9
  645.1 35.5 %shard_map.310 = (bf16[608,2176]{1,0:T(8,128)(2,1)}, bf16[608,2176]{1,0:T(8,128)(2,1)}, bf16[608,2048]{1,0:T(8,128)(2,1)}, bf16[608,2048]{1,0:T(8,128)(2,1)}, bf...) custom-call(s32[1]{0:T(128)} %bitcast.18.expert, ...), custom_call_target="tpu_custom_call", output_to_operand_aliasing={{4}: (8, {}), {5}: (9, {}), {6}: (10, {}), {7}: (11, {}), {... | custom-call | flops 21038628864 | bytes 43671552 | tf_op jit(solution)/shard_map/pallas_call | solution.py:501
  680.8 6.0 convolution_add_fusion
  686.8 5.6 convolution_convert_fusion.6
  692.4 6.8 fusion.27
  702.2 7.0 reshape.506
  723.2 5.6 fusion.21
  739.5 24.3 %collective-permute-done.25 = bf16[320,2176]{1,0:T(8,128)(2,1)S(1)} collective-permute-done((bf16[320,2176]{1,0:T(8,128)(2,1)}, bf16[320,2176]{1,0:T(8,128)(2,1)S(1)}, u32[]{:S(2)}, u32[]{:S(2)}) %collective-permute-start.25) | collective-permute-done | bytes 1392672 | tf_op jit(solution)/shard_map/ppermute | solution.py:527
  787.3 20.5 %collective-permute-done.27 = bf16[320,2176]{1,0:T(8,128)(2,1)S(1)} collective-permute-done((bf16[320,2176]{1,0:T(8,128)(2,1)S(1)}, bf16[320,2176]{1,0:T(8,128)(2,1)S(1)}, u32[]{:S(2)}, u32[]{:S(2)}) %collective-permute-start.27) | collective-permute-done | bytes 1392672 | tf_op jit(solution)/shard_map/ppermute | solution.py:527
  825.7 6.8 fusion.94
  832.5 7.1 convolution_convert_fusion.14.grad
  844.9 10.5 all-to-all-done.13
  855.4 6.1 reduce-scatter.5.cloned.1.call-done
  862.6 6.4 fusion.182
  873.8 6.3 fusion.37
  886.9 31.8 %shard_map.311 = (bf16[320,2048]{1,0:T(8,128)(2,1)S(1)}, bf16[320,1024]{1,0:T(8,128)(2,1)S(1)}, bf16[1280,2048]{1,0:T(8,128)(2,1)}, bf16[1280,2048]{1,0:T(8,128)(2,1)}, f32[1280,128]{1,0:T(8,128)S(1)}) custom-call(s32[1]{0:T(128)} %bitcast.11.link, f32[320,3072]{1,0:T(8,128)} %fusion.174.nope.rope, f32[320,3072]{1,0:T(8,128)} %fusion.174.nope.rope, ...), custom_call_target="tpu_custom_call" | custom-call | flops 6643777536 | bytes 30801920 | tf_op jit(solution)/shard_map/pallas_call | solution.py:337
  919.5 17.0 %collective-permute-done.33 = bf16[256,2112]{0,1:T(8,128)(2,1)} collective-permute-done((bf16[256,2112]{0,1:T(8,128)(2,1)}, bf16[256,2112]{0,1:T(8,128)(2,1)}, u32[]{:S(2)}, u32[]{:S(2)}) %collective-permute-start.33) | collective-permute-done | bytes 1081376 | tf_op jit(solution)/shard_map/ppermute | solution.py:527
  943.3 5.6 convolution_convert_fusion.13
  966.5 9.8 fusion.172
  976.2 16.4 %collective-permute-done.35 = bf16[320,576]{1,0:T(8,128)(2,1)} collective-permute-done((bf16[320,576]{1,0:T(8,128)(2,1)}, bf16[320,576]{1,0:T(8,128)(2,1)}, u32[]{:S(2)}, u32[]{:S(2)}) %collective-permute-start.35) | collective-permute-done | bytes 368672 | tf_op jit(solution)/shard_map/ppermute | solution.py:557
  995.0 19.5 %collective-permute-done.37 = bf16[256,2112]{0,1:T(8,128)(2,1)} collective-permute-done((bf16[256,2112]{0,1:T(8,128)(2,1)}, bf16[256,2112]{0,1:T(8,128)(2,1)}, u32[]{:S(2)}, u32[]{:S(2)}) %collective-permute-start.37) | collective-permute-done | bytes 1081376 | tf_op jit(solution)/shard_map/ppermute | solution.py:527
  1014.7 21.3 %convolution_bitcast_fusion.4 = f32[1,704,2048]{2,1,0:T(8,128)} fusion(bf16[4864,704]{1,0:T(8,128)(2,1)} %get-tuple-element.304, bf16[4864,2048]{1,0:T(8,128)(2,1)} %get-tuple-element.305), kind=kOutput, calls=%fused_computation.51 | convolution fusion | flops 14025752576 | bytes 32538624 | tf_op jit(solution)/shard_map/ra,rb->ab/dot_general | solution.py:1041
  1036.1 21.1 %convolution_bitcast_fusion.5 = f32[1,2048,704]{1,2,0:T(8,128)} fusion(bf16[4864,2048]{1,0:T(8,128)(2,1)S(1)} %bitcast.233, bf16[4864,704]{1,0:T(8,128)(2,1)} %get-tuple-element.303), kind=kOutput, calls=%fused_computation.52 | convolution fusion | flops 14025752576 | bytes 32538624 | tf_op jit(solution)/shard_map/ra,rb->ab/dot_general | solution.py:1041
  1059.2 10.8 convolution_convert_fusion.1
  1070.0 7.7 reshape.514
  1083.0 10.7 collective-permute-start.38
  1101.1 11.5 fusion.41
  1115.7 13.1 collective-permute-done.40
  1128.9 5.7 collective-permute-done.41
  1134.5 5.6 collective-permute-done.42
  1143.8 26.1 %collective-permute-start.43 = (bf16[64,2048]{1,0:T(8,128)(2,1)S(1)}, bf16[64,2048]{1,0:T(8,128)(2,1)}, u32[]{:S(2)}, u32[]{:S(2)}) collective-permute-start(bf16[64,2048]{1,0:T(8,128)(2,1)S(1)} %get-tuple-element.402), channel_id=1, source_target_pairs={{0,8},{8,16},{16,24},{24,0},{1,9},{9,17},{17,25},{25,1},{2,10},{10... | collective-permute-start | bytes 786440 | tf_op jit(solution)/shard_map/ppermute | solution.py:557
  1178.4 9.2 collective-permute-done.44
  1189.4 21.0 %convolution_bitcast_fusion.6 = f32[1,2048,704]{1,2,0:T(8,128)} fusion(bf16[4864,2048]{1,0:T(8,128)(2,1)} %get-tuple-element.301, bf16[4864,704]{1,0:T(8,128)(2,1)} %get-tuple-element.302), kind=kOutput, calls=%fused_computation.53 | convolution fusion | flops 14025752576 | bytes 32538624 | tf_op jit(solution)/shard_map/ra,rb->ab/dot_general | solution.py:1041
  1230.9 15.4 %collective-permute-done.47 = bf16[64,3072]{1,0:T(8,128)(2,1)S(1)} collective-permute-done((bf16[64,3072]{1,0:T(8,128)(2,1)S(1)}, bf16[64,3072]{1,0:T(8,128)(2,1)S(1)}, u32[]{:S(2)}, u32[]{:S(2)}) %collective-permute-start.47) | collective-permute-done | bytes 393248 | tf_op jit(solution)/shard_map/ppermute | solution.py:557
  1249.4 8.9 collective-permute-start.49
  1268.8 14.7 %collective-permute-done.50 = bf16[64,3072]{1,0:T(8,128)(2,1)S(1)} collective-permute-done((bf16[64,3072]{1,0:T(8,128)(2,1)S(1)}, bf16[64,3072]{1,0:T(8,128)(2,1)S(1)}, u32[]{:S(2)}, u32[]{:S(2)}) %collective-permute-start.50) | collective-permute-done | bytes 393248 | tf_op jit(solution)/shard_map/ppermute | solution.py:557
  1287.4 8.9 collective-permute-start.52
  1306.0 8.7 collective-permute-done.53
  1335.0 9.9 collective-permute-done.56
  (624 shorter events, 441.9 us)
Async XLA Ops:
  7.2 58.3 %all-gather.6.cloned.1.call-start = ((), (), s32[]{:S(2)}) async-start(), calls=%async_computation.20 | async-start | bytes 2764800 | tf_op jit(solution)/shard_map/all_gather | solution.py:548
  19.4 42.4 %all-to-all-start = ((bf16[4,152,2048]{2,1,0:T(8,128)(2,1)}), bf16[4,152,2048]{2,1,0:T(8,128)(2,1)}, u32[]{:S(2)}, u32[]{:S(2)}) async-start(bf16[4,152,2048]{2,1,0:T(8,128)(2,1)} %convolution_convert_fusion.12), calls=%async_computation | async-start | bytes 4980736 | tf_op jit(solution)/shard_map/all_to_all | solution.py:532
  24.7 141.6 %all-gather.8.cloned.1.call-start = ((), (), s32[]{:S(2)}) async-start(), calls=%async_computation.21 | async-start | bytes 14155776 | tf_op jit(solution)/shard_map/all_gather | solution.py:548
  24.7 34.5 %collective-permute-start.3 = (bf16[320,2048]{1,0:T(8,128)(2,1)}, bf16[320,2048]{1,0:T(8,128)(2,1)}, u32[]{:S(2)}, u32[]{:S(2)}) collective-permute-start(bf16[320,2048]{1,0:T(8,128)(2,1)} %bitcast.278), channel_id=1, source_target_pairs={{0,8},{8,16},{16,24},{24,0},{1,9},{9,17},{17,25},{25,1},{2,10},{10... | collective-permute-start | bytes 3932168 | tf_op jit(solution)/shard_map/ppermute | solution.py:527
  27.2 31.7 %collective-permute-start = (s32[320,6]{0,1:T(8,128)S(1)}, s32[320,6]{0,1:T(8,128)S(1)}, u32[]{:S(2)}, u32[]{:S(2)}) collective-permute-start(s32[320,6]{0,1:T(8,128)S(1)} %bitcast.286), channel_id=1, source_target_pairs={{0,8},{8,16},{16,24},{24,0},{1,9},{9,17},{17,25},{25,1},{2,10},{10... | collective-permute-start | bytes 23048 | tf_op jit(solution)/shard_map/ppermute | solution.py:557
  28.8 30.4 %collective-permute-start.1 = (s32[320,6]{0,1:T(8,128)S(1)}, s32[320,6]{0,1:T(8,128)S(1)}, u32[]{:S(2)}, u32[]{:S(2)}) collective-permute-start(s32[320,6]{0,1:T(8,128)S(1)} %bitcast.287), channel_id=1, source_target_pairs={{0,16},{8,24},{16,0},{24,8},{1,17},{9,25},{17,1},{25,9},{2,18},{10... | collective-permute-start | bytes 23048 | tf_op jit(solution)/shard_map/ppermute | solution.py:557
  29.9 29.3 %collective-permute-start.2 = (s32[320,6]{0,1:T(8,128)S(1)}, s32[320,6]{0,1:T(8,128)S(1)}, u32[]{:S(2)}, u32[]{:S(2)}) collective-permute-start(s32[320,6]{0,1:T(8,128)S(1)} %bitcast.288), channel_id=1, source_target_pairs={{0,24},{8,0},{16,8},{24,16},{1,25},{9,1},{17,9},{25,17},{2,26},{10... | collective-permute-start | bytes 23048 | tf_op jit(solution)/shard_map/ppermute | solution.py:557
  67.1 63.2 %collective-permute-start.8 = (bf16[4,152,2048]{2,1,0:T(8,128)(2,1)}, bf16[4,152,2048]{2,1,0:T(8,128)(2,1)}, u32[]{:S(2)}, u32[]{:S(2)}) collective-permute-start(bf16[4,152,2048]{2,1,0:T(8,128)(2,1)} %all-to-all-done), channel_id=1, source_target_pairs={{0,1},{1,0},{2,3},{3,2},{4,5},{5,4},{6,7},{7,6},{8,9},{9,8},{10,11... | collective-permute-start | bytes 7471112 | tf_op jit(solution)/shard_map/ppermute | solution.py:544
  69.4 60.9 %collective-permute-start.7 = (bf16[320,2048]{1,0:T(8,128)(2,1)}, bf16[320,2048]{1,0:T(8,128)(2,1)}, u32[]{:S(2)}, u32[]{:S(2)}) collective-permute-start(bf16[320,2048]{1,0:T(8,128)(2,1)} %collective-permute-done.3), channel_id=1, source_target_pairs={{0,8},{8,16},{16,24},{24,0},{1,9},{9,17},{17,25},{25,1},{2,10},{10... | collective-permute-start | bytes 3932168 | tf_op jit(solution)/shard_map/ppermute | solution.py:527
  75.2 55.0 %all-to-all-start.1 = ((bf16[4,152,2048]{2,1,0:T(8,128)(2,1)}), bf16[4,152,2048]{2,1,0:T(8,128)(2,1)}, u32[]{:S(2)}, u32[]{:S(2)}) async-start(bf16[4,152,2048]{2,1,0:T(8,128)(2,1)} %convolution_convert_fusion.11), calls=%async_computation.1 | async-start | bytes 4980736 | tf_op jit(solution)/shard_map/all_to_all | solution.py:532
  79.9 143.7 %all-gather.10.cloned.1.call-start = ((), (), s32[]{:S(2)}) async-start(), calls=%async_computation.22 | async-start | bytes 4718592 | tf_op jit(solution)/shard_map/all_gather | solution.py:548
  86.4 42.4 %collective-permute-start.5 = (bf16[320,576]{1,0:T(8,128)(2,1)S(1)}, bf16[320,576]{1,0:T(8,128)(2,1)S(1)}, u32[]{:S(2)}, u32[]{:S(2)}) collective-permute-start(bf16[320,576]{1,0:T(8,128)(2,1)S(1)} %pad_maximum_fusion.13), channel_id=1, source_target_pairs={{0,16},{8,24},{16,0},{24,8},{1,17},{9,25},{17,1},{25,9},{2,18},{10... | collective-permute-start | bytes 1105928 | tf_op jit(solution)/shard_map/ppermute | solution.py:557
  87.7 41.0 %collective-permute-start.6 = (bf16[320,576]{1,0:T(8,128)(2,1)S(1)}, bf16[320,576]{1,0:T(8,128)(2,1)S(1)}, u32[]{:S(2)}, u32[]{:S(2)}) collective-permute-start(bf16[320,576]{1,0:T(8,128)(2,1)S(1)} %pad_maximum_fusion.13), channel_id=1, source_target_pairs={{0,24},{8,0},{16,8},{24,16},{1,25},{9,1},{17,9},{25,17},{2,26},{10... | collective-permute-start | bytes 1105928 | tf_op jit(solution)/shard_map/ppermute | solution.py:557
  166.3 45.4 %collective-permute-start.10 = (bf16[4,152,2048]{2,1,0:T(8,128)(2,1)}, bf16[4,152,2048]{2,1,0:T(8,128)(2,1)}, u32[]{:S(2)}, u32[]{:S(2)}) collective-permute-start(bf16[4,152,2048]{2,1,0:T(8,128)(2,1)} %all-to-all-done.1), channel_id=1, source_target_pairs={{0,1},{1,0},{2,3},{3,2},{4,5},{5,4},{6,7},{7,6},{8,9},{9,8},{10,11... | collective-permute-start | bytes 7471112 | tf_op jit(solution)/shard_map/ppermute | solution.py:544
  170.8 40.8 %all-to-all-start.2 = ((bf16[4,152,2048]{2,1,0:T(8,128)(2,1)}), bf16[4,152,2048]{2,1,0:T(8,128)(2,1)}, u32[]{:S(2)}, u32[]{:S(2)}) async-start(bf16[4,152,2048]{2,1,0:T(8,128)(2,1)} %convolution_convert_fusion.10), calls=%async_computation.2 | async-start | bytes 4980736 | tf_op jit(solution)/shard_map/all_to_all | solution.py:532
  175.4 128.6 %all-gather.12.cloned.1.call-start = ((), (), s32[]{:S(2)}) async-start(), calls=%async_computation.23 | async-start | bytes 9437184 | tf_op jit(solution)/shard_map/all_gather | solution.py:548
  175.5 33.3 %collective-permute-start.9 = (bf16[320,2048]{1,0:T(8,128)(2,1)}, bf16[320,2048]{1,0:T(8,128)(2,1)}, u32[]{:S(2)}, u32[]{:S(2)}) collective-permute-start(bf16[320,2048]{1,0:T(8,128)(2,1)} %collective-permute-done.7), channel_id=1, source_target_pairs={{0,8},{8,16},{16,24},{24,0},{1,9},{9,17},{17,25},{25,1},{2,10},{10... | collective-permute-start | bytes 3932168 | tf_op jit(solution)/shard_map/ppermute | solution.py:527
  239.7 62.5 %collective-permute-start.11 = (bf16[4,152,2048]{2,1,0:T(8,128)(2,1)}, bf16[4,152,2048]{2,1,0:T(8,128)(2,1)}, u32[]{:S(2)}, u32[]{:S(2)}) collective-permute-start(bf16[4,152,2048]{2,1,0:T(8,128)(2,1)} %all-to-all-done.2), channel_id=1, source_target_pairs={{0,1},{1,0},{2,3},{3,2},{4,5},{5,4},{6,7},{7,6},{8,9},{9,8},{10,11... | collective-permute-start | bytes 7471112 | tf_op jit(solution)/shard_map/ppermute | solution.py:544
  245.3 56.8 %all-to-all-start.3 = ((bf16[4,152,2048]{2,1,0:T(8,128)(2,1)}), bf16[4,152,2048]{2,1,0:T(8,128)(2,1)}, u32[]{:S(2)}, u32[]{:S(2)}) async-start(bf16[4,152,2048]{2,1,0:T(8,128)(2,1)} %convolution_convert_fusion.9), calls=%async_computation.3 | async-start | bytes 4980736 | tf_op jit(solution)/shard_map/all_to_all | solution.py:532
  249.8 159.3 %all-gather.14.cloned.1.call-start = ((), (), s32[]{:S(2)}) async-start(), calls=%async_computation.24 | async-start | bytes 9732096 | tf_op jit(solution)/shard_map/all_gather | solution.py:548
  311.4 48.9 %collective-permute-start.13 = (bf16[4,152,2048]{2,1,0:T(8,128)(2,1)}, bf16[4,152,2048]{2,1,0:T(8,128)(2,1)}, u32[]{:S(2)}, u32[]{:S(2)}) collective-permute-start(bf16[4,152,2048]{2,1,0:T(8,128)(2,1)} %all-to-all-done.3), channel_id=1, source_target_pairs={{0,1},{1,0},{2,3},{3,2},{4,5},{5,4},{6,7},{7,6},{8,9},{9,8},{10,11... | collective-permute-start | bytes 7471112 | tf_op jit(solution)/shard_map/ppermute | solution.py:544
  317.0 43.3 %all-to-all-start.4 = ((bf16[4,152,2176]{2,1,0:T(8,128)(2,1)}), bf16[4,152,2176]{2,1,0:T(8,128)(2,1)}, u32[]{:S(2)}, u32[]{:S(2)}) async-start(bf16[4,152,2176]{2,1,0:T(8,128)(2,1)} %convolution_convert_fusion.5), calls=%async_computation.4 | async-start | bytes 5292032 | tf_op jit(solution)/shard_map/all_to_all | solution.py:532
  321.6 34.6 %collective-permute-start.12 = (bf16[320,2176]{1,0:T(8,128)(2,1)S(1)}, bf16[320,2176]{1,0:T(8,128)(2,1)}, u32[]{:S(2)}, u32[]{:S(2)}) collective-permute-start(bf16[320,2176]{1,0:T(8,128)(2,1)S(1)} %concatenate.90), channel_id=1, source_target_pairs={{0,8},{8,16},{16,24},{24,0},{1,9},{9,17},{17,25},{25,1},{2,10},{10... | collective-permute-start | bytes 4177928 | tf_op jit(solution)/shard_map/ppermute | solution.py:527
  364.8 44.3 %all-to-all-start.5 = ((bf16[4,152,2176]{2,1,0:T(8,128)(2,1)}), bf16[4,152,2176]{2,1,0:T(8,128)(2,1)}, u32[]{:S(2)}, u32[]{:S(2)}) async-start(bf16[4,152,2176]{2,1,0:T(8,128)(2,1)} %convolution_convert_fusion.4), calls=%async_computation.5 | async-start | bytes 5292032 | tf_op jit(solution)/shard_map/all_to_all | solution.py:532
  369.3 39.7 %collective-permute-start.15 = (bf16[320,2176]{1,0:T(8,128)(2,1)}, bf16[320,2176]{1,0:T(8,128)(2,1)}, u32[]{:S(2)}, u32[]{:S(2)}) collective-permute-start(bf16[320,2176]{1,0:T(8,128)(2,1)} %collective-permute-done.12), channel_id=1, source_target_pairs={{0,8},{8,16},{16,24},{24,0},{1,9},{9,17},{17,25},{25,1},{2,10},{10... | collective-permute-start | bytes 4177928 | tf_op jit(solution)/shard_map/ppermute | solution.py:527
  424.5 36.6 %collective-permute-start.16 = (bf16[4,152,2176]{2,1,0:T(8,128)(2,1)}, bf16[4,152,2176]{2,1,0:T(8,128)(2,1)}, u32[]{:S(2)}, u32[]{:S(2)}) collective-permute-start(bf16[4,152,2176]{2,1,0:T(8,128)(2,1)} %bitcast.297), channel_id=1, source_target_pairs={{0,1},{1,0},{2,3},{3,2},{4,5},{5,4},{6,7},{7,6},{8,9},{9,8},{10,11... | collective-permute-start | bytes 7938056 | tf_op jit(solution)/shard_map/ppermute | solution.py:544
  424.7 40.2 %collective-permute-start.17 = (bf16[4,152,2176]{2,1,0:T(8,128)(2,1)}, bf16[4,152,2176]{2,1,0:T(8,128)(2,1)}, u32[]{:S(2)}, u32[]{:S(2)}) collective-permute-start(bf16[4,152,2176]{2,1,0:T(8,128)(2,1)} %all-to-all-done.5), channel_id=1, source_target_pairs={{0,1},{1,0},{2,3},{3,2},{4,5},{5,4},{6,7},{7,6},{8,9},{9,8},{10,11... | collective-permute-start | bytes 7938056 | tf_op jit(solution)/shard_map/ppermute | solution.py:544
  425.0 75.4 %collective-permute-start.18 = (bf16[320,2176]{1,0:T(8,128)(2,1)}, bf16[320,2176]{1,0:T(8,128)(2,1)}, u32[]{:S(2)}, u32[]{:S(2)}) collective-permute-start(bf16[320,2176]{1,0:T(8,128)(2,1)} %collective-permute-done.15), channel_id=1, source_target_pairs={{0,8},{8,16},{16,24},{24,0},{1,9},{9,17},{17,25},{25,1},{2,10},{10... | collective-permute-start | bytes 4177928 | tf_op jit(solution)/shard_map/ppermute | solution.py:527
  442.4 58.1 %all-to-all-start.6 = ((bf16[4,152,2176]{2,1,0:T(8,128)(2,1)}), bf16[4,152,2176]{2,1,0:T(8,128)(2,1)}, u32[]{:S(2)}, u32[]{:S(2)}) async-start(bf16[4,152,2176]{2,1,0:T(8,128)(2,1)} %convolution_convert_fusion.3), calls=%async_computation.6 | async-start | bytes 5292032 | tf_op jit(solution)/shard_map/all_to_all | solution.py:532
  500.5 49.6 %collective-permute-start.19 = (bf16[4,152,2176]{2,1,0:T(8,128)(2,1)}, bf16[4,152,2176]{2,1,0:T(8,128)(2,1)}, u32[]{:S(2)}, u32[]{:S(2)}) collective-permute-start(bf16[4,152,2176]{2,1,0:T(8,128)(2,1)} %bitcast.296), channel_id=1, source_target_pairs={{0,1},{1,0},{2,3},{3,2},{4,5},{5,4},{6,7},{7,6},{8,9},{9,8},{10,11... | collective-permute-start | bytes 7938056 | tf_op jit(solution)/shard_map/ppermute | solution.py:544
  508.8 45.9 %collective-permute-start.20 = (bf16[4,152,2176]{2,1,0:T(8,128)(2,1)}, bf16[4,152,2176]{2,1,0:T(8,128)(2,1)}, u32[]{:S(2)}, u32[]{:S(2)}) collective-permute-start(bf16[4,152,2176]{2,1,0:T(8,128)(2,1)} %all-to-all-done.6), channel_id=1, source_target_pairs={{0,1},{1,0},{2,3},{3,2},{4,5},{5,4},{6,7},{7,6},{8,9},{9,8},{10,11... | collective-permute-start | bytes 7938056 | tf_op jit(solution)/shard_map/ppermute | solution.py:544
  509.3 36.2 %all-to-all-start.7 = ((bf16[4,152,2176]{2,1,0:T(8,128)(2,1)}), bf16[4,152,2176]{2,1,0:T(8,128)(2,1)}, u32[]{:S(2)}, u32[]{:S(2)}) async-start(bf16[4,152,2176]{2,1,0:T(8,128)(2,1)} %add_convert_fusion.3), calls=%async_computation.7 | async-start | bytes 5292032 | tf_op jit(solution)/shard_map/all_to_all | solution.py:532
  545.5 44.7 %all-to-all-start.8 = ((bf16[4,152,2176]{2,1,0:T(8,128)(2,1)}), bf16[4,152,2176]{2,1,0:T(8,128)(2,1)}, u32[]{:S(2)}, u32[]{:S(2)}) async-start(bf16[4,152,2176]{2,1,0:T(8,128)(2,1)} %convolution_convert_fusion.2), calls=%async_computation.8 | async-start | bytes 5292032 | tf_op jit(solution)/shard_map/all_to_all | solution.py:532
  590.2 31.9 %collective-permute-start.21 = (bf16[4,152,2176]{2,1,0:T(8,128)(2,1)}, bf16[4,152,2176]{2,1,0:T(8,128)(2,1)}, u32[]{:S(2)}, u32[]{:S(2)}) collective-permute-start(bf16[4,152,2176]{2,1,0:T(8,128)(2,1)} %bitcast.299), channel_id=1, source_target_pairs={{0,1},{1,0},{2,3},{3,2},{4,5},{5,4},{6,7},{7,6},{8,9},{9,8},{10,11... | collective-permute-start | bytes 7938056 | tf_op jit(solution)/shard_map/ppermute | solution.py:544
  598.5 36.6 %collective-permute-start.22 = (bf16[4,152,2176]{2,1,0:T(8,128)(2,1)}, bf16[4,152,2176]{2,1,0:T(8,128)(2,1)}, u32[]{:S(2)}, u32[]{:S(2)}) collective-permute-start(bf16[4,152,2176]{2,1,0:T(8,128)(2,1)} %all-to-all-done.8), channel_id=1, source_target_pairs={{0,1},{1,0},{2,3},{3,2},{4,5},{5,4},{6,7},{7,6},{8,9},{9,8},{10,11... | collective-permute-start | bytes 7938056 | tf_op jit(solution)/shard_map/ppermute | solution.py:544
  599.0 36.1 %all-to-all-start.9 = ((bf16[4,152,2176]{2,1,0:T(8,128)(2,1)}), bf16[4,152,2176]{2,1,0:T(8,128)(2,1)}, u32[]{:S(2)}, u32[]{:S(2)}) async-start(bf16[4,152,2176]{2,1,0:T(8,128)(2,1)} %add_convert_fusion.2), calls=%async_computation.9 | async-start | bytes 5292032 | tf_op jit(solution)/shard_map/all_to_all | solution.py:532
  610.7 123.7 %collective-permute-start.26 = (bf16[4,152,2048]{2,1,0:T(8,128)(2,1)}, bf16[4,152,2048]{2,1,0:T(8,128)(2,1)}, u32[]{:S(2)}, u32[]{:S(2)}) collective-permute-start(bf16[4,152,2048]{2,1,0:T(8,128)(2,1)} %bitcast.57), channel_id=1, source_target_pairs={{0,1},{1,0},{2,3},{3,2},{4,5},{5,4},{6,7},{7,6},{8,9},{9,8},{10,11... | collective-permute-start | bytes 7471112 | tf_op jit(solution)/shard_map/ppermute | solution.py:544
  635.0 45.6 %all-to-all-start.10 = ((bf16[4,152,2176]{2,1,0:T(8,128)(2,1)}), bf16[4,152,2176]{2,1,0:T(8,128)(2,1)}, u32[]{:S(2)}, u32[]{:S(2)}) async-start(bf16[4,152,2176]{2,1,0:T(8,128)(2,1)} %add_convert_fusion.1), calls=%async_computation.10 | async-start | bytes 5292032 | tf_op jit(solution)/shard_map/all_to_all | solution.py:532
  643.5 37.1 %collective-permute-start.23 = (bf16[320,2176]{1,0:T(8,128)(2,1)S(1)}, bf16[320,2176]{1,0:T(8,128)(2,1)}, u32[]{:S(2)}, u32[]{:S(2)}) collective-permute-start(bf16[320,2176]{1,0:T(8,128)(2,1)S(1)} %fusion.22), channel_id=1, source_target_pairs={{0,8},{8,16},{16,24},{24,0},{1,9},{9,17},{17,25},{25,1},{2,10},{10... | collective-permute-start | bytes 4177928 | tf_op jit(solution)/shard_map/ppermute | solution.py:527
  680.7 33.1 %collective-permute-start.24 = (bf16[4,152,2176]{2,1,0:T(8,128)(2,1)}, bf16[4,152,2176]{2,1,0:T(8,128)(2,1)}, u32[]{:S(2)}, u32[]{:S(2)}) collective-permute-start(bf16[4,152,2176]{2,1,0:T(8,128)(2,1)} %bitcast.298), channel_id=1, source_target_pairs={{0,1},{1,0},{2,3},{3,2},{4,5},{5,4},{6,7},{7,6},{8,9},{9,8},{10,11... | collective-permute-start | bytes 7938056 | tf_op jit(solution)/shard_map/ppermute | solution.py:544
  718.4 45.4 %all-to-all-start.11 = ((bf16[4,152,2176]{2,1,0:T(8,128)(2,1)}), bf16[4,152,2176]{2,1,0:T(8,128)(2,1)}, u32[]{:S(2)}, u32[]{:S(2)}) async-start(bf16[4,152,2176]{2,1,0:T(8,128)(2,1)} %add_convert_fusion), calls=%async_computation.11 | async-start | bytes 5292032 | tf_op jit(solution)/shard_map/all_to_all | solution.py:532
  723.1 138.4 %reduce-scatter.5.cloned.1.call-start = ((), (), s32[]{:S(2)}) async-start(), calls=%async_computation.25 | async-start | bytes 9732096 | tf_op jit(solution)/shard_map/reduce_scatter | solution.py:552
  728.8 35.0 %collective-permute-start.25 = (bf16[320,2176]{1,0:T(8,128)(2,1)}, bf16[320,2176]{1,0:T(8,128)(2,1)S(1)}, u32[]{:S(2)}, u32[]{:S(2)}) collective-permute-start(bf16[320,2176]{1,0:T(8,128)(2,1)} %fusion.21), channel_id=1, source_target_pairs={{0,8},{8,16},{16,24},{24,0},{1,9},{9,17},{17,25},{25,1},{2,10},{10... | collective-permute-start | bytes 4177928 | tf_op jit(solution)/shard_map/ppermute | solution.py:527
  764.4 43.4 %all-to-all-start.12 = ((bf16[4,152,2048]{2,1,0:T(8,128)(2,1)}), bf16[4,152,2048]{2,1,0:T(8,128)(2,1)}, u32[]{:S(2)}, u32[]{:S(2)}) async-start(bf16[4,152,2048]{2,1,0:T(8,128)(2,1)} %fusion.13), calls=%async_computation.12 | async-start | bytes 4980736 | tf_op jit(solution)/shard_map/all_to_all | solution.py:532
  773.4 34.4 %collective-permute-start.27 = (bf16[320,2176]{1,0:T(8,128)(2,1)S(1)}, bf16[320,2176]{1,0:T(8,128)(2,1)S(1)}, u32[]{:S(2)}, u32[]{:S(2)}) collective-permute-start(bf16[320,2176]{1,0:T(8,128)(2,1)S(1)} %fusion.20), channel_id=1, source_target_pairs={{0,8},{8,16},{16,24},{24,0},{1,9},{9,17},{17,25},{25,1},{2,10},{10... | collective-permute-start | bytes 4177928 | tf_op jit(solution)/shard_map/ppermute | solution.py:527
  812.9 32.1 %collective-permute-start.30 = (bf16[320,2048]{1,0:T(8,128)(2,1)}, bf16[320,2048]{1,0:T(8,128)(2,1)}, u32[]{:S(2)}, u32[]{:S(2)}) collective-permute-start(bf16[320,2048]{1,0:T(8,128)(2,1)} %fusion.38), channel_id=1, source_target_pairs={{0,8},{8,16},{16,24},{24,0},{1,9},{9,17},{17,25},{25,1},{2,10},{10... | collective-permute-start | bytes 3932168 | tf_op jit(solution)/shard_map/ppermute | solution.py:527
  812.9 42.5 %all-to-all-start.13 = ((bf16[4,152,2048]{2,1,0:T(8,128)(2,1)}), bf16[4,152,2048]{2,1,0:T(8,128)(2,1)}, u32[]{:S(2)}, u32[]{:S(2)}) async-start(bf16[4,152,2048]{2,1,0:T(8,128)(2,1)} %fusion.12), calls=%async_computation.13 | async-start | bytes 4980736 | tf_op jit(solution)/shard_map/all_to_all | solution.py:532
  817.5 197.0 %reduce-scatter.7.cloned.1.call-start = ((), (), s32[]{:S(2)}) async-start(), calls=%async_computation.26 | async-start | bytes 9437184 | tf_op jit(solution)/shard_map/reduce_scatter | solution.py:552
  869.0 67.6 %all-to-all-start.14 = ((bf16[4,152,2048]{2,1,0:T(8,128)(2,1)}), bf16[4,152,2048]{2,1,0:T(8,128)(2,1)}, u32[]{:S(2)}, u32[]{:S(2)}) async-start(bf16[4,152,2048]{2,1,0:T(8,128)(2,1)} %fusion.11), calls=%async_computation.15 | async-start | bytes 4980736 | tf_op jit(solution)/shard_map/all_to_all | solution.py:532
  880.2 56.4 %collective-permute-start.32 = (bf16[320,2048]{1,0:T(8,128)(2,1)}, bf16[320,2048]{1,0:T(8,128)(2,1)}, u32[]{:S(2)}, u32[]{:S(2)}) collective-permute-start(bf16[320,2048]{1,0:T(8,128)(2,1)} %fusion.37), channel_id=1, source_target_pairs={{0,8},{8,16},{16,24},{24,0},{1,9},{9,17},{17,25},{25,1},{2,10},{10... | collective-permute-start | bytes 3932168 | tf_op jit(solution)/shard_map/ppermute | solution.py:527
  880.9 55.6 %collective-permute-start.33 = (bf16[256,2112]{0,1:T(8,128)(2,1)}, bf16[256,2112]{0,1:T(8,128)(2,1)}, u32[]{:S(2)}, u32[]{:S(2)}) collective-permute-start(bf16[256,2112]{0,1:T(8,128)(2,1)} %reduce-scatter.5.cloned.1.call-done), channel_id=1, source_target_pairs={{0,8},{8,16},{16,24},{24,0},{1,9},{9,17},{17,25},{25,1},{2,10},{10... | collective-permute-start | bytes 3244040 | tf_op jit(solution)/shard_map/ppermute | solution.py:527
  953.3 61.2 %all-to-all-start.15 = ((bf16[4,152,2048]{2,1,0:T(8,128)(2,1)}), bf16[4,152,2048]{2,1,0:T(8,128)(2,1)}, u32[]{:S(2)}, u32[]{:S(2)}) async-start(bf16[4,152,2048]{2,1,0:T(8,128)(2,1)} %fusion.10), calls=%async_computation.17 | async-start | bytes 4980736 | tf_op jit(solution)/shard_map/all_to_all | solution.py:532
  957.8 231.5 %reduce-scatter.9.cloned.1.call-start = ((), (), s32[]{:S(2)}) async-start(), calls=%async_computation.27 | async-start | bytes 14155776 | tf_op jit(solution)/shard_map/reduce_scatter | solution.py:552
  960.4 32.2 %collective-permute-start.35 = (bf16[320,576]{1,0:T(8,128)(2,1)}, bf16[320,576]{1,0:T(8,128)(2,1)}, u32[]{:S(2)}, u32[]{:S(2)}) collective-permute-start(bf16[320,576]{1,0:T(8,128)(2,1)} %get-tuple-element.423), channel_id=1, source_target_pairs={{0,16},{8,24},{16,0},{24,8},{1,17},{9,25},{17,1},{25,9},{2,18},{10... | collective-permute-start | bytes 1105928 | tf_op jit(solution)/shard_map/ppermute | solution.py:557
  960.5 32.2 %collective-permute-start.36 = (bf16[320,576]{1,0:T(8,128)(2,1)}, bf16[320,576]{1,0:T(8,128)(2,1)}, u32[]{:S(2)}, u32[]{:S(2)}) collective-permute-start(bf16[320,576]{1,0:T(8,128)(2,1)} %get-tuple-element.422), channel_id=1, source_target_pairs={{0,24},{8,0},{16,8},{24,16},{1,25},{9,1},{17,9},{25,17},{2,26},{10... | collective-permute-start | bytes 1105928 | tf_op jit(solution)/shard_map/ppermute | solution.py:557
  964.3 50.2 %collective-permute-start.37 = (bf16[256,2112]{0,1:T(8,128)(2,1)}, bf16[256,2112]{0,1:T(8,128)(2,1)}, u32[]{:S(2)}, u32[]{:S(2)}) collective-permute-start(bf16[256,2112]{0,1:T(8,128)(2,1)} %collective-permute-done.33), channel_id=1, source_target_pairs={{0,8},{8,16},{16,24},{24,0},{1,9},{9,17},{17,25},{25,1},{2,10},{10... | collective-permute-start | bytes 3244040 | tf_op jit(solution)/shard_map/ppermute | solution.py:527
  1014.5 270.9 %reduce-scatter.11.cloned.1.call-start = ((), (), s32[]{:S(2)}) async-start(), calls=%async_computation.28 | async-start | bytes 8257536 | tf_op jit(solution)/shard_map/reduce_scatter | solution.py:552
  1083.0 106.3 %collective-permute-start.38 = (bf16[320,2048]{1,0:T(8,128)(2,1)}, bf16[320,2048]{1,0:T(8,128)(2,1)}, u32[]{:S(2)}, u32[]{:S(2)}) collective-permute-start(bf16[320,2048]{1,0:T(8,128)(2,1)} %fusion.36), channel_id=1, source_target_pairs={{0,8},{8,16},{16,24},{24,0},{1,9},{9,17},{17,25},{25,1},{2,10},{10... | collective-permute-start | bytes 3932168 | tf_op jit(solution)/shard_map/ppermute | solution.py:527
  1094.6 34.3 %collective-permute-start.40 = (bf16[64,2048]{1,0:T(8,128)(2,1)}, bf16[64,2048]{1,0:T(8,128)(2,1)}, u32[]{:S(2)}, u32[]{:S(2)}) collective-permute-start(bf16[64,2048]{1,0:T(8,128)(2,1)} %get-tuple-element.431), channel_id=1, source_target_pairs={{0,8},{8,16},{16,24},{24,0},{1,9},{9,17},{17,25},{25,1},{2,10},{10... | collective-permute-start | bytes 786440 | tf_op jit(solution)/shard_map/ppermute | solution.py:557
  1094.6 39.9 %collective-permute-start.41 = (bf16[64,2048]{1,0:T(8,128)(2,1)}, bf16[64,2048]{1,0:T(8,128)(2,1)}, u32[]{:S(2)}, u32[]{:S(2)}) collective-permute-start(bf16[64,2048]{1,0:T(8,128)(2,1)} %get-tuple-element.433), channel_id=1, source_target_pairs={{0,16},{8,24},{16,0},{24,8},{1,17},{9,25},{17,1},{25,9},{2,18},{10... | collective-permute-start | bytes 786440 | tf_op jit(solution)/shard_map/ppermute | solution.py:557
  1094.6 45.5 %collective-permute-start.42 = (bf16[64,2048]{1,0:T(8,128)(2,1)}, bf16[64,2048]{1,0:T(8,128)(2,1)}, u32[]{:S(2)}, u32[]{:S(2)}) collective-permute-start(bf16[64,2048]{1,0:T(8,128)(2,1)} %get-tuple-element.432), channel_id=1, source_target_pairs={{0,24},{8,0},{16,8},{24,16},{1,25},{9,1},{17,9},{25,17},{2,26},{10... | collective-permute-start | bytes 786440 | tf_op jit(solution)/shard_map/ppermute | solution.py:557
  1113.1 76.2 %collective-permute-start.39 = (bf16[256,2112]{0,1:T(8,128)(2,1)}, bf16[256,2112]{0,1:T(8,128)(2,1)S(1)}, u32[]{:S(2)}, u32[]{:S(2)}) collective-permute-start(bf16[256,2112]{0,1:T(8,128)(2,1)} %collective-permute-done.37), channel_id=1, source_target_pairs={{0,8},{8,16},{16,24},{24,0},{1,9},{9,17},{17,25},{25,1},{2,10},{10... | collective-permute-start | bytes 3244040 | tf_op jit(solution)/shard_map/ppermute | solution.py:527
  1143.8 32.8 %collective-permute-start.43 = (bf16[64,2048]{1,0:T(8,128)(2,1)S(1)}, bf16[64,2048]{1,0:T(8,128)(2,1)}, u32[]{:S(2)}, u32[]{:S(2)}) collective-permute-start(bf16[64,2048]{1,0:T(8,128)(2,1)S(1)} %get-tuple-element.402), channel_id=1, source_target_pairs={{0,8},{8,16},{16,24},{24,0},{1,9},{9,17},{17,25},{25,1},{2,10},{10... | collective-permute-start | bytes 786440 | tf_op jit(solution)/shard_map/ppermute | solution.py:557
  1217.7 28.5 %collective-permute-start.47 = (bf16[64,3072]{1,0:T(8,128)(2,1)S(1)}, bf16[64,3072]{1,0:T(8,128)(2,1)S(1)}, u32[]{:S(2)}, u32[]{:S(2)}) collective-permute-start(bf16[64,3072]{1,0:T(8,128)(2,1)S(1)} %get-tuple-element.428), channel_id=1, source_target_pairs={{0,16},{8,24},{16,0},{24,8},{1,17},{9,25},{17,1},{25,9},{2,18},{10... | collective-permute-start | bytes 1179656 | tf_op jit(solution)/shard_map/ppermute | solution.py:557
  (159 other events, 4885.0 us)
Sparse Core Ops, SparseCore 0:
  13.9 51.5 all-gather.5
  67.4 98.7 all-gather.7
  168.2 55.4 all-gather.9
  225.4 78.5 all-gather.11
  306.3 99.8 all-gather.13
  764.0 97.4 reduce-scatter.4
  865.3 80.3 reduce-scatter.6
  1014.6 100.7 reduce-scatter.8
  1189.5 70.7 reduce-scatter.10

commit v3 on v2

--- a/solution.py
+++ b/solution.py
@@ -406,35 +406,42 @@
     for load in loads:
         load.start()
 
-    def stores(half):
+    def store(half, which):
         span = pl.ds(first_row + half * count, count)
         pairs = [
-            (back.at[half], (back_mine, back_theirs)[half]),
-            (out.at[half], (out_mine, out_theirs)[half]),
             (rows.at[half, :, pl.ds(0, width)], all_rows.at[span, :]),
             (grads.at[half], all_grads.at[span, :]),
             (act.at[half], all_act.at[span, :]),
             (grad_gate.at[half], all_gate.at[span, :]),
             (grad_up.at[half], all_up.at[span, :]),
+            (back.at[half], (back_mine, back_theirs)[half]),
+            (out.at[half], (out_mine, out_theirs)[half]),
         ]
-        return [
-            pltpu.make_async_copy(source, target, out_sems.at[half, i])
-            for i, (source, target) in enumerate(pairs)
-        ]
+        source, target = pairs[which]
+        return pltpu.make_async_copy(source, target, out_sems.at[half, which])
 
     def one_half(turn, carry):
         half = 1 - turn
 
-        @pl.when(turn == 0)
-        def _():
-            for load in loads[:5]:
-                load.wait()
-
-        @pl.when(turn == 1)
-        def _():
-            for load in loads[5:]:
-                load.wait()
-
+        def await_loads(first, second):
+            for when, which in enumerate((first, second)):
+                if which:
+
+                    @pl.when(turn == when)
+                    def _(which=which):
+                        for i in which:
+                            loads[i].wait()
+
+        def start_stores(which):
+            for when in range(2):
+
+                @pl.when(turn == when)
+                def _(when=when):
+                    for i in which:
+                        store(1 - when, i).start()
+
+        await_loads((0, 1), (5,))
+        start_stores((0,))
         extra = rows[half, :, width:].astype(single)
         slot_weight = jnp.sum(
             jnp.where(here | (lane == expert[0] + experts), extra, 0.0), axis=1, keepdims=True
@@ -443,7 +450,12 @@
         for lo in range(0, hidden, 256):
             hi = min(lo + 256, hidden)
             gate_pre = product(rows[half, :, :width], gate_w[lo:hi, :], NT)
+            if lo == 0:
+                await_loads((2,), ())
             up_pre = product(rows[half, :, :width], up_w[lo:hi, :], NT)
+            if lo == 0:
+                await_loads((3, 4), (6,))
+                start_stores((1,))
             grad_act = product(grads[half], down_w[lo:hi, :], NT)
             sigmoid = 1.0 / (1.0 + jnp.exp(-gate_pre))
             silu = gate_pre * sigmoid
@@ -457,6 +469,7 @@
                 grad_act * up_pre * sigmoid * (1.0 + gate_pre * (1.0 - sigmoid))
             ).astype(bfloat)
             grad_up[half, :, lo:hi] = (grad_act * silu).astype(bfloat)
+        start_stores((2, 3, 4))
         back[half, :, width:] = jnp.where(here, total, 0.0).astype(bfloat)
         step = min(512, width)
         for lo in range(0, width, step):
@@ -464,26 +477,17 @@
             part = matmul(grad_gate[half], gate_w[:, lo:hi])
             part = part + matmul(grad_up[half], up_w[:, lo:hi])
             back[half, :, lo:hi] = part.astype(bfloat)
+        start_stores((5,))
         for lo in range(0, width, step):
             hi = lo + step
             out[half, :, lo:hi] = matmul(act[half], down_w[:, lo:hi]).astype(bfloat)
-
-        @pl.when(turn == 0)
-        def _():
-            for store in stores(1):
-                store.start()
-
-        @pl.when(turn == 1)
-        def _():
-            for store in stores(0):
-                store.start()
-
+        start_stores((6,))
         return carry
 
     lax.fori_loop(0, 2, one_half, 0)
     for half in range(2):
-        for store in stores(half):
-            store.wait()
+        for which in range(7):
+            store(half, which).wait()
 
 
 def expert_call(
@@ -557,12 +561,29 @@
     return lax.ppermute(value, "ctx", [(i, (i + shift) % size) for i in range(size)])
 
 
+def column_shares(value, device):
+    size = lax.axis_size("ctx")
+    count = value.shape[1] // size
+
+    def share(owner):
+        return lax.dynamic_slice_in_dim(value, owner % size * count, count, axis=1)
+
+    return [share(device)] + [along_ctx(share(device + k), k) for k in range(1, size)]
+
+
+def all_columns_of(part, device):
+    pieces = [part] + [along_ctx(part, shift) for shift in range(1, lax.axis_size("ctx"))]
+    return in_order([piece.astype(single) for piece in pieces], device, 1)
+
+
+def ctx_spread(part, device):
+    pieces = [part] + [along_ctx(part, shift) for shift in range(1, lax.axis_size("ctx"))]
+    return in_order([piece.astype(single) for piece in pieces], device)
+
+
 def sum_ctx(value):
-    size = lax.axis_size("ctx")
     device = lax.axis_index("ctx")
-    low = ctx_total(value, device).astype(bfloat)
-    pieces = [low] + [along_ctx(low, shift) for shift in range(1, size)]
-    return in_order([piece.astype(single) for piece in pieces], device)
+    return ctx_spread(ctx_total(value, device).astype(bfloat), device)
 
 
 def in_order(pieces, device, axis=0):
@@ -659,14 +680,7 @@
 
     hidden_part = fsdp_size * hidden_dev
     part_down = lax.dynamic_slice_in_dim(shared_down, device * hidden_dev, hidden_dev, axis=0)
-    part_shared = jnp.concatenate(
-        [
-            hidden_columns(shared_gate),
-            hidden_columns(shared_up),
-            part_down.reshape(shard_rows, hidden_part),
-        ],
-        axis=1,
-    )
+    part_shared = jnp.concatenate([hidden_columns(shared_gate), hidden_columns(shared_up)], axis=1)
 
     own_rows = jnp.arange(tokens, dtype=jnp.int32)
     link_table = continuation_prompt[0]
@@ -818,12 +832,28 @@
         grad_next, theirs, mine = more_grad_rows()
         grad_theirs.append(theirs)
         grad_mine.append(mine)
-    full_output, shared_shard, attended_low, grad_mine, grad_theirs = together(
-        full_output, part_shared, attended_low, grad_mine, grad_theirs
+    grad_group = jnp.concatenate(grad_ring)
+    (
+        full_output,
+        shared_shard,
+        down_shard,
+        attended_low,
+        grad_mine,
+        grad_theirs,
+        grad_group,
+    ) = together(
+        full_output,
+        part_shared,
+        part_down,
+        attended_low,
+        grad_mine,
+        grad_theirs,
+        grad_group,
     )
     grad_theirs.append(to_core(grad_mine[-1]))
 
     part_shared = gather_rows(shared_shard)
+    part_down = gather_rows(down_shard)
     hidden = inputs_full + matmul(attended_low, full_output)
     ffn_in, ffn_normal, ffn_inverse = rms_forward(hidden, gain_ffn)
     ffn_low = ffn_in.astype(bfloat)
@@ -870,45 +900,43 @@
             expert_down[0],
             kept,
         )
-        shaped = [rows.reshape(chips, slots, -1) for rows in results]
-        out_sends.append(shaped[2:])
-        return shaped[:2]
-
-    def shared_step(first):
-        rows = jnp.concatenate([block[:, :model_width] for block in ffn_ring[first : first + 2]])
-        grads = jnp.concatenate(grad_ring[first : first + 2])
+        return [rows.reshape(chips, slots, -1) for rows in results]
+
+    def shared_step(step):
+        rows = (shared_rows + ffn_ring[len(shared_rows) :])[step][:, :model_width]
         gate_pre = matmul(rows, part_gate)
         up_pre = matmul(rows, part_up)
         act = (jax.nn.silu(gate_pre) * up_pre).astype(bfloat)
-        grad_act = jnp.einsum("td,fd->tf", grads, part_down, preferred_element_type=single)
+        grad_act = jnp.einsum(
+            "td,fd->tf",
+            shared_grad_rows[step * tokens : (step + 1) * tokens],
+            part_down,
+            preferred_element_type=single,
+        )
         grad_gate, grad_up = silu_grads(grad_act, gate_pre, up_pre)
         back = jnp.einsum("tf,df->td", grad_gate, part_gate, preferred_element_type=single)
         back = back + jnp.einsum("tf,df->td", grad_up, part_up, preferred_element_type=single)
-        return rows, grads, act, grad_gate, grad_up, back
-
-    def shared_grads():
-        rows, grads, act, grad_gate, grad_up = [
-            jnp.concatenate([part[i] for part in shared]) for i in range(5)
+        return rows, act, grad_gate, grad_up, back
+
+    def shared_grads(group):
+        act, grad_gate, grad_up = [
+            jnp.concatenate([shared[step][i] for step in range(ctx_size)]) for i in range(1, 4)
         ]
         pieces = [
             jnp.einsum("ta,tb->ab", left, right, preferred_element_type=single).astype(bfloat)
-            for left, right in ((rows, grad_gate), (rows, grad_up), (act, grads))
+            for left, right in ((group, grad_gate), (group, grad_up), (act, shared_grad_rows))
         ]
         return jnp.concatenate(pieces[:2] + [pieces[2].reshape(model_width, hidden_part)], axis=1)
 
-    def block_rows(parts, step):
-        first = step % 2 * tokens
-        return parts[step // 2][first : first + tokens]
-
+    last = ctx_size - 1
     ffn_ring = [ffn_wide]
-    shared = []
-    mines, backs, added, returned, out_added = {}, {}, {}, {}, {}
+    attended_ring = [attended_low]
+    shared, mines, theirs, backs, added, returned, out_added, out_steps = ({} for _ in range(8))
     moving = None
-    first_part = None
 
     def block_part(step):
         part = put_rows(step, returned[step])
-        return part + jnp.pad(block_rows([p[5] for p in shared], step), ((0, 0), (0, EXTRA)))
+        return part + jnp.pad(shared[step][4], ((0, 0), (0, EXTRA)))
 
     def hop(step):
         part = block_part(step)
@@ -916,79 +944,95 @@
             part = part + moving.astype(single)
         return ring_next(part.astype(bfloat))
 
-    for tick in range(ctx_size + 1):
+    for tick in range(ctx_size + 5):
         sent = {}
-        if tick < ctx_size:
+        if tick <= last:
             sent["mine"] = to_chips(pick_rows(tick, ffn_ring[tick]))
-            if tick + 1 < ctx_size:
-                sent["ring"] = ring_next(ffn_ring[tick])
-        else:
-            sent["returned"] = to_chips(added[tick - 2])
-        if tick >= 1:
-            sent["back"] = expert_step(tick - 1, *mines[tick - 1])
-        if 1 <= tick - 3 <= ctx_size - 3:
-            sent["moving"] = hop(tick - 3)
+        if tick < last:
+            sent["ring"] = ring_next(ffn_ring[tick])
+        if 0 <= tick - 1 <= last:
+            sent["theirs"] = to_core(mines[tick - 1])
+        if 0 <= tick - 2 <= last:
+            sent["back"] = expert_step(tick - 2, mines[tick - 2], theirs[tick - 2])
+        if 0 <= tick - 3 <= last:
+            sent["added"] = add_halves(*backs[tick - 3])
+        if 0 <= tick - 4 <= last:
+            sent["returned"] = to_chips(added[tick - 4])
+        if 1 <= tick - 4 <= last:
+            shared[tick - 4] = shared_step(tick - 4)
+            sent["shared"] = shared[tick - 4]
+        if 1 <= tick - 5 <= last:
+            sent["moving"] = hop(tick - 5)
         if tick == 0:
-            sent["theirs"] = grad_theirs[-1]
+            sent["grads"] = grad_theirs[-1]
         if tick == 1:
-            sent["shared"] = part_shared
+            sent["weights"] = (part_shared, part_down)
+        if tick == 4:
+            sent["shared_in"] = (ffn_ring, grad_group, part_gate, part_up, part_down)
+        if tick == ctx_size + 3:
+            sent["shared_all"] = shared
+            sent["group"] = jnp.concatenate(
+                [block[:, :model_width] for block in shared_rows + ffn_ring[len(shared_rows) :]]
+            )
+            sent["out"] = add_halves(*out_sends[1])
+        if tick == ctx_size + 4:
+            sent["shared_grads"] = shared_grads(ffn_group)
+            sent["out_step"] = to_chips(out_added[1])
+        if last <= tick < 2 * last:
+            sent["attended"] = ring_next(attended_ring[-1])
+        if tick == ctx_size + 2:
+            shared[0] = shared_step(0)
+            sent["first"] = shared[0]
+        if tick == ctx_size + 4:
+            sent["out"] = add_halves(*out_sends[2])
         names = sorted(sent)
         sent = dict(zip(names, together(*(sent[name] for name in names))))
-        if tick + 1 < ctx_size:
+        if "mine" in sent:
+            mines[tick] = sent["mine"]
+        if "ring" in sent:
             ffn_ring.append(sent["ring"])
-        if tick >= 1:
-            backs[tick - 1] = sent["back"]
-        if tick == ctx_size:
-            returned[tick - 2] = sent["returned"]
+        if "theirs" in sent:
+            theirs[tick - 1] = sent["theirs"]
+        if "back" in sent:
+            backs[tick - 2] = sent["back"][:2]
+            out_sends.append(sent["back"][2:])
+        if "added" in sent:
+            added[tick - 3] = sent["added"]
+        if "returned" in sent:
+            returned[tick - 4] = sent["returned"]
+        if "shared_in" in sent:
+            shared_rows, shared_grad_rows, part_gate, part_up, part_down = sent["shared_in"]
+        if "shared" in sent:
+            shared[tick - 4] = sent["shared"]
+        if "first" in sent:
+            shared[0] = sent["first"]
+        if "shared_all" in sent:
+            shared = sent["shared_all"]
+        if "attended" in sent:
+            attended_ring.append(sent["attended"])
+        if "out" in sent:
+            out_added[tick - ctx_size - 2] = sent["out"]
+        if "group" in sent:
+            ffn_group = sent["group"]
+        if "out_step" in sent:
+            out_steps[1] = sent["out_step"]
         moving = sent.get("moving", moving)
         if tick == 0:
-            grad_theirs[-1] = sent["theirs"]
+            grad_theirs[-1] = sent["grads"]
         if tick == 1:
-            part_gate = sent["shared"][:, :hidden_part]
-            part_up = sent["shared"][:, hidden_part : 2 * hidden_part]
-            part_down = sent["shared"][:, 2 * hidden_part :].reshape(hidden_part, model_width)
-
-        sends = {}
-        if tick < ctx_size:
-            sends["theirs"] = to_core(sent["mine"])
-            sends["mine"] = sent["mine"]
-        if tick >= 1:
-            sends["added"] = add_halves(*backs[tick - 1])
-        if 2 <= tick < ctx_size:
-            sends["returned"] = to_chips(added[tick - 2])
-        for pair in range(ctx_size // 2):
-            if tick == min(2 * pair + 2, ctx_size - 1):
-                shared.append(shared_step(2 * pair))
-        if tick == 3:
-            sends["first"] = block_part(0)
-        if tick == ctx_size:
-            sends["returned"] = to_chips(sends["added"])
-            sends["moving"] = hop(ctx_size - 2)
-            sends["shared_grads"] = shared_grads()
-            sends["out"] = add_halves(*out_sends[1])
-        names = sorted(sends)
-        sends = dict(zip(names, together(*(sends[name] for name in names))))
-        if tick < ctx_size:
-            mines[tick] = (sends["mine"], sends["theirs"])
-        if tick >= 1:
-            added[tick - 1] = sends["added"]
-        if 2 <= tick < ctx_size:
-            returned[tick - 2] = sends["returned"]
-        if tick == 3:
-            first_part = sends["first"]
-        if tick == ctx_size:
-            returned[ctx_size - 1] = sends["returned"]
-            moving = sends["moving"]
-            out_added = sends["out"]
-
-    shared_part = scatter_rows(sends["shared_grads"])
-    out_steps = {}
+            part_gate = sent["weights"][0][:, :hidden_part]
+            part_up = sent["weights"][0][:, hidden_part:]
+            part_down = sent["weights"][1]
+
+    while len(attended_ring) < ctx_size:
+        attended_ring.append(ring_next(attended_ring[-1]))
+    shared_part = scatter_rows(sent["shared_grads"])
+    first_part = block_part(0)
 
     def next_out(step):
         ahead = (step + 1) % ctx_size
-        return to_chips(out_added), add_halves(*out_sends[ahead]) if step else out_added
-
-    moving, (out_steps[1], out_added) = together(hop(ctx_size - 1), next_out(1))
+        return to_chips(out_added[step]), add_halves(*out_sends[ahead]) if step else out_added[step]
+
     grad_wide = moving.astype(single) + first_part
     grad_ffn = grad_wide[:, :model_width]
     grad_gate_pair = jnp.where(
@@ -1013,37 +1057,27 @@
     grad_attn_low = grad_hidden.astype(bfloat)
 
     def out_hop(step, moving):
-        part = put_rows(step, out_steps[step]) + block_rows(shared_out, step)
+        part = put_rows(step, out_steps[step]) + matmul(shared[step][1], part_down)
         if moving is not None:
             part = part + moving.astype(single)
         return ring_next(part.astype(bfloat))
 
-    shared_out = [matmul(part[2], part_down) for part in shared]
-    out_next = next_out(2)
-    out_moving = out_hop(1, None)
     grad_attended = jnp.einsum(
         "td,vd->tv", grad_attn_low, full_output, preferred_element_type=single
     ).astype(bfloat)
-    grad_w_output = jnp.einsum(
-        "tv,td->vd", attended_low, grad_attn_low, preferred_element_type=single
-    )
-    grad_attended, out_next, shared_part, grad_w_output, out_moving = together(
-        grad_attended, out_next, shared_part, grad_w_output, out_moving
-    )
-    out_steps[2], out_added = out_next
-    output_part = scatter_rows(grad_w_output)
-    shared_ring = [shared_part]
-
-    out_moving = out_hop(2, out_moving)
-    shared_next = ring_next(shared_part)
+    out_next = next_out(2)
+    out_moving = out_hop(1, None)
+    att_shares = column_shares(grad_attn_low, device)
+    grad_attended, out_next, out_moving = together(grad_attended, out_next, out_moving)
+    out_steps[2], out_added[3] = out_next
 
     def weight_grad(left, right):
         return jnp.einsum("ra,rb->ab", left, right, preferred_element_type=single)
 
-    all_rows, all_grads, all_act, all_gate, all_up = kept
-    grad_piece_down = weight_grad(all_act, all_grads)
-    grad_piece_gate = weight_grad(all_rows, all_gate)
-    grad_piece_up = weight_grad(all_rows, all_up)
+    grad_w_output = weight_grad(jnp.concatenate(attended_ring), jnp.concatenate(att_shares))
+
+    out_next = next_out(3)
+    out_moving = out_hop(2, out_moving)
 
     log_rows = log_total[:, :HEADS].T.reshape(HEADS // 2, 2, tokens)
     grad_nope, grad_rope, grad_key_part, grad_value_part, rope_pair_grad = attend_back(
@@ -1060,7 +1094,6 @@
         log_rows,
         grad_attended,
     )
-    out_next = next_out(3)
     (
         grad_nope,
         grad_rope,
@@ -1069,7 +1102,8 @@
         rope_pair_grad,
         out_next,
         out_moving,
-        shared_next,
+        shared_part,
+        grad_w_output,
     ) = together(
         grad_nope,
         grad_rope,
@@ -1078,38 +1112,47 @@
         rope_pair_grad,
         out_next,
         out_moving,
-        shared_next,
-    )
-    out_steps[3], out_added = out_next
-    shared_ring.append(shared_next)
-    shared_next = ring_next(shared_next)
-    grad_kv_block = jnp.concatenate([grad_key_part, grad_value_part], axis=1)
+        shared_part,
+        grad_w_output,
+    )
+    out_steps[3], out_added[4 % ctx_size] = out_next
+    out_next = next_out(0) if ctx_size == 4 else next_out(4)
+    out_moving = out_hop(3, out_moving)
+    output_part = scatter_rows(grad_w_output)
     grad_key_rope = rope_pair_grad[:, :ROPE] + rope_pair_grad[:, ROPE:]
-    grad_w_up = jnp.einsum("tc,tk->ck", latent_group, grad_kv_block, preferred_element_type=single)
+    keys_width = HEADS * NOPE
     grad_latent_group = jnp.einsum(
-        "tk,ck->tc", grad_kv_block, full_up, preferred_element_type=single
+        "tk,ck->tc", grad_key_part, full_up[:, :keys_width], preferred_element_type=single
+    ) + jnp.einsum(
+        "tk,ck->tc", grad_value_part, full_up[:, keys_width:], preferred_element_type=single
     )
     grad_query_pre = jnp.concatenate([grad_nope, grad_rope], axis=1)
-    grad_w_query = jnp.einsum(
-        "td,tq->dq", normed_low, grad_query_pre, preferred_element_type=single
-    )
+    grad_w_query = weight_grad(normed_low, grad_query_pre)
     grad_keys_own = ctx_total(
         by_block(jnp.concatenate([grad_latent_group, grad_key_rope], axis=1).astype(bfloat)), device
     )
-    out_next = next_out(4 % ctx_size)
-    grad_keys_own, output_part, grad_w_query, out_next, shared_next = together(
-        grad_keys_own, output_part, grad_w_query, out_next, shared_next
-    )
-    out_steps[4 % ctx_size], out_added = out_next
-    shared_ring.append(shared_next)
-    out_moving = out_hop(3, out_moving)
-    for step in range(4, ctx_size):
-        out_moving = out_hop(step, out_moving)
-        out_steps[(step + 1) % ctx_size], out_added = next_out((step + 1) % ctx_size)
+    grad_keys_own, output_part, grad_w_query, out_next, out_moving = together(
+        grad_keys_own, output_part, grad_w_query, out_next, out_moving
+    )
+    if ctx_size == 4:
+        out_steps[0] = out_next[0]
+    else:
+        out_steps[4], out_added[5] = out_next
+        for step in range(4, ctx_size):
+            if step > 4:
+                out_steps[step], out_added[(step + 1) % ctx_size] = next_out(step)
+            out_moving = out_hop(step, out_moving)
+        out_steps[0] = to_chips(out_added[0])
     query_part = scatter_rows(grad_w_query)
-    sum_output = sum_ctx(output_part)
-    while len(shared_ring) < ctx_size:
-        shared_ring.append(ring_next(shared_ring[-1]))
+    shared_ring = [shared_part, ring_next(shared_part)]
+    sum_output = all_columns_of(output_part, device)
+    grad_w_up = jnp.concatenate(
+        [
+            weight_grad(latent_group, part).astype(bfloat).reshape(model_width, -1)
+            for part in (grad_key_part, grad_value_part)
+        ],
+        axis=1,
+    )
     grad_latent = grad_keys_own[:, :KV_RANK]
     grad_rope_own = grad_keys_own[:, KV_RANK:]
     grad_latent_in, grad_gain_latent = rms_backward(
@@ -1133,7 +1176,7 @@
         grad_gain_latent.reshape(fsdp_size, -1),
         ((0, 0), (0, shard_rows - latent_gain.shape[0])),
     ).reshape(-1)
-    up_width = grad_w_up.size // model_width
+    up_width = grad_w_up.shape[1]
     small = jnp.concatenate(
         [
             grad_w_router,
@@ -1145,24 +1188,41 @@
     ).astype(bfloat)
     packed_grads = jnp.concatenate(
         [
-            grad_w_up.astype(bfloat).reshape(model_width, up_width),
+            grad_w_up,
             grad_w_down.astype(bfloat),
             jnp.pad(small, ((0, 0), (0, -small.shape[1] % 128))),
         ],
         axis=1,
     )
-    query_part, out_moving, shared_ring, packed_grads, sum_output = together(
-        query_part, out_moving, shared_ring, packed_grads, sum_output
-    )
-    first_out = put_rows(0, out_steps[0]) + block_rows(shared_out, 0)
+    packed_grads, shared_ring, kept = together(packed_grads, shared_ring, kept)
+    all_rows, all_grads, all_act, all_gate, all_up = kept
+    grad_piece_down = weight_grad(all_act, all_grads)
+    while len(shared_ring) < ctx_size:
+        shared_ring.append(ring_next(shared_ring[-1]))
+    query_part, packed_grads, shared_ring, sum_output, grad_piece_down, kept = together(
+        query_part, packed_grads, shared_ring, sum_output, grad_piece_down, kept
+    )
+    packed_part = scatter_rows(with_layout_constraint(packed_grads, by_rows))
+    all_rows, all_grads, all_act, all_gate, all_up = kept
+    grad_piece_gate = weight_grad(all_rows, all_gate)
+    query_total = ctx_total(query_part, device).astype(bfloat)
+    query_total, grad_piece_gate, kept = together(query_total, grad_piece_gate, kept)
+    all_rows, all_grads, all_act, all_gate, all_up = kept
+    grad_piece_up = weight_grad(all_rows, all_up)
+    sum_query = ctx_spread(query_total, device)
+    first_out = put_rows(0, out_steps[0]) + matmul(shared[0][1], part_down)
     layer_output = (hidden + out_moving.astype(single) + first_out).astype(bfloat)
-    packed_part = scatter_rows(with_layout_constraint(packed_grads, by_rows))
-    sum_query = sum_ctx(query_part)
-    packed_part, sum_query = together(packed_part, sum_query)
+    packed_part, sum_query, grad_piece_up = together(packed_part, sum_query, grad_piece_up)
     sum_packed = with_layout_constraint(
         sum_ctx(with_layout_constraint(packed_part, by_rows)), by_rows
     )
-    sum_up = sum_packed[:, :up_width].reshape(latent_up.shape)
+    sum_up = jnp.concatenate(
+        [
+            part.reshape(latent_up.shape[0], -1)
+            for part in (sum_packed[:, : up_width // 2], sum_packed[:, up_width // 2 : up_width])
+        ],
+        axis=1,
+    )
     sum_down = sum_packed[:, up_width : up_width + down_width]
     sum_small = sum_packed[:, up_width + grad_w_down.shape[1] :]
     sum_router = sum_small[:, :experts]

time: 1370 us -> 1380 us (level)
  waiting for transfers between devices: 423 us -> 359 us
  local copies, waits for them, and re-layouts: 118 us -> 171 us
  other arithmetic: 85.4 us -> 107 us
  starting transfers between devices: 194 us -> 176 us
  matrix products: 325 us -> 342 us
    all_to_all x16, waiting for transfers between devices: 48.8 us -> 8.44 us  [to_chips(): lax.all_to_all(value, 'fsdp', split_axis=0, concat_axis=0, tiled=True, ax...]
    ppermute x27, starting transfers between devices: 88.6 us -> 52.5 us  [along_ctx(): lax.ppermute(value, 'ctx', [(i, (i + shift) % size) for i in range(size)])]
    ppermute x27, waiting for transfers between devices: 173 us -> 138 us  [along_ctx(): lax.ppermute(value, 'ctx', [(i, (i + shift) % size) for i in range(size)])]
    dot_general x3 -> x7, matrix products: 63.5 us -> 95.5 us  [weight_grad(): return jnp.einsum('ra,rb->ab', left, right, preferred_element_type=single)]
    optimization_barrier x0 -> x8, local copies, waits for them, and re-layouts: none -> 25 us  [together(): return lax.optimization_barrier(values)]
    concatenate x1 -> x3, local copies, waits for them, and re-layouts: 0.84 us -> 23.6 us  [the longest x1 9.99 us: local(): grad_group = jnp.concatenate(grad_ring)]
    dot_general x6, matrix products: 45.4 us -> 29.2 us  [the longest x4 18 us: shared_step(): jnp.einsum('td,fd->tf', shared_grad_rows[step * tokens:(step + 1) * token...]
    ppermute x15 -> x18, waiting for transfers between devices: 142 us -> 155 us  [ring_next(): lax.ppermute(value, 'ctx', [(i, (i + 1) % size) for i in range(size)])]
  transfers between devices with their start and end apart: 83 -> 87, of which waited for: 35 -> 26; matrix products, arithmetic and copies ran while one was open for 35% -> 39% of each run, Pallas kernels for 15% -> 14%
where the time goes in v3:
time: 1380 us; the launch traced here: 1370 us
  waiting for transfers between devices  359 us (26%)
  matrix products  342 us (25%)
  Pallas kernels  199 us (14%)
  starting transfers between devices  176 us (13%)
  local copies, waits for them, and re-layouts  171 us (12%)
  other arithmetic  107 us (8%)
  between operations  17.2 us (1%)
    ppermute x18, waiting for transfers between devices, ring_next(): lax.ppermute(value, 'ctx', [(i, (i + 1) % size) for i in range(size)])  155 us
    pallas_call x4, Pallas kernels, expert_call(): pl.pallas_call(functools.partial(expert_kernel, step * 2 * count, experts...  141 us
    ppermute x27, waiting for transfers between devices, along_ctx(): lax.ppermute(value, 'ctx', [(i, (i + shift) % size) for i in range(size)])  138 us
    dot_general x7, matrix products, weight_grad(): return jnp.einsum('ra,rb->ab', left, right, preferred_element_type=single)  95.5 us
    dot_general x21, matrix products, matmul(): return jnp.dot(left, right, preferred_element_type=single)  76.8 us
    all_to_all x16, starting transfers between devices, to_chips(): lax.all_to_all(value, 'fsdp', split_axis=0, concat_axis=0, tiled=True, ax...  74.4 us
    ppermute x27, starting transfers between devices, along_ctx(): lax.ppermute(value, 'ctx', [(i, (i + shift) % size) for i in range(size)])  52.5 us
    all_gather x6, waiting for transfers between devices, gather_rows(): return lax.all_gather(value, 'fsdp', axis=0, tiled=True)  49.6 us
  transfers between devices with their start and end apart: 87, of which 26 were waited for; matrix products, arithmetic and copies ran while one was open for 39% of the time, Pallas kernels for 14%

profile of v3, /device:TPU:0, one launch (start us, length us, event | category | flops | bytes accessed | tf_op | source)
XLA Modules:
  0.0 1371.1 jit_solution(3433861060812192689)
XLA Ops:
  19.1 5.3 all-to-all-start
  32.5 26.0 %collective-permute-done = s32[320,6]{0,1:T(8,128)S(1)} collective-permute-done((s32[320,6]{0,1:T(8,128)S(1)}, s32[320,6]{0,1:T(8,128)S(1)}, u32[]{:S(2)}, u32[]{:S(2)}) %collective-permute-start) | collective-permute-done | bytes 7712 | tf_op jit(solution)/shard_map/ppermute | solution.py:561
  92.4 20.7 %collective-permute-done.4 = bf16[320,576]{1,0:T(8,128)(2,1)S(1)} collective-permute-done((bf16[320,576]{1,0:T(8,128)(2,1)S(1)}, bf16[320,576]{1,0:T(8,128)(2,1)S(1)}, u32[]{:S(2)}, u32[]{:S(2)}) %collective-permute-start.4) | collective-permute-done | bytes 368672 | tf_op jit(solution)/shard_map/ppermute | solution.py:561
  113.0 16.9 %collective-permute-done.5 = bf16[320,576]{1,0:T(8,128)(2,1)S(1)} collective-permute-done((bf16[320,576]{1,0:T(8,128)(2,1)S(1)}, bf16[320,576]{1,0:T(8,128)(2,1)S(1)}, u32[]{:S(2)}, u32[]{:S(2)}) %collective-permute-start.5) | collective-permute-done | bytes 368672 | tf_op jit(solution)/shard_map/ppermute | solution.py:561
  131.4 33.4 %all-gather.9.cloned.1.call-done = bf16[2048,3072]{1,0:T(8,128)(2,1)} async-done(((bf16[256,3072]{1,0:T(8,128)(2,1)}), bf16[2048,3072]{1,0:T(8,128)(2,1)}) %all-gather.9.cloned.1.call-update) | async-done | bytes 12582928 | tf_op jit(solution)/shard_map/all_gather | solution.py:552
  175.8 9.5 fusion.178.nope.rope
  185.3 22.1 %collective-permute-done.9 = bf16[320,2048]{1,0:T(8,128)(2,1)} collective-permute-done((bf16[320,2048]{1,0:T(8,128)(2,1)}, bf16[320,2048]{1,0:T(8,128)(2,1)}, u32[]{:S(2)}, u32[]{:S(2)}) %collective-permute-start.9) | collective-permute-done | bytes 1310752 | tf_op jit(solution)/shard_map/ppermute | solution.py:531
  210.2 12.0 all-gather.11.cloned.1.call-done
  261.8 10.0 concatenate.82
  271.8 10.6 convolution_convert_fusion.keys.values
  282.4 26.4 %shard_map.306 = (bf16[320,2048]{1,0:T(8,128)(2,1)S(1)}, f32[320,128]{1,0:T(8,128)S(1)}) custom-call(s32[1]{0:T(128)} %bitcast.13.link, f32[320,3072]{1,0:T(8,128)S(1)} %copy-done.2, f32[320,3072]{1,0:T(8,128)S(1)} %copy-done.2, f32[320,128]{1,0:T(8,128)S(1)} %get-tuple-element.583.cos, f32[320,128]{1,0:T(8,128)S(1)} %get-tuple-element.584.sin, ...), custom_call_target="tpu_custom_call" | custom-call | flops 2214592512 | bytes 16384000 | tf_op jit(solution)/shard_map/pallas_call | solution.py:312
  309.0 10.2 all-gather.15.cloned.1.call-start
  319.5 8.8 multiply_reduce_fusion.2
  330.8 5.3 convolution_convert_fusion.4
  340.8 5.1 maximum_maximum_fusion
  351.1 33.3 %collective-permute-done.13 = bf16[320,2176]{1,0:T(8,128)(2,1)} collective-permute-done((bf16[320,2176]{1,0:T(8,128)(2,1)}, bf16[320,2176]{1,0:T(8,128)(2,1)}, u32[]{:S(2)}, u32[]{:S(2)}) %collective-permute-start.13) | collective-permute-done | bytes 1392672 | tf_op jit(solution)/shard_map/ppermute | solution.py:531
  393.6 35.2 %collective-permute-done.14 = bf16[320,2176]{1,0:T(8,128)(2,1)} collective-permute-done((bf16[320,2176]{1,0:T(8,128)(2,1)}, bf16[320,2176]{1,0:T(8,128)(2,1)}, u32[]{:S(2)}, u32[]{:S(2)}) %collective-permute-start.14) | collective-permute-done | bytes 1392672 | tf_op jit(solution)/shard_map/ppermute | solution.py:531
  442.6 35.5 %shard_map.307 = (bf16[608,2176]{1,0:T(8,128)(2,1)}, bf16[608,2176]{1,0:T(8,128)(2,1)}, bf16[608,2048]{1,0:T(8,128)(2,1)}, bf16[608,2048]{1,0:T(8,128)(2,1)}, bf...) custom-call(s32[1]{0:T(128)} %bitcast.20.expert, ...), custom_call_target="tpu_custom_call" | custom-call | flops 21038628864 | bytes 43671552 | tf_op jit(solution)/shard_map/pallas_call | solution.py:505
  489.1 35.3 %shard_map.308 = (bf16[608,2176]{1,0:T(8,128)(2,1)}, bf16[608,2176]{1,0:T(8,128)(2,1)}, bf16[608,2048]{1,0:T(8,128)(2,1)}, bf16[608,2048]{1,0:T(8,128)(2,1)}, bf...) custom-call(s32[1]{0:T(128)} %bitcast.20.expert, ...), custom_call_target="tpu_custom_call", output_to_operand_aliasing={{4}: (8, {}), {5}: (9, {}), {6}: (10, {}), {7}: (11, {}), {... | custom-call | flops 21038628864 | bytes 43671552 | tf_op jit(solution)/shard_map/pallas_call | solution.py:505
  529.0 6.2 fusion.181
  541.5 35.4 %shard_map.309 = (bf16[608,2176]{1,0:T(8,128)(2,1)}, bf16[608,2176]{1,0:T(8,128)(2,1)}, bf16[608,2048]{1,0:T(8,128)(2,1)}, bf16[608,2048]{1,0:T(8,128)(2,1)}, bf...) custom-call(s32[1]{0:T(128)} %bitcast.20.expert, ...), custom_call_target="tpu_custom_call", output_to_operand_aliasing={{4}: (8, {}), {5}: (9, {}), {6}: (10, {}), {7}: (11, {}), {... | custom-call | flops 21038628864 | bytes 43671552 | tf_op jit(solution)/shard_map/pallas_call | solution.py:505
  589.8 5.0 fusion.162
  600.5 5.0 fusion.166
  611.7 5.4 fusion.73
  638.0 35.2 %shard_map.310 = (bf16[608,2176]{1,0:T(8,128)(2,1)}, bf16[608,2176]{1,0:T(8,128)(2,1)}, bf16[608,2048]{1,0:T(8,128)(2,1)}, bf16[608,2048]{1,0:T(8,128)(2,1)}, bf...) custom-call(s32[1]{0:T(128)} %bitcast.20.expert, ...), custom_call_target="tpu_custom_call", output_to_operand_aliasing={{4}: (8, {}), {5}: (9, {}), {6}: (10, {}), {7}: (11, {}), {... | custom-call | flops 21038628864 | bytes 43671552 | tf_op jit(solution)/shard_map/pallas_call | solution.py:505
  699.4 5.0 all-to-all-start.10
  721.3 26.4 %collective-permute-done.27 = bf16[320,2176]{1,0:T(8,128)(2,1)S(1)} collective-permute-done((bf16[320,2176]{1,0:T(8,128)(2,1)S(1)}, bf16[320,2176]{1,0:T(8,128)(2,1)S(1)}, u32[]{:S(2)}, u32[]{:S(2)}) %collective-permute-start.27) | collective-permute-done | bytes 1392672 | tf_op jit(solution)/shard_map/ppermute | solution.py:531
  753.5 5.2 multiply_convert_fusion.1
  760.8 10.0 concatenate.84
  783.1 26.0 %collective-permute-done.28 = bf16[320,2176]{1,0:T(8,128)(2,1)} collective-permute-done((bf16[320,2176]{1,0:T(8,128)(2,1)S(1)}, bf16[320,2176]{1,0:T(8,128)(2,1)}, u32[]{:S(2)}, u32[]{:S(2)}) %collective-permute-start.28) | collective-permute-done | bytes 1392672 | tf_op jit(solution)/shard_map/ppermute | solution.py:531
  818.2 8.7 convolution_convert_fusion.7
  827.0 8.2 convolution_convert_fusion.6
  835.3 5.9 convolution_convert_fusion.5
  841.2 7.0 reshape.511
  852.7 7.2 pad_maximum_fusion
  866.5 5.7 add_convert_fusion.4
  888.7 5.5 fusion.41
  920.0 16.4 %collective-permute-done.36 = bf16[320,512]{0,1:T(8,128)(2,1)S(1)} collective-permute-done((bf16[320,512]{0,1:T(8,128)(2,1)S(1)}, bf16[320,512]{0,1:T(8,128)(2,1)S(1)}, u32[]{:S(2)}, u32[]{:S(2)}) %collective-permute-start.36) | collective-permute-done | bytes 327712 | tf_op jit(solution)/shard_map/ppermute | solution.py:561
  936.4 16.3 %collective-permute-done.37 = bf16[320,512]{0,1:T(8,128)(2,1)S(1)} collective-permute-done((bf16[320,512]{0,1:T(8,128)(2,1)S(1)}, bf16[320,512]{0,1:T(8,128)(2,1)S(1)}, u32[]{:S(2)}, u32[]{:S(2)}) %collective-permute-start.37) | collective-permute-done | bytes 327712 | tf_op jit(solution)/shard_map/ppermute | solution.py:561
  962.5 5.4 fusion.40
  967.9 8.1 collective-permute-start.35
  976.0 5.8 fusion.2
  983.5 31.0 %shard_map.311 = (bf16[320,2048]{1,0:T(8,128)(2,1)S(1)}, bf16[320,1024]{1,0:T(8,128)(2,1)S(1)}, bf16[1280,2048]{1,0:T(8,128)(2,1)}, bf16[1280,2048]{1,0:T(8,128)(2,1)}, f32[1280,128]{1,0:T(8,128)S(1)}) custom-call(s32[1]{0:T(128)} %bitcast.13.link, f32[320,3072]{1,0:T(8,128)} %fusion.178.nope.rope, f32[320,3072]{1,0:T(8,128)} %fusion.178.nope.rope, ...), custom_call_target="tpu_custom_call" | custom-call | flops 6643777536 | bytes 30801920 | tf_op jit(solution)/shard_map/pallas_call | solution.py:337
  1015.5 5.3 fusion.39
  1026.5 6.8 fusion.33
  1048.1 9.6 fusion.176
  1057.7 5.9 collective-permute-done.39
  1063.6 16.4 %collective-permute-done.40 = bf16[320,576]{1,0:T(8,128)(2,1)} collective-permute-done((bf16[320,576]{1,0:T(8,128)(2,1)S(1)}, bf16[320,576]{1,0:T(8,128)(2,1)}, u32[]{:S(2)}, u32[]{:S(2)}) %collective-permute-start.40) | collective-permute-done | bytes 368672 | tf_op jit(solution)/shard_map/ppermute | solution.py:561
  1086.0 5.5 fusion.192
  1093.4 7.6 convolution_convert_fusion.14
  1105.5 7.8 convolution_convert_fusion.13
  1117.8 5.6 collective-permute-start.43
  1131.4 11.4 fusion.29
  1146.5 6.3 fusion.1
  1153.6 20.8 %fusion.193 = f32[704,2048]{1,0:T(8,128)} fusion(bf16[4864,704]{1,0:T(8,128)(2,1)} %get-tuple-element.403, bf16[4864,2048]{1,0:T(8,128)(2,1)} %get-tuple-element.404), kind=kOutput, calls=%fused_computation.407 | convolution fusion | flops 14025752576 | bytes 32538624 | tf_op jit(solution)/shard_map/ra,rb->ab/dot_general | solution.py:1075
  1180.7 6.9 collective-permute-done.44
  1187.6 5.8 collective-permute-start.45
  1193.4 5.9 fusion.72
  1211.2 5.6 collective-permute-done.45
  1237.1 23.8 %fusion.194 = f32[2048,704]{0,1:T(8,128)} fusion(bf16[4864,2048]{1,0:T(8,128)(2,1)} %get-tuple-element.414, bf16[4864,704]{1,0:T(8,128)(2,1)} %get-tuple-element.411), kind=kOutput, calls=%fused_computation.408 | convolution fusion | flops 14025752576 | bytes 32538624 | tf_op jit(solution)/shard_map/ra,rb->ab/dot_general | solution.py:1075
  1271.5 20.0 %fusion.195 = f32[2048,704]{0,1:T(8,128)} fusion(bf16[4864,2048]{1,0:T(8,128)(2,1)S(1)} %bitcast.268, bf16[4864,704]{1,0:T(8,128)(2,1)} %get-tuple-element.415), kind=kOutput, calls=%fused_computation.409 | convolution fusion | flops 14025752576 | bytes 32538624 | tf_op jit(solution)/shard_map/ra,rb->ab/dot_general | solution.py:1075
  1313.1 6.5 collective-permute-done.56
  1321.6 5.5 collective-permute-start.58
  1339.9 9.9 collective-permute-done.59
  (746 shorter events, 497.6 us)
Async XLA Ops:
  7.2 58.3 %all-gather.7.cloned.1.call-start = ((), (), s32[]{:S(2)}) async-start(), calls=%async_computation.20 | async-start | bytes 2764800 | tf_op jit(solution)/shard_map/all_gather | solution.py:552
  19.1 42.3 %all-to-all-start = ((bf16[4,152,2048]{2,1,0:T(8,128)(2,1)}), bf16[4,152,2048]{2,1,0:T(8,128)(2,1)}, u32[]{:S(2)}, u32[]{:S(2)}) async-start(bf16[4,152,2048]{2,1,0:T(8,128)(2,1)} %convolution_convert_fusion.12), calls=%async_computation | async-start | bytes 4980736 | tf_op jit(solution)/shard_map/all_to_all | solution.py:536
  24.4 140.4 %all-gather.9.cloned.1.call-start = ((), (), s32[]{:S(2)}) async-start(), calls=%async_computation.21 | async-start | bytes 14155776 | tf_op jit(solution)/shard_map/all_gather | solution.py:552
  68.6 62.8 %collective-permute-start.8 = (bf16[4,152,2048]{2,1,0:T(8,128)(2,1)}, bf16[4,152,2048]{2,1,0:T(8,128)(2,1)}, u32[]{:S(2)}, u32[]{:S(2)}) collective-permute-start(bf16[4,152,2048]{2,1,0:T(8,128)(2,1)} %all-to-all-done), channel_id=1, source_target_pairs={{0,1},{1,0},{2,3},{3,2},{4,5},{5,4},{6,7},{7,6},{8,9},{9,8},{10,11... | collective-permute-start | bytes 7471112 | tf_op jit(solution)/shard_map/ppermute | solution.py:548
  70.4 61.0 %collective-permute-start.7 = (bf16[320,2048]{1,0:T(8,128)(2,1)}, bf16[320,2048]{1,0:T(8,128)(2,1)}, u32[]{:S(2)}, u32[]{:S(2)}) collective-permute-start(bf16[320,2048]{1,0:T(8,128)(2,1)} %collective-permute-done.3), channel_id=1, source_target_pairs={{0,8},{8,16},{16,24},{24,0},{1,9},{9,17},{17,25},{25,1},{2,10},{10... | collective-permute-start | bytes 3932168 | tf_op jit(solution)/shard_map/ppermute | solution.py:531
  77.0 54.4 %all-to-all-start.1 = ((bf16[4,152,2048]{2,1,0:T(8,128)(2,1)}), bf16[4,152,2048]{2,1,0:T(8,128)(2,1)}, u32[]{:S(2)}, u32[]{:S(2)}) async-start(bf16[4,152,2048]{2,1,0:T(8,128)(2,1)} %convolution_convert_fusion.11), calls=%async_computation.1 | async-start | bytes 4980736 | tf_op jit(solution)/shard_map/all_to_all | solution.py:536
  81.6 140.6 %all-gather.11.cloned.1.call-start = ((), (), s32[]{:S(2)}) async-start(), calls=%async_computation.22 | async-start | bytes 4718592 | tf_op jit(solution)/shard_map/all_gather | solution.py:552
  88.5 41.4 %collective-permute-start.5 = (bf16[320,576]{1,0:T(8,128)(2,1)S(1)}, bf16[320,576]{1,0:T(8,128)(2,1)S(1)}, u32[]{:S(2)}, u32[]{:S(2)}) collective-permute-start(bf16[320,576]{1,0:T(8,128)(2,1)S(1)} %pad_maximum_fusion.5), channel_id=1, source_target_pairs={{0,16},{8,24},{16,0},{24,8},{1,17},{9,25},{17,1},{25,9},{2,18},{10... | collective-permute-start | bytes 1105928 | tf_op jit(solution)/shard_map/ppermute | solution.py:561
  90.1 39.9 %collective-permute-start.6 = (bf16[320,576]{1,0:T(8,128)(2,1)S(1)}, bf16[320,576]{1,0:T(8,128)(2,1)S(1)}, u32[]{:S(2)}, u32[]{:S(2)}) collective-permute-start(bf16[320,576]{1,0:T(8,128)(2,1)S(1)} %pad_maximum_fusion.5), channel_id=1, source_target_pairs={{0,24},{8,0},{16,8},{24,16},{1,25},{9,1},{17,9},{25,17},{2,26},{10... | collective-permute-start | bytes 1105928 | tf_op jit(solution)/shard_map/ppermute | solution.py:561
  164.9 45.4 %collective-permute-start.10 = (bf16[4,152,2048]{2,1,0:T(8,128)(2,1)}, bf16[4,152,2048]{2,1,0:T(8,128)(2,1)}, u32[]{:S(2)}, u32[]{:S(2)}) collective-permute-start(bf16[4,152,2048]{2,1,0:T(8,128)(2,1)} %all-to-all-done.1), channel_id=1, source_target_pairs={{0,1},{1,0},{2,3},{3,2},{4,5},{5,4},{6,7},{7,6},{8,9},{9,8},{10,11... | collective-permute-start | bytes 7471112 | tf_op jit(solution)/shard_map/ppermute | solution.py:548
  169.4 40.8 %all-to-all-start.2 = ((bf16[4,152,2048]{2,1,0:T(8,128)(2,1)}), bf16[4,152,2048]{2,1,0:T(8,128)(2,1)}, u32[]{:S(2)}, u32[]{:S(2)}) async-start(bf16[4,152,2048]{2,1,0:T(8,128)(2,1)} %convolution_convert_fusion.10), calls=%async_computation.2 | async-start | bytes 4980736 | tf_op jit(solution)/shard_map/all_to_all | solution.py:536
  174.0 135.0 %all-gather.13.cloned.1.call-start = ((), (), s32[]{:S(2)}) async-start(), calls=%async_computation.23 | async-start | bytes 9437184 | tf_op jit(solution)/shard_map/all_gather | solution.py:552
  242.5 66.4 %collective-permute-start.11 = (bf16[4,152,2048]{2,1,0:T(8,128)(2,1)}, bf16[4,152,2048]{2,1,0:T(8,128)(2,1)}, u32[]{:S(2)}, u32[]{:S(2)}) collective-permute-start(bf16[4,152,2048]{2,1,0:T(8,128)(2,1)} %all-to-all-done.2), channel_id=1, source_target_pairs={{0,1},{1,0},{2,3},{3,2},{4,5},{5,4},{6,7},{7,6},{8,9},{9,8},{10,11... | collective-permute-start | bytes 7471112 | tf_op jit(solution)/shard_map/ppermute | solution.py:548
  248.4 60.5 %all-to-all-start.3 = ((bf16[4,152,2048]{2,1,0:T(8,128)(2,1)}), bf16[4,152,2048]{2,1,0:T(8,128)(2,1)}, u32[]{:S(2)}, u32[]{:S(2)}) async-start(bf16[4,152,2048]{2,1,0:T(8,128)(2,1)} %convolution_convert_fusion.9), calls=%async_computation.3 | async-start | bytes 4980736 | tf_op jit(solution)/shard_map/all_to_all | solution.py:536
  252.9 178.7 %all-gather.17.cloned.1.call-start = ((), (), s32[]{:S(2)}) async-start(), calls=%async_computation.25 | async-start | bytes 3244032 | tf_op jit(solution)/shard_map/all_gather | solution.py:552
  309.0 122.7 %all-gather.15.cloned.1.call-start = ((), (), s32[]{:S(2)}) async-start(), calls=%async_computation.24 | async-start | bytes 6488064 | tf_op jit(solution)/shard_map/all_gather | solution.py:552
  319.2 65.2 %collective-permute-start.12 = (bf16[4,152,2048]{2,1,0:T(8,128)(2,1)}, bf16[4,152,2048]{2,1,0:T(8,128)(2,1)}, u32[]{:S(2)}, u32[]{:S(2)}) collective-permute-start(bf16[4,152,2048]{2,1,0:T(8,128)(2,1)} %all-to-all-done.3), channel_id=1, source_target_pairs={{0,1},{1,0},{2,3},{3,2},{4,5},{5,4},{6,7},{7,6},{8,9},{9,8},{10,11... | collective-permute-start | bytes 7471112 | tf_op jit(solution)/shard_map/ppermute | solution.py:548
  336.2 48.2 %all-to-all-start.4 = ((bf16[4,152,2176]{2,1,0:T(8,128)(2,1)}), bf16[4,152,2176]{2,1,0:T(8,128)(2,1)}, u32[]{:S(2)}, u32[]{:S(2)}) async-start(bf16[4,152,2176]{2,1,0:T(8,128)(2,1)} %convolution_convert_fusion.4), calls=%async_computation.4 | async-start | bytes 5292032 | tf_op jit(solution)/shard_map/all_to_all | solution.py:536
  349.5 34.9 %collective-permute-start.13 = (bf16[320,2176]{1,0:T(8,128)(2,1)}, bf16[320,2176]{1,0:T(8,128)(2,1)}, u32[]{:S(2)}, u32[]{:S(2)}) collective-permute-start(bf16[320,2176]{1,0:T(8,128)(2,1)} %copy.278), channel_id=1, source_target_pairs={{0,8},{8,16},{16,24},{24,0},{1,9},{9,17},{17,25},{25,1},{2,10},{10... | collective-permute-start | bytes 4177928 | tf_op jit(solution)/shard_map/ppermute | solution.py:531
  384.4 47.2 %collective-permute-start.15 = (bf16[4,152,2176]{2,1,0:T(8,128)(2,1)}, bf16[4,152,2176]{2,1,0:T(8,128)(2,1)}, u32[]{:S(2)}, u32[]{:S(2)}) collective-permute-start(bf16[4,152,2176]{2,1,0:T(8,128)(2,1)} %all-to-all-done.4), channel_id=1, source_target_pairs={{0,1},{1,0},{2,3},{3,2},{4,5},{5,4},{6,7},{7,6},{8,9},{9,8},{10,11... | collective-permute-start | bytes 7938056 | tf_op jit(solution)/shard_map/ppermute | solution.py:548
  388.8 42.8 %all-to-all-start.5 = ((bf16[4,152,2176]{2,1,0:T(8,128)(2,1)}), bf16[4,152,2176]{2,1,0:T(8,128)(2,1)}, u32[]{:S(2)}, u32[]{:S(2)}) async-start(bf16[4,152,2176]{2,1,0:T(8,128)(2,1)} %convolution_convert_fusion.3), calls=%async_computation.5 | async-start | bytes 5292032 | tf_op jit(solution)/shard_map/all_to_all | solution.py:536
  393.5 35.3 %collective-permute-start.14 = (bf16[320,2176]{1,0:T(8,128)(2,1)}, bf16[320,2176]{1,0:T(8,128)(2,1)}, u32[]{:S(2)}, u32[]{:S(2)}) collective-permute-start(bf16[320,2176]{1,0:T(8,128)(2,1)} %collective-permute-done.13), channel_id=1, source_target_pairs={{0,8},{8,16},{16,24},{24,0},{1,9},{9,17},{17,25},{25,1},{2,10},{10... | collective-permute-start | bytes 4177928 | tf_op jit(solution)/shard_map/ppermute | solution.py:531
  431.6 46.5 %collective-permute-start.17 = (bf16[4,152,2176]{2,1,0:T(8,128)(2,1)}, bf16[4,152,2176]{2,1,0:T(8,128)(2,1)}, u32[]{:S(2)}, u32[]{:S(2)}) collective-permute-start(bf16[4,152,2176]{2,1,0:T(8,128)(2,1)} %all-to-all-done.5), channel_id=1, source_target_pairs={{0,1},{1,0},{2,3},{3,2},{4,5},{5,4},{6,7},{7,6},{8,9},{9,8},{10,11... | collective-permute-start | bytes 7938056 | tf_op jit(solution)/shard_map/ppermute | solution.py:548
  436.2 41.9 %all-to-all-start.6 = ((bf16[4,152,2176]{2,1,0:T(8,128)(2,1)}), bf16[4,152,2176]{2,1,0:T(8,128)(2,1)}, u32[]{:S(2)}, u32[]{:S(2)}) async-start(bf16[4,152,2176]{2,1,0:T(8,128)(2,1)} %convolution_convert_fusion.2), calls=%async_computation.6 | async-start | bytes 5292032 | tf_op jit(solution)/shard_map/all_to_all | solution.py:536
  440.8 37.4 %collective-permute-start.16 = (bf16[320,2176]{1,0:T(8,128)(2,1)}, bf16[320,2176]{1,0:T(8,128)(2,1)}, u32[]{:S(2)}, u32[]{:S(2)}) collective-permute-start(bf16[320,2176]{1,0:T(8,128)(2,1)} %collective-permute-done.14), channel_id=1, source_target_pairs={{0,8},{8,16},{16,24},{24,0},{1,9},{9,17},{17,25},{25,1},{2,10},{10... | collective-permute-start | bytes 4177928 | tf_op jit(solution)/shard_map/ppermute | solution.py:531
  478.1 46.3 %collective-permute-start.18 = (bf16[4,152,2176]{2,1,0:T(8,128)(2,1)}, bf16[4,152,2176]{2,1,0:T(8,128)(2,1)}, u32[]{:S(2)}, u32[]{:S(2)}) collective-permute-start(bf16[4,152,2176]{2,1,0:T(8,128)(2,1)} %bitcast.333), channel_id=1, source_target_pairs={{0,1},{1,0},{2,3},{3,2},{4,5},{5,4},{6,7},{7,6},{8,9},{9,8},{10,11... | collective-permute-start | bytes 7938056 | tf_op jit(solution)/shard_map/ppermute | solution.py:548
  478.4 49.9 %collective-permute-start.19 = (bf16[320,2048]{1,0:T(8,128)(2,1)S(1)}, bf16[320,2048]{1,0:T(8,128)(2,1)}, u32[]{:S(2)}, u32[]{:S(2)}) collective-permute-start(bf16[320,2048]{1,0:T(8,128)(2,1)S(1)} %get-tuple-element.244), channel_id=1, source_target_pairs={{0,8},{8,16},{16,24},{24,0},{1,9},{9,17},{17,25},{25,1},{2,10},{10... | collective-permute-start | bytes 3932168 | tf_op jit(solution)/shard_map/ppermute | solution.py:531
  484.3 44.1 %all-to-all-start.7 = ((bf16[4,152,2176]{2,1,0:T(8,128)(2,1)}), bf16[4,152,2176]{2,1,0:T(8,128)(2,1)}, u32[]{:S(2)}, u32[]{:S(2)}) async-start(bf16[4,152,2176]{2,1,0:T(8,128)(2,1)} %convolution_convert_fusion.1), calls=%async_computation.7 | async-start | bytes 5292032 | tf_op jit(solution)/shard_map/all_to_all | solution.py:536
  489.0 39.3 %collective-permute-start.20 = (bf16[4,152,2176]{2,1,0:T(8,128)(2,1)}, bf16[4,152,2176]{2,1,0:T(8,128)(2,1)}, u32[]{:S(2)}, u32[]{:S(2)}) collective-permute-start(bf16[4,152,2176]{2,1,0:T(8,128)(2,1)} %all-to-all-done.6), channel_id=1, source_target_pairs={{0,1},{1,0},{2,3},{3,2},{4,5},{5,4},{6,7},{7,6},{8,9},{9,8},{10,11... | collective-permute-start | bytes 7938056 | tf_op jit(solution)/shard_map/ppermute | solution.py:548
  528.4 53.0 %collective-permute-start.21 = (bf16[4,152,2176]{2,1,0:T(8,128)(2,1)}, bf16[4,152,2176]{2,1,0:T(8,128)(2,1)}, u32[]{:S(2)}, u32[]{:S(2)}) collective-permute-start(bf16[4,152,2176]{2,1,0:T(8,128)(2,1)} %bitcast.331), channel_id=1, source_target_pairs={{0,1},{1,0},{2,3},{3,2},{4,5},{5,4},{6,7},{7,6},{8,9},{9,8},{10,11... | collective-permute-start | bytes 7938056 | tf_op jit(solution)/shard_map/ppermute | solution.py:548
  528.9 48.0 %collective-permute-start.29 = (bf16[4,152,2048]{2,1,0:T(8,128)(2,1)}, bf16[4,152,2048]{2,1,0:T(8,128)(2,1)}, u32[]{:S(2)}, u32[]{:S(2)}) collective-permute-start(bf16[4,152,2048]{2,1,0:T(8,128)(2,1)} %bitcast.336), channel_id=1, source_target_pairs={{0,1},{1,0},{2,3},{3,2},{4,5},{5,4},{6,7},{7,6},{8,9},{9,8},{10,11... | collective-permute-start | bytes 7471112 | tf_op jit(solution)/shard_map/ppermute | solution.py:548
  535.2 50.2 %collective-permute-start.23 = (bf16[4,152,2176]{2,1,0:T(8,128)(2,1)}, bf16[4,152,2176]{2,1,0:T(8,128)(2,1)}, u32[]{:S(2)}, u32[]{:S(2)}) collective-permute-start(bf16[4,152,2176]{2,1,0:T(8,128)(2,1)} %all-to-all-done.7), channel_id=1, source_target_pairs={{0,1},{1,0},{2,3},{3,2},{4,5},{5,4},{6,7},{7,6},{8,9},{9,8},{10,11... | collective-permute-start | bytes 7938056 | tf_op jit(solution)/shard_map/ppermute | solution.py:548
  535.6 49.7 %collective-permute-start.22 = (bf16[320,2048]{1,0:T(8,128)(2,1)}, bf16[320,2048]{1,0:T(8,128)(2,1)}, u32[]{:S(2)}, u32[]{:S(2)}) collective-permute-start(bf16[320,2048]{1,0:T(8,128)(2,1)} %collective-permute-done.19), channel_id=1, source_target_pairs={{0,8},{8,16},{16,24},{24,0},{1,9},{9,17},{17,25},{25,1},{2,10},{10... | collective-permute-start | bytes 3932168 | tf_op jit(solution)/shard_map/ppermute | solution.py:531
  537.1 48.3 %all-to-all-start.8 = ((bf16[4,152,2176]{2,1,0:T(8,128)(2,1)}), bf16[4,152,2176]{2,1,0:T(8,128)(2,1)S(1)}, u32[]{:S(2)}, u32[]{:S(2)}) async-start(bf16[4,152,2176]{2,1,0:T(8,128)(2,1)} %add_convert_fusion.3), calls=%async_computation.8 | async-start | bytes 5292032 | tf_op jit(solution)/shard_map/all_to_all | solution.py:536
  625.2 58.6 %collective-permute-start.24 = (bf16[4,152,2176]{2,1,0:T(8,128)(2,1)}, bf16[4,152,2176]{2,1,0:T(8,128)(2,1)}, u32[]{:S(2)}, u32[]{:S(2)}) collective-permute-start(bf16[4,152,2176]{2,1,0:T(8,128)(2,1)} %bitcast.54), channel_id=1, source_target_pairs={{0,1},{1,0},{2,3},{3,2},{4,5},{5,4},{6,7},{7,6},{8,9},{9,8},{10,11... | collective-permute-start | bytes 7938056 | tf_op jit(solution)/shard_map/ppermute | solution.py:548
  625.2 62.5 %collective-permute-start.25 = (bf16[320,2048]{1,0:T(8,128)(2,1)}, bf16[320,2048]{1,0:T(8,128)(2,1)}, u32[]{:S(2)}, u32[]{:S(2)}) collective-permute-start(bf16[320,2048]{1,0:T(8,128)(2,1)} %collective-permute-done.22), channel_id=1, source_target_pairs={{0,8},{8,16},{16,24},{24,0},{1,9},{9,17},{17,25},{25,1},{2,10},{10... | collective-permute-start | bytes 3932168 | tf_op jit(solution)/shard_map/ppermute | solution.py:531
  625.8 61.9 %all-to-all-start.9 = ((bf16[4,152,2176]{2,1,0:T(8,128)(2,1)}), bf16[4,152,2176]{2,1,0:T(8,128)(2,1)}, u32[]{:S(2)}, u32[]{:S(2)}) async-start(bf16[4,152,2176]{2,1,0:T(8,128)(2,1)} %add_convert_fusion.2), calls=%async_computation.9 | async-start | bytes 5292032 | tf_op jit(solution)/shard_map/all_to_all | solution.py:536
  635.0 143.5 %collective-permute-start.31 = (bf16[4,152,2048]{2,1,0:T(8,128)(2,1)}, bf16[4,152,2048]{2,1,0:T(8,128)(2,1)}, u32[]{:S(2)}, u32[]{:S(2)}) collective-permute-start(bf16[4,152,2048]{2,1,0:T(8,128)(2,1)} %bitcast.56), channel_id=1, source_target_pairs={{0,1},{1,0},{2,3},{3,2},{4,5},{5,4},{6,7},{7,6},{8,9},{9,8},{10,11... | collective-permute-start | bytes 7471112 | tf_op jit(solution)/shard_map/ppermute | solution.py:548
  699.4 48.3 %all-to-all-start.10 = ((bf16[4,152,2176]{2,1,0:T(8,128)(2,1)}), bf16[4,152,2176]{2,1,0:T(8,128)(2,1)}, u32[]{:S(2)}, u32[]{:S(2)}) async-start(bf16[4,152,2176]{2,1,0:T(8,128)(2,1)} %add_convert_fusion.1), calls=%async_computation.10 | async-start | bytes 5292032 | tf_op jit(solution)/shard_map/all_to_all | solution.py:536
  713.2 34.5 %collective-permute-start.27 = (bf16[320,2176]{1,0:T(8,128)(2,1)S(1)}, bf16[320,2176]{1,0:T(8,128)(2,1)S(1)}, u32[]{:S(2)}, u32[]{:S(2)}) collective-permute-start(bf16[320,2176]{1,0:T(8,128)(2,1)S(1)} %fusion.22), channel_id=1, source_target_pairs={{0,8},{8,16},{16,24},{24,0},{1,9},{9,17},{17,25},{25,1},{2,10},{10... | collective-permute-start | bytes 4177928 | tf_op jit(solution)/shard_map/ppermute | solution.py:531
  748.8 60.4 %all-to-all-start.11 = ((bf16[4,152,2176]{2,1,0:T(8,128)(2,1)}), bf16[4,152,2176]{2,1,0:T(8,128)(2,1)}, u32[]{:S(2)}, u32[]{:S(2)}) async-start(bf16[4,152,2176]{2,1,0:T(8,128)(2,1)} %add_convert_fusion), calls=%async_computation.11 | async-start | bytes 5292032 | tf_op jit(solution)/shard_map/all_to_all | solution.py:536
  813.8 46.2 %collective-permute-start.30 = (bf16[320,2176]{1,0:T(8,128)(2,1)}, bf16[320,2176]{1,0:T(8,128)(2,1)}, u32[]{:S(2)}, u32[]{:S(2)}) collective-permute-start(bf16[320,2176]{1,0:T(8,128)(2,1)} %fusion.20), channel_id=1, source_target_pairs={{0,8},{8,16},{16,24},{24,0},{1,9},{9,17},{17,25},{25,1},{2,10},{10... | collective-permute-start | bytes 4177928 | tf_op jit(solution)/shard_map/ppermute | solution.py:531
  813.8 46.2 %all-to-all-start.12 = ((bf16[4,152,2048]{2,1,0:T(8,128)(2,1)}), bf16[4,152,2048]{2,1,0:T(8,128)(2,1)S(1)}, u32[]{:S(2)}, u32[]{:S(2)}) async-start(bf16[4,152,2048]{2,1,0:T(8,128)(2,1)} %add_convert_fusion.7), calls=%async_computation.12 | async-start | bytes 4980736 | tf_op jit(solution)/shard_map/all_to_all | solution.py:536
  818.0 197.5 %reduce-scatter.5.cloned.1.call-start = ((), (), s32[]{:S(2)}) async-start(), calls=%async_computation.26 | async-start | bytes 9732096 | tf_op jit(solution)/shard_map/reduce_scatter | solution.py:556
  894.2 63.6 %collective-permute-start.33 = (bf16[320,2048]{1,0:T(8,128)(2,1)}, bf16[320,2048]{1,0:T(8,128)(2,1)}, u32[]{:S(2)}, u32[]{:S(2)}) collective-permute-start(bf16[320,2048]{1,0:T(8,128)(2,1)} %fusion.41), channel_id=1, source_target_pairs={{0,8},{8,16},{16,24},{24,0},{1,9},{9,17},{17,25},{25,1},{2,10},{10... | collective-permute-start | bytes 3932168 | tf_op jit(solution)/shard_map/ppermute | solution.py:531
  894.2 63.6 %all-to-all-start.13 = ((bf16[4,152,2048]{2,1,0:T(8,128)(2,1)}), bf16[4,152,2048]{2,1,0:T(8,128)(2,1)}, u32[]{:S(2)}, u32[]{:S(2)}) async-start(bf16[4,152,2048]{2,1,0:T(8,128)(2,1)} %add_convert_fusion.6), calls=%async_computation.13 | async-start | bytes 4980736 | tf_op jit(solution)/shard_map/all_to_all | solution.py:536
  909.2 43.4 %collective-permute-start.37 = (bf16[320,512]{0,1:T(8,128)(2,1)S(1)}, bf16[320,512]{0,1:T(8,128)(2,1)S(1)}, u32[]{:S(2)}, u32[]{:S(2)}) collective-permute-start(bf16[320,512]{0,1:T(8,128)(2,1)S(1)} %get-tuple-element.554), channel_id=1, source_target_pairs={{0,16},{8,24},{16,0},{24,8},{1,17},{9,25},{17,1},{25,9},{2,18},{10... | collective-permute-start | bytes 983048 | tf_op jit(solution)/shard_map/ppermute | solution.py:561
  913.5 39.1 %collective-permute-start.38 = (bf16[320,512]{0,1:T(8,128)(2,1)S(1)}, bf16[320,512]{0,1:T(8,128)(2,1)S(1)}, u32[]{:S(2)}, u32[]{:S(2)}) collective-permute-start(bf16[320,512]{0,1:T(8,128)(2,1)S(1)} %get-tuple-element.553), channel_id=1, source_target_pairs={{0,24},{8,0},{16,8},{24,16},{1,25},{9,1},{17,9},{25,17},{2,26},{10... | collective-permute-start | bytes 983048 | tf_op jit(solution)/shard_map/ppermute | solution.py:561
  957.8 57.7 %all-to-all-start.14 = ((bf16[4,152,2048]{2,1,0:T(8,128)(2,1)}), bf16[4,152,2048]{2,1,0:T(8,128)(2,1)}, u32[]{:S(2)}, u32[]{:S(2)}) async-start(bf16[4,152,2048]{2,1,0:T(8,128)(2,1)} %add_convert_fusion.5), calls=%async_computation.14 | async-start | bytes 4980736 | tf_op jit(solution)/shard_map/all_to_all | solution.py:536
  962.4 123.1 %reduce-scatter.7.cloned.1.call-start = ((), (), s32[]{:S(2)}) async-start(), calls=%async_computation.27 | async-start | bytes 2359296 | tf_op jit(solution)/shard_map/reduce_scatter | solution.py:556
  967.9 47.6 %collective-permute-start.35 = (bf16[320,2048]{1,0:T(8,128)(2,1)}, bf16[320,2048]{1,0:T(8,128)(2,1)}, u32[]{:S(2)}, u32[]{:S(2)}) collective-permute-start(bf16[320,2048]{1,0:T(8,128)(2,1)} %fusion.40), channel_id=1, source_target_pairs={{0,8},{8,16},{16,24},{24,0},{1,9},{9,17},{17,25},{25,1},{2,10},{10... | collective-permute-start | bytes 3932168 | tf_op jit(solution)/shard_map/ppermute | solution.py:531
  1020.9 60.7 %collective-permute-start.42 = (bf16[320,2048]{1,0:T(8,128)(2,1)}, bf16[320,2048]{1,0:T(8,128)(2,1)}, u32[]{:S(2)}, u32[]{:S(2)}) collective-permute-start(bf16[320,2048]{1,0:T(8,128)(2,1)} %fusion.39), channel_id=1, source_target_pairs={{0,8},{8,16},{16,24},{24,0},{1,9},{9,17},{17,25},{25,1},{2,10},{10... | collective-permute-start | bytes 3932168 | tf_op jit(solution)/shard_map/ppermute | solution.py:531
  1037.8 43.7 %all-to-all-start.15 = ((bf16[4,152,2048]{2,1,0:T(8,128)(2,1)}), bf16[4,152,2048]{2,1,0:T(8,128)(2,1)}, u32[]{:S(2)}, u32[]{:S(2)}) async-start(bf16[4,152,2048]{2,1,0:T(8,128)(2,1)} %add_convert_fusion.4), calls=%async_computation.17 | async-start | bytes 4980736 | tf_op jit(solution)/shard_map/all_to_all | solution.py:536
  1042.4 174.4 %reduce-scatter.9.cloned.1.call-start = ((), (), s32[]{:S(2)}) async-start(), calls=%async_computation.28 | async-start | bytes 14155776 | tf_op jit(solution)/shard_map/reduce_scatter | solution.py:556
  1042.8 37.1 %collective-permute-start.40 = (bf16[320,576]{1,0:T(8,128)(2,1)S(1)}, bf16[320,576]{1,0:T(8,128)(2,1)}, u32[]{:S(2)}, u32[]{:S(2)}) collective-permute-start(bf16[320,576]{1,0:T(8,128)(2,1)S(1)} %get-tuple-element.547), channel_id=1, source_target_pairs={{0,16},{8,24},{16,0},{24,8},{1,17},{9,25},{17,1},{25,9},{2,18},{10... | collective-permute-start | bytes 1105928 | tf_op jit(solution)/shard_map/ppermute | solution.py:561
  1085.5 213.8 %reduce-scatter.11.cloned.1.call-start = ((), (), s32[]{:S(2)}) async-start(), calls=%async_computation.29 | async-start | bytes 8257536 | tf_op jit(solution)/shard_map/reduce_scatter | solution.py:556
  1117.8 35.1 %collective-permute-start.43 = (bf16[256,2112]{0,1:T(8,128)(2,1)}, bf16[256,2112]{0,1:T(8,128)(2,1)}, u32[]{:S(2)}, u32[]{:S(2)}) collective-permute-start(bf16[256,2112]{0,1:T(8,128)(2,1)} %reduce-scatter.5.cloned.1.call-done), channel_id=1, source_target_pairs={{0,8},{8,16},{16,24},{24,0},{1,9},{9,17},{17,25},{25,1},{2,10},{10... | collective-permute-start | bytes 3244040 | tf_op jit(solution)/shard_map/ppermute | solution.py:531
  1123.4 82.3 %collective-permute-start.46 = (bf16[256,512]{1,0:T(8,128)(2,1)S(1)}, bf16[256,512]{1,0:T(8,128)(2,1)}, u32[]{:S(2)}, u32[]{:S(2)}) collective-permute-start(bf16[256,512]{1,0:T(8,128)(2,1)S(1)} %copy-done.89), channel_id=1, source_target_pairs={{0,8},{8,16},{16,24},{24,0},{1,9},{9,17},{17,25},{25,1},{2,10},{10... | collective-permute-start | bytes 786440 | tf_op jit(solution)/shard_map/ppermute | solution.py:561
  1123.5 84.1 %collective-permute-start.47 = (bf16[256,512]{1,0:T(8,128)(2,1)S(1)}, bf16[256,512]{1,0:T(8,128)(2,1)}, u32[]{:S(2)}, u32[]{:S(2)}) collective-permute-start(bf16[256,512]{1,0:T(8,128)(2,1)S(1)} %copy-done.89), channel_id=1, source_target_pairs={{0,16},{8,24},{16,0},{24,8},{1,17},{9,25},{17,1},{25,9},{2,18},{10... | collective-permute-start | bytes 786440 | tf_op jit(solution)/shard_map/ppermute | solution.py:561
  1123.5 85.9 %collective-permute-start.48 = (bf16[256,512]{1,0:T(8,128)(2,1)S(1)}, bf16[256,512]{1,0:T(8,128)(2,1)}, u32[]{:S(2)}, u32[]{:S(2)}) collective-permute-start(bf16[256,512]{1,0:T(8,128)(2,1)S(1)} %copy-done.89), channel_id=1, source_target_pairs={{0,24},{8,0},{16,8},{24,16},{1,25},{9,1},{17,9},{25,17},{2,26},{10... | collective-permute-start | bytes 786440 | tf_op jit(solution)/shard_map/ppermute | solution.py:561
  1152.8 34.7 %collective-permute-start.44 = (bf16[256,2112]{0,1:T(8,128)(2,1)}, bf16[256,2112]{0,1:T(8,128)(2,1)}, u32[]{:S(2)}, u32[]{:S(2)}) collective-permute-start(bf16[256,2112]{0,1:T(8,128)(2,1)} %collective-permute-done.43), channel_id=1, source_target_pairs={{0,8},{8,16},{16,24},{24,0},{1,9},{9,17},{17,25},{25,1},{2,10},{10... | collective-permute-start | bytes 3244040 | tf_op jit(solution)/shard_map/ppermute | solution.py:531
  1218.9 46.9 %collective-permute-start.49 = (bf16[64,3072]{1,0:T(8,128)(2,1)}, bf16[64,3072]{1,0:T(8,128)(2,1)}, u32[]{:S(2)}, u32[]{:S(2)}) collective-permute-start(bf16[64,3072]{1,0:T(8,128)(2,1)} %get-tuple-element.550), channel_id=1, source_target_pairs={{0,8},{8,16},{16,24},{24,0},{1,9},{9,17},{17,25},{25,1},{2,10},{10... | collective-permute-start | bytes 1179656 | tf_op jit(solution)/shard_map/ppermute | solution.py:561
  1221.4 44.4 %collective-permute-start.50 = (bf16[64,3072]{1,0:T(8,128)(2,1)S(1)}, bf16[64,3072]{1,0:T(8,128)(2,1)}, u32[]{:S(2)}, u32[]{:S(2)}) collective-permute-start(bf16[64,3072]{1,0:T(8,128)(2,1)S(1)} %get-tuple-element.552), channel_id=1, source_target_pairs={{0,16},{8,24},{16,0},{24,8},{1,17},{9,25},{17,1},{25,9},{2,18},{10... | collective-permute-start | bytes 1179656 | tf_op jit(solution)/shard_map/ppermute | solution.py:561
  1223.6 42.2 %collective-permute-start.51 = (bf16[64,3072]{1,0:T(8,128)(2,1)S(1)}, bf16[64,3072]{1,0:T(8,128)(2,1)}, u32[]{:S(2)}, u32[]{:S(2)}) collective-permute-start(bf16[64,3072]{1,0:T(8,128)(2,1)S(1)} %get-tuple-element.551), channel_id=1, source_target_pairs={{0,24},{8,0},{16,8},{24,16},{1,25},{9,1},{17,9},{25,17},{2,26},{10... | collective-permute-start | bytes 1179656 | tf_op jit(solution)/shard_map/ppermute | solution.py:561
  (211 other events, 3897.3 us)
Sparse Core Ops, SparseCore 0:
  13.9 51.5 all-gather.6
  67.4 97.3 all-gather.8
  166.7 55.4 all-gather.10
  224.0 81.0 all-gather.12
  309.1 32.6 all-gather.16
  344.0 82.2 all-gather.14
  860.1 102.9 reduce-scatter.4
  1026.6 58.8 reduce-scatter.6
  1089.0 92.4 reduce-scatter.8
  1226.3 64.9 reduce-scatter.10

commit v4 on v3

--- a/solution.py
+++ b/solution.py
@@ -902,41 +902,41 @@
         )
         return [rows.reshape(chips, slots, -1) for rows in results]
 
-    def shared_step(step):
-        rows = (shared_rows + ffn_ring[len(shared_rows) :])[step][:, :model_width]
+    def shared_step(rows, grad_act):
         gate_pre = matmul(rows, part_gate)
         up_pre = matmul(rows, part_up)
         act = (jax.nn.silu(gate_pre) * up_pre).astype(bfloat)
-        grad_act = jnp.einsum(
-            "td,fd->tf",
-            shared_grad_rows[step * tokens : (step + 1) * tokens],
-            part_down,
-            preferred_element_type=single,
-        )
         grad_gate, grad_up = silu_grads(grad_act, gate_pre, up_pre)
         back = jnp.einsum("tf,df->td", grad_gate, part_gate, preferred_element_type=single)
         back = back + jnp.einsum("tf,df->td", grad_up, part_up, preferred_element_type=single)
-        return rows, act, grad_gate, grad_up, back
-
-    def shared_grads(group):
+        return act, grad_gate, grad_up, back
+
+    def shared_grads():
+        group = jnp.concatenate(groups)
         act, grad_gate, grad_up = [
-            jnp.concatenate([shared[step][i] for step in range(ctx_size)]) for i in range(1, 4)
+            jnp.concatenate([part[i] for part in shared]) for i in range(3)
         ]
         pieces = [
             jnp.einsum("ta,tb->ab", left, right, preferred_element_type=single).astype(bfloat)
-            for left, right in ((group, grad_gate), (group, grad_up), (act, shared_grad_rows))
+            for left, right in ((group, grad_gate), (group, grad_up), (act, grad_group))
         ]
         return jnp.concatenate(pieces[:2] + [pieces[2].reshape(model_width, hidden_part)], axis=1)
 
     last = ctx_size - 1
     ffn_ring = [ffn_wide]
     attended_ring = [attended_low]
-    shared, mines, theirs, backs, added, returned, out_added, out_steps = ({} for _ in range(8))
+    mines, theirs, backs, added, returned, out_added, out_steps = ({} for _ in range(7))
+    shared, groups = [], []
+    together_blocks = 4
     moving = None
+
+    def of_block(which, step):
+        first = step % together_blocks * tokens
+        return shared[step // together_blocks][which][first : first + tokens]
 
     def block_part(step):
         part = put_rows(step, returned[step])
-        return part + jnp.pad(shared[step][4], ((0, 0), (0, EXTRA)))
+        return part + jnp.pad(of_block(3, step), ((0, 0), (0, EXTRA)))
 
     def hop(step):
         part = block_part(step)
@@ -958,31 +958,38 @@
             sent["added"] = add_halves(*backs[tick - 3])
         if 0 <= tick - 4 <= last:
             sent["returned"] = to_chips(added[tick - 4])
-        if 1 <= tick - 4 <= last:
-            shared[tick - 4] = shared_step(tick - 4)
-            sent["shared"] = shared[tick - 4]
+        first = tick - 4
+        if 0 <= first <= last and first % together_blocks == 0:
+            sent["group"] = jnp.concatenate(
+                [
+                    block[:, :model_width]
+                    for block in ffn_ring[first : first + together_blocks]
+                ]
+            )
+        first = tick - 5
+        if 0 <= first <= last and first % together_blocks == 0:
+            rows = groups[-1].shape[0]
+            shared.append(
+                shared_step(groups[-1], grad_act[first * tokens : first * tokens + rows])
+            )
+            sent["shared"] = shared[-1]
         if 1 <= tick - 5 <= last:
             sent["moving"] = hop(tick - 5)
         if tick == 0:
             sent["grads"] = grad_theirs[-1]
         if tick == 1:
             sent["weights"] = (part_shared, part_down)
-        if tick == 4:
-            sent["shared_in"] = (ffn_ring, grad_group, part_gate, part_up, part_down)
+            sent["grad_act"] = jnp.einsum(
+                "td,fd->tf", grad_group, part_down, preferred_element_type=single
+            )
         if tick == ctx_size + 3:
-            sent["shared_all"] = shared
-            sent["group"] = jnp.concatenate(
-                [block[:, :model_width] for block in shared_rows + ffn_ring[len(shared_rows) :]]
-            )
+            sent["shared_all"] = (shared, groups, grad_group)
             sent["out"] = add_halves(*out_sends[1])
         if tick == ctx_size + 4:
-            sent["shared_grads"] = shared_grads(ffn_group)
+            sent["shared_grads"] = shared_grads()
             sent["out_step"] = to_chips(out_added[1])
         if last <= tick < 2 * last:
             sent["attended"] = ring_next(attended_ring[-1])
-        if tick == ctx_size + 2:
-            shared[0] = shared_step(0)
-            sent["first"] = shared[0]
         if tick == ctx_size + 4:
             sent["out"] = add_halves(*out_sends[2])
         names = sorted(sent)
@@ -1000,20 +1007,16 @@
             added[tick - 3] = sent["added"]
         if "returned" in sent:
             returned[tick - 4] = sent["returned"]
-        if "shared_in" in sent:
-            shared_rows, shared_grad_rows, part_gate, part_up, part_down = sent["shared_in"]
+        if "group" in sent:
+            groups.append(sent["group"])
         if "shared" in sent:
-            shared[tick - 4] = sent["shared"]
-        if "first" in sent:
-            shared[0] = sent["first"]
+            shared[-1] = sent["shared"]
         if "shared_all" in sent:
-            shared = sent["shared_all"]
+            shared, groups, grad_group = sent["shared_all"]
         if "attended" in sent:
             attended_ring.append(sent["attended"])
         if "out" in sent:
             out_added[tick - ctx_size - 2] = sent["out"]
-        if "group" in sent:
-            ffn_group = sent["group"]
         if "out_step" in sent:
             out_steps[1] = sent["out_step"]
         moving = sent.get("moving", moving)
@@ -1023,6 +1026,7 @@
             part_gate = sent["weights"][0][:, :hidden_part]
             part_up = sent["weights"][0][:, hidden_part:]
             part_down = sent["weights"][1]
+            grad_act = sent["grad_act"]
 
     while len(attended_ring) < ctx_size:
         attended_ring.append(ring_next(attended_ring[-1]))
@@ -1057,7 +1061,7 @@
     grad_attn_low = grad_hidden.astype(bfloat)
 
     def out_hop(step, moving):
-        part = put_rows(step, out_steps[step]) + matmul(shared[step][1], part_down)
+        part = put_rows(step, out_steps[step]) + matmul(of_block(0, step), part_down)
         if moving is not None:
             part = part + moving.astype(single)
         return ring_next(part.astype(bfloat))
@@ -1065,19 +1069,17 @@
     grad_attended = jnp.einsum(
         "td,vd->tv", grad_attn_low, full_output, preferred_element_type=single
     ).astype(bfloat)
-    out_next = next_out(2)
+    out_steps[2] = to_chips(out_added[2])
     out_moving = out_hop(1, None)
     att_shares = column_shares(grad_attn_low, device)
-    grad_attended, out_next, out_moving = together(grad_attended, out_next, out_moving)
-    out_steps[2], out_added[3] = out_next
+    grad_attended, out_sends = together(grad_attended, out_sends)
 
     def weight_grad(left, right):
         return jnp.einsum("ra,rb->ab", left, right, preferred_element_type=single)
 
     grad_w_output = weight_grad(jnp.concatenate(attended_ring), jnp.concatenate(att_shares))
 
-    out_next = next_out(3)
-    out_moving = out_hop(2, out_moving)
+    out_added[3] = add_halves(*out_sends[3])
 
     log_rows = log_total[:, :HEADS].T.reshape(HEADS // 2, 2, tokens)
     grad_nope, grad_rope, grad_key_part, grad_value_part, rope_pair_grad = attend_back(
@@ -1100,7 +1102,8 @@
         grad_key_part,
         grad_value_part,
         rope_pair_grad,
-        out_next,
+        out_steps[2],
+        out_added[3],
         out_moving,
         shared_part,
         grad_w_output,
@@ -1110,14 +1113,14 @@
         grad_key_part,
         grad_value_part,
         rope_pair_grad,
-        out_next,
+        out_steps[2],
+        out_added[3],
         out_moving,
         shared_part,
         grad_w_output,
     )
-    out_steps[3], out_added[4 % ctx_size] = out_next
-    out_next = next_out(0) if ctx_size == 4 else next_out(4)
-    out_moving = out_hop(3, out_moving)
+    out_next = next_out(3)
+    out_moving = out_hop(2, out_moving)
     output_part = scatter_rows(grad_w_output)
     grad_key_rope = rope_pair_grad[:, :ROPE] + rope_pair_grad[:, ROPE:]
     keys_width = HEADS * NOPE
@@ -1134,17 +1137,15 @@
     grad_keys_own, output_part, grad_w_query, out_next, out_moving = together(
         grad_keys_own, output_part, grad_w_query, out_next, out_moving
     )
-    if ctx_size == 4:
-        out_steps[0] = out_next[0]
-    else:
-        out_steps[4], out_added[5] = out_next
-        for step in range(4, ctx_size):
-            if step > 4:
-                out_steps[step], out_added[(step + 1) % ctx_size] = next_out(step)
-            out_moving = out_hop(step, out_moving)
-        out_steps[0] = to_chips(out_added[0])
+    out_steps[3], out_added[4 % ctx_size] = out_next
+    for step in range(3, ctx_size):
+        if step > 3:
+            out_steps[step], out_added[(step + 1) % ctx_size] = next_out(step)
+        out_moving = out_hop(step, out_moving)
+    out_steps[0] = to_chips(out_added[0])
     query_part = scatter_rows(grad_w_query)
     shared_ring = [shared_part, ring_next(shared_part)]
+    shared_ring.append(ring_next(shared_ring[-1]))
     sum_output = all_columns_of(output_part, device)
     grad_w_up = jnp.concatenate(
         [
@@ -1194,25 +1195,31 @@
         ],
         axis=1,
     )
-    packed_grads, shared_ring, kept = together(packed_grads, shared_ring, kept)
+    (
+        query_part,
+        packed_grads,
+        shared_ring,
+        kept,
+        out_moving,
+        out_steps[0],
+        sum_output,
+    ) = together(
+        query_part, packed_grads, shared_ring, kept, out_moving, out_steps[0], sum_output
+    )
+    packed_part = scatter_rows(with_layout_constraint(packed_grads, by_rows))
     all_rows, all_grads, all_act, all_gate, all_up = kept
     grad_piece_down = weight_grad(all_act, all_grads)
+    grad_piece_gate = weight_grad(all_rows, all_gate)
+    sum_query = sum_ctx(query_part)
+    packed_part, sum_query, grad_piece_down, grad_piece_gate, kept = together(
+        packed_part, sum_query, grad_piece_down, grad_piece_gate, kept
+    )
+    all_rows, all_grads, all_act, all_gate, all_up = kept
+    grad_piece_up = weight_grad(all_rows, all_up)
     while len(shared_ring) < ctx_size:
         shared_ring.append(ring_next(shared_ring[-1]))
-    query_part, packed_grads, shared_ring, sum_output, grad_piece_down, kept = together(
-        query_part, packed_grads, shared_ring, sum_output, grad_piece_down, kept
-    )
-    packed_part = scatter_rows(with_layout_constraint(packed_grads, by_rows))
-    all_rows, all_grads, all_act, all_gate, all_up = kept
-    grad_piece_gate = weight_grad(all_rows, all_gate)
-    query_total = ctx_total(query_part, device).astype(bfloat)
-    query_total, grad_piece_gate, kept = together(query_total, grad_piece_gate, kept)
-    all_rows, all_grads, all_act, all_gate, all_up = kept
-    grad_piece_up = weight_grad(all_rows, all_up)
-    sum_query = ctx_spread(query_total, device)
-    first_out = put_rows(0, out_steps[0]) + matmul(shared[0][1], part_down)
+    first_out = put_rows(0, out_steps[0]) + matmul(of_block(0, 0), part_down)
     layer_output = (hidden + out_moving.astype(single) + first_out).astype(bfloat)
-    packed_part, sum_query, grad_piece_up = together(packed_part, sum_query, grad_piece_up)
     sum_packed = with_layout_constraint(
         sum_ctx(with_layout_constraint(packed_part, by_rows)), by_rows
     )

time: 1380 us -> 1310 us (0.949)
  local copies, waits for them, and re-layouts: 171 us -> 113 us
  waiting for transfers between devices: 359 us -> 408 us
  matrix products: 342 us -> 310 us
  starting transfers between devices: 176 us -> 147 us
    ppermute x27, waiting for transfers between devices: 138 us -> 166 us  [along_ctx(): lax.ppermute(value, 'ctx', [(i, (i + shift) % size) for i in range(size)])]
    optimization_barrier x8 -> x0, local copies, waits for them, and re-layouts: 25 us -> none  [together(): return lax.optimization_barrier(values)]
    concatenate x3 -> x0, local copies, waits for them, and re-layouts: 23.6 us -> none  [the longest x1 9.99 us: local(): grad_group = jnp.concatenate(grad_ring)]
    all_to_all x16, waiting for transfers between devices: 8.44 us -> 30.6 us  [to_chips(): lax.all_to_all(value, 'fsdp', split_axis=0, concat_axis=0, tiled=True, ax...]
    dot_general x21 -> x15, matrix products: 76.8 us -> 67.1 us  [matmul(): return jnp.dot(left, right, preferred_element_type=single)]
    unnamed x388 -> x308, local copies, waits for them, and re-layouts: 36.5 us -> 30.3 us
  transfers between devices with their start and end apart: 87 -> 87, of which waited for: 26 -> 30; matrix products, arithmetic and copies ran while one was open for 39% -> 35% of each run, Pallas kernels for 14% -> 15%
where the time goes in v4:
time: 1310 us; the launch traced here: 1300 us
  waiting for transfers between devices  408 us (31%)
  matrix products  310 us (24%)
  Pallas kernels  200 us (15%)
  starting transfers between devices  147 us (11%)
  local copies, waits for them, and re-layouts  113 us (9%)
  other arithmetic  102 us (8%)
  between operations  16.9 us (1%)
    ppermute x27, waiting for transfers between devices, along_ctx(): lax.ppermute(value, 'ctx', [(i, (i + shift) % size) for i in range(size)])  166 us
    ppermute x18, waiting for transfers between devices, ring_next(): lax.ppermute(value, 'ctx', [(i, (i + 1) % size) for i in range(size)])  152 us
    pallas_call x4, Pallas kernels, expert_call(): pl.pallas_call(functools.partial(expert_kernel, step * 2 * count, experts...  141 us
    dot_general x7, matrix products, weight_grad(): return jnp.einsum('ra,rb->ab', left, right, preferred_element_type=single)  94.5 us
    all_to_all x16, starting transfers between devices, to_chips(): lax.all_to_all(value, 'fsdp', split_axis=0, concat_axis=0, tiled=True, ax...  73.7 us
    dot_general x15, matrix products, matmul(): return jnp.dot(left, right, preferred_element_type=single)  67.1 us
    all_gather x6, waiting for transfers between devices, gather_rows(): return lax.all_gather(value, 'fsdp', axis=0, tiled=True)  58 us
    ppermute x27, starting transfers between devices, along_ctx(): lax.ppermute(value, 'ctx', [(i, (i + shift) % size) for i in range(size)])  43.9 us
  transfers between devices with their start and end apart: 87, of which 30 were waited for; matrix products, arithmetic and copies ran while one was open for 35% of the time, Pallas kernels for 15%

profile of v4, /device:TPU:0, one launch (start us, length us, event | category | flops | bytes accessed | tf_op | source)
XLA Modules:
  0.0 1295.7 jit_solution(11964427635123675980)
XLA Ops:
  19.8 5.3 all-to-all-start
  33.1 26.0 %collective-permute-done = s32[320,6]{0,1:T(8,128)S(1)} collective-permute-done((s32[320,6]{0,1:T(8,128)S(1)}, s32[320,6]{0,1:T(8,128)S(1)}, u32[]{:S(2)}, u32[]{:S(2)}) %collective-permute-start) | collective-permute-done | bytes 7712 | tf_op jit(solution)/shard_map/ppermute | solution.py:561
  75.7 4.7 all-to-all-start.1
  90.9 20.1 %collective-permute-done.4 = bf16[320,576]{1,0:T(8,128)(2,1)S(1)} collective-permute-done((bf16[320,576]{1,0:T(8,128)(2,1)S(1)}, bf16[320,576]{1,0:T(8,128)(2,1)S(1)}, u32[]{:S(2)}, u32[]{:S(2)}) %collective-permute-start.4) | collective-permute-done | bytes 368672 | tf_op jit(solution)/shard_map/ppermute | solution.py:561
  111.0 16.9 %collective-permute-done.5 = bf16[320,576]{1,0:T(8,128)(2,1)S(1)} collective-permute-done((bf16[320,576]{1,0:T(8,128)(2,1)S(1)}, bf16[320,576]{1,0:T(8,128)(2,1)S(1)}, u32[]{:S(2)}, u32[]{:S(2)}) %collective-permute-start.5) | collective-permute-done | bytes 368672 | tf_op jit(solution)/shard_map/ppermute | solution.py:561
  129.3 36.9 %all-gather.9.cloned.1.call-done = bf16[2048,3072]{1,0:T(8,128)(2,1)} async-done(((bf16[256,3072]{1,0:T(8,128)(2,1)}), bf16[2048,3072]{1,0:T(8,128)(2,1)}) %all-gather.9.cloned.1.call-update) | async-done | bytes 12582928 | tf_op jit(solution)/shard_map/all_gather | solution.py:552
  177.1 9.3 fusion.149.nope.rope
  186.4 22.3 %collective-permute-done.9 = bf16[320,2048]{1,0:T(8,128)(2,1)} collective-permute-done((bf16[320,2048]{1,0:T(8,128)(2,1)}, bf16[320,2048]{1,0:T(8,128)(2,1)}, u32[]{:S(2)}, u32[]{:S(2)}) %collective-permute-start.9) | collective-permute-done | bytes 1310752 | tf_op jit(solution)/shard_map/ppermute | solution.py:531
  211.6 12.0 all-gather.11.cloned.1.call-done
  246.4 10.5 convolution_convert_fusion.keys.values
  256.9 26.5 %shard_map.306 = (bf16[320,2048]{1,0:T(8,128)(2,1)S(1)}, f32[320,128]{1,0:T(8,128)S(1)}) custom-call(s32[1]{0:T(128)} %bitcast.11.link, f32[320,3072]{1,0:T(8,128)S(1)} %copy-done.2, f32[320,3072]{1,0:T(8,128)S(1)} %copy-done.2, f32[320,128]{1,0:T(8,128)S(1)} %get-tuple-element.520.cos, f32[320,128]{1,0:T(8,128)S(1)} %get-tuple-element.521.sin, ...), custom_call_target="tpu_custom_call" | custom-call | flops 2214592512 | bytes 16384000 | tf_op jit(solution)/shard_map/pallas_call | solution.py:312
  283.4 5.6 pad_maximum_fusion.1
  289.0 8.4 all-to-all-done.3
  301.0 6.7 multiply_reduce_fusion.2
  320.1 4.7 all-to-all-start.4
  326.1 33.6 %collective-permute-done.13 = bf16[320,2176]{1,0:T(8,128)(2,1)} collective-permute-done((bf16[320,2176]{1,0:T(8,128)(2,1)}, bf16[320,2176]{1,0:T(8,128)(2,1)}, u32[]{:S(2)}, u32[]{:S(2)}) %collective-permute-start.13) | collective-permute-done | bytes 1392672 | tf_op jit(solution)/shard_map/ppermute | solution.py:531
  371.4 9.1 fusion.158
  380.5 24.5 %collective-permute-done.14 = bf16[320,2176]{1,0:T(8,128)(2,1)} collective-permute-done((bf16[320,2176]{1,0:T(8,128)(2,1)}, bf16[320,2176]{1,0:T(8,128)(2,1)}, u32[]{:S(2)}, u32[]{:S(2)}) %collective-permute-start.14) | collective-permute-done | bytes 1392672 | tf_op jit(solution)/shard_map/ppermute | solution.py:531
  405.0 12.1 all-to-all-done.5
  430.8 35.5 %shard_map.307 = (bf16[608,2176]{1,0:T(8,128)(2,1)}, bf16[608,2176]{1,0:T(8,128)(2,1)}, bf16[608,2048]{1,0:T(8,128)(2,1)}, bf16[608,2048]{1,0:T(8,128)(2,1)}, bf...) custom-call(s32[1]{0:T(128)} %bitcast.18.expert, ...), custom_call_target="tpu_custom_call" | custom-call | flops 21038628864 | bytes 43671552 | tf_op jit(solution)/shard_map/pallas_call | solution.py:505
  477.4 4.8 all-to-all-start.7
  482.4 35.3 %shard_map.308 = (bf16[608,2176]{1,0:T(8,128)(2,1)}, bf16[608,2176]{1,0:T(8,128)(2,1)}, bf16[608,2048]{1,0:T(8,128)(2,1)}, bf16[608,2048]{1,0:T(8,128)(2,1)}, bf...) custom-call(s32[1]{0:T(128)} %bitcast.18.expert, ...), custom_call_target="tpu_custom_call", output_to_operand_aliasing={{4}: (8, {}), {5}: (9, {}), {6}: (10, {}), {7}: (11, {}), {... | custom-call | flops 21038628864 | bytes 43671552 | tf_op jit(solution)/shard_map/pallas_call | solution.py:505
  524.5 5.2 pad_maximum_fusion.2
  535.9 35.4 %shard_map.309 = (bf16[608,2176]{1,0:T(8,128)(2,1)}, bf16[608,2176]{1,0:T(8,128)(2,1)}, bf16[608,2048]{1,0:T(8,128)(2,1)}, bf16[608,2048]{1,0:T(8,128)(2,1)}, bf...) custom-call(s32[1]{0:T(128)} %bitcast.18.expert, ...), custom_call_target="tpu_custom_call", output_to_operand_aliasing={{4}: (8, {}), {5}: (9, {}), {6}: (10, {}), {7}: (11, {}), {... | custom-call | flops 21038628864 | bytes 43671552 | tf_op jit(solution)/shard_map/pallas_call | solution.py:505
  575.3 10.2 fusion.46
  585.4 9.1 fusion.43
  599.9 35.3 %shard_map.310 = (bf16[608,2176]{1,0:T(8,128)(2,1)}, bf16[608,2176]{1,0:T(8,128)(2,1)}, bf16[608,2048]{1,0:T(8,128)(2,1)}, bf16[608,2048]{1,0:T(8,128)(2,1)}, bf...) custom-call(s32[1]{0:T(128)} %bitcast.18.expert, ...), custom_call_target="tpu_custom_call", output_to_operand_aliasing={{4}: (8, {}), {5}: (9, {}), {6}: (10, {}), {7}: (11, {}), {... | custom-call | flops 21038628864 | bytes 43671552 | tf_op jit(solution)/shard_map/pallas_call | solution.py:505
  635.3 5.6 multiply_convert_fusion
  640.9 7.5 fusion.41
  648.5 7.2 convolution_add_fusion
  676.0 28.9 %collective-permute-done.27 = bf16[320,2176]{1,0:T(8,128)(2,1)S(1)} collective-permute-done((bf16[320,2176]{1,0:T(8,128)(2,1)S(1)}, bf16[320,2176]{1,0:T(8,128)(2,1)S(1)}, u32[]{:S(2)}, u32[]{:S(2)}) %collective-permute-start.27) | collective-permute-done | bytes 1392672 | tf_op jit(solution)/shard_map/ppermute | solution.py:531
  723.4 24.8 %collective-permute-done.28 = bf16[320,2176]{1,0:T(8,128)(2,1)} collective-permute-done((bf16[320,2176]{1,0:T(8,128)(2,1)S(1)}, bf16[320,2176]{1,0:T(8,128)(2,1)}, u32[]{:S(2)}, u32[]{:S(2)}) %collective-permute-start.28) | collective-permute-done | bytes 1392672 | tf_op jit(solution)/shard_map/ppermute | solution.py:531
  760.9 8.6 convolution_convert_fusion.5
  769.5 7.8 convolution_convert_fusion.6
  777.4 5.2 convolution_convert_fusion.7
  782.6 7.0 reshape.511
  794.1 7.6 pad_maximum_fusion
  805.0 5.0 fusion.83
  826.9 4.9 all-to-all-start.13
  839.6 31.5 %shard_map.311 = (bf16[320,2048]{1,0:T(8,128)(2,1)S(1)}, bf16[320,1024]{1,0:T(8,128)(2,1)S(1)}, bf16[1280,2048]{1,0:T(8,128)(2,1)}, bf16[1280,2048]{1,0:T(8,128)(2,1)}, f32[1280,128]{1,0:T(8,128)S(1)}) custom-call(s32[1]{0:T(128)} %bitcast.11.link, f32[320,3072]{1,0:T(8,128)} %fusion.149.nope.rope, f32[320,3072]{1,0:T(8,128)} %fusion.149.nope.rope, ...), custom_call_target="tpu_custom_call" | custom-call | flops 6643777536 | bytes 30801920 | tf_op jit(solution)/shard_map/pallas_call | solution.py:337
  876.7 5.8 fusion.2
  882.5 5.2 add_convert_fusion.5
  891.9 15.3 %collective-permute-done.33 = bf16[320,2048]{1,0:T(8,128)(2,1)} collective-permute-done((bf16[320,2048]{1,0:T(8,128)(2,1)}, bf16[320,2048]{1,0:T(8,128)(2,1)}, u32[]{:S(2)}, u32[]{:S(2)}) %collective-permute-start.33) | collective-permute-done | bytes 1310752 | tf_op jit(solution)/shard_map/ppermute | solution.py:531
  907.2 7.6 fusion.48
  914.8 6.8 fusion.23
  935.0 5.4 fusion.31
  943.9 10.0 fusion.147
  953.9 39.8 %collective-permute-done.38 = bf16[320,576]{1,0:T(8,128)(2,1)} collective-permute-done((bf16[320,576]{1,0:T(8,128)(2,1)}, bf16[320,576]{1,0:T(8,128)(2,1)}, u32[]{:S(2)}, u32[]{:S(2)}) %collective-permute-start.38) | collective-permute-done | bytes 368672 | tf_op jit(solution)/shard_map/ppermute | solution.py:561
  996.7 4.7 fusion.79
  1006.0 7.9 convolution_convert_fusion.13
  1018.4 6.6 convolution_convert_fusion.14
  1040.8 11.8 fusion.35
  1052.9 5.2 fusion.30
  1059.9 4.9 all-to-all-start.15
  1071.3 5.7 fusion.60
  1081.2 21.3 %collective-permute-done.46 = bf16[256,512]{1,0:T(8,128)(2,1)} collective-permute-done((bf16[256,512]{1,0:T(8,128)(2,1)S(1)}, bf16[256,512]{1,0:T(8,128)(2,1)}, u32[]{:S(2)}, u32[]{:S(2)}) %collective-permute-start.46) | collective-permute-done | bytes 262176 | tf_op jit(solution)/shard_map/ppermute | solution.py:561
  1126.9 23.4 %fusion.159 = f32[704,2048]{1,0:T(8,128)} fusion(bf16[4864,704]{1,0:T(8,128)(2,1)} %get-tuple-element.355, bf16[4864,2048]{1,0:T(8,128)(2,1)} %get-tuple-element.356), kind=kOutput, calls=%fused_computation.361 | convolution fusion | flops 14025752576 | bytes 32538624 | tf_op jit(solution)/shard_map/ra,rb->ab/dot_general | solution.py:1078
  1150.3 20.0 %fusion.160 = f32[2048,704]{0,1:T(8,128)} fusion(bf16[4864,2048]{1,0:T(8,128)(2,1)S(1)} %bitcast.240, bf16[4864,704]{1,0:T(8,128)(2,1)} %get-tuple-element.358), kind=kOutput, calls=%fused_computation.362 | convolution fusion | flops 14025752576 | bytes 32538624 | tf_op jit(solution)/shard_map/ra,rb->ab/dot_general | solution.py:1078
  1183.7 5.5 collective-permute-done.51
  1189.3 15.2 %collective-permute-done.52 = bf16[64,3072]{1,0:T(8,128)(2,1)S(1)} collective-permute-done((bf16[64,3072]{1,0:T(8,128)(2,1)S(1)}, bf16[64,3072]{1,0:T(8,128)(2,1)S(1)}, u32[]{:S(2)}, u32[]{:S(2)}) %collective-permute-start.52) | collective-permute-done | bytes 393248 | tf_op jit(solution)/shard_map/ppermute | solution.py:561
  1216.8 7.2 collective-permute-start.56
  1236.8 10.8 collective-permute-done.55
  1249.1 20.9 %convolution_bitcast_fusion.4 = f32[1,2048,704]{1,2,0:T(8,128)} fusion(bf16[4864,2048]{1,0:T(8,128)(2,1)} %get-tuple-element.367, bf16[4864,704]{1,0:T(8,128)(2,1)} %get-tuple-element.368), kind=kOutput, calls=%fused_computation.48 | convolution fusion | flops 14025752576 | bytes 32538624 | tf_op jit(solution)/shard_map/ra,rb->ab/dot_general | solution.py:1078
  1273.9 9.7 collective-permute-done.58
  (649 shorter events, 384.9 us)
Async XLA Ops:
  7.2 58.3 %all-gather.7.cloned.1.call-start = ((), (), s32[]{:S(2)}) async-start(), calls=%async_computation.20 | async-start | bytes 2764800 | tf_op jit(solution)/shard_map/all_gather | solution.py:552
  19.8 42.4 %all-to-all-start = ((bf16[4,152,2048]{2,1,0:T(8,128)(2,1)}), bf16[4,152,2048]{2,1,0:T(8,128)(2,1)}, u32[]{:S(2)}, u32[]{:S(2)}) async-start(bf16[4,152,2048]{2,1,0:T(8,128)(2,1)} %convolution_convert_fusion.12), calls=%async_computation | async-start | bytes 4980736 | tf_op jit(solution)/shard_map/all_to_all | solution.py:536
  25.1 141.1 %all-gather.9.cloned.1.call-start = ((), (), s32[]{:S(2)}) async-start(), calls=%async_computation.21 | async-start | bytes 14155776 | tf_op jit(solution)/shard_map/all_gather | solution.py:552
  68.4 61.0 %collective-permute-start.7 = (bf16[320,2048]{1,0:T(8,128)(2,1)}, bf16[320,2048]{1,0:T(8,128)(2,1)}, u32[]{:S(2)}, u32[]{:S(2)}) collective-permute-start(bf16[320,2048]{1,0:T(8,128)(2,1)} %collective-permute-done.3), channel_id=1, source_target_pairs={{0,8},{8,16},{16,24},{24,0},{1,9},{9,17},{17,25},{25,1},{2,10},{10... | collective-permute-start | bytes 3932168 | tf_op jit(solution)/shard_map/ppermute | solution.py:531
  69.9 59.4 %collective-permute-start.8 = (bf16[4,152,2048]{2,1,0:T(8,128)(2,1)}, bf16[4,152,2048]{2,1,0:T(8,128)(2,1)}, u32[]{:S(2)}, u32[]{:S(2)}) collective-permute-start(bf16[4,152,2048]{2,1,0:T(8,128)(2,1)} %all-to-all-done), channel_id=1, source_target_pairs={{0,1},{1,0},{2,3},{3,2},{4,5},{5,4},{6,7},{7,6},{8,9},{9,8},{10,11... | collective-permute-start | bytes 7471112 | tf_op jit(solution)/shard_map/ppermute | solution.py:548
  75.7 53.6 %all-to-all-start.1 = ((bf16[4,152,2048]{2,1,0:T(8,128)(2,1)}), bf16[4,152,2048]{2,1,0:T(8,128)(2,1)}, u32[]{:S(2)}, u32[]{:S(2)}) async-start(bf16[4,152,2048]{2,1,0:T(8,128)(2,1)} %convolution_convert_fusion.11), calls=%async_computation.1 | async-start | bytes 4980736 | tf_op jit(solution)/shard_map/all_to_all | solution.py:536
  80.4 143.2 %all-gather.11.cloned.1.call-start = ((), (), s32[]{:S(2)}) async-start(), calls=%async_computation.22 | async-start | bytes 4718592 | tf_op jit(solution)/shard_map/all_gather | solution.py:552
  87.0 40.8 %collective-permute-start.5 = (bf16[320,576]{1,0:T(8,128)(2,1)S(1)}, bf16[320,576]{1,0:T(8,128)(2,1)S(1)}, u32[]{:S(2)}, u32[]{:S(2)}) collective-permute-start(bf16[320,576]{1,0:T(8,128)(2,1)S(1)} %pad_maximum_fusion.7), channel_id=1, source_target_pairs={{0,16},{8,24},{16,0},{24,8},{1,17},{9,25},{17,1},{25,9},{2,18},{10... | collective-permute-start | bytes 1105928 | tf_op jit(solution)/shard_map/ppermute | solution.py:561
  88.3 39.5 %collective-permute-start.6 = (bf16[320,576]{1,0:T(8,128)(2,1)S(1)}, bf16[320,576]{1,0:T(8,128)(2,1)S(1)}, u32[]{:S(2)}, u32[]{:S(2)}) collective-permute-start(bf16[320,576]{1,0:T(8,128)(2,1)S(1)} %pad_maximum_fusion.7), channel_id=1, source_target_pairs={{0,24},{8,0},{16,8},{24,16},{1,25},{9,1},{17,9},{25,17},{2,26},{10... | collective-permute-start | bytes 1105928 | tf_op jit(solution)/shard_map/ppermute | solution.py:561
  166.2 45.4 %collective-permute-start.10 = (bf16[4,152,2048]{2,1,0:T(8,128)(2,1)}, bf16[4,152,2048]{2,1,0:T(8,128)(2,1)}, u32[]{:S(2)}, u32[]{:S(2)}) collective-permute-start(bf16[4,152,2048]{2,1,0:T(8,128)(2,1)} %all-to-all-done.1), channel_id=1, source_target_pairs={{0,1},{1,0},{2,3},{3,2},{4,5},{5,4},{6,7},{7,6},{8,9},{9,8},{10,11... | collective-permute-start | bytes 7471112 | tf_op jit(solution)/shard_map/ppermute | solution.py:548
  170.8 40.8 %all-to-all-start.2 = ((bf16[4,152,2048]{2,1,0:T(8,128)(2,1)}), bf16[4,152,2048]{2,1,0:T(8,128)(2,1)}, u32[]{:S(2)}, u32[]{:S(2)}) async-start(bf16[4,152,2048]{2,1,0:T(8,128)(2,1)} %convolution_convert_fusion.10), calls=%async_computation.2 | async-start | bytes 4980736 | tf_op jit(solution)/shard_map/all_to_all | solution.py:536
  175.3 125.1 %all-gather.13.cloned.1.call-start = ((), (), s32[]{:S(2)}) async-start(), calls=%async_computation.23 | async-start | bytes 9437184 | tf_op jit(solution)/shard_map/all_gather | solution.py:552
  236.9 60.5 %collective-permute-start.11 = (bf16[4,152,2048]{2,1,0:T(8,128)(2,1)}, bf16[4,152,2048]{2,1,0:T(8,128)(2,1)}, u32[]{:S(2)}, u32[]{:S(2)}) collective-permute-start(bf16[4,152,2048]{2,1,0:T(8,128)(2,1)} %all-to-all-done.2), channel_id=1, source_target_pairs={{0,1},{1,0},{2,3},{3,2},{4,5},{5,4},{6,7},{7,6},{8,9},{9,8},{10,11... | collective-permute-start | bytes 7471112 | tf_op jit(solution)/shard_map/ppermute | solution.py:548
  241.7 55.7 %all-to-all-start.3 = ((bf16[4,152,2048]{2,1,0:T(8,128)(2,1)}), bf16[4,152,2048]{2,1,0:T(8,128)(2,1)}, u32[]{:S(2)}, u32[]{:S(2)}) async-start(bf16[4,152,2048]{2,1,0:T(8,128)(2,1)} %convolution_convert_fusion.9), calls=%async_computation.3 | async-start | bytes 4980736 | tf_op jit(solution)/shard_map/all_to_all | solution.py:536
  246.3 125.0 %all-gather.15.cloned.1.call-start = ((), (), s32[]{:S(2)}) async-start(), calls=%async_computation.24 | async-start | bytes 3244032 | tf_op jit(solution)/shard_map/all_gather | solution.py:552
  300.5 119.4 %all-gather.17.cloned.1.call-start = ((), (), s32[]{:S(2)}) async-start(), calls=%async_computation.25 | async-start | bytes 6488064 | tf_op jit(solution)/shard_map/all_gather | solution.py:552
  311.2 49.6 %collective-permute-start.12 = (bf16[4,152,2048]{2,1,0:T(8,128)(2,1)}, bf16[4,152,2048]{2,1,0:T(8,128)(2,1)}, u32[]{:S(2)}, u32[]{:S(2)}) collective-permute-start(bf16[4,152,2048]{2,1,0:T(8,128)(2,1)} %all-to-all-done.3), channel_id=1, source_target_pairs={{0,1},{1,0},{2,3},{3,2},{4,5},{5,4},{6,7},{7,6},{8,9},{9,8},{10,11... | collective-permute-start | bytes 7471112 | tf_op jit(solution)/shard_map/ppermute | solution.py:548
  320.1 40.7 %all-to-all-start.4 = ((bf16[4,152,2176]{2,1,0:T(8,128)(2,1)}), bf16[4,152,2176]{2,1,0:T(8,128)(2,1)}, u32[]{:S(2)}, u32[]{:S(2)}) async-start(bf16[4,152,2176]{2,1,0:T(8,128)(2,1)} %convolution_convert_fusion.4), calls=%async_computation.4 | async-start | bytes 5292032 | tf_op jit(solution)/shard_map/all_to_all | solution.py:536
  360.7 56.3 %collective-permute-start.15 = (bf16[4,152,2176]{2,1,0:T(8,128)(2,1)}, bf16[4,152,2176]{2,1,0:T(8,128)(2,1)}, u32[]{:S(2)}, u32[]{:S(2)}) collective-permute-start(bf16[4,152,2176]{2,1,0:T(8,128)(2,1)} %all-to-all-done.4), channel_id=1, source_target_pairs={{0,1},{1,0},{2,3},{3,2},{4,5},{5,4},{6,7},{7,6},{8,9},{9,8},{10,11... | collective-permute-start | bytes 7938056 | tf_op jit(solution)/shard_map/ppermute | solution.py:548
  365.3 51.8 %all-to-all-start.5 = ((bf16[4,152,2176]{2,1,0:T(8,128)(2,1)}), bf16[4,152,2176]{2,1,0:T(8,128)(2,1)}, u32[]{:S(2)}, u32[]{:S(2)}) async-start(bf16[4,152,2176]{2,1,0:T(8,128)(2,1)} %convolution_convert_fusion.3), calls=%async_computation.5 | async-start | bytes 5292032 | tf_op jit(solution)/shard_map/all_to_all | solution.py:536
  419.9 46.5 %collective-permute-start.17 = (bf16[4,152,2176]{2,1,0:T(8,128)(2,1)}, bf16[4,152,2176]{2,1,0:T(8,128)(2,1)}, u32[]{:S(2)}, u32[]{:S(2)}) collective-permute-start(bf16[4,152,2176]{2,1,0:T(8,128)(2,1)} %all-to-all-done.5), channel_id=1, source_target_pairs={{0,1},{1,0},{2,3},{3,2},{4,5},{5,4},{6,7},{7,6},{8,9},{9,8},{10,11... | collective-permute-start | bytes 7938056 | tf_op jit(solution)/shard_map/ppermute | solution.py:548
  424.5 41.8 %all-to-all-start.6 = ((bf16[4,152,2176]{2,1,0:T(8,128)(2,1)}), bf16[4,152,2176]{2,1,0:T(8,128)(2,1)}, u32[]{:S(2)}, u32[]{:S(2)}) async-start(bf16[4,152,2176]{2,1,0:T(8,128)(2,1)} %convolution_convert_fusion.2), calls=%async_computation.6 | async-start | bytes 5292032 | tf_op jit(solution)/shard_map/all_to_all | solution.py:536
  429.1 37.2 %collective-permute-start.16 = (bf16[320,2176]{1,0:T(8,128)(2,1)}, bf16[320,2176]{1,0:T(8,128)(2,1)}, u32[]{:S(2)}, u32[]{:S(2)}) collective-permute-start(bf16[320,2176]{1,0:T(8,128)(2,1)} %collective-permute-done.14), channel_id=1, source_target_pairs={{0,8},{8,16},{16,24},{24,0},{1,9},{9,17},{17,25},{25,1},{2,10},{10... | collective-permute-start | bytes 4177928 | tf_op jit(solution)/shard_map/ppermute | solution.py:531
  466.3 53.9 %collective-permute-start.18 = (bf16[4,152,2176]{2,1,0:T(8,128)(2,1)}, bf16[4,152,2176]{2,1,0:T(8,128)(2,1)}, u32[]{:S(2)}, u32[]{:S(2)}) collective-permute-start(bf16[4,152,2176]{2,1,0:T(8,128)(2,1)} %bitcast.307), channel_id=1, source_target_pairs={{0,1},{1,0},{2,3},{3,2},{4,5},{5,4},{6,7},{7,6},{8,9},{9,8},{10,11... | collective-permute-start | bytes 7938056 | tf_op jit(solution)/shard_map/ppermute | solution.py:548
  466.4 57.7 %collective-permute-start.19 = (bf16[320,2048]{1,0:T(8,128)(2,1)S(1)}, bf16[320,2048]{1,0:T(8,128)(2,1)}, u32[]{:S(2)}, u32[]{:S(2)}) collective-permute-start(bf16[320,2048]{1,0:T(8,128)(2,1)S(1)} %get-tuple-element.216), channel_id=1, source_target_pairs={{0,8},{8,16},{16,24},{24,0},{1,9},{9,17},{17,25},{25,1},{2,10},{10... | collective-permute-start | bytes 3932168 | tf_op jit(solution)/shard_map/ppermute | solution.py:531
  477.4 46.7 %all-to-all-start.7 = ((bf16[4,152,2176]{2,1,0:T(8,128)(2,1)}), bf16[4,152,2176]{2,1,0:T(8,128)(2,1)}, u32[]{:S(2)}, u32[]{:S(2)}) async-start(bf16[4,152,2176]{2,1,0:T(8,128)(2,1)} %convolution_convert_fusion.1), calls=%async_computation.7 | async-start | bytes 5292032 | tf_op jit(solution)/shard_map/all_to_all | solution.py:536
  482.2 41.9 %collective-permute-start.20 = (bf16[4,152,2176]{2,1,0:T(8,128)(2,1)}, bf16[4,152,2176]{2,1,0:T(8,128)(2,1)}, u32[]{:S(2)}, u32[]{:S(2)}) collective-permute-start(bf16[4,152,2176]{2,1,0:T(8,128)(2,1)} %all-to-all-done.6), channel_id=1, source_target_pairs={{0,1},{1,0},{2,3},{3,2},{4,5},{5,4},{6,7},{7,6},{8,9},{9,8},{10,11... | collective-permute-start | bytes 7938056 | tf_op jit(solution)/shard_map/ppermute | solution.py:548
  524.1 47.2 %collective-permute-start.21 = (bf16[4,152,2176]{2,1,0:T(8,128)(2,1)}, bf16[4,152,2176]{2,1,0:T(8,128)(2,1)}, u32[]{:S(2)}, u32[]{:S(2)}) collective-permute-start(bf16[4,152,2176]{2,1,0:T(8,128)(2,1)} %bitcast.305), channel_id=1, source_target_pairs={{0,1},{1,0},{2,3},{3,2},{4,5},{5,4},{6,7},{7,6},{8,9},{9,8},{10,11... | collective-permute-start | bytes 7938056 | tf_op jit(solution)/shard_map/ppermute | solution.py:548
  529.8 45.5 %collective-permute-start.22 = (bf16[320,2048]{1,0:T(8,128)(2,1)}, bf16[320,2048]{1,0:T(8,128)(2,1)}, u32[]{:S(2)}, u32[]{:S(2)}) collective-permute-start(bf16[320,2048]{1,0:T(8,128)(2,1)} %collective-permute-done.19), channel_id=1, source_target_pairs={{0,8},{8,16},{16,24},{24,0},{1,9},{9,17},{17,25},{25,1},{2,10},{10... | collective-permute-start | bytes 3932168 | tf_op jit(solution)/shard_map/ppermute | solution.py:531
  531.3 44.0 %all-to-all-start.8 = ((bf16[4,152,2176]{2,1,0:T(8,128)(2,1)}), bf16[4,152,2176]{2,1,0:T(8,128)(2,1)S(1)}, u32[]{:S(2)}, u32[]{:S(2)}) async-start(bf16[4,152,2176]{2,1,0:T(8,128)(2,1)} %add_convert_fusion.3), calls=%async_computation.8 | async-start | bytes 5292032 | tf_op jit(solution)/shard_map/all_to_all | solution.py:536
  535.8 39.4 %collective-permute-start.23 = (bf16[4,152,2176]{2,1,0:T(8,128)(2,1)}, bf16[4,152,2176]{2,1,0:T(8,128)(2,1)}, u32[]{:S(2)}, u32[]{:S(2)}) collective-permute-start(bf16[4,152,2176]{2,1,0:T(8,128)(2,1)} %all-to-all-done.7), channel_id=1, source_target_pairs={{0,1},{1,0},{2,3},{3,2},{4,5},{5,4},{6,7},{7,6},{8,9},{9,8},{10,11... | collective-permute-start | bytes 7938056 | tf_op jit(solution)/shard_map/ppermute | solution.py:548
  594.5 61.2 %collective-permute-start.24 = (bf16[4,152,2176]{2,1,0:T(8,128)(2,1)}, bf16[4,152,2176]{2,1,0:T(8,128)(2,1)}, u32[]{:S(2)}, u32[]{:S(2)}) collective-permute-start(bf16[4,152,2176]{2,1,0:T(8,128)(2,1)} %bitcast.52), channel_id=1, source_target_pairs={{0,1},{1,0},{2,3},{3,2},{4,5},{5,4},{6,7},{7,6},{8,9},{9,8},{10,11... | collective-permute-start | bytes 7938056 | tf_op jit(solution)/shard_map/ppermute | solution.py:548
  595.0 64.6 %collective-permute-start.25 = (bf16[320,2048]{1,0:T(8,128)(2,1)}, bf16[320,2048]{1,0:T(8,128)(2,1)}, u32[]{:S(2)}, u32[]{:S(2)}) collective-permute-start(bf16[320,2048]{1,0:T(8,128)(2,1)} %collective-permute-done.22), channel_id=1, source_target_pairs={{0,8},{8,16},{16,24},{24,0},{1,9},{9,17},{17,25},{25,1},{2,10},{10... | collective-permute-start | bytes 3932168 | tf_op jit(solution)/shard_map/ppermute | solution.py:531
  595.5 64.1 %all-to-all-start.9 = ((bf16[4,152,2176]{2,1,0:T(8,128)(2,1)}), bf16[4,152,2176]{2,1,0:T(8,128)(2,1)S(1)}, u32[]{:S(2)}, u32[]{:S(2)}) async-start(bf16[4,152,2176]{2,1,0:T(8,128)(2,1)} %add_convert_fusion.2), calls=%async_computation.9 | async-start | bytes 5292032 | tf_op jit(solution)/shard_map/all_to_all | solution.py:536
  659.6 55.4 %collective-permute-start.29 = (bf16[4,152,2048]{2,1,0:T(8,128)(2,1)}, bf16[4,152,2048]{2,1,0:T(8,128)(2,1)}, u32[]{:S(2)}, u32[]{:S(2)}) collective-permute-start(bf16[4,152,2048]{2,1,0:T(8,128)(2,1)} %bitcast.308), channel_id=1, source_target_pairs={{0,1},{1,0},{2,3},{3,2},{4,5},{5,4},{6,7},{7,6},{8,9},{9,8},{10,11... | collective-permute-start | bytes 7471112 | tf_op jit(solution)/shard_map/ppermute | solution.py:548
  660.1 44.9 %all-to-all-start.10 = ((bf16[4,152,2176]{2,1,0:T(8,128)(2,1)}), bf16[4,152,2176]{2,1,0:T(8,128)(2,1)}, u32[]{:S(2)}, u32[]{:S(2)}) async-start(bf16[4,152,2176]{2,1,0:T(8,128)(2,1)} %add_convert_fusion.1), calls=%async_computation.10 | async-start | bytes 5292032 | tf_op jit(solution)/shard_map/all_to_all | solution.py:536
  672.1 47.2 %collective-permute-start.31 = (bf16[4,152,2048]{2,1,0:T(8,128)(2,1)}, bf16[4,152,2048]{2,1,0:T(8,128)(2,1)}, u32[]{:S(2)}, u32[]{:S(2)}) collective-permute-start(bf16[4,152,2048]{2,1,0:T(8,128)(2,1)} %bitcast.54), channel_id=1, source_target_pairs={{0,1},{1,0},{2,3},{3,2},{4,5},{5,4},{6,7},{7,6},{8,9},{9,8},{10,11... | collective-permute-start | bytes 7471112 | tf_op jit(solution)/shard_map/ppermute | solution.py:548
  706.0 42.2 %all-to-all-start.11 = ((bf16[4,152,2176]{2,1,0:T(8,128)(2,1)}), bf16[4,152,2176]{2,1,0:T(8,128)(2,1)S(1)}, u32[]{:S(2)}, u32[]{:S(2)}) async-start(bf16[4,152,2176]{2,1,0:T(8,128)(2,1)} %add_convert_fusion), calls=%async_computation.11 | async-start | bytes 5292032 | tf_op jit(solution)/shard_map/all_to_all | solution.py:536
  756.9 44.9 %collective-permute-start.30 = (bf16[320,2176]{1,0:T(8,128)(2,1)}, bf16[320,2176]{1,0:T(8,128)(2,1)}, u32[]{:S(2)}, u32[]{:S(2)}) collective-permute-start(bf16[320,2176]{1,0:T(8,128)(2,1)} %fusion.16), channel_id=1, source_target_pairs={{0,8},{8,16},{16,24},{24,0},{1,9},{9,17},{17,25},{25,1},{2,10},{10... | collective-permute-start | bytes 4177928 | tf_op jit(solution)/shard_map/ppermute | solution.py:531
  756.9 44.9 %all-to-all-start.12 = ((bf16[4,152,2048]{2,1,0:T(8,128)(2,1)}), bf16[4,152,2048]{2,1,0:T(8,128)(2,1)S(1)}, u32[]{:S(2)}, u32[]{:S(2)}) async-start(bf16[4,152,2048]{2,1,0:T(8,128)(2,1)} %add_convert_fusion.7), calls=%async_computation.12 | async-start | bytes 4980736 | tf_op jit(solution)/shard_map/all_to_all | solution.py:536
  760.9 146.3 %reduce-scatter.5.cloned.1.call-start = ((), (), s32[]{:S(2)}) async-start(), calls=%async_computation.26 | async-start | bytes 9732096 | tf_op jit(solution)/shard_map/reduce_scatter | solution.py:556
  823.1 59.4 %collective-permute-start.32 = (bf16[4,152,2048]{2,1,0:T(8,128)(2,1)}, bf16[4,152,2048]{2,1,0:T(8,128)(2,1)}, u32[]{:S(2)}, u32[]{:S(2)}) collective-permute-start(bf16[4,152,2048]{2,1,0:T(8,128)(2,1)} %bitcast.62), channel_id=1, source_target_pairs={{0,1},{1,0},{2,3},{3,2},{4,5},{5,4},{6,7},{7,6},{8,9},{9,8},{10,11... | collective-permute-start | bytes 7471112 | tf_op jit(solution)/shard_map/ppermute | solution.py:548
  826.9 80.3 %all-to-all-start.13 = ((bf16[4,152,2048]{2,1,0:T(8,128)(2,1)}), bf16[4,152,2048]{2,1,0:T(8,128)(2,1)}, u32[]{:S(2)}, u32[]{:S(2)}) async-start(bf16[4,152,2048]{2,1,0:T(8,128)(2,1)} %add_convert_fusion.6), calls=%async_computation.13 | async-start | bytes 4980736 | tf_op jit(solution)/shard_map/all_to_all | solution.py:536
  831.8 163.4 %reduce-scatter.7.cloned.1.call-start = ((), (), s32[]{:S(2)}) async-start(), calls=%async_computation.27 | async-start | bytes 2359296 | tf_op jit(solution)/shard_map/reduce_scatter | solution.py:556
  833.3 40.3 %collective-permute-start.36 = (bf16[320,512]{1,0:T(8,128)(2,1)S(1)}, bf16[320,512]{1,0:T(8,128)(2,1)S(1)}, u32[]{:S(2)}, u32[]{:S(2)}) collective-permute-start(bf16[320,512]{1,0:T(8,128)(2,1)S(1)} %get-tuple-element.493), channel_id=1, source_target_pairs={{0,24},{8,0},{16,8},{24,16},{1,25},{9,1},{17,9},{25,17},{2,26},{10... | collective-permute-start | bytes 983048 | tf_op jit(solution)/shard_map/ppermute | solution.py:561
  837.3 39.4 %collective-permute-start.35 = (bf16[320,512]{1,0:T(8,128)(2,1)S(1)}, bf16[320,512]{1,0:T(8,128)(2,1)S(1)}, u32[]{:S(2)}, u32[]{:S(2)}) collective-permute-start(bf16[320,512]{1,0:T(8,128)(2,1)S(1)} %get-tuple-element.494), channel_id=1, source_target_pairs={{0,16},{8,24},{16,0},{24,8},{1,17},{9,25},{17,1},{25,9},{2,18},{10... | collective-permute-start | bytes 983048 | tf_op jit(solution)/shard_map/ppermute | solution.py:561
  837.3 39.4 %collective-permute-start.34 = (bf16[320,512]{1,0:T(8,128)(2,1)S(1)}, bf16[320,512]{1,0:T(8,128)(2,1)S(1)}, u32[]{:S(2)}, u32[]{:S(2)}) collective-permute-start(bf16[320,512]{1,0:T(8,128)(2,1)S(1)} %get-tuple-element.495), channel_id=1, source_target_pairs={{0,8},{8,16},{16,24},{24,0},{1,9},{9,17},{17,25},{25,1},{2,10},{10... | collective-permute-start | bytes 983048 | tf_op jit(solution)/shard_map/ppermute | solution.py:561
  837.9 49.8 %collective-permute-start.40 = (bf16[4,152,2048]{2,1,0:T(8,128)(2,1)}, bf16[4,152,2048]{2,1,0:T(8,128)(2,1)}, u32[]{:S(2)}, u32[]{:S(2)}) collective-permute-start(bf16[4,152,2048]{2,1,0:T(8,128)(2,1)} %bitcast.34), channel_id=1, source_target_pairs={{0,1},{1,0},{2,3},{3,2},{4,5},{5,4},{6,7},{7,6},{8,9},{9,8},{10,11... | collective-permute-start | bytes 7471112 | tf_op jit(solution)/shard_map/ppermute | solution.py:548
  929.0 64.6 %collective-permute-start.38 = (bf16[320,576]{1,0:T(8,128)(2,1)}, bf16[320,576]{1,0:T(8,128)(2,1)}, u32[]{:S(2)}, u32[]{:S(2)}) collective-permute-start(bf16[320,576]{1,0:T(8,128)(2,1)} %get-tuple-element.484), channel_id=1, source_target_pairs={{0,16},{8,24},{16,0},{24,8},{1,17},{9,25},{17,1},{25,9},{2,18},{10... | collective-permute-start | bytes 1105928 | tf_op jit(solution)/shard_map/ppermute | solution.py:561
  930.2 63.5 %collective-permute-start.37 = (bf16[320,576]{1,0:T(8,128)(2,1)}, bf16[320,576]{1,0:T(8,128)(2,1)}, u32[]{:S(2)}, u32[]{:S(2)}) collective-permute-start(bf16[320,576]{1,0:T(8,128)(2,1)} %get-tuple-element.482), channel_id=1, source_target_pairs={{0,8},{8,16},{16,24},{24,0},{1,9},{9,17},{17,25},{25,1},{2,10},{10... | collective-permute-start | bytes 1105928 | tf_op jit(solution)/shard_map/ppermute | solution.py:561
  930.4 64.8 %all-to-all-start.14 = ((bf16[4,152,2048]{2,1,0:T(8,128)(2,1)}), bf16[4,152,2048]{2,1,0:T(8,128)(2,1)}, u32[]{:S(2)}, u32[]{:S(2)}) async-start(bf16[4,152,2048]{2,1,0:T(8,128)(2,1)} %add_convert_fusion.5), calls=%async_computation.16 | async-start | bytes 4980736 | tf_op jit(solution)/shard_map/all_to_all | solution.py:536
  934.9 175.4 %reduce-scatter.9.cloned.1.call-start = ((), (), s32[]{:S(2)}) async-start(), calls=%async_computation.28 | async-start | bytes 14155776 | tf_op jit(solution)/shard_map/reduce_scatter | solution.py:556
  940.4 54.8 %collective-permute-start.41 = (bf16[320,2048]{1,0:T(8,128)(2,1)}, bf16[320,2048]{1,0:T(8,128)(2,1)}, u32[]{:S(2)}, u32[]{:S(2)}) collective-permute-start(bf16[320,2048]{1,0:T(8,128)(2,1)} %fusion.31), channel_id=1, source_target_pairs={{0,8},{8,16},{16,24},{24,0},{1,9},{9,17},{17,25},{25,1},{2,10},{10... | collective-permute-start | bytes 3932168 | tf_op jit(solution)/shard_map/ppermute | solution.py:531
  1032.2 74.0 %collective-permute-start.43 = (bf16[256,2112]{0,1:T(8,128)(2,1)}, bf16[256,2112]{0,1:T(8,128)(2,1)}, u32[]{:S(2)}, u32[]{:S(2)}) collective-permute-start(bf16[256,2112]{0,1:T(8,128)(2,1)} %collective-permute-done.42), channel_id=1, source_target_pairs={{0,8},{8,16},{16,24},{24,0},{1,9},{9,17},{17,25},{25,1},{2,10},{10... | collective-permute-start | bytes 3244040 | tf_op jit(solution)/shard_map/ppermute | solution.py:531
  1032.2 47.2 %collective-permute-start.45 = (bf16[256,512]{1,0:T(8,128)(2,1)S(1)}, bf16[256,512]{1,0:T(8,128)(2,1)}, u32[]{:S(2)}, u32[]{:S(2)}) collective-permute-start(bf16[256,512]{1,0:T(8,128)(2,1)S(1)} %copy-done.76), channel_id=1, source_target_pairs={{0,8},{8,16},{16,24},{24,0},{1,9},{9,17},{17,25},{25,1},{2,10},{10... | collective-permute-start | bytes 786440 | tf_op jit(solution)/shard_map/ppermute | solution.py:561
  1032.2 70.3 %collective-permute-start.46 = (bf16[256,512]{1,0:T(8,128)(2,1)S(1)}, bf16[256,512]{1,0:T(8,128)(2,1)}, u32[]{:S(2)}, u32[]{:S(2)}) collective-permute-start(bf16[256,512]{1,0:T(8,128)(2,1)S(1)} %copy-done.76), channel_id=1, source_target_pairs={{0,16},{8,24},{16,0},{24,8},{1,17},{9,25},{17,1},{25,9},{2,18},{10... | collective-permute-start | bytes 786440 | tf_op jit(solution)/shard_map/ppermute | solution.py:561
  1036.6 67.8 %collective-permute-start.47 = (bf16[256,512]{1,0:T(8,128)(2,1)S(1)}, bf16[256,512]{1,0:T(8,128)(2,1)}, u32[]{:S(2)}, u32[]{:S(2)}) collective-permute-start(bf16[256,512]{1,0:T(8,128)(2,1)S(1)} %copy-done.76), channel_id=1, source_target_pairs={{0,24},{8,0},{16,8},{24,16},{1,25},{9,1},{17,9},{25,17},{2,26},{10... | collective-permute-start | bytes 786440 | tf_op jit(solution)/shard_map/ppermute | solution.py:561
  1058.1 48.1 %collective-permute-start.44 = (bf16[320,2048]{1,0:T(8,128)(2,1)}, bf16[320,2048]{1,0:T(8,128)(2,1)}, u32[]{:S(2)}, u32[]{:S(2)}) collective-permute-start(bf16[320,2048]{1,0:T(8,128)(2,1)} %fusion.30), channel_id=1, source_target_pairs={{0,8},{8,16},{16,24},{24,0},{1,9},{9,17},{17,25},{25,1},{2,10},{10... | collective-permute-start | bytes 3932168 | tf_op jit(solution)/shard_map/ppermute | solution.py:531
  1059.9 49.6 %all-to-all-start.15 = ((bf16[4,152,2048]{2,1,0:T(8,128)(2,1)}), bf16[4,152,2048]{2,1,0:T(8,128)(2,1)}, u32[]{:S(2)}, u32[]{:S(2)}) async-start(bf16[4,152,2048]{2,1,0:T(8,128)(2,1)} %add_convert_fusion.4), calls=%async_computation.18 | async-start | bytes 4980736 | tf_op jit(solution)/shard_map/all_to_all | solution.py:536
  1064.7 150.1 %reduce-scatter.11.cloned.1.call-start = ((), (), s32[]{:S(2)}) async-start(), calls=%async_computation.29 | async-start | bytes 8257536 | tf_op jit(solution)/shard_map/reduce_scatter | solution.py:556
  1112.8 59.8 %collective-permute-start.50 = (bf16[64,3072]{1,0:T(8,128)(2,1)}, bf16[64,3072]{1,0:T(8,128)(2,1)}, u32[]{:S(2)}, u32[]{:S(2)}) collective-permute-start(bf16[64,3072]{1,0:T(8,128)(2,1)} %get-tuple-element.488), channel_id=1, source_target_pairs={{0,24},{8,0},{16,8},{24,16},{1,25},{9,1},{17,9},{25,17},{2,26},{10... | collective-permute-start | bytes 1179656 | tf_op jit(solution)/shard_map/ppermute | solution.py:561
  1115.1 57.6 %collective-permute-start.49 = (bf16[64,3072]{1,0:T(8,128)(2,1)}, bf16[64,3072]{1,0:T(8,128)(2,1)}, u32[]{:S(2)}, u32[]{:S(2)}) collective-permute-start(bf16[64,3072]{1,0:T(8,128)(2,1)} %get-tuple-element.489), channel_id=1, source_target_pairs={{0,16},{8,24},{16,0},{24,8},{1,17},{9,25},{17,1},{25,9},{2,18},{10... | collective-permute-start | bytes 1179656 | tf_op jit(solution)/shard_map/ppermute | solution.py:561
  1115.1 57.6 %collective-permute-start.48 = (bf16[64,3072]{1,0:T(8,128)(2,1)}, bf16[64,3072]{1,0:T(8,128)(2,1)}, u32[]{:S(2)}, u32[]{:S(2)}) collective-permute-start(bf16[64,3072]{1,0:T(8,128)(2,1)} %get-tuple-element.487), channel_id=1, source_target_pairs={{0,8},{8,16},{16,24},{24,0},{1,9},{9,17},{17,25},{25,1},{2,10},{10... | collective-permute-start | bytes 1179656 | tf_op jit(solution)/shard_map/ppermute | solution.py:561
  1115.8 88.8 %collective-permute-start.60 = (bf16[256,2112]{0,1:T(8,128)(2,1)}, bf16[256,2112]{0,1:T(8,128)(2,1)S(1)}, u32[]{:S(2)}, u32[]{:S(2)}) collective-permute-start(bf16[256,2112]{0,1:T(8,128)(2,1)} %collective-permute-done.43), channel_id=1, source_target_pairs={{0,8},{8,16},{16,24},{24,0},{1,9},{9,17},{17,25},{25,1},{2,10},{10... | collective-permute-start | bytes 3244040 | tf_op jit(solution)/shard_map/ppermute | solution.py:531
  (172 other events, 4579.7 us)
Sparse Core Ops, SparseCore 0:
  13.9 51.5 all-gather.6
  67.4 98.7 all-gather.8
  168.1 55.4 all-gather.10
  225.3 75.0 all-gather.12
  302.7 49.7 all-gather.14
  354.8 64.9 all-gather.16
  802.0 100.2 reduce-scatter.4
  914.9 58.6 reduce-scatter.6
  995.4 114.8 reduce-scatter.8
  1113.6 66.5 reduce-scatter.10

commit v5 on v4

--- a/solution.py
+++ b/solution.py
@@ -852,7 +852,6 @@
     )
     grad_theirs.append(to_core(grad_mine[-1]))
 
-    part_shared = gather_rows(shared_shard)
     part_down = gather_rows(down_shard)
     hidden = inputs_full + matmul(attended_low, full_output)
     ffn_in, ffn_normal, ffn_inverse = rms_forward(hidden, gain_ffn)
@@ -920,7 +919,7 @@
             jnp.einsum("ta,tb->ab", left, right, preferred_element_type=single).astype(bfloat)
             for left, right in ((group, grad_gate), (group, grad_up), (act, grad_group))
         ]
-        return jnp.concatenate(pieces[:2] + [pieces[2].reshape(model_width, hidden_part)], axis=1)
+        return pieces
 
     last = ctx_size - 1
     ffn_ring = [ffn_wide]
@@ -977,16 +976,24 @@
             sent["moving"] = hop(tick - 5)
         if tick == 0:
             sent["grads"] = grad_theirs[-1]
+        if tick == 0:
+            sent["shard"] = shared_shard
+        if tick == 3:
+            sent["weights"] = part_shared
         if tick == 1:
-            sent["weights"] = (part_shared, part_down)
+            sent["down"] = part_down
             sent["grad_act"] = jnp.einsum(
                 "td,fd->tf", grad_group, part_down, preferred_element_type=single
             )
+        if tick == ctx_size + 2:
+            sent["shared_all"] = (shared, groups, grad_group)
         if tick == ctx_size + 3:
-            sent["shared_all"] = (shared, groups, grad_group)
+            sent["shared_grads"] = shared_grads()
             sent["out"] = add_halves(*out_sends[1])
         if tick == ctx_size + 4:
-            sent["shared_grads"] = shared_grads()
+            sent["shared_packed"] = jnp.concatenate(
+                shared_pieces[:2] + [shared_pieces[2].reshape(model_width, hidden_part)], axis=1
+            )
             sent["out_step"] = to_chips(out_added[1])
         if last <= tick < 2 * last:
             sent["attended"] = ring_next(attended_ring[-1])
@@ -1011,6 +1018,8 @@
             groups.append(sent["group"])
         if "shared" in sent:
             shared[-1] = sent["shared"]
+        if "shared_grads" in sent:
+            shared_pieces = list(sent["shared_grads"])
         if "shared_all" in sent:
             shared, groups, grad_group = sent["shared_all"]
         if "attended" in sent:
@@ -1022,15 +1031,18 @@
         moving = sent.get("moving", moving)
         if tick == 0:
             grad_theirs[-1] = sent["grads"]
-        if tick == 1:
-            part_gate = sent["weights"][0][:, :hidden_part]
-            part_up = sent["weights"][0][:, hidden_part:]
-            part_down = sent["weights"][1]
+        if "shard" in sent:
+            part_shared = gather_rows(sent["shard"])
+        if "down" in sent:
+            part_down = sent["down"]
             grad_act = sent["grad_act"]
+        if "weights" in sent:
+            part_gate = sent["weights"][:, :hidden_part]
+            part_up = sent["weights"][:, hidden_part:]
 
     while len(attended_ring) < ctx_size:
         attended_ring.append(ring_next(attended_ring[-1]))
-    shared_part = scatter_rows(sent["shared_grads"])
+    shared_part = scatter_rows(sent["shared_packed"])
     first_part = block_part(0)
 
     def next_out(step):
@@ -1070,7 +1082,7 @@
         "td,vd->tv", grad_attn_low, full_output, preferred_element_type=single
     ).astype(bfloat)
     out_steps[2] = to_chips(out_added[2])
-    out_moving = out_hop(1, None)
+    out_moving = out_hop(2, out_hop(1, None))
     att_shares = column_shares(grad_attn_low, device)
     grad_attended, out_sends = together(grad_attended, out_sends)
 
@@ -1120,7 +1132,6 @@
         grad_w_output,
     )
     out_next = next_out(3)
-    out_moving = out_hop(2, out_moving)
     output_part = scatter_rows(grad_w_output)
     grad_key_rope = rope_pair_grad[:, :ROPE] + rope_pair_grad[:, ROPE:]
     keys_width = HEADS * NOPE

time: 1310 us -> 1270 us (0.969)
  waiting for transfers between devices: 408 us -> 370 us
    ppermute x27, waiting for transfers between devices: 166 us -> 149 us  [along_ctx(): lax.ppermute(value, 'ctx', [(i, (i + shift) % size) for i in range(size)])]
    unnamed x308 -> x266, local copies, waits for them, and re-layouts: 30.3 us -> 26 us
  transfers between devices with their start and end apart: 87 -> 87, of which waited for: 30 -> 32; matrix products, arithmetic and copies ran while one was open for 35% -> 39% of each run, Pallas kernels for 15% -> 16%
where the time goes in v5:
time: 1270 us; the launch traced here: 1260 us
  waiting for transfers between devices  370 us (29%)
  matrix products  311 us (24%)
  Pallas kernels  199 us (16%)
  starting transfers between devices  151 us (12%)
  local copies, waits for them, and re-layouts  108 us (9%)
  other arithmetic  106 us (8%)
  between operations  16.8 us (1%)
    ppermute x27, waiting for transfers between devices, along_ctx(): lax.ppermute(value, 'ctx', [(i, (i + shift) % size) for i in range(size)])  149 us
    pallas_call x4, Pallas kernels, expert_call(): pl.pallas_call(functools.partial(expert_kernel, step * 2 * count, experts...  141 us
    ppermute x18, waiting for transfers between devices, ring_next(): lax.ppermute(value, 'ctx', [(i, (i + 1) % size) for i in range(size)])  141 us
    dot_general x7, matrix products, weight_grad(): return jnp.einsum('ra,rb->ab', left, right, preferred_element_type=single)  93.3 us
    all_to_all x16, starting transfers between devices, to_chips(): lax.all_to_all(value, 'fsdp', split_axis=0, concat_axis=0, tiled=True, ax...  74.8 us
    dot_general x15, matrix products, matmul(): return jnp.dot(left, right, preferred_element_type=single)  64.7 us
    all_gather x6, waiting for transfers between devices, gather_rows(): return lax.all_gather(value, 'fsdp', axis=0, tiled=True)  51.9 us
    ppermute x27, starting transfers between devices, along_ctx(): lax.ppermute(value, 'ctx', [(i, (i + shift) % size) for i in range(size)])  46.6 us
  transfers between devices with their start and end apart: 87, of which 32 were waited for; matrix products, arithmetic and copies ran while one was open for 39% of the time, Pallas kernels for 16%

profile of v5, /device:TPU:0, one launch (start us, length us, event | category | flops | bytes accessed | tf_op | source)
XLA Modules:
  0.0 1260.9 jit_solution(9544433408910082173)
XLA Ops:
  19.8 5.3 all-to-all-start
  33.1 26.0 %collective-permute-done = s32[320,6]{0,1:T(8,128)S(1)} collective-permute-done((s32[320,6]{0,1:T(8,128)S(1)}, s32[320,6]{0,1:T(8,128)S(1)}, u32[]{:S(2)}, u32[]{:S(2)}) %collective-permute-start) | collective-permute-done | bytes 7712 | tf_op jit(solution)/shard_map/ppermute | solution.py:561
  91.9 19.6 %collective-permute-done.4 = bf16[320,576]{1,0:T(8,128)(2,1)S(1)} collective-permute-done((bf16[320,576]{1,0:T(8,128)(2,1)S(1)}, bf16[320,576]{1,0:T(8,128)(2,1)S(1)}, u32[]{:S(2)}, u32[]{:S(2)}) %collective-permute-start.4) | collective-permute-done | bytes 368672 | tf_op jit(solution)/shard_map/ppermute | solution.py:561
  111.5 16.9 %collective-permute-done.5 = bf16[320,576]{1,0:T(8,128)(2,1)S(1)} collective-permute-done((bf16[320,576]{1,0:T(8,128)(2,1)S(1)}, bf16[320,576]{1,0:T(8,128)(2,1)S(1)}, u32[]{:S(2)}, u32[]{:S(2)}) %collective-permute-start.5) | collective-permute-done | bytes 368672 | tf_op jit(solution)/shard_map/ppermute | solution.py:561
  129.9 34.6 %all-gather.9.cloned.1.call-done = bf16[2048,3072]{1,0:T(8,128)(2,1)} async-done(((bf16[256,3072]{1,0:T(8,128)(2,1)}), bf16[2048,3072]{1,0:T(8,128)(2,1)}) %all-gather.9.cloned.1.call-update) | async-done | bytes 12582928 | tf_op jit(solution)/shard_map/all_gather | solution.py:552
  175.8 9.3 fusion.149.nope.rope
  185.1 22.3 %collective-permute-done.9 = bf16[320,2048]{1,0:T(8,128)(2,1)} collective-permute-done((bf16[320,2048]{1,0:T(8,128)(2,1)}, bf16[320,2048]{1,0:T(8,128)(2,1)}, u32[]{:S(2)}, u32[]{:S(2)}) %collective-permute-start.9) | collective-permute-done | bytes 1310752 | tf_op jit(solution)/shard_map/ppermute | solution.py:531
  210.0 12.0 all-gather.11.cloned.1.call-done
  247.4 10.7 convolution_convert_fusion.keys.values
  258.1 26.6 %shard_map.306 = (bf16[320,2048]{1,0:T(8,128)(2,1)S(1)}, f32[320,128]{1,0:T(8,128)S(1)}) custom-call(s32[1]{0:T(128)} %bitcast.11.link, f32[320,3072]{1,0:T(8,128)S(1)} %copy-done.2, f32[320,3072]{1,0:T(8,128)S(1)} %copy-done.2, f32[320,128]{1,0:T(8,128)S(1)} %get-tuple-element.525.cos, f32[320,128]{1,0:T(8,128)S(1)} %get-tuple-element.526.sin, ...), custom_call_target="tpu_custom_call" | custom-call | flops 2214592512 | bytes 16384000 | tf_op jit(solution)/shard_map/pallas_call | solution.py:312
  284.7 5.5 pad_maximum_fusion.1
  290.1 9.3 all-to-all-done.3
  301.3 6.7 multiply_reduce_fusion.2
  326.6 33.3 %collective-permute-done.13 = bf16[320,2176]{1,0:T(8,128)(2,1)} collective-permute-done((bf16[320,2176]{1,0:T(8,128)(2,1)}, bf16[320,2176]{1,0:T(8,128)(2,1)}, u32[]{:S(2)}, u32[]{:S(2)}) %collective-permute-start.13) | collective-permute-done | bytes 1392672 | tf_op jit(solution)/shard_map/ppermute | solution.py:531
  372.8 9.1 fusion.157
  381.9 24.5 %collective-permute-done.14 = bf16[320,2176]{1,0:T(8,128)(2,1)} collective-permute-done((bf16[320,2176]{1,0:T(8,128)(2,1)}, bf16[320,2176]{1,0:T(8,128)(2,1)}, u32[]{:S(2)}, u32[]{:S(2)}) %collective-permute-start.14) | collective-permute-done | bytes 1392672 | tf_op jit(solution)/shard_map/ppermute | solution.py:531
  420.0 35.5 %shard_map.307 = (bf16[608,2176]{1,0:T(8,128)(2,1)}, bf16[608,2176]{1,0:T(8,128)(2,1)}, bf16[608,2048]{1,0:T(8,128)(2,1)}, bf16[608,2048]{1,0:T(8,128)(2,1)}, bf...) custom-call(s32[1]{0:T(128)} %bitcast.18.expert, ...), custom_call_target="tpu_custom_call" | custom-call | flops 21038628864 | bytes 43671552 | tf_op jit(solution)/shard_map/pallas_call | solution.py:505
  471.7 35.4 %shard_map.308 = (bf16[608,2176]{1,0:T(8,128)(2,1)}, bf16[608,2176]{1,0:T(8,128)(2,1)}, bf16[608,2048]{1,0:T(8,128)(2,1)}, bf16[608,2048]{1,0:T(8,128)(2,1)}, bf...) custom-call(s32[1]{0:T(128)} %bitcast.18.expert, ...), custom_call_target="tpu_custom_call", output_to_operand_aliasing={{4}: (8, {}), {5}: (9, {}), {6}: (10, {}), {7}: (11, {}), {... | custom-call | flops 21038628864 | bytes 43671552 | tf_op jit(solution)/shard_map/pallas_call | solution.py:505
  514.0 5.2 pad_maximum_fusion.2
  520.7 4.8 all-to-all-start.8
  526.1 35.3 %shard_map.309 = (bf16[608,2176]{1,0:T(8,128)(2,1)}, bf16[608,2176]{1,0:T(8,128)(2,1)}, bf16[608,2048]{1,0:T(8,128)(2,1)}, bf16[608,2048]{1,0:T(8,128)(2,1)}, bf...) custom-call(s32[1]{0:T(128)} %bitcast.18.expert, ...), custom_call_target="tpu_custom_call", output_to_operand_aliasing={{4}: (8, {}), {5}: (9, {}), {6}: (10, {}), {7}: (11, {}), {... | custom-call | flops 21038628864 | bytes 43671552 | tf_op jit(solution)/shard_map/pallas_call | solution.py:505
  565.5 9.3 fusion.46
  574.8 7.5 fusion.43
  587.6 35.3 %shard_map.310 = (bf16[608,2176]{1,0:T(8,128)(2,1)}, bf16[608,2176]{1,0:T(8,128)(2,1)}, bf16[608,2048]{1,0:T(8,128)(2,1)}, bf16[608,2048]{1,0:T(8,128)(2,1)}, bf...) custom-call(s32[1]{0:T(128)} %bitcast.18.expert, ...), custom_call_target="tpu_custom_call", output_to_operand_aliasing={{4}: (8, {}), {5}: (9, {}), {6}: (10, {}), {7}: (11, {}), {... | custom-call | flops 21038628864 | bytes 43671552 | tf_op jit(solution)/shard_map/pallas_call | solution.py:505
  623.0 5.4 multiply_convert_fusion
  628.4 7.5 fusion.41
  636.0 7.1 convolution_add_fusion
  669.7 24.9 %collective-permute-done.27 = bf16[320,2176]{1,0:T(8,128)(2,1)S(1)} collective-permute-done((bf16[320,2176]{1,0:T(8,128)(2,1)S(1)}, bf16[320,2176]{1,0:T(8,128)(2,1)S(1)}, u32[]{:S(2)}, u32[]{:S(2)}) %collective-permute-start.27) | collective-permute-done | bytes 1392672 | tf_op jit(solution)/shard_map/ppermute | solution.py:531
  694.6 6.4 fusion.153
  710.0 8.6 convolution_convert_fusion.6
  718.7 5.2 convolution_convert_fusion.5
  723.9 5.2 convolution_convert_fusion.7
  729.1 10.0 collective-permute-done.28
  745.5 5.6 fusion.16
  756.4 7.0 reshape.511
  768.0 7.3 pad_maximum_fusion
  775.3 9.4 collective-permute-done.30
  785.2 4.9 fusion.81
  794.9 5.9 fusion.31
  821.4 31.0 %shard_map.311 = (bf16[320,2048]{1,0:T(8,128)(2,1)S(1)}, bf16[320,1024]{1,0:T(8,128)(2,1)S(1)}, bf16[1280,2048]{1,0:T(8,128)(2,1)}, bf16[1280,2048]{1,0:T(8,128)(2,1)}, f32[1280,128]{1,0:T(8,128)S(1)}) custom-call(s32[1]{0:T(128)} %bitcast.11.link, f32[320,3072]{1,0:T(8,128)} %fusion.149.nope.rope, f32[320,3072]{1,0:T(8,128)} %fusion.149.nope.rope, ...), custom_call_target="tpu_custom_call" | custom-call | flops 6643777536 | bytes 30801920 | tf_op jit(solution)/shard_map/pallas_call | solution.py:337
  853.4 5.3 fusion.32
  865.4 5.6 fusion.2
  871.1 5.2 add_convert_fusion.5
  880.4 12.6 %collective-permute-done.34 = bf16[320,2048]{1,0:T(8,128)(2,1)} collective-permute-done((bf16[320,2048]{1,0:T(8,128)(2,1)}, bf16[320,2048]{1,0:T(8,128)(2,1)}, u32[]{:S(2)}, u32[]{:S(2)}) %collective-permute-start.34) | collective-permute-done | bytes 1310752 | tf_op jit(solution)/shard_map/ppermute | solution.py:531
  893.4 7.6 fusion.48
  901.0 6.8 fusion.23
  926.6 9.8 fusion.147
  936.3 22.5 %collective-permute-done.39 = bf16[320,576]{1,0:T(8,128)(2,1)} collective-permute-done((bf16[320,576]{1,0:T(8,128)(2,1)S(1)}, bf16[320,576]{1,0:T(8,128)(2,1)}, u32[]{:S(2)}, u32[]{:S(2)}) %collective-permute-start.39) | collective-permute-done | bytes 368672 | tf_op jit(solution)/shard_map/ppermute | solution.py:561
  972.9 7.8 convolution_convert_fusion.13
  983.9 7.1 convolution_convert_fusion.14
  1010.8 11.9 fusion.35
  1023.8 5.3 fusion.30
  1041.8 6.1 fusion.60
  1053.1 17.2 %collective-permute-done.46 = bf16[256,512]{1,0:T(8,128)(2,1)} collective-permute-done((bf16[256,512]{1,0:T(8,128)(2,1)}, bf16[256,512]{1,0:T(8,128)(2,1)}, u32[]{:S(2)}, u32[]{:S(2)}) %collective-permute-start.46) | collective-permute-done | bytes 262176 | tf_op jit(solution)/shard_map/ppermute | solution.py:561
  1073.9 5.5 all-to-all-done.15
  1092.8 23.2 %fusion.158 = f32[704,2048]{1,0:T(8,128)} fusion(bf16[4864,704]{1,0:T(8,128)(2,1)} %get-tuple-element.361, bf16[4864,2048]{1,0:T(8,128)(2,1)} %get-tuple-element.362), kind=kOutput, calls=%fused_computation.360 | convolution fusion | flops 14025752576 | bytes 32538624 | tf_op jit(solution)/shard_map/ra,rb->ab/dot_general | solution.py:1090
  1116.1 18.8 %fusion.159 = f32[2048,704]{0,1:T(8,128)} fusion(bf16[4864,2048]{1,0:T(8,128)(2,1)} %get-tuple-element.373, bf16[4864,704]{1,0:T(8,128)(2,1)S(1)} %bitcast.240), kind=kOutput, calls=%fused_computation.361 | convolution fusion | flops 14025752576 | bytes 32538624 | tf_op jit(solution)/shard_map/ra,rb->ab/dot_general | solution.py:1090
  1136.2 5.9 collective-permute-done.49
  1151.5 5.4 collective-permute-done.51
  1157.0 15.0 %collective-permute-done.52 = bf16[64,3072]{1,0:T(8,128)(2,1)S(1)} collective-permute-done((bf16[64,3072]{1,0:T(8,128)(2,1)S(1)}, bf16[64,3072]{1,0:T(8,128)(2,1)S(1)}, u32[]{:S(2)}, u32[]{:S(2)}) %collective-permute-start.52) | collective-permute-done | bytes 393248 | tf_op jit(solution)/shard_map/ppermute | solution.py:561
  1182.5 8.3 collective-permute-start.56
  1206.5 6.6 collective-permute-done.55
  1214.4 20.9 %convolution_bitcast_fusion.4 = f32[1,2048,704]{1,2,0:T(8,128)} fusion(bf16[4864,2048]{1,0:T(8,128)(2,1)} %get-tuple-element.373, bf16[4864,704]{1,0:T(8,128)(2,1)} %get-tuple-element.374), kind=kOutput, calls=%fused_computation.48 | convolution fusion | flops 14025752576 | bytes 32538624 | tf_op jit(solution)/shard_map/ra,rb->ab/dot_general | solution.py:1090
  1239.1 9.7 collective-permute-done.58
  (609 shorter events, 402.8 us)
Async XLA Ops:
  7.2 58.3 %all-gather.7.cloned.1.call-start = ((), (), s32[]{:S(2)}) async-start(), calls=%async_computation.20 | async-start | bytes 2764800 | tf_op jit(solution)/shard_map/all_gather | solution.py:552
  19.8 42.4 %all-to-all-start = ((bf16[4,152,2048]{2,1,0:T(8,128)(2,1)}), bf16[4,152,2048]{2,1,0:T(8,128)(2,1)}, u32[]{:S(2)}, u32[]{:S(2)}) async-start(bf16[4,152,2048]{2,1,0:T(8,128)(2,1)} %convolution_convert_fusion.12), calls=%async_computation | async-start | bytes 4980736 | tf_op jit(solution)/shard_map/all_to_all | solution.py:536
  25.1 139.4 %all-gather.9.cloned.1.call-start = ((), (), s32[]{:S(2)}) async-start(), calls=%async_computation.21 | async-start | bytes 14155776 | tf_op jit(solution)/shard_map/all_gather | solution.py:552
  68.9 60.9 %collective-permute-start.7 = (bf16[320,2048]{1,0:T(8,128)(2,1)}, bf16[320,2048]{1,0:T(8,128)(2,1)}, u32[]{:S(2)}, u32[]{:S(2)}) collective-permute-start(bf16[320,2048]{1,0:T(8,128)(2,1)} %collective-permute-done.3), channel_id=1, source_target_pairs={{0,8},{8,16},{16,24},{24,0},{1,9},{9,17},{17,25},{25,1},{2,10},{10... | collective-permute-start | bytes 3932168 | tf_op jit(solution)/shard_map/ppermute | solution.py:531
  70.5 59.4 %collective-permute-start.8 = (bf16[4,152,2048]{2,1,0:T(8,128)(2,1)}, bf16[4,152,2048]{2,1,0:T(8,128)(2,1)}, u32[]{:S(2)}, u32[]{:S(2)}) collective-permute-start(bf16[4,152,2048]{2,1,0:T(8,128)(2,1)} %all-to-all-done), channel_id=1, source_target_pairs={{0,1},{1,0},{2,3},{3,2},{4,5},{5,4},{6,7},{7,6},{8,9},{9,8},{10,11... | collective-permute-start | bytes 7471112 | tf_op jit(solution)/shard_map/ppermute | solution.py:548
  76.9 52.9 %all-to-all-start.1 = ((bf16[4,152,2048]{2,1,0:T(8,128)(2,1)}), bf16[4,152,2048]{2,1,0:T(8,128)(2,1)}, u32[]{:S(2)}, u32[]{:S(2)}) async-start(bf16[4,152,2048]{2,1,0:T(8,128)(2,1)} %convolution_convert_fusion.11), calls=%async_computation.1 | async-start | bytes 4980736 | tf_op jit(solution)/shard_map/all_to_all | solution.py:536
  81.6 140.4 %all-gather.11.cloned.1.call-start = ((), (), s32[]{:S(2)}) async-start(), calls=%async_computation.22 | async-start | bytes 4718592 | tf_op jit(solution)/shard_map/all_gather | solution.py:552
  88.1 40.3 %collective-permute-start.5 = (bf16[320,576]{1,0:T(8,128)(2,1)S(1)}, bf16[320,576]{1,0:T(8,128)(2,1)S(1)}, u32[]{:S(2)}, u32[]{:S(2)}) collective-permute-start(bf16[320,576]{1,0:T(8,128)(2,1)S(1)} %pad_maximum_fusion.7), channel_id=1, source_target_pairs={{0,16},{8,24},{16,0},{24,8},{1,17},{9,25},{17,1},{25,9},{2,18},{10... | collective-permute-start | bytes 1105928 | tf_op jit(solution)/shard_map/ppermute | solution.py:561
  89.6 38.8 %collective-permute-start.6 = (bf16[320,576]{1,0:T(8,128)(2,1)S(1)}, bf16[320,576]{1,0:T(8,128)(2,1)S(1)}, u32[]{:S(2)}, u32[]{:S(2)}) collective-permute-start(bf16[320,576]{1,0:T(8,128)(2,1)S(1)} %pad_maximum_fusion.7), channel_id=1, source_target_pairs={{0,24},{8,0},{16,8},{24,16},{1,25},{9,1},{17,9},{25,17},{2,26},{10... | collective-permute-start | bytes 1105928 | tf_op jit(solution)/shard_map/ppermute | solution.py:561
  164.5 45.5 %collective-permute-start.10 = (bf16[4,152,2048]{2,1,0:T(8,128)(2,1)}, bf16[4,152,2048]{2,1,0:T(8,128)(2,1)}, u32[]{:S(2)}, u32[]{:S(2)}) collective-permute-start(bf16[4,152,2048]{2,1,0:T(8,128)(2,1)} %all-to-all-done.1), channel_id=1, source_target_pairs={{0,1},{1,0},{2,3},{3,2},{4,5},{5,4},{6,7},{7,6},{8,9},{9,8},{10,11... | collective-permute-start | bytes 7471112 | tf_op jit(solution)/shard_map/ppermute | solution.py:548
  169.1 40.9 %all-to-all-start.2 = ((bf16[4,152,2048]{2,1,0:T(8,128)(2,1)}), bf16[4,152,2048]{2,1,0:T(8,128)(2,1)}, u32[]{:S(2)}, u32[]{:S(2)}) async-start(bf16[4,152,2048]{2,1,0:T(8,128)(2,1)} %convolution_convert_fusion.10), calls=%async_computation.2 | async-start | bytes 4980736 | tf_op jit(solution)/shard_map/all_to_all | solution.py:536
  173.8 127.6 %all-gather.13.cloned.1.call-start = ((), (), s32[]{:S(2)}) async-start(), calls=%async_computation.23 | async-start | bytes 9437184 | tf_op jit(solution)/shard_map/all_gather | solution.py:552
  238.1 61.3 %collective-permute-start.11 = (bf16[4,152,2048]{2,1,0:T(8,128)(2,1)}, bf16[4,152,2048]{2,1,0:T(8,128)(2,1)}, u32[]{:S(2)}, u32[]{:S(2)}) collective-permute-start(bf16[4,152,2048]{2,1,0:T(8,128)(2,1)} %all-to-all-done.2), channel_id=1, source_target_pairs={{0,1},{1,0},{2,3},{3,2},{4,5},{5,4},{6,7},{7,6},{8,9},{9,8},{10,11... | collective-permute-start | bytes 7471112 | tf_op jit(solution)/shard_map/ppermute | solution.py:548
  242.6 56.8 %all-to-all-start.3 = ((bf16[4,152,2048]{2,1,0:T(8,128)(2,1)}), bf16[4,152,2048]{2,1,0:T(8,128)(2,1)}, u32[]{:S(2)}, u32[]{:S(2)}) async-start(bf16[4,152,2048]{2,1,0:T(8,128)(2,1)} %convolution_convert_fusion.9), calls=%async_computation.3 | async-start | bytes 4980736 | tf_op jit(solution)/shard_map/all_to_all | solution.py:536
  247.2 125.6 %all-gather.15.cloned.1.call-start = ((), (), s32[]{:S(2)}) async-start(), calls=%async_computation.24 | async-start | bytes 3244032 | tf_op jit(solution)/shard_map/all_gather | solution.py:552
  311.5 50.2 %collective-permute-start.12 = (bf16[4,152,2048]{2,1,0:T(8,128)(2,1)}, bf16[4,152,2048]{2,1,0:T(8,128)(2,1)}, u32[]{:S(2)}, u32[]{:S(2)}) collective-permute-start(bf16[4,152,2048]{2,1,0:T(8,128)(2,1)} %all-to-all-done.3), channel_id=1, source_target_pairs={{0,1},{1,0},{2,3},{3,2},{4,5},{5,4},{6,7},{7,6},{8,9},{9,8},{10,11... | collective-permute-start | bytes 7471112 | tf_op jit(solution)/shard_map/ppermute | solution.py:548
  320.4 41.3 %all-to-all-start.4 = ((bf16[4,152,2176]{2,1,0:T(8,128)(2,1)}), bf16[4,152,2176]{2,1,0:T(8,128)(2,1)}, u32[]{:S(2)}, u32[]{:S(2)}) async-start(bf16[4,152,2176]{2,1,0:T(8,128)(2,1)} %convolution_convert_fusion.4), calls=%async_computation.4 | async-start | bytes 5292032 | tf_op jit(solution)/shard_map/all_to_all | solution.py:536
  325.0 188.5 %all-gather.17.cloned.1.call-start = ((), (), s32[]{:S(2)}) async-start(), calls=%async_computation.25 | async-start | bytes 6488064 | tf_op jit(solution)/shard_map/all_gather | solution.py:552
  325.0 34.9 %collective-permute-start.13 = (bf16[320,2176]{1,0:T(8,128)(2,1)}, bf16[320,2176]{1,0:T(8,128)(2,1)}, u32[]{:S(2)}, u32[]{:S(2)}) collective-permute-start(bf16[320,2176]{1,0:T(8,128)(2,1)} %concatenate.74), channel_id=1, source_target_pairs={{0,8},{8,16},{16,24},{24,0},{1,9},{9,17},{17,25},{25,1},{2,10},{10... | collective-permute-start | bytes 4177928 | tf_op jit(solution)/shard_map/ppermute | solution.py:531
  361.7 47.8 %collective-permute-start.15 = (bf16[4,152,2176]{2,1,0:T(8,128)(2,1)}, bf16[4,152,2176]{2,1,0:T(8,128)(2,1)}, u32[]{:S(2)}, u32[]{:S(2)}) collective-permute-start(bf16[4,152,2176]{2,1,0:T(8,128)(2,1)} %all-to-all-done.4), channel_id=1, source_target_pairs={{0,1},{1,0},{2,3},{3,2},{4,5},{5,4},{6,7},{7,6},{8,9},{9,8},{10,11... | collective-permute-start | bytes 7938056 | tf_op jit(solution)/shard_map/ppermute | solution.py:548
  366.2 43.3 %all-to-all-start.5 = ((bf16[4,152,2176]{2,1,0:T(8,128)(2,1)}), bf16[4,152,2176]{2,1,0:T(8,128)(2,1)}, u32[]{:S(2)}, u32[]{:S(2)}) async-start(bf16[4,152,2176]{2,1,0:T(8,128)(2,1)} %convolution_convert_fusion.3), calls=%async_computation.5 | async-start | bytes 5292032 | tf_op jit(solution)/shard_map/all_to_all | solution.py:536
  370.9 35.5 %collective-permute-start.14 = (bf16[320,2176]{1,0:T(8,128)(2,1)}, bf16[320,2176]{1,0:T(8,128)(2,1)}, u32[]{:S(2)}, u32[]{:S(2)}) collective-permute-start(bf16[320,2176]{1,0:T(8,128)(2,1)} %collective-permute-done.13), channel_id=1, source_target_pairs={{0,8},{8,16},{16,24},{24,0},{1,9},{9,17},{17,25},{25,1},{2,10},{10... | collective-permute-start | bytes 4177928 | tf_op jit(solution)/shard_map/ppermute | solution.py:531
  409.5 46.1 %collective-permute-start.17 = (bf16[4,152,2176]{2,1,0:T(8,128)(2,1)}, bf16[4,152,2176]{2,1,0:T(8,128)(2,1)}, u32[]{:S(2)}, u32[]{:S(2)}) collective-permute-start(bf16[4,152,2176]{2,1,0:T(8,128)(2,1)} %all-to-all-done.5), channel_id=1, source_target_pairs={{0,1},{1,0},{2,3},{3,2},{4,5},{5,4},{6,7},{7,6},{8,9},{9,8},{10,11... | collective-permute-start | bytes 7938056 | tf_op jit(solution)/shard_map/ppermute | solution.py:548
  413.9 41.7 %all-to-all-start.6 = ((bf16[4,152,2176]{2,1,0:T(8,128)(2,1)}), bf16[4,152,2176]{2,1,0:T(8,128)(2,1)}, u32[]{:S(2)}, u32[]{:S(2)}) async-start(bf16[4,152,2176]{2,1,0:T(8,128)(2,1)} %convolution_convert_fusion.2), calls=%async_computation.6 | async-start | bytes 5292032 | tf_op jit(solution)/shard_map/all_to_all | solution.py:536
  418.5 37.1 %collective-permute-start.16 = (bf16[320,2176]{1,0:T(8,128)(2,1)}, bf16[320,2176]{1,0:T(8,128)(2,1)}, u32[]{:S(2)}, u32[]{:S(2)}) collective-permute-start(bf16[320,2176]{1,0:T(8,128)(2,1)} %collective-permute-done.14), channel_id=1, source_target_pairs={{0,8},{8,16},{16,24},{24,0},{1,9},{9,17},{17,25},{25,1},{2,10},{10... | collective-permute-start | bytes 4177928 | tf_op jit(solution)/shard_map/ppermute | solution.py:531
  455.6 54.0 %collective-permute-start.18 = (bf16[4,152,2176]{2,1,0:T(8,128)(2,1)}, bf16[4,152,2176]{2,1,0:T(8,128)(2,1)}, u32[]{:S(2)}, u32[]{:S(2)}) collective-permute-start(bf16[4,152,2176]{2,1,0:T(8,128)(2,1)} %bitcast.311), channel_id=1, source_target_pairs={{0,1},{1,0},{2,3},{3,2},{4,5},{5,4},{6,7},{7,6},{8,9},{9,8},{10,11... | collective-permute-start | bytes 7938056 | tf_op jit(solution)/shard_map/ppermute | solution.py:548
  455.9 57.5 %collective-permute-start.19 = (bf16[320,2048]{1,0:T(8,128)(2,1)S(1)}, bf16[320,2048]{1,0:T(8,128)(2,1)}, u32[]{:S(2)}, u32[]{:S(2)}) collective-permute-start(bf16[320,2048]{1,0:T(8,128)(2,1)S(1)} %get-tuple-element.219), channel_id=1, source_target_pairs={{0,8},{8,16},{16,24},{24,0},{1,9},{9,17},{17,25},{25,1},{2,10},{10... | collective-permute-start | bytes 3932168 | tf_op jit(solution)/shard_map/ppermute | solution.py:531
  466.8 46.6 %all-to-all-start.7 = ((bf16[4,152,2176]{2,1,0:T(8,128)(2,1)}), bf16[4,152,2176]{2,1,0:T(8,128)(2,1)}, u32[]{:S(2)}, u32[]{:S(2)}) async-start(bf16[4,152,2176]{2,1,0:T(8,128)(2,1)} %convolution_convert_fusion.1), calls=%async_computation.7 | async-start | bytes 5292032 | tf_op jit(solution)/shard_map/all_to_all | solution.py:536
  471.6 41.9 %collective-permute-start.20 = (bf16[4,152,2176]{2,1,0:T(8,128)(2,1)}, bf16[4,152,2176]{2,1,0:T(8,128)(2,1)}, u32[]{:S(2)}, u32[]{:S(2)}) collective-permute-start(bf16[4,152,2176]{2,1,0:T(8,128)(2,1)} %all-to-all-done.6), channel_id=1, source_target_pairs={{0,1},{1,0},{2,3},{3,2},{4,5},{5,4},{6,7},{7,6},{8,9},{9,8},{10,11... | collective-permute-start | bytes 7938056 | tf_op jit(solution)/shard_map/ppermute | solution.py:548
  513.5 47.9 %collective-permute-start.21 = (bf16[4,152,2176]{2,1,0:T(8,128)(2,1)}, bf16[4,152,2176]{2,1,0:T(8,128)(2,1)}, u32[]{:S(2)}, u32[]{:S(2)}) collective-permute-start(bf16[4,152,2176]{2,1,0:T(8,128)(2,1)} %bitcast.309), channel_id=1, source_target_pairs={{0,1},{1,0},{2,3},{3,2},{4,5},{5,4},{6,7},{7,6},{8,9},{9,8},{10,11... | collective-permute-start | bytes 7938056 | tf_op jit(solution)/shard_map/ppermute | solution.py:548
  519.2 46.2 %collective-permute-start.22 = (bf16[320,2048]{1,0:T(8,128)(2,1)}, bf16[320,2048]{1,0:T(8,128)(2,1)}, u32[]{:S(2)}, u32[]{:S(2)}) collective-permute-start(bf16[320,2048]{1,0:T(8,128)(2,1)} %collective-permute-done.19), channel_id=1, source_target_pairs={{0,8},{8,16},{16,24},{24,0},{1,9},{9,17},{17,25},{25,1},{2,10},{10... | collective-permute-start | bytes 3932168 | tf_op jit(solution)/shard_map/ppermute | solution.py:531
  520.7 44.7 %all-to-all-start.8 = ((bf16[4,152,2176]{2,1,0:T(8,128)(2,1)}), bf16[4,152,2176]{2,1,0:T(8,128)(2,1)}, u32[]{:S(2)}, u32[]{:S(2)}) async-start(bf16[4,152,2176]{2,1,0:T(8,128)(2,1)} %add_convert_fusion.3), calls=%async_computation.8 | async-start | bytes 5292032 | tf_op jit(solution)/shard_map/all_to_all | solution.py:536
  525.5 40.0 %collective-permute-start.23 = (bf16[4,152,2176]{2,1,0:T(8,128)(2,1)}, bf16[4,152,2176]{2,1,0:T(8,128)(2,1)}, u32[]{:S(2)}, u32[]{:S(2)}) collective-permute-start(bf16[4,152,2176]{2,1,0:T(8,128)(2,1)} %all-to-all-done.7), channel_id=1, source_target_pairs={{0,1},{1,0},{2,3},{3,2},{4,5},{5,4},{6,7},{7,6},{8,9},{9,8},{10,11... | collective-permute-start | bytes 7938056 | tf_op jit(solution)/shard_map/ppermute | solution.py:548
  525.6 136.1 %collective-permute-start.29 = (bf16[4,152,2048]{2,1,0:T(8,128)(2,1)}, bf16[4,152,2048]{2,1,0:T(8,128)(2,1)}, u32[]{:S(2)}, u32[]{:S(2)}) collective-permute-start(bf16[4,152,2048]{2,1,0:T(8,128)(2,1)} %bitcast.312), channel_id=1, source_target_pairs={{0,1},{1,0},{2,3},{3,2},{4,5},{5,4},{6,7},{7,6},{8,9},{9,8},{10,11... | collective-permute-start | bytes 7471112 | tf_op jit(solution)/shard_map/ppermute | solution.py:548
  582.3 60.7 %collective-permute-start.24 = (bf16[4,152,2176]{2,1,0:T(8,128)(2,1)}, bf16[4,152,2176]{2,1,0:T(8,128)(2,1)}, u32[]{:S(2)}, u32[]{:S(2)}) collective-permute-start(bf16[4,152,2176]{2,1,0:T(8,128)(2,1)} %bitcast.52), channel_id=1, source_target_pairs={{0,1},{1,0},{2,3},{3,2},{4,5},{5,4},{6,7},{7,6},{8,9},{9,8},{10,11... | collective-permute-start | bytes 7938056 | tf_op jit(solution)/shard_map/ppermute | solution.py:548
  582.4 64.5 %collective-permute-start.25 = (bf16[320,2048]{1,0:T(8,128)(2,1)}, bf16[320,2048]{1,0:T(8,128)(2,1)S(1)}, u32[]{:S(2)}, u32[]{:S(2)}) collective-permute-start(bf16[320,2048]{1,0:T(8,128)(2,1)} %collective-permute-done.22), channel_id=1, source_target_pairs={{0,8},{8,16},{16,24},{24,0},{1,9},{9,17},{17,25},{25,1},{2,10},{10... | collective-permute-start | bytes 3932168 | tf_op jit(solution)/shard_map/ppermute | solution.py:531
  582.9 64.0 %all-to-all-start.9 = ((bf16[4,152,2176]{2,1,0:T(8,128)(2,1)}), bf16[4,152,2176]{2,1,0:T(8,128)(2,1)}, u32[]{:S(2)}, u32[]{:S(2)}) async-start(bf16[4,152,2176]{2,1,0:T(8,128)(2,1)} %add_convert_fusion.2), calls=%async_computation.9 | async-start | bytes 5292032 | tf_op jit(solution)/shard_map/all_to_all | solution.py:536
  650.9 43.6 %all-to-all-start.10 = ((bf16[4,152,2176]{2,1,0:T(8,128)(2,1)}), bf16[4,152,2176]{2,1,0:T(8,128)(2,1)}, u32[]{:S(2)}, u32[]{:S(2)}) async-start(bf16[4,152,2176]{2,1,0:T(8,128)(2,1)} %add_convert_fusion.1), calls=%async_computation.10 | async-start | bytes 5292032 | tf_op jit(solution)/shard_map/all_to_all | solution.py:536
  665.7 86.5 %collective-permute-start.31 = (bf16[4,152,2048]{2,1,0:T(8,128)(2,1)}, bf16[4,152,2048]{2,1,0:T(8,128)(2,1)}, u32[]{:S(2)}, u32[]{:S(2)}) collective-permute-start(bf16[4,152,2048]{2,1,0:T(8,128)(2,1)} %bitcast.54), channel_id=1, source_target_pairs={{0,1},{1,0},{2,3},{3,2},{4,5},{5,4},{6,7},{7,6},{8,9},{9,8},{10,11... | collective-permute-start | bytes 7471112 | tf_op jit(solution)/shard_map/ppermute | solution.py:548
  705.3 35.6 %all-to-all-start.11 = ((bf16[4,152,2176]{2,1,0:T(8,128)(2,1)}), bf16[4,152,2176]{2,1,0:T(8,128)(2,1)}, u32[]{:S(2)}, u32[]{:S(2)}) async-start(bf16[4,152,2176]{2,1,0:T(8,128)(2,1)} %add_convert_fusion), calls=%async_computation.11 | async-start | bytes 5292032 | tf_op jit(solution)/shard_map/all_to_all | solution.py:536
  740.9 43.8 %all-to-all-start.12 = ((bf16[4,152,2048]{2,1,0:T(8,128)(2,1)}), bf16[4,152,2048]{2,1,0:T(8,128)(2,1)}, u32[]{:S(2)}, u32[]{:S(2)}) async-start(bf16[4,152,2048]{2,1,0:T(8,128)(2,1)} %add_convert_fusion.7), calls=%async_computation.12 | async-start | bytes 4980736 | tf_op jit(solution)/shard_map/all_to_all | solution.py:536
  745.4 147.6 %reduce-scatter.5.cloned.1.call-start = ((), (), s32[]{:S(2)}) async-start(), calls=%async_computation.26 | async-start | bytes 9732096 | tf_op jit(solution)/shard_map/reduce_scatter | solution.py:556
  790.1 63.3 %all-to-all-start.13 = ((bf16[4,152,2048]{2,1,0:T(8,128)(2,1)}), bf16[4,152,2048]{2,1,0:T(8,128)(2,1)}, u32[]{:S(2)}, u32[]{:S(2)}) async-start(bf16[4,152,2048]{2,1,0:T(8,128)(2,1)} %add_convert_fusion.6), calls=%async_computation.13 | async-start | bytes 4980736 | tf_op jit(solution)/shard_map/all_to_all | solution.py:536
  794.9 166.5 %reduce-scatter.7.cloned.1.call-start = ((), (), s32[]{:S(2)}) async-start(), calls=%async_computation.27 | async-start | bytes 2359296 | tf_op jit(solution)/shard_map/reduce_scatter | solution.py:556
  800.8 51.6 %collective-permute-start.33 = (bf16[320,2048]{1,0:T(8,128)(2,1)}, bf16[320,2048]{1,0:T(8,128)(2,1)}, u32[]{:S(2)}, u32[]{:S(2)}) collective-permute-start(bf16[320,2048]{1,0:T(8,128)(2,1)} %fusion.31), channel_id=1, source_target_pairs={{0,8},{8,16},{16,24},{24,0},{1,9},{9,17},{17,25},{25,1},{2,10},{10... | collective-permute-start | bytes 3932168 | tf_op jit(solution)/shard_map/ppermute | solution.py:531
  812.6 58.5 %collective-permute-start.32 = (bf16[4,152,2048]{2,1,0:T(8,128)(2,1)}, bf16[4,152,2048]{2,1,0:T(8,128)(2,1)}, u32[]{:S(2)}, u32[]{:S(2)}) collective-permute-start(bf16[4,152,2048]{2,1,0:T(8,128)(2,1)} %bitcast.62), channel_id=1, source_target_pairs={{0,1},{1,0},{2,3},{3,2},{4,5},{5,4},{6,7},{7,6},{8,9},{9,8},{10,11... | collective-permute-start | bytes 7471112 | tf_op jit(solution)/shard_map/ppermute | solution.py:548
  817.5 41.3 %collective-permute-start.37 = (bf16[320,512]{1,0:T(8,128)(2,1)}, bf16[320,512]{1,0:T(8,128)(2,1)}, u32[]{:S(2)}, u32[]{:S(2)}) collective-permute-start(bf16[320,512]{1,0:T(8,128)(2,1)} %get-tuple-element.498), channel_id=1, source_target_pairs={{0,24},{8,0},{16,8},{24,16},{1,25},{9,1},{17,9},{25,17},{2,26},{10... | collective-permute-start | bytes 983048 | tf_op jit(solution)/shard_map/ppermute | solution.py:561
  821.2 40.4 %collective-permute-start.36 = (bf16[320,512]{1,0:T(8,128)(2,1)}, bf16[320,512]{1,0:T(8,128)(2,1)}, u32[]{:S(2)}, u32[]{:S(2)}) collective-permute-start(bf16[320,512]{1,0:T(8,128)(2,1)} %get-tuple-element.499), channel_id=1, source_target_pairs={{0,16},{8,24},{16,0},{24,8},{1,17},{9,25},{17,1},{25,9},{2,18},{10... | collective-permute-start | bytes 983048 | tf_op jit(solution)/shard_map/ppermute | solution.py:561
  821.2 55.0 %collective-permute-start.41 = (bf16[4,152,2048]{2,1,0:T(8,128)(2,1)}, bf16[4,152,2048]{2,1,0:T(8,128)(2,1)}, u32[]{:S(2)}, u32[]{:S(2)}) collective-permute-start(bf16[4,152,2048]{2,1,0:T(8,128)(2,1)} %bitcast.34), channel_id=1, source_target_pairs={{0,1},{1,0},{2,3},{3,2},{4,5},{5,4},{6,7},{7,6},{8,9},{9,8},{10,11... | collective-permute-start | bytes 7471112 | tf_op jit(solution)/shard_map/ppermute | solution.py:548
  915.0 46.4 %all-to-all-start.14 = ((bf16[4,152,2048]{2,1,0:T(8,128)(2,1)}), bf16[4,152,2048]{2,1,0:T(8,128)(2,1)}, u32[]{:S(2)}, u32[]{:S(2)}) async-start(bf16[4,152,2048]{2,1,0:T(8,128)(2,1)} %add_convert_fusion.5), calls=%async_computation.16 | async-start | bytes 4980736 | tf_op jit(solution)/shard_map/all_to_all | solution.py:536
  919.5 161.3 %reduce-scatter.9.cloned.1.call-start = ((), (), s32[]{:S(2)}) async-start(), calls=%async_computation.28 | async-start | bytes 14155776 | tf_op jit(solution)/shard_map/reduce_scatter | solution.py:556
  922.5 36.3 %collective-permute-start.39 = (bf16[320,576]{1,0:T(8,128)(2,1)S(1)}, bf16[320,576]{1,0:T(8,128)(2,1)}, u32[]{:S(2)}, u32[]{:S(2)}) collective-permute-start(bf16[320,576]{1,0:T(8,128)(2,1)S(1)} %get-tuple-element.489), channel_id=1, source_target_pairs={{0,16},{8,24},{16,0},{24,8},{1,17},{9,25},{17,1},{25,9},{2,18},{10... | collective-permute-start | bytes 1105928 | tf_op jit(solution)/shard_map/ppermute | solution.py:561
  923.0 35.8 %collective-permute-start.38 = (bf16[320,576]{1,0:T(8,128)(2,1)S(1)}, bf16[320,576]{1,0:T(8,128)(2,1)}, u32[]{:S(2)}, u32[]{:S(2)}) collective-permute-start(bf16[320,576]{1,0:T(8,128)(2,1)S(1)} %get-tuple-element.487), channel_id=1, source_target_pairs={{0,8},{8,16},{16,24},{24,0},{1,9},{9,17},{17,25},{25,1},{2,10},{10... | collective-permute-start | bytes 1105928 | tf_op jit(solution)/shard_map/ppermute | solution.py:561
  999.3 74.6 %collective-permute-start.43 = (bf16[256,2112]{0,1:T(8,128)(2,1)}, bf16[256,2112]{0,1:T(8,128)(2,1)}, u32[]{:S(2)}, u32[]{:S(2)}) collective-permute-start(bf16[256,2112]{0,1:T(8,128)(2,1)} %collective-permute-done.42), channel_id=1, source_target_pairs={{0,8},{8,16},{16,24},{24,0},{1,9},{9,17},{17,25},{25,1},{2,10},{10... | collective-permute-start | bytes 3244040 | tf_op jit(solution)/shard_map/ppermute | solution.py:531
  999.3 52.0 %collective-permute-start.45 = (bf16[256,512]{1,0:T(8,128)(2,1)}, bf16[256,512]{1,0:T(8,128)(2,1)}, u32[]{:S(2)}, u32[]{:S(2)}) collective-permute-start(bf16[256,512]{1,0:T(8,128)(2,1)} %reduce-scatter.7.cloned.1.call-done), channel_id=1, source_target_pairs={{0,8},{8,16},{16,24},{24,0},{1,9},{9,17},{17,25},{25,1},{2,10},{10... | collective-permute-start | bytes 786440 | tf_op jit(solution)/shard_map/ppermute | solution.py:561
  1001.7 68.6 %collective-permute-start.46 = (bf16[256,512]{1,0:T(8,128)(2,1)}, bf16[256,512]{1,0:T(8,128)(2,1)}, u32[]{:S(2)}, u32[]{:S(2)}) collective-permute-start(bf16[256,512]{1,0:T(8,128)(2,1)} %reduce-scatter.7.cloned.1.call-done), channel_id=1, source_target_pairs={{0,16},{8,24},{16,0},{24,8},{1,17},{9,25},{17,1},{25,9},{2,18},{10... | collective-permute-start | bytes 786440 | tf_op jit(solution)/shard_map/ppermute | solution.py:561
  1003.7 68.4 %collective-permute-start.47 = (bf16[256,512]{1,0:T(8,128)(2,1)}, bf16[256,512]{1,0:T(8,128)(2,1)}, u32[]{:S(2)}, u32[]{:S(2)}) collective-permute-start(bf16[256,512]{1,0:T(8,128)(2,1)} %reduce-scatter.7.cloned.1.call-done), channel_id=1, source_target_pairs={{0,24},{8,0},{16,8},{24,16},{1,25},{9,1},{17,9},{25,17},{2,26},{10... | collective-permute-start | bytes 786440 | tf_op jit(solution)/shard_map/ppermute | solution.py:561
  1029.0 44.9 %collective-permute-start.44 = (bf16[320,2048]{1,0:T(8,128)(2,1)}, bf16[320,2048]{1,0:T(8,128)(2,1)}, u32[]{:S(2)}, u32[]{:S(2)}) collective-permute-start(bf16[320,2048]{1,0:T(8,128)(2,1)} %fusion.30), channel_id=1, source_target_pairs={{0,8},{8,16},{16,24},{24,0},{1,9},{9,17},{17,25},{25,1},{2,10},{10... | collective-permute-start | bytes 3932168 | tf_op jit(solution)/shard_map/ppermute | solution.py:531
  1030.4 49.0 %all-to-all-start.15 = ((bf16[4,152,2048]{2,1,0:T(8,128)(2,1)}), bf16[4,152,2048]{2,1,0:T(8,128)(2,1)}, u32[]{:S(2)}, u32[]{:S(2)}) async-start(bf16[4,152,2048]{2,1,0:T(8,128)(2,1)} %add_convert_fusion.4), calls=%async_computation.18 | async-start | bytes 4980736 | tf_op jit(solution)/shard_map/all_to_all | solution.py:536
  1035.0 146.4 %reduce-scatter.11.cloned.1.call-start = ((), (), s32[]{:S(2)}) async-start(), calls=%async_computation.29 | async-start | bytes 8257536 | tf_op jit(solution)/shard_map/reduce_scatter | solution.py:556
  1082.3 53.9 %collective-permute-start.50 = (bf16[64,3072]{1,0:T(8,128)(2,1)S(1)}, bf16[64,3072]{1,0:T(8,128)(2,1)S(1)}, u32[]{:S(2)}, u32[]{:S(2)}) collective-permute-start(bf16[64,3072]{1,0:T(8,128)(2,1)S(1)} %get-tuple-element.493), channel_id=1, source_target_pairs={{0,24},{8,0},{16,8},{24,16},{1,25},{9,1},{17,9},{25,17},{2,26},{10... | collective-permute-start | bytes 1179656 | tf_op jit(solution)/shard_map/ppermute | solution.py:561
  1085.9 56.2 %collective-permute-start.49 = (bf16[64,3072]{1,0:T(8,128)(2,1)S(1)}, bf16[64,3072]{1,0:T(8,128)(2,1)S(1)}, u32[]{:S(2)}, u32[]{:S(2)}) collective-permute-start(bf16[64,3072]{1,0:T(8,128)(2,1)S(1)} %get-tuple-element.494), channel_id=1, source_target_pairs={{0,16},{8,24},{16,0},{24,8},{1,17},{9,25},{17,1},{25,9},{2,18},{10... | collective-permute-start | bytes 1179656 | tf_op jit(solution)/shard_map/ppermute | solution.py:561
  1085.9 56.2 %collective-permute-start.48 = (bf16[64,3072]{1,0:T(8,128)(2,1)S(1)}, bf16[64,3072]{1,0:T(8,128)(2,1)S(1)}, u32[]{:S(2)}, u32[]{:S(2)}) collective-permute-start(bf16[64,3072]{1,0:T(8,128)(2,1)S(1)} %get-tuple-element.492), channel_id=1, source_target_pairs={{0,8},{8,16},{16,24},{24,0},{1,9},{9,17},{17,25},{25,1},{2,10},{10... | collective-permute-start | bytes 1179656 | tf_op jit(solution)/shard_map/ppermute | solution.py:561
  1086.5 85.5 %collective-permute-start.60 = (bf16[256,2112]{0,1:T(8,128)(2,1)}, bf16[256,2112]{0,1:T(8,128)(2,1)S(1)}, u32[]{:S(2)}, u32[]{:S(2)}) collective-permute-start(bf16[256,2112]{0,1:T(8,128)(2,1)} %collective-permute-done.43), channel_id=1, source_target_pairs={{0,8},{8,16},{16,24},{24,0},{1,9},{9,17},{17,25},{25,1},{2,10},{10... | collective-permute-start | bytes 3244040 | tf_op jit(solution)/shard_map/ppermute | solution.py:531
  (151 other events, 3007.5 us)
Sparse Core Ops, SparseCore 0:
  13.9 51.5 all-gather.6
  67.4 97.0 all-gather.8
  166.4 55.5 all-gather.10
  223.8 77.4 all-gather.12
  303.6 50.6 all-gather.14
  361.9 81.5 all-gather.16
  784.8 80.8 reduce-scatter.4
  901.1 57.0 reduce-scatter.6
  961.7 119.0 reduce-scatter.8
  1084.1 67.1 reduce-scatter.10

commit v6 on v5

--- a/solution.py
+++ b/solution.py
@@ -999,6 +999,7 @@
             sent["attended"] = ring_next(attended_ring[-1])
         if tick == ctx_size + 4:
             sent["out"] = add_halves(*out_sends[2])
+            sent["out_third"] = add_halves(*out_sends[3])
         names = sorted(sent)
         sent = dict(zip(names, together(*(sent[name] for name in names))))
         if "mine" in sent:
@@ -1026,6 +1027,8 @@
             attended_ring.append(sent["attended"])
         if "out" in sent:
             out_added[tick - ctx_size - 2] = sent["out"]
+        if "out_third" in sent:
+            out_added[3] = sent["out_third"]
         if "out_step" in sent:
             out_steps[1] = sent["out_step"]
         moving = sent.get("moving", moving)
@@ -1091,7 +1094,8 @@
 
     grad_w_output = weight_grad(jnp.concatenate(attended_ring), jnp.concatenate(att_shares))
 
-    out_added[3] = add_halves(*out_sends[3])
+    out_steps[3] = to_chips(out_added[3])
+    out_added[4 % ctx_size] = add_halves(*out_sends[4 % ctx_size])
 
     log_rows = log_total[:, :HEADS].T.reshape(HEADS // 2, 2, tokens)
     grad_nope, grad_rope, grad_key_part, grad_value_part, rope_pair_grad = attend_back(
@@ -1115,7 +1119,8 @@
         grad_value_part,
         rope_pair_grad,
         out_steps[2],
-        out_added[3],
+        out_steps[3],
+        out_added[4 % ctx_size],
         out_moving,
         shared_part,
         grad_w_output,
@@ -1126,12 +1131,13 @@
         grad_value_part,
         rope_pair_grad,
         out_steps[2],
-        out_added[3],
+        out_steps[3],
+        out_added[4 % ctx_size],
         out_moving,
         shared_part,
         grad_w_output,
     )
-    out_next = next_out(3)
+    out_next = next_out(4 % ctx_size)
     output_part = scatter_rows(grad_w_output)
     grad_key_rope = rope_pair_grad[:, :ROPE] + rope_pair_grad[:, ROPE:]
     keys_width = HEADS * NOPE
@@ -1148,12 +1154,13 @@
     grad_keys_own, output_part, grad_w_query, out_next, out_moving = together(
         grad_keys_own, output_part, grad_w_query, out_next, out_moving
     )
-    out_steps[3], out_added[4 % ctx_size] = out_next
+    out_steps[4 % ctx_size], out_added[5] = out_next
     for step in range(3, ctx_size):
-        if step > 3:
+        if step > 4:
             out_steps[step], out_added[(step + 1) % ctx_size] = next_out(step)
         out_moving = out_hop(step, out_moving)
-    out_steps[0] = to_chips(out_added[0])
+    if ctx_size > 4:
+        out_steps[0] = to_chips(out_added[0])
     query_part = scatter_rows(grad_w_query)
     shared_ring = [shared_part, ring_next(shared_part)]
     shared_ring.append(ring_next(shared_ring[-1]))

time: 1270 us -> 1280 us (level)
  starting transfers between devices: 151 us -> 171 us
  waiting for transfers between devices: 370 us -> 354 us
    ppermute x27, waiting for transfers between devices: 149 us -> 135 us  [along_ctx(): lax.ppermute(value, 'ctx', [(i, (i + shift) % size) for i in range(size)])]
  transfers between devices with their start and end apart: 87 -> 87, of which waited for: 32 -> 28; matrix products, arithmetic and copies ran while one was open for 39% -> 39% of each run, Pallas kernels for 16% -> 16%
where the time goes in v6:
time: 1280 us; the launch traced here: 1270 us
  waiting for transfers between devices  354 us (28%)
  matrix products  311 us (24%)
  Pallas kernels  199 us (16%)
  starting transfers between devices  171 us (13%)
  local copies, waits for them, and re-layouts  110 us (9%)
  other arithmetic  107 us (8%)
  between operations  17.2 us (1%)
    pallas_call x4, Pallas kernels, expert_call(): pl.pallas_call(functools.partial(expert_kernel, step * 2 * count, experts...  142 us
    ppermute x27, waiting for transfers between devices, along_ctx(): lax.ppermute(value, 'ctx', [(i, (i + shift) % size) for i in range(size)])  135 us
    ppermute x18, waiting for transfers between devices, ring_next(): lax.ppermute(value, 'ctx', [(i, (i + 1) % size) for i in range(size)])  134 us
    dot_general x7, matrix products, weight_grad(): return jnp.einsum('ra,rb->ab', left, right, preferred_element_type=single)  93.2 us
    all_to_all x16, starting transfers between devices, to_chips(): lax.all_to_all(value, 'fsdp', split_axis=0, concat_axis=0, tiled=True, ax...  75.5 us
    dot_general x15, matrix products, matmul(): return jnp.dot(left, right, preferred_element_type=single)  65.1 us
    ppermute x27, starting transfers between devices, along_ctx(): lax.ppermute(value, 'ctx', [(i, (i + shift) % size) for i in range(size)])  58.6 us
    all_gather x6, waiting for transfers between devices, gather_rows(): return lax.all_gather(value, 'fsdp', axis=0, tiled=True)  51.9 us
  transfers between devices with their start and end apart: 87, of which 28 were waited for; matrix products, arithmetic and copies ran while one was open for 39% of the time, Pallas kernels for 16%

profile of v6, /device:TPU:0, one launch (start us, length us, event | category | flops | bytes accessed | tf_op | source)
XLA Modules:
  0.0 1267.7 jit_solution(17985993702857807950)
XLA Ops:
  19.8 5.3 all-to-all-start
  33.1 26.0 %collective-permute-done = s32[320,6]{0,1:T(8,128)S(1)} collective-permute-done((s32[320,6]{0,1:T(8,128)S(1)}, s32[320,6]{0,1:T(8,128)S(1)}, u32[]{:S(2)}, u32[]{:S(2)}) %collective-permute-start) | collective-permute-done | bytes 7712 | tf_op jit(solution)/shard_map/ppermute | solution.py:561
  91.9 19.6 %collective-permute-done.4 = bf16[320,576]{1,0:T(8,128)(2,1)S(1)} collective-permute-done((bf16[320,576]{1,0:T(8,128)(2,1)S(1)}, bf16[320,576]{1,0:T(8,128)(2,1)S(1)}, u32[]{:S(2)}, u32[]{:S(2)}) %collective-permute-start.4) | collective-permute-done | bytes 368672 | tf_op jit(solution)/shard_map/ppermute | solution.py:561
  111.5 16.9 %collective-permute-done.5 = bf16[320,576]{1,0:T(8,128)(2,1)S(1)} collective-permute-done((bf16[320,576]{1,0:T(8,128)(2,1)S(1)}, bf16[320,576]{1,0:T(8,128)(2,1)S(1)}, u32[]{:S(2)}, u32[]{:S(2)}) %collective-permute-start.5) | collective-permute-done | bytes 368672 | tf_op jit(solution)/shard_map/ppermute | solution.py:561
  129.9 34.7 %all-gather.9.cloned.1.call-done = bf16[2048,3072]{1,0:T(8,128)(2,1)} async-done(((bf16[256,3072]{1,0:T(8,128)(2,1)}), bf16[2048,3072]{1,0:T(8,128)(2,1)}) %all-gather.9.cloned.1.call-update) | async-done | bytes 12582928 | tf_op jit(solution)/shard_map/all_gather | solution.py:552
  175.6 9.3 fusion.149.nope.rope
  184.9 22.3 %collective-permute-done.9 = bf16[320,2048]{1,0:T(8,128)(2,1)} collective-permute-done((bf16[320,2048]{1,0:T(8,128)(2,1)}, bf16[320,2048]{1,0:T(8,128)(2,1)}, u32[]{:S(2)}, u32[]{:S(2)}) %collective-permute-start.9) | collective-permute-done | bytes 1310752 | tf_op jit(solution)/shard_map/ppermute | solution.py:531
  210.1 12.0 all-gather.11.cloned.1.call-done
  247.5 10.7 convolution_convert_fusion.keys.values
  258.2 26.6 %shard_map.306 = (bf16[320,2048]{1,0:T(8,128)(2,1)S(1)}, f32[320,128]{1,0:T(8,128)S(1)}) custom-call(s32[1]{0:T(128)} %bitcast.11.link, f32[320,3072]{1,0:T(8,128)S(1)} %copy-done.2, f32[320,3072]{1,0:T(8,128)S(1)} %copy-done.2, f32[320,128]{1,0:T(8,128)S(1)} %get-tuple-element.523.cos, f32[320,128]{1,0:T(8,128)S(1)} %get-tuple-element.524.sin, ...), custom_call_target="tpu_custom_call" | custom-call | flops 2214592512 | bytes 16384000 | tf_op jit(solution)/shard_map/pallas_call | solution.py:312
  284.8 5.5 pad_maximum_fusion.1
  290.3 9.2 all-to-all-done.3
  301.4 6.7 multiply_reduce_fusion.2
  326.7 33.3 %collective-permute-done.13 = bf16[320,2176]{1,0:T(8,128)(2,1)} collective-permute-done((bf16[320,2176]{1,0:T(8,128)(2,1)}, bf16[320,2176]{1,0:T(8,128)(2,1)}, u32[]{:S(2)}, u32[]{:S(2)}) %collective-permute-start.13) | collective-permute-done | bytes 1392672 | tf_op jit(solution)/shard_map/ppermute | solution.py:531
  370.9 13.9 %collective-permute-start.14 = (bf16[320,2176]{1,0:T(8,128)(2,1)}, bf16[320,2176]{1,0:T(8,128)(2,1)}, u32[]{:S(2)}, u32[]{:S(2)}) collective-permute-start(bf16[320,2176]{1,0:T(8,128)(2,1)} %collective-permute-done.13), channel_id=1, source_target_pairs={{0,8},{8,16},{16,24},{24,0},{1,9},{9,17},{17,25},{25,1},{2,10},{10... | collective-permute-start | bytes 4177928 | tf_op jit(solution)/shard_map/ppermute | solution.py:531
  384.7 9.1 fusion.157
  393.8 24.5 %collective-permute-done.14 = bf16[320,2176]{1,0:T(8,128)(2,1)} collective-permute-done((bf16[320,2176]{1,0:T(8,128)(2,1)}, bf16[320,2176]{1,0:T(8,128)(2,1)}, u32[]{:S(2)}, u32[]{:S(2)}) %collective-permute-start.14) | collective-permute-done | bytes 1392672 | tf_op jit(solution)/shard_map/ppermute | solution.py:531
  427.6 35.5 %shard_map.307 = (bf16[608,2176]{1,0:T(8,128)(2,1)}, bf16[608,2176]{1,0:T(8,128)(2,1)}, bf16[608,2048]{1,0:T(8,128)(2,1)}, bf16[608,2048]{1,0:T(8,128)(2,1)}, bf...) custom-call(s32[1]{0:T(128)} %bitcast.18.expert, ...), custom_call_target="tpu_custom_call" | custom-call | flops 21038628864 | bytes 43671552 | tf_op jit(solution)/shard_map/pallas_call | solution.py:505
  479.0 35.4 %shard_map.308 = (bf16[608,2176]{1,0:T(8,128)(2,1)}, bf16[608,2176]{1,0:T(8,128)(2,1)}, bf16[608,2048]{1,0:T(8,128)(2,1)}, bf16[608,2048]{1,0:T(8,128)(2,1)}, bf...) custom-call(s32[1]{0:T(128)} %bitcast.18.expert, ...), custom_call_target="tpu_custom_call", output_to_operand_aliasing={{4}: (8, {}), {5}: (9, {}), {6}: (10, {}), {7}: (11, {}), {... | custom-call | flops 21038628864 | bytes 43671552 | tf_op jit(solution)/shard_map/pallas_call | solution.py:505
  521.3 5.2 pad_maximum_fusion.2
  533.4 35.4 %shard_map.309 = (bf16[608,2176]{1,0:T(8,128)(2,1)}, bf16[608,2176]{1,0:T(8,128)(2,1)}, bf16[608,2048]{1,0:T(8,128)(2,1)}, bf16[608,2048]{1,0:T(8,128)(2,1)}, bf...) custom-call(s32[1]{0:T(128)} %bitcast.18.expert, ...), custom_call_target="tpu_custom_call", output_to_operand_aliasing={{4}: (8, {}), {5}: (9, {}), {6}: (10, {}), {7}: (11, {}), {... | custom-call | flops 21038628864 | bytes 43671552 | tf_op jit(solution)/shard_map/pallas_call | solution.py:505
  572.8 9.3 fusion.46
  582.2 7.5 fusion.43
  592.1 5.0 all-to-all-start.9
  597.3 35.3 %shard_map.310 = (bf16[608,2176]{1,0:T(8,128)(2,1)}, bf16[608,2176]{1,0:T(8,128)(2,1)}, bf16[608,2048]{1,0:T(8,128)(2,1)}, bf16[608,2048]{1,0:T(8,128)(2,1)}, bf...) custom-call(s32[1]{0:T(128)} %bitcast.18.expert, ...), custom_call_target="tpu_custom_call", output_to_operand_aliasing={{4}: (8, {}), {5}: (9, {}), {6}: (10, {}), {7}: (11, {}), {... | custom-call | flops 21038628864 | bytes 43671552 | tf_op jit(solution)/shard_map/pallas_call | solution.py:505
  632.6 5.4 multiply_convert_fusion
  638.0 7.5 fusion.41
  645.6 7.1 convolution_add_fusion
  656.9 5.1 add_convert_fusion.7
  683.5 25.8 %collective-permute-done.27 = bf16[320,2176]{1,0:T(8,128)(2,1)S(1)} collective-permute-done((bf16[320,2176]{1,0:T(8,128)(2,1)S(1)}, bf16[320,2176]{1,0:T(8,128)(2,1)S(1)}, u32[]{:S(2)}, u32[]{:S(2)}) %collective-permute-start.27) | collective-permute-done | bytes 1392672 | tf_op jit(solution)/shard_map/ppermute | solution.py:531
  709.4 6.4 fusion.153
  724.8 8.6 convolution_convert_fusion.6
  733.5 5.2 convolution_convert_fusion.5
  738.7 5.2 convolution_convert_fusion.7
  743.9 10.3 collective-permute-done.28
  760.5 5.6 fusion.16
  770.2 7.0 reshape.511
  781.7 7.3 pad_maximum_fusion
  789.0 10.5 collective-permute-done.30
  809.8 5.9 fusion.31
  836.8 31.0 %shard_map.311 = (bf16[320,2048]{1,0:T(8,128)(2,1)S(1)}, bf16[320,1024]{1,0:T(8,128)(2,1)S(1)}, bf16[1280,2048]{1,0:T(8,128)(2,1)}, bf16[1280,2048]{1,0:T(8,128)(2,1)}, f32[1280,128]{1,0:T(8,128)S(1)}) custom-call(s32[1]{0:T(128)} %bitcast.11.link, f32[320,3072]{1,0:T(8,128)} %fusion.149.nope.rope, f32[320,3072]{1,0:T(8,128)} %fusion.149.nope.rope, ...), custom_call_target="tpu_custom_call" | custom-call | flops 6643777536 | bytes 30801920 | tf_op jit(solution)/shard_map/pallas_call | solution.py:337
  872.6 5.4 fusion.32
  881.2 5.7 fusion.2
  886.9 5.0 add_convert_fusion.4
  891.9 13.7 %all-to-all-done.14 = bf16[4,152,2048]{2,1,0:T(8,128)(2,1)} async-done(((bf16[4,152,2048]{2,1,0:T(8,128)(2,1)}), bf16[4,152,2048]{2,1,0:T(8,128)(2,1)}, u32[]{:S(2)}, u32[]{:S(2)}) %all-to-all-start.14) | async-done | bytes 2490400 | tf_op jit(solution)/shard_map/all_to_all | solution.py:536
  905.7 5.1 collective-permute-done.35
  911.2 7.6 fusion.48
  918.8 6.8 fusion.23
  944.0 9.8 fusion.147
  953.8 22.7 %collective-permute-done.40 = bf16[320,576]{1,0:T(8,128)(2,1)} collective-permute-done((bf16[320,576]{1,0:T(8,128)(2,1)S(1)}, bf16[320,576]{1,0:T(8,128)(2,1)}, u32[]{:S(2)}, u32[]{:S(2)}) %collective-permute-start.40) | collective-permute-done | bytes 368672 | tf_op jit(solution)/shard_map/ppermute | solution.py:561
  990.4 7.9 convolution_convert_fusion.13
  1001.4 7.1 convolution_convert_fusion.14
  1026.9 11.8 fusion.35
  1039.8 5.4 fusion.30
  1052.5 6.1 fusion.60
  1063.8 21.2 %collective-permute-done.46 = bf16[256,512]{1,0:T(8,128)(2,1)} collective-permute-done((bf16[256,512]{1,0:T(8,128)(2,1)}, bf16[256,512]{1,0:T(8,128)(2,1)}, u32[]{:S(2)}, u32[]{:S(2)}) %collective-permute-start.46) | collective-permute-done | bytes 262176 | tf_op jit(solution)/shard_map/ppermute | solution.py:561
  1090.2 16.3 %collective-permute-start.49 = (bf16[64,3072]{1,0:T(8,128)(2,1)S(1)}, bf16[64,3072]{1,0:T(8,128)(2,1)S(1)}, u32[]{:S(2)}, u32[]{:S(2)}) collective-permute-start(bf16[64,3072]{1,0:T(8,128)(2,1)S(1)} %get-tuple-element.492), channel_id=1, source_target_pairs={{0,16},{8,24},{16,0},{24,8},{1,17},{9,25},{17,1},{25,9},{2,18},{10... | collective-permute-start | bytes 1179656 | tf_op jit(solution)/shard_map/ppermute | solution.py:561
  1112.5 23.1 %fusion.158 = f32[704,2048]{1,0:T(8,128)} fusion(bf16[4864,704]{1,0:T(8,128)(2,1)} %get-tuple-element.359, bf16[4864,2048]{1,0:T(8,128)(2,1)} %get-tuple-element.360), kind=kOutput, calls=%fused_computation.360 | convolution fusion | flops 14025752576 | bytes 32538624 | tf_op jit(solution)/shard_map/ra,rb->ab/dot_general | solution.py:1093
  1135.6 18.8 %fusion.159 = f32[2048,704]{0,1:T(8,128)} fusion(bf16[4864,2048]{1,0:T(8,128)(2,1)} %get-tuple-element.371, bf16[4864,704]{1,0:T(8,128)(2,1)S(1)} %bitcast.240), kind=kOutput, calls=%fused_computation.361 | convolution fusion | flops 14025752576 | bytes 32538624 | tf_op jit(solution)/shard_map/ra,rb->ab/dot_general | solution.py:1093
  1170.4 11.5 collective-permute-done.52
  1192.4 8.4 collective-permute-start.56
  1215.4 5.2 collective-permute-done.55
  1221.9 20.9 %convolution_bitcast_fusion.4 = f32[1,2048,704]{1,2,0:T(8,128)} fusion(bf16[4864,2048]{1,0:T(8,128)(2,1)} %get-tuple-element.371, bf16[4864,704]{1,0:T(8,128)(2,1)} %get-tuple-element.372), kind=kOutput, calls=%fused_computation.48 | convolution fusion | flops 14025752576 | bytes 32538624 | tf_op jit(solution)/shard_map/ra,rb->ab/dot_general | solution.py:1093
  1246.6 8.8 collective-permute-done.58
  (609 shorter events, 388.8 us)
Async XLA Ops:
  7.2 58.3 %all-gather.7.cloned.1.call-start = ((), (), s32[]{:S(2)}) async-start(), calls=%async_computation.20 | async-start | bytes 2764800 | tf_op jit(solution)/shard_map/all_gather | solution.py:552
  19.8 42.4 %all-to-all-start = ((bf16[4,152,2048]{2,1,0:T(8,128)(2,1)}), bf16[4,152,2048]{2,1,0:T(8,128)(2,1)}, u32[]{:S(2)}, u32[]{:S(2)}) async-start(bf16[4,152,2048]{2,1,0:T(8,128)(2,1)} %convolution_convert_fusion.12), calls=%async_computation | async-start | bytes 4980736 | tf_op jit(solution)/shard_map/all_to_all | solution.py:536
  25.1 139.5 %all-gather.9.cloned.1.call-start = ((), (), s32[]{:S(2)}) async-start(), calls=%async_computation.21 | async-start | bytes 14155776 | tf_op jit(solution)/shard_map/all_gather | solution.py:552
  68.9 60.9 %collective-permute-start.7 = (bf16[320,2048]{1,0:T(8,128)(2,1)}, bf16[320,2048]{1,0:T(8,128)(2,1)}, u32[]{:S(2)}, u32[]{:S(2)}) collective-permute-start(bf16[320,2048]{1,0:T(8,128)(2,1)} %collective-permute-done.3), channel_id=1, source_target_pairs={{0,8},{8,16},{16,24},{24,0},{1,9},{9,17},{17,25},{25,1},{2,10},{10... | collective-permute-start | bytes 3932168 | tf_op jit(solution)/shard_map/ppermute | solution.py:531
  70.5 59.4 %collective-permute-start.8 = (bf16[4,152,2048]{2,1,0:T(8,128)(2,1)}, bf16[4,152,2048]{2,1,0:T(8,128)(2,1)}, u32[]{:S(2)}, u32[]{:S(2)}) collective-permute-start(bf16[4,152,2048]{2,1,0:T(8,128)(2,1)} %all-to-all-done), channel_id=1, source_target_pairs={{0,1},{1,0},{2,3},{3,2},{4,5},{5,4},{6,7},{7,6},{8,9},{9,8},{10,11... | collective-permute-start | bytes 7471112 | tf_op jit(solution)/shard_map/ppermute | solution.py:548
  76.9 52.9 %all-to-all-start.1 = ((bf16[4,152,2048]{2,1,0:T(8,128)(2,1)}), bf16[4,152,2048]{2,1,0:T(8,128)(2,1)}, u32[]{:S(2)}, u32[]{:S(2)}) async-start(bf16[4,152,2048]{2,1,0:T(8,128)(2,1)} %convolution_convert_fusion.11), calls=%async_computation.1 | async-start | bytes 4980736 | tf_op jit(solution)/shard_map/all_to_all | solution.py:536
  81.6 140.5 %all-gather.11.cloned.1.call-start = ((), (), s32[]{:S(2)}) async-start(), calls=%async_computation.22 | async-start | bytes 4718592 | tf_op jit(solution)/shard_map/all_gather | solution.py:552
  88.0 40.3 %collective-permute-start.5 = (bf16[320,576]{1,0:T(8,128)(2,1)S(1)}, bf16[320,576]{1,0:T(8,128)(2,1)S(1)}, u32[]{:S(2)}, u32[]{:S(2)}) collective-permute-start(bf16[320,576]{1,0:T(8,128)(2,1)S(1)} %pad_maximum_fusion.7), channel_id=1, source_target_pairs={{0,16},{8,24},{16,0},{24,8},{1,17},{9,25},{17,1},{25,9},{2,18},{10... | collective-permute-start | bytes 1105928 | tf_op jit(solution)/shard_map/ppermute | solution.py:561
  89.6 38.8 %collective-permute-start.6 = (bf16[320,576]{1,0:T(8,128)(2,1)S(1)}, bf16[320,576]{1,0:T(8,128)(2,1)S(1)}, u32[]{:S(2)}, u32[]{:S(2)}) collective-permute-start(bf16[320,576]{1,0:T(8,128)(2,1)S(1)} %pad_maximum_fusion.7), channel_id=1, source_target_pairs={{0,24},{8,0},{16,8},{24,16},{1,25},{9,1},{17,9},{25,17},{2,26},{10... | collective-permute-start | bytes 1105928 | tf_op jit(solution)/shard_map/ppermute | solution.py:561
  164.6 45.5 %collective-permute-start.10 = (bf16[4,152,2048]{2,1,0:T(8,128)(2,1)}, bf16[4,152,2048]{2,1,0:T(8,128)(2,1)}, u32[]{:S(2)}, u32[]{:S(2)}) collective-permute-start(bf16[4,152,2048]{2,1,0:T(8,128)(2,1)} %all-to-all-done.1), channel_id=1, source_target_pairs={{0,1},{1,0},{2,3},{3,2},{4,5},{5,4},{6,7},{7,6},{8,9},{9,8},{10,11... | collective-permute-start | bytes 7471112 | tf_op jit(solution)/shard_map/ppermute | solution.py:548
  169.1 41.0 %all-to-all-start.2 = ((bf16[4,152,2048]{2,1,0:T(8,128)(2,1)}), bf16[4,152,2048]{2,1,0:T(8,128)(2,1)}, u32[]{:S(2)}, u32[]{:S(2)}) async-start(bf16[4,152,2048]{2,1,0:T(8,128)(2,1)} %convolution_convert_fusion.10), calls=%async_computation.2 | async-start | bytes 4980736 | tf_op jit(solution)/shard_map/all_to_all | solution.py:536
  173.8 127.5 %all-gather.13.cloned.1.call-start = ((), (), s32[]{:S(2)}) async-start(), calls=%async_computation.23 | async-start | bytes 9437184 | tf_op jit(solution)/shard_map/all_gather | solution.py:552
  238.1 61.3 %collective-permute-start.11 = (bf16[4,152,2048]{2,1,0:T(8,128)(2,1)}, bf16[4,152,2048]{2,1,0:T(8,128)(2,1)}, u32[]{:S(2)}, u32[]{:S(2)}) collective-permute-start(bf16[4,152,2048]{2,1,0:T(8,128)(2,1)} %all-to-all-done.2), channel_id=1, source_target_pairs={{0,1},{1,0},{2,3},{3,2},{4,5},{5,4},{6,7},{7,6},{8,9},{9,8},{10,11... | collective-permute-start | bytes 7471112 | tf_op jit(solution)/shard_map/ppermute | solution.py:548
  242.6 56.8 %all-to-all-start.3 = ((bf16[4,152,2048]{2,1,0:T(8,128)(2,1)}), bf16[4,152,2048]{2,1,0:T(8,128)(2,1)}, u32[]{:S(2)}, u32[]{:S(2)}) async-start(bf16[4,152,2048]{2,1,0:T(8,128)(2,1)} %convolution_convert_fusion.9), calls=%async_computation.3 | async-start | bytes 4980736 | tf_op jit(solution)/shard_map/all_to_all | solution.py:536
  247.2 137.6 %all-gather.15.cloned.1.call-start = ((), (), s32[]{:S(2)}) async-start(), calls=%async_computation.24 | async-start | bytes 3244032 | tf_op jit(solution)/shard_map/all_gather | solution.py:552
  311.6 50.2 %collective-permute-start.12 = (bf16[4,152,2048]{2,1,0:T(8,128)(2,1)}, bf16[4,152,2048]{2,1,0:T(8,128)(2,1)}, u32[]{:S(2)}, u32[]{:S(2)}) collective-permute-start(bf16[4,152,2048]{2,1,0:T(8,128)(2,1)} %all-to-all-done.3), channel_id=1, source_target_pairs={{0,1},{1,0},{2,3},{3,2},{4,5},{5,4},{6,7},{7,6},{8,9},{9,8},{10,11... | collective-permute-start | bytes 7471112 | tf_op jit(solution)/shard_map/ppermute | solution.py:548
  320.5 41.3 %all-to-all-start.4 = ((bf16[4,152,2176]{2,1,0:T(8,128)(2,1)}), bf16[4,152,2176]{2,1,0:T(8,128)(2,1)}, u32[]{:S(2)}, u32[]{:S(2)}) async-start(bf16[4,152,2176]{2,1,0:T(8,128)(2,1)} %convolution_convert_fusion.4), calls=%async_computation.4 | async-start | bytes 5292032 | tf_op jit(solution)/shard_map/all_to_all | solution.py:536
  325.0 195.7 %all-gather.17.cloned.1.call-start = ((), (), s32[]{:S(2)}) async-start(), calls=%async_computation.25 | async-start | bytes 6488064 | tf_op jit(solution)/shard_map/all_gather | solution.py:552
  361.8 56.5 %collective-permute-start.15 = (bf16[4,152,2176]{2,1,0:T(8,128)(2,1)}, bf16[4,152,2176]{2,1,0:T(8,128)(2,1)}, u32[]{:S(2)}, u32[]{:S(2)}) collective-permute-start(bf16[4,152,2176]{2,1,0:T(8,128)(2,1)} %all-to-all-done.4), channel_id=1, source_target_pairs={{0,1},{1,0},{2,3},{3,2},{4,5},{5,4},{6,7},{7,6},{8,9},{9,8},{10,11... | collective-permute-start | bytes 7938056 | tf_op jit(solution)/shard_map/ppermute | solution.py:548
  366.3 52.1 %all-to-all-start.5 = ((bf16[4,152,2176]{2,1,0:T(8,128)(2,1)}), bf16[4,152,2176]{2,1,0:T(8,128)(2,1)}, u32[]{:S(2)}, u32[]{:S(2)}) async-start(bf16[4,152,2176]{2,1,0:T(8,128)(2,1)} %convolution_convert_fusion.3), calls=%async_computation.5 | async-start | bytes 5292032 | tf_op jit(solution)/shard_map/all_to_all | solution.py:536
  370.9 47.4 %collective-permute-start.14 = (bf16[320,2176]{1,0:T(8,128)(2,1)}, bf16[320,2176]{1,0:T(8,128)(2,1)}, u32[]{:S(2)}, u32[]{:S(2)}) collective-permute-start(bf16[320,2176]{1,0:T(8,128)(2,1)} %collective-permute-done.13), channel_id=1, source_target_pairs={{0,8},{8,16},{16,24},{24,0},{1,9},{9,17},{17,25},{25,1},{2,10},{10... | collective-permute-start | bytes 4177928 | tf_op jit(solution)/shard_map/ppermute | solution.py:531
  418.3 44.8 %collective-permute-start.17 = (bf16[4,152,2176]{2,1,0:T(8,128)(2,1)}, bf16[4,152,2176]{2,1,0:T(8,128)(2,1)}, u32[]{:S(2)}, u32[]{:S(2)}) collective-permute-start(bf16[4,152,2176]{2,1,0:T(8,128)(2,1)} %all-to-all-done.5), channel_id=1, source_target_pairs={{0,1},{1,0},{2,3},{3,2},{4,5},{5,4},{6,7},{7,6},{8,9},{9,8},{10,11... | collective-permute-start | bytes 7938056 | tf_op jit(solution)/shard_map/ppermute | solution.py:548
  422.7 40.4 %all-to-all-start.6 = ((bf16[4,152,2176]{2,1,0:T(8,128)(2,1)}), bf16[4,152,2176]{2,1,0:T(8,128)(2,1)}, u32[]{:S(2)}, u32[]{:S(2)}) async-start(bf16[4,152,2176]{2,1,0:T(8,128)(2,1)} %convolution_convert_fusion.2), calls=%async_computation.6 | async-start | bytes 5292032 | tf_op jit(solution)/shard_map/all_to_all | solution.py:536
  427.5 35.6 %collective-permute-start.16 = (bf16[320,2176]{1,0:T(8,128)(2,1)}, bf16[320,2176]{1,0:T(8,128)(2,1)}, u32[]{:S(2)}, u32[]{:S(2)}) collective-permute-start(bf16[320,2176]{1,0:T(8,128)(2,1)} %collective-permute-done.14), channel_id=1, source_target_pairs={{0,8},{8,16},{16,24},{24,0},{1,9},{9,17},{17,25},{25,1},{2,10},{10... | collective-permute-start | bytes 4177928 | tf_op jit(solution)/shard_map/ppermute | solution.py:531
  463.1 53.7 %collective-permute-start.18 = (bf16[4,152,2176]{2,1,0:T(8,128)(2,1)}, bf16[4,152,2176]{2,1,0:T(8,128)(2,1)}, u32[]{:S(2)}, u32[]{:S(2)}) collective-permute-start(bf16[4,152,2176]{2,1,0:T(8,128)(2,1)} %bitcast.311), channel_id=1, source_target_pairs={{0,1},{1,0},{2,3},{3,2},{4,5},{5,4},{6,7},{7,6},{8,9},{9,8},{10,11... | collective-permute-start | bytes 7938056 | tf_op jit(solution)/shard_map/ppermute | solution.py:548
  463.5 57.2 %collective-permute-start.19 = (bf16[320,2048]{1,0:T(8,128)(2,1)S(1)}, bf16[320,2048]{1,0:T(8,128)(2,1)}, u32[]{:S(2)}, u32[]{:S(2)}) collective-permute-start(bf16[320,2048]{1,0:T(8,128)(2,1)S(1)} %get-tuple-element.218), channel_id=1, source_target_pairs={{0,8},{8,16},{16,24},{24,0},{1,9},{9,17},{17,25},{25,1},{2,10},{10... | collective-permute-start | bytes 3932168 | tf_op jit(solution)/shard_map/ppermute | solution.py:531
  473.9 46.8 %all-to-all-start.7 = ((bf16[4,152,2176]{2,1,0:T(8,128)(2,1)}), bf16[4,152,2176]{2,1,0:T(8,128)(2,1)}, u32[]{:S(2)}, u32[]{:S(2)}) async-start(bf16[4,152,2176]{2,1,0:T(8,128)(2,1)} %convolution_convert_fusion.1), calls=%async_computation.7 | async-start | bytes 5292032 | tf_op jit(solution)/shard_map/all_to_all | solution.py:536
  478.9 41.9 %collective-permute-start.20 = (bf16[4,152,2176]{2,1,0:T(8,128)(2,1)}, bf16[4,152,2176]{2,1,0:T(8,128)(2,1)}, u32[]{:S(2)}, u32[]{:S(2)}) collective-permute-start(bf16[4,152,2176]{2,1,0:T(8,128)(2,1)} %all-to-all-done.6), channel_id=1, source_target_pairs={{0,1},{1,0},{2,3},{3,2},{4,5},{5,4},{6,7},{7,6},{8,9},{9,8},{10,11... | collective-permute-start | bytes 7938056 | tf_op jit(solution)/shard_map/ppermute | solution.py:548
  520.8 48.0 %collective-permute-start.21 = (bf16[4,152,2176]{2,1,0:T(8,128)(2,1)}, bf16[4,152,2176]{2,1,0:T(8,128)(2,1)}, u32[]{:S(2)}, u32[]{:S(2)}) collective-permute-start(bf16[4,152,2176]{2,1,0:T(8,128)(2,1)} %bitcast.309), channel_id=1, source_target_pairs={{0,1},{1,0},{2,3},{3,2},{4,5},{5,4},{6,7},{7,6},{8,9},{9,8},{10,11... | collective-permute-start | bytes 7938056 | tf_op jit(solution)/shard_map/ppermute | solution.py:548
  526.6 46.2 %collective-permute-start.22 = (bf16[320,2048]{1,0:T(8,128)(2,1)}, bf16[320,2048]{1,0:T(8,128)(2,1)}, u32[]{:S(2)}, u32[]{:S(2)}) collective-permute-start(bf16[320,2048]{1,0:T(8,128)(2,1)} %collective-permute-done.19), channel_id=1, source_target_pairs={{0,8},{8,16},{16,24},{24,0},{1,9},{9,17},{17,25},{25,1},{2,10},{10... | collective-permute-start | bytes 3932168 | tf_op jit(solution)/shard_map/ppermute | solution.py:531
  528.1 44.8 %all-to-all-start.8 = ((bf16[4,152,2176]{2,1,0:T(8,128)(2,1)}), bf16[4,152,2176]{2,1,0:T(8,128)(2,1)}, u32[]{:S(2)}, u32[]{:S(2)}) async-start(bf16[4,152,2176]{2,1,0:T(8,128)(2,1)} %add_convert_fusion.3), calls=%async_computation.8 | async-start | bytes 5292032 | tf_op jit(solution)/shard_map/all_to_all | solution.py:536
  532.8 40.0 %collective-permute-start.23 = (bf16[4,152,2176]{2,1,0:T(8,128)(2,1)}, bf16[4,152,2176]{2,1,0:T(8,128)(2,1)}, u32[]{:S(2)}, u32[]{:S(2)}) collective-permute-start(bf16[4,152,2176]{2,1,0:T(8,128)(2,1)} %all-to-all-done.7), channel_id=1, source_target_pairs={{0,1},{1,0},{2,3},{3,2},{4,5},{5,4},{6,7},{7,6},{8,9},{9,8},{10,11... | collective-permute-start | bytes 7938056 | tf_op jit(solution)/shard_map/ppermute | solution.py:548
  532.9 124.1 %collective-permute-start.29 = (bf16[4,152,2048]{2,1,0:T(8,128)(2,1)}, bf16[4,152,2048]{2,1,0:T(8,128)(2,1)}, u32[]{:S(2)}, u32[]{:S(2)}) collective-permute-start(bf16[4,152,2048]{2,1,0:T(8,128)(2,1)} %bitcast.312), channel_id=1, source_target_pairs={{0,1},{1,0},{2,3},{3,2},{4,5},{5,4},{6,7},{7,6},{8,9},{9,8},{10,11... | collective-permute-start | bytes 7471112 | tf_op jit(solution)/shard_map/ppermute | solution.py:548
  589.7 62.9 %collective-permute-start.24 = (bf16[4,152,2176]{2,1,0:T(8,128)(2,1)}, bf16[4,152,2176]{2,1,0:T(8,128)(2,1)}, u32[]{:S(2)}, u32[]{:S(2)}) collective-permute-start(bf16[4,152,2176]{2,1,0:T(8,128)(2,1)} %bitcast.52), channel_id=1, source_target_pairs={{0,1},{1,0},{2,3},{3,2},{4,5},{5,4},{6,7},{7,6},{8,9},{9,8},{10,11... | collective-permute-start | bytes 7938056 | tf_op jit(solution)/shard_map/ppermute | solution.py:548
  589.8 66.7 %collective-permute-start.25 = (bf16[320,2048]{1,0:T(8,128)(2,1)}, bf16[320,2048]{1,0:T(8,128)(2,1)S(1)}, u32[]{:S(2)}, u32[]{:S(2)}) collective-permute-start(bf16[320,2048]{1,0:T(8,128)(2,1)} %collective-permute-done.22), channel_id=1, source_target_pairs={{0,8},{8,16},{16,24},{24,0},{1,9},{9,17},{17,25},{25,1},{2,10},{10... | collective-permute-start | bytes 3932168 | tf_op jit(solution)/shard_map/ppermute | solution.py:531
  592.1 64.5 %all-to-all-start.9 = ((bf16[4,152,2176]{2,1,0:T(8,128)(2,1)}), bf16[4,152,2176]{2,1,0:T(8,128)(2,1)}, u32[]{:S(2)}, u32[]{:S(2)}) async-start(bf16[4,152,2176]{2,1,0:T(8,128)(2,1)} %add_convert_fusion.2), calls=%async_computation.9 | async-start | bytes 5292032 | tf_op jit(solution)/shard_map/all_to_all | solution.py:536
  597.0 78.0 %collective-permute-start.31 = (bf16[4,152,2048]{2,1,0:T(8,128)(2,1)}, bf16[4,152,2048]{2,1,0:T(8,128)(2,1)}, u32[]{:S(2)}, u32[]{:S(2)}) collective-permute-start(bf16[4,152,2048]{2,1,0:T(8,128)(2,1)} %bitcast.313), channel_id=1, source_target_pairs={{0,1},{1,0},{2,3},{3,2},{4,5},{5,4},{6,7},{7,6},{8,9},{9,8},{10,11... | collective-permute-start | bytes 7471112 | tf_op jit(solution)/shard_map/ppermute | solution.py:548
  665.5 43.8 %all-to-all-start.10 = ((bf16[4,152,2176]{2,1,0:T(8,128)(2,1)}), bf16[4,152,2176]{2,1,0:T(8,128)(2,1)}, u32[]{:S(2)}, u32[]{:S(2)}) async-start(bf16[4,152,2176]{2,1,0:T(8,128)(2,1)} %add_convert_fusion.1), calls=%async_computation.10 | async-start | bytes 5292032 | tf_op jit(solution)/shard_map/all_to_all | solution.py:536
  674.3 35.1 %collective-permute-start.27 = (bf16[320,2176]{1,0:T(8,128)(2,1)S(1)}, bf16[320,2176]{1,0:T(8,128)(2,1)S(1)}, u32[]{:S(2)}, u32[]{:S(2)}) collective-permute-start(bf16[320,2176]{1,0:T(8,128)(2,1)S(1)} %fusion.18), channel_id=1, source_target_pairs={{0,8},{8,16},{16,24},{24,0},{1,9},{9,17},{17,25},{25,1},{2,10},{10... | collective-permute-start | bytes 4177928 | tf_op jit(solution)/shard_map/ppermute | solution.py:531
  679.3 86.8 %collective-permute-start.32 = (bf16[4,152,2048]{2,1,0:T(8,128)(2,1)}, bf16[4,152,2048]{2,1,0:T(8,128)(2,1)}, u32[]{:S(2)}, u32[]{:S(2)}) collective-permute-start(bf16[4,152,2048]{2,1,0:T(8,128)(2,1)} %bitcast.62), channel_id=1, source_target_pairs={{0,1},{1,0},{2,3},{3,2},{4,5},{5,4},{6,7},{7,6},{8,9},{9,8},{10,11... | collective-permute-start | bytes 7471112 | tf_op jit(solution)/shard_map/ppermute | solution.py:548
  720.0 35.9 %all-to-all-start.11 = ((bf16[4,152,2176]{2,1,0:T(8,128)(2,1)}), bf16[4,152,2176]{2,1,0:T(8,128)(2,1)}, u32[]{:S(2)}, u32[]{:S(2)}) async-start(bf16[4,152,2176]{2,1,0:T(8,128)(2,1)} %add_convert_fusion), calls=%async_computation.11 | async-start | bytes 5292032 | tf_op jit(solution)/shard_map/all_to_all | solution.py:536
  755.9 43.6 %all-to-all-start.12 = ((bf16[4,152,2048]{2,1,0:T(8,128)(2,1)}), bf16[4,152,2048]{2,1,0:T(8,128)(2,1)}, u32[]{:S(2)}, u32[]{:S(2)}) async-start(bf16[4,152,2048]{2,1,0:T(8,128)(2,1)} %add_convert_fusion.7), calls=%async_computation.12 | async-start | bytes 4980736 | tf_op jit(solution)/shard_map/all_to_all | solution.py:536
  760.4 150.3 %reduce-scatter.5.cloned.1.call-start = ((), (), s32[]{:S(2)}) async-start(), calls=%async_computation.26 | async-start | bytes 9732096 | tf_op jit(solution)/shard_map/reduce_scatter | solution.py:556
  805.0 62.8 %all-to-all-start.13 = ((bf16[4,152,2048]{2,1,0:T(8,128)(2,1)}), bf16[4,152,2048]{2,1,0:T(8,128)(2,1)}, u32[]{:S(2)}, u32[]{:S(2)}) async-start(bf16[4,152,2048]{2,1,0:T(8,128)(2,1)} %add_convert_fusion.6), calls=%async_computation.13 | async-start | bytes 4980736 | tf_op jit(solution)/shard_map/all_to_all | solution.py:536
  815.6 57.0 %collective-permute-start.34 = (bf16[320,2048]{1,0:T(8,128)(2,1)}, bf16[320,2048]{1,0:T(8,128)(2,1)}, u32[]{:S(2)}, u32[]{:S(2)}) collective-permute-start(bf16[320,2048]{1,0:T(8,128)(2,1)} %fusion.31), channel_id=1, source_target_pairs={{0,8},{8,16},{16,24},{24,0},{1,9},{9,17},{17,25},{25,1},{2,10},{10... | collective-permute-start | bytes 3932168 | tf_op jit(solution)/shard_map/ppermute | solution.py:531
  827.5 59.4 %collective-permute-start.33 = (bf16[4,152,2048]{2,1,0:T(8,128)(2,1)}, bf16[4,152,2048]{2,1,0:T(8,128)(2,1)}, u32[]{:S(2)}, u32[]{:S(2)}) collective-permute-start(bf16[4,152,2048]{2,1,0:T(8,128)(2,1)} %bitcast.34), channel_id=1, source_target_pairs={{0,1},{1,0},{2,3},{3,2},{4,5},{5,4},{6,7},{7,6},{8,9},{9,8},{10,11... | collective-permute-start | bytes 7471112 | tf_op jit(solution)/shard_map/ppermute | solution.py:548
  832.4 48.7 %collective-permute-start.38 = (bf16[320,512]{1,0:T(8,128)(2,1)}, bf16[320,512]{1,0:T(8,128)(2,1)}, u32[]{:S(2)}, u32[]{:S(2)}) collective-permute-start(bf16[320,512]{1,0:T(8,128)(2,1)} %get-tuple-element.496), channel_id=1, source_target_pairs={{0,24},{8,0},{16,8},{24,16},{1,25},{9,1},{17,9},{25,17},{2,26},{10... | collective-permute-start | bytes 983048 | tf_op jit(solution)/shard_map/ppermute | solution.py:561
  836.2 45.0 %collective-permute-start.37 = (bf16[320,512]{1,0:T(8,128)(2,1)}, bf16[320,512]{1,0:T(8,128)(2,1)}, u32[]{:S(2)}, u32[]{:S(2)}) collective-permute-start(bf16[320,512]{1,0:T(8,128)(2,1)} %get-tuple-element.497), channel_id=1, source_target_pairs={{0,16},{8,24},{16,0},{24,8},{1,17},{9,25},{17,1},{25,9},{2,18},{10... | collective-permute-start | bytes 983048 | tf_op jit(solution)/shard_map/ppermute | solution.py:561
  836.2 45.0 %collective-permute-start.36 = (bf16[320,512]{1,0:T(8,128)(2,1)}, bf16[320,512]{1,0:T(8,128)(2,1)}, u32[]{:S(2)}, u32[]{:S(2)}) collective-permute-start(bf16[320,512]{1,0:T(8,128)(2,1)} %get-tuple-element.498), channel_id=1, source_target_pairs={{0,8},{8,16},{16,24},{24,0},{1,9},{9,17},{17,25},{25,1},{2,10},{10... | collective-permute-start | bytes 983048 | tf_op jit(solution)/shard_map/ppermute | solution.py:561
  867.7 38.0 %all-to-all-start.14 = ((bf16[4,152,2048]{2,1,0:T(8,128)(2,1)}), bf16[4,152,2048]{2,1,0:T(8,128)(2,1)}, u32[]{:S(2)}, u32[]{:S(2)}) async-start(bf16[4,152,2048]{2,1,0:T(8,128)(2,1)} %add_convert_fusion.5), calls=%async_computation.14 | async-start | bytes 4980736 | tf_op jit(solution)/shard_map/all_to_all | solution.py:536
  872.3 106.6 %reduce-scatter.7.cloned.1.call-start = ((), (), s32[]{:S(2)}) async-start(), calls=%async_computation.27 | async-start | bytes 2359296 | tf_op jit(solution)/shard_map/reduce_scatter | solution.py:556
  932.7 46.2 %all-to-all-start.15 = ((bf16[4,152,2048]{2,1,0:T(8,128)(2,1)}), bf16[4,152,2048]{2,1,0:T(8,128)(2,1)}, u32[]{:S(2)}, u32[]{:S(2)}) async-start(bf16[4,152,2048]{2,1,0:T(8,128)(2,1)} %add_convert_fusion.4), calls=%async_computation.17 | async-start | bytes 4980736 | tf_op jit(solution)/shard_map/all_to_all | solution.py:536
  937.2 151.4 %reduce-scatter.9.cloned.1.call-start = ((), (), s32[]{:S(2)}) async-start(), calls=%async_computation.28 | async-start | bytes 14155776 | tf_op jit(solution)/shard_map/reduce_scatter | solution.py:556
  941.0 35.4 %collective-permute-start.40 = (bf16[320,576]{1,0:T(8,128)(2,1)S(1)}, bf16[320,576]{1,0:T(8,128)(2,1)}, u32[]{:S(2)}, u32[]{:S(2)}) collective-permute-start(bf16[320,576]{1,0:T(8,128)(2,1)S(1)} %get-tuple-element.487), channel_id=1, source_target_pairs={{0,16},{8,24},{16,0},{24,8},{1,17},{9,25},{17,1},{25,9},{2,18},{10... | collective-permute-start | bytes 1105928 | tf_op jit(solution)/shard_map/ppermute | solution.py:561
  978.9 212.3 %reduce-scatter.11.cloned.1.call-start = ((), (), s32[]{:S(2)}) async-start(), calls=%async_computation.29 | async-start | bytes 8257536 | tf_op jit(solution)/shard_map/reduce_scatter | solution.py:556
  1015.6 73.0 %collective-permute-start.43 = (bf16[256,2112]{0,1:T(8,128)(2,1)}, bf16[256,2112]{0,1:T(8,128)(2,1)}, u32[]{:S(2)}, u32[]{:S(2)}) collective-permute-start(bf16[256,2112]{0,1:T(8,128)(2,1)} %collective-permute-done.42), channel_id=1, source_target_pairs={{0,8},{8,16},{16,24},{24,0},{1,9},{9,17},{17,25},{25,1},{2,10},{10... | collective-permute-start | bytes 3244040 | tf_op jit(solution)/shard_map/ppermute | solution.py:531
  1015.6 46.4 %collective-permute-start.45 = (bf16[256,512]{1,0:T(8,128)(2,1)}, bf16[256,512]{1,0:T(8,128)(2,1)}, u32[]{:S(2)}, u32[]{:S(2)}) collective-permute-start(bf16[256,512]{1,0:T(8,128)(2,1)} %reduce-scatter.7.cloned.1.call-done), channel_id=1, source_target_pairs={{0,8},{8,16},{16,24},{24,0},{1,9},{9,17},{17,25},{25,1},{2,10},{10... | collective-permute-start | bytes 786440 | tf_op jit(solution)/shard_map/ppermute | solution.py:561
  1017.3 67.7 %collective-permute-start.46 = (bf16[256,512]{1,0:T(8,128)(2,1)}, bf16[256,512]{1,0:T(8,128)(2,1)}, u32[]{:S(2)}, u32[]{:S(2)}) collective-permute-start(bf16[256,512]{1,0:T(8,128)(2,1)} %reduce-scatter.7.cloned.1.call-done), channel_id=1, source_target_pairs={{0,16},{8,24},{16,0},{24,8},{1,17},{9,25},{17,1},{25,9},{2,18},{10... | collective-permute-start | bytes 786440 | tf_op jit(solution)/shard_map/ppermute | solution.py:561
  1020.0 66.8 %collective-permute-start.47 = (bf16[256,512]{1,0:T(8,128)(2,1)}, bf16[256,512]{1,0:T(8,128)(2,1)}, u32[]{:S(2)}, u32[]{:S(2)}) collective-permute-start(bf16[256,512]{1,0:T(8,128)(2,1)} %reduce-scatter.7.cloned.1.call-done), channel_id=1, source_target_pairs={{0,24},{8,0},{16,8},{24,16},{1,25},{9,1},{17,9},{25,17},{2,26},{10... | collective-permute-start | bytes 786440 | tf_op jit(solution)/shard_map/ppermute | solution.py:561
  1045.1 43.5 %collective-permute-start.44 = (bf16[320,2048]{1,0:T(8,128)(2,1)}, bf16[320,2048]{1,0:T(8,128)(2,1)}, u32[]{:S(2)}, u32[]{:S(2)}) collective-permute-start(bf16[320,2048]{1,0:T(8,128)(2,1)} %fusion.30), channel_id=1, source_target_pairs={{0,8},{8,16},{16,24},{24,0},{1,9},{9,17},{17,25},{25,1},{2,10},{10... | collective-permute-start | bytes 3932168 | tf_op jit(solution)/shard_map/ppermute | solution.py:531
  1090.1 65.6 %collective-permute-start.50 = (bf16[64,3072]{1,0:T(8,128)(2,1)S(1)}, bf16[64,3072]{1,0:T(8,128)(2,1)S(1)}, u32[]{:S(2)}, u32[]{:S(2)}) collective-permute-start(bf16[64,3072]{1,0:T(8,128)(2,1)S(1)} %get-tuple-element.491), channel_id=1, source_target_pairs={{0,24},{8,0},{16,8},{24,16},{1,25},{9,1},{17,9},{25,17},{2,26},{10... | collective-permute-start | bytes 1179656 | tf_op jit(solution)/shard_map/ppermute | solution.py:561
  1090.2 65.5 %collective-permute-start.49 = (bf16[64,3072]{1,0:T(8,128)(2,1)S(1)}, bf16[64,3072]{1,0:T(8,128)(2,1)S(1)}, u32[]{:S(2)}, u32[]{:S(2)}) collective-permute-start(bf16[64,3072]{1,0:T(8,128)(2,1)S(1)} %get-tuple-element.492), channel_id=1, source_target_pairs={{0,16},{8,24},{16,0},{24,8},{1,17},{9,25},{17,1},{25,9},{2,18},{10... | collective-permute-start | bytes 1179656 | tf_op jit(solution)/shard_map/ppermute | solution.py:561
  1106.5 49.2 %collective-permute-start.48 = (bf16[64,3072]{1,0:T(8,128)(2,1)S(1)}, bf16[64,3072]{1,0:T(8,128)(2,1)S(1)}, u32[]{:S(2)}, u32[]{:S(2)}) collective-permute-start(bf16[64,3072]{1,0:T(8,128)(2,1)S(1)} %get-tuple-element.490), channel_id=1, source_target_pairs={{0,8},{8,16},{16,24},{24,0},{1,9},{9,17},{17,25},{25,1},{2,10},{10... | collective-permute-start | bytes 1179656 | tf_op jit(solution)/shard_map/ppermute | solution.py:561
  1108.5 73.5 %collective-permute-start.60 = (bf16[256,2112]{0,1:T(8,128)(2,1)}, bf16[256,2112]{0,1:T(8,128)(2,1)S(1)}, u32[]{:S(2)}, u32[]{:S(2)}) collective-permute-start(bf16[256,2112]{0,1:T(8,128)(2,1)} %collective-permute-done.43), channel_id=1, source_target_pairs={{0,8},{8,16},{16,24},{24,0},{1,9},{9,17},{17,25},{25,1},{2,10},{10... | collective-permute-start | bytes 3244040 | tf_op jit(solution)/shard_map/ppermute | solution.py:531
  (151 other events, 2997.9 us)
Sparse Core Ops, SparseCore 0:
  13.9 51.5 all-gather.6
  67.4 97.0 all-gather.8
  166.4 55.6 all-gather.10
  223.8 77.4 all-gather.12
  303.6 50.6 all-gather.14
  361.9 65.1 all-gather.16
  799.7 97.6 reduce-scatter.4
  918.9 56.6 reduce-scatter.6
  979.1 92.0 reduce-scatter.8
  1088.8 82.1 reduce-scatter.10
